TPU v7x, 32 devices: a whole 2x2x4 slice. The times are simulated.
32 devices in a mesh: shard: 4 (over y, x), replica: 8 (over z, core).
Axes of the slice: x: 2, y: 2, z: 4, core: 2. Of those that a mesh axis runs over, the one named last changes fastest.
Arguments:
- tokens: bfloat16 [2, 8, 1024, 2048], P(None, 'replica', 'shard'), may hold values from -6 to 6
- gain_attn: bfloat16 [2048], P('shard'), may hold values from 0.099609375 to 1.8984375
- w_query: bfloat16 [2048, 2048], P('shard'), may hold values from -0.5 to 0.5
- w_key: bfloat16 [512, 2048], P('shard'), may hold values from -0.5 to 0.5
- w_value: bfloat16 [512, 2048], P('shard'), may hold values from -0.125 to 0.125
- w_out: bfloat16 [2048, 2048], P('shard'), may hold values from -2 to 2
- gain_ff: bfloat16 [2048], P('shard'), may hold values from 0.099609375 to 1.8984375
- w_gate: bfloat16 [8192, 2048], P('shard'), may hold values from -0.125 to 0.125
- w_up: bfloat16 [8192, 2048], P('shard'), may hold values from -0.125 to 0.125
- w_down: bfloat16 [8192, 2048], P('shard'), may hold values from -0.25 to 0.25
- cotangent: bfloat16 [2, 8, 1024, 2048], P(None, 'replica', 'shard'), may hold values from -6 to 6
- segment_ids: int32 [2, 8, 1024], P(None, 'replica', 'shard'), may hold values from 0 to 12, as said below
- parents: int32 [2, 8, 13], P(None, 'replica'), may hold values from 0 to 4, as said below
Outputs:
- output: bfloat16 [2, 8, 1024, 2048], P(None, 'replica', 'shard')
- input_grad: float32 [2, 8, 1024, 2048], P(None, 'replica', 'shard')
- grad_gain_attn: float32 [2048], P('shard')
- grad_query: float32 [2048, 2048], P('shard')
- grad_key: float32 [512, 2048], P('shard')
- grad_value: float32 [512, 2048], P('shard')
- grad_out: float32 [2048, 2048], P('shard')
- grad_gain_ff: float32 [2048], P('shard')
- grad_gate: float32 [8192, 2048], P('shard')
- grad_up: float32 [8192, 2048], P('shard')
- grad_down: float32 [8192, 2048], P('shard')
Inputs may be any that keep to these rules, and one draw needn't show every extreme that they name: `segment_ids`: segment numbers never fall along a tree, begin at 0 (the trunk), and each of the 13 segments holds one token or more. `parents`: segment 0 is its own parent; segments 1 to 4 are children of segment 0; each later segment is a child of one of segments 1 to 4, and every one of those has a child.
All inputs are finite; a program needn't handle non-finite values.
Results may differ from a plain program's by a relative error of at most 0.02.
Values may be sent and summed in bfloat16 or wider, within the bound.
A program may use at most 384 MiB of HBM per device.

v0:
```python
import math

import jax
import jax.numpy as jnp
from jax import lax
from jax.sharding import PartitionSpec as P

HEADS = 32
KV_HEADS = 8
HEAD_DIM = 64


EPSILON = 1e-05
RESIDUAL = 0.22
ATTN_SCALE = 0.015625
ROPE_BASE = 10000000.0
NEGATIVE = -1e30


def tree_layout(segment_row, parent_row):
    seg_numbers = jnp.arange(parent_row.shape[0], dtype=jnp.int32)
    member = (segment_row[:, None] == seg_numbers[None, :]).astype(jnp.int32)
    lengths = jnp.sum(member, axis=0)
    starts = jnp.cumsum(lengths) - lengths
    parent_hit = parent_row[:, None] == seg_numbers[None, :]
    grandparent = jnp.sum(jnp.where(parent_hit, parent_row[None, :], 0), axis=1)
    itself = seg_numbers[:, None] == seg_numbers[None, :]
    related = itself | parent_hit | (grandparent[:, None] == seg_numbers[None, :])
    before = jnp.sum(jnp.where(related & jnp.logical_not(itself), lengths[None, :], 0), axis=1)
    position = jnp.arange(segment_row.shape[0], dtype=jnp.int32) + jnp.dot(member, before - starts)
    return (position, related.astype(jnp.int32), member)


def rotate(values, position, sign):
    half = values.shape[-1] // 2
    fraction = jnp.arange(half, dtype=jnp.float32) * (2.0 / values.shape[-1])
    freq = jnp.exp(-math.log(ROPE_BASE) * fraction)
    angle = position.astype(jnp.float32)[:, None] * freq[None, :]
    cosine = jnp.concatenate([jnp.cos(angle), jnp.cos(angle)], axis=-1)[:, None, :]
    sine = jnp.concatenate([jnp.sin(angle), jnp.sin(angle)], axis=-1)[:, None, :]
    turned = jnp.concatenate([-values[..., half:], values[..., :half]], axis=-1)
    return values * cosine + sign * turned * sine


def contract_last(left, right):
    return lax.dot_general(
        left, right, (((1,), (1,)), ((), ())), preferred_element_type=jnp.float32
    )


def contract_first(left, right):
    return lax.dot_general(
        left, right, (((0,), (0,)), ((), ())), preferred_element_type=jnp.float32
    )


def norm_back(values, scale, gain, grad_in):
    scaled = values * scale
    weighted = grad_in * gain
    back = scale * (weighted - scaled * jnp.mean(weighted * scaled, axis=-1, keepdims=True))
    return (back, jnp.sum(grad_in * scaled, axis=0))


def block_mask(member, related, begin, block_rows):
    member_block = lax.slice_in_dim(member, begin, begin + block_rows, axis=0)
    link = jnp.dot(jnp.dot(member_block, related), member.T)
    query_index = begin + jnp.arange(block_rows, dtype=jnp.int32)
    key_index = jnp.arange(member.shape[0], dtype=jnp.int32)
    return ((link > 0) & (key_index[None, :] <= query_index[:, None]))[None, None]


def body(
    tokens,
    gain_attn,
    w_query,
    w_key,
    w_value,
    w_out,
    gain_ff,
    w_gate,
    w_up,
    w_down,
    cotangent,
    segment_ids,
    parents,
):
    width = tokens.shape[3]
    group = HEADS // KV_HEADS
    all_segments = lax.all_gather(segment_ids, "shard", axis=2, tiled=True)
    tree_rows = all_segments.shape[2]
    block_rows = min(512, tree_rows)
    sums = [
        jnp.zeros(w.shape, jnp.float32)
        for w in (gain_attn, w_query, w_key, w_value, w_out, gain_ff, w_gate, w_up, w_down)
    ]
    gains = (
        lax.all_gather(gain_attn, "shard", axis=0, tiled=True),
        lax.all_gather(gain_ff, "shard", axis=0, tiled=True),
    )
    gain_first = gains[0].astype(jnp.float32)
    gain_second = gains[1].astype(jnp.float32)
    gain_attn_acc = jnp.zeros((width,), jnp.float32)
    gain_ff_acc = jnp.zeros((width,), jnp.float32)
    results = []
    input_grads = []
    for batch_index in range(tokens.shape[0]):
        inputs = tokens[batch_index, 0].astype(jnp.float32)
        position_all, related, member = tree_layout(
            all_segments[batch_index, 0], parents[batch_index, 0]
        )
        scale_first = lax.rsqrt(jnp.mean(inputs * inputs, axis=-1, keepdims=True) + EPSILON)
        normed = (inputs * scale_first * gain_first).astype(jnp.bfloat16)
        normed_all = lax.all_gather(normed, "shard", axis=0, tiled=True)
        own_heads = w_key.shape[0] // HEAD_DIM
        query_h = rotate(
            contract_last(normed_all, w_query).reshape(tree_rows, own_heads * group, HEAD_DIM),
            position_all,
            1.0,
        )
        query_h = query_h.astype(jnp.bfloat16).reshape(tree_rows, own_heads, group, HEAD_DIM)
        key_h = rotate(
            contract_last(normed_all, w_key).reshape(tree_rows, own_heads, HEAD_DIM),
            position_all,
            1.0,
        ).astype(jnp.bfloat16)
        value_h = (
            contract_last(normed_all, w_value)
            .astype(jnp.bfloat16)
            .reshape(tree_rows, own_heads, HEAD_DIM)
        )
        masks = []
        log_totals = []
        pieces = []
        for begin in range(0, tree_rows, block_rows):
            allowed_blk = block_mask(member, related, begin, block_rows)
            query_blk = query_h[begin : begin + block_rows]
            scores = (
                jnp.einsum("qhgd,khd->hgqk", query_blk, key_h, preferred_element_type=jnp.float32)
                * ATTN_SCALE
            )
            masked = jnp.where(allowed_blk, scores, NEGATIVE)
            top = jnp.max(masked, axis=-1, keepdims=True)
            expo = jnp.exp(masked - top)
            total = jnp.sum(expo, axis=-1, keepdims=True)
            masks.append(allowed_blk)
            log_totals.append(top + jnp.log(total))
            probs_low = (expo / total).astype(jnp.bfloat16)
            mixed = jnp.einsum(
                "hgqk,khd->qhgd", probs_low, value_h, preferred_element_type=jnp.float32
            )
            pieces.append(mixed.reshape(block_rows, own_heads * group * HEAD_DIM))
        attended_h = jnp.concatenate(pieces, axis=0).astype(jnp.bfloat16)
        attn_branch = lax.psum_scatter(
            jnp.dot(attended_h, w_out, preferred_element_type=jnp.float32),
            "shard",
            scatter_dimension=0,
            tiled=True,
        )
        middle = inputs + RESIDUAL * attn_branch
        scale_second = lax.rsqrt(jnp.mean(middle * middle, axis=-1, keepdims=True) + EPSILON)
        normed_ff = (middle * scale_second * gain_second).astype(jnp.bfloat16)
        rows_all = lax.all_gather(normed_ff, "shard", axis=0, tiled=True)
        gate = contract_last(rows_all, w_gate)
        upper = contract_last(rows_all, w_up)
        hidden = (gate * jax.nn.sigmoid(gate) * upper).astype(jnp.bfloat16)
        down_branch = lax.psum_scatter(
            jnp.dot(hidden, w_down, preferred_element_type=jnp.float32).astype(jnp.bfloat16),
            "shard",
            scatter_dimension=0,
            tiled=True,
        ).astype(jnp.float32)
        results.append((middle + RESIDUAL * down_branch).astype(jnp.bfloat16))
        cot = cotangent[batch_index, 0].astype(jnp.float32)
        down_grad = (RESIDUAL * cot).astype(jnp.bfloat16)
        cot_all = lax.all_gather(down_grad, "shard", axis=0, tiled=True)
        gate = contract_last(rows_all, w_gate)
        upper = contract_last(rows_all, w_up)
        sigma = jax.nn.sigmoid(gate)
        hidden = (gate * sigma * upper).astype(jnp.bfloat16)
        hidden_grad = contract_last(cot_all, w_down)
        gate_grad = (hidden_grad * upper * sigma * (1.0 + gate * (1.0 - sigma))).astype(
            jnp.bfloat16
        )
        up_grad = (hidden_grad * gate * sigma).astype(jnp.bfloat16)
        sums[6] = sums[6] + contract_first(gate_grad, rows_all)
        sums[7] = sums[7] + contract_first(up_grad, rows_all)
        sums[8] = sums[8] + contract_first(hidden, cot_all)
        ff_normed_grad = lax.psum_scatter(
            jnp.dot(gate_grad, w_gate, preferred_element_type=jnp.float32)
            + jnp.dot(up_grad, w_up, preferred_element_type=jnp.float32),
            "shard",
            scatter_dimension=0,
            tiled=True,
        )
        middle_back, gain_ff_term = norm_back(middle, scale_second, gain_second, ff_normed_grad)
        middle_grad = cot + middle_back
        out_grad = (RESIDUAL * middle_grad).astype(jnp.bfloat16)
        out_all = lax.all_gather(out_grad, "shard", axis=0, tiled=True)
        sums[4] = sums[4] + contract_first(attended_h, out_all)
        attended_grad = (
            contract_last(out_all, w_out)
            .astype(jnp.bfloat16)
            .reshape(tree_rows, own_heads, group, HEAD_DIM)
        )
        value_term = jnp.zeros((tree_rows, own_heads, HEAD_DIM), jnp.float32)
        key_term = jnp.zeros((tree_rows, own_heads, HEAD_DIM), jnp.float32)
        query_parts = []
        for block_index, begin in enumerate(range(0, tree_rows, block_rows)):
            query_blk = query_h[begin : begin + block_rows]
            grad_blk = attended_grad[begin : begin + block_rows]
            scores = (
                jnp.einsum("qhgd,khd->hgqk", query_blk, key_h, preferred_element_type=jnp.float32)
                * ATTN_SCALE
            )
            probs = jnp.exp(
                jnp.where(masks[block_index], scores, NEGATIVE) - log_totals[block_index]
            )
            probs_low = probs.astype(jnp.bfloat16)
            probs_grad = jnp.einsum(
                "qhgd,khd->hgqk", grad_blk, value_h, preferred_element_type=jnp.float32
            )
            value_term = value_term + jnp.einsum(
                "hgqk,qhgd->khd", probs_low, grad_blk, preferred_element_type=jnp.float32
            )
            score_grad = (
                probs * (probs_grad - jnp.sum(probs_grad * probs, axis=-1, keepdims=True))
            ).astype(jnp.bfloat16)
            query_parts.append(
                jnp.einsum("hgqk,khd->qhgd", score_grad, key_h, preferred_element_type=jnp.float32)
                * ATTN_SCALE
            )
            key_term = (
                key_term
                + jnp.einsum(
                    "hgqk,qhgd->khd", score_grad, query_blk, preferred_element_type=jnp.float32
                )
                * ATTN_SCALE
            )
        query_grad = jnp.concatenate(query_parts, axis=0)
        query_raw = rotate(
            query_grad.reshape(tree_rows, own_heads * group, HEAD_DIM), position_all, -1.0
        )
        query_raw = query_raw.reshape(tree_rows, own_heads * group * HEAD_DIM).astype(jnp.bfloat16)
        key_raw = (
            rotate(key_term, position_all, -1.0)
            .reshape(tree_rows, own_heads * HEAD_DIM)
            .astype(jnp.bfloat16)
        )
        value_raw = value_term.reshape(tree_rows, own_heads * HEAD_DIM).astype(jnp.bfloat16)
        sums[1] = sums[1] + contract_first(query_raw, normed_all)
        sums[2] = sums[2] + contract_first(key_raw, normed_all)
        sums[3] = sums[3] + contract_first(value_raw, normed_all)
        normed_grad = lax.psum_scatter(
            (
                jnp.dot(query_raw, w_query, preferred_element_type=jnp.float32)
                + jnp.dot(key_raw, w_key, preferred_element_type=jnp.float32)
                + jnp.dot(value_raw, w_value, preferred_element_type=jnp.float32)
            ).astype(jnp.bfloat16),
            "shard",
            scatter_dimension=0,
            tiled=True,
        ).astype(jnp.float32)
        input_back, gain_attn_term = norm_back(inputs, scale_first, gain_first, normed_grad)
        input_grads.append(middle_grad + input_back)
        gain_attn_acc = gain_attn_acc + gain_attn_term
        gain_ff_acc = gain_ff_acc + gain_ff_term
    owned_gains = (
        lax.psum_scatter(gain_attn_acc, "shard", scatter_dimension=0, tiled=True),
        lax.psum_scatter(gain_ff_acc, "shard", scatter_dimension=0, tiled=True),
    )
    sums[0] = owned_gains[0]
    sums[5] = owned_gains[1]
    totals = (
        lax.psum(sums[0].astype(jnp.bfloat16), "replica").astype(jnp.float32),
        lax.psum(sums[1].astype(jnp.bfloat16), "replica").astype(jnp.float32),
        lax.psum(sums[2].astype(jnp.bfloat16), "replica").astype(jnp.float32),
        lax.psum(sums[3].astype(jnp.bfloat16), "replica").astype(jnp.float32),
        lax.psum(sums[4].astype(jnp.bfloat16), "replica").astype(jnp.float32),
        lax.psum(sums[5].astype(jnp.bfloat16), "replica").astype(jnp.float32),
        lax.psum(sums[6].astype(jnp.bfloat16), "replica").astype(jnp.float32),
        lax.psum(sums[7].astype(jnp.bfloat16), "replica").astype(jnp.float32),
        lax.psum(sums[8].astype(jnp.bfloat16), "replica").astype(jnp.float32),
    )
    output = jnp.stack(results)[:, None]
    input_grad = jnp.stack(input_grads)[:, None]
    return (
        output,
        input_grad,
        totals[0],
        totals[1],
        totals[2],
        totals[3],
        totals[4],
        totals[5],
        totals[6],
        totals[7],
        totals[8],
    )


def solution(mesh):
    in_specs = (
        P(None, "replica", "shard", None),
        P("shard"),
        P("shard", None),
        P("shard", None),
        P("shard", None),
        P("shard", None),
        P("shard"),
        P("shard", None),
        P("shard", None),
        P("shard", None),
        P(None, "replica", "shard", None),
        P(None, "replica", "shard"),
        P(None, "replica", None),
    )
    out_specs = (
        P(None, "replica", "shard", None),
        P(None, "replica", "shard", None),
        P("shard"),
        P("shard", None),
        P("shard", None),
        P("shard", None),
        P("shard", None),
        P("shard"),
        P("shard", None),
        P("shard", None),
        P("shard", None),
    )
    return jax.shard_map(body, mesh=mesh, in_specs=in_specs, out_specs=out_specs, check_vma=False)
```

profile of v0, /device:TPU:0, one launch (start us, length us, event | category | flops | bytes accessed | tf_op | source)
XLA Modules:
  0.0 1901.9 jit_solution(17890299135495085045)
XLA Ops:
  44.1 32.7 %all-gather.15.cloned.1.call-done = bf16[1024,2048]{1,0:T(8,128)(2,1)} async-done(((bf16[256,2048]{1,0:T(8,128)(2,1)}), bf16[1024,2048]{1,0:T(8,128)(2,1)}) %all-gather.15.cloned.1.call-update) | async-done | bytes 4194320 | tf_op jit(solution)/shard_map/all_gather | solution.py:113
  229.1 89.6 %reduce-scatter.9.cloned.1.call-done = f32[256,2048]{1,0:T(8,128)} async-done(((f32[1024,2048]{1,0:T(8,128)}), f32[256,2048]{1,0:T(8,128)}) %reduce-scatter.9.cloned.1.call-update) | async-done | bytes 2097168 | tf_op jit(solution)/shard_map/reduce_scatter | solution.py:153
  329.8 49.3 %all-gather.13.cloned.1.call-done = bf16[1024,2048]{1,0:T(8,128)(2,1)} async-done(((bf16[256,2048]{1,0:T(8,128)(2,1)}), bf16[1024,2048]{1,0:T(8,128)(2,1)}) %all-gather.13.cloned.1.call-update) | async-done | bytes 4194320 | tf_op jit(solution)/shard_map/all_gather | solution.py:162
  379.1 15.9 fusion.186
  408.2 25.9 %all-gather.19.cloned.1.call-done = bf16[1024,2048]{1,0:T(8,128)(2,1)} async-done(((bf16[256,2048]{1,0:T(8,128)(2,1)}), bf16[1024,2048]{1,0:T(8,128)(2,1)}) %all-gather.19.cloned.1.call-update) | async-done | bytes 4194320 | tf_op jit(solution)/shard_map/all_gather | solution.py:175
  434.1 22.0 %multiply_convert_fusion.2 = (bf16[1024,2048]{1,0:T(8,128)(2,1)}, bf16[1024,2048]{1,0:T(8,128)(2,1)}, bf16[1024,2048]{1,0:T(8,128)(2,1)}) fusion(f32[1024,2048]{1,0:T(8,128)} %fusion.185, f32[1024,2048]{1,0:T(8,128)} %fusion.186, bf16[1024,2048]{1,0:T(8,128)(2,1)} %all-gather.19.cloned.1.call-done, bf16[2048,2048]{1,0:T(8,128)(2,1)} %param.22), kind=kOutput, calls=%fused_computation.59 | convolution fusion | flops 8623489024 | bytes 41943040 | tf_op jit(solution)/shard_map/dot_general | solution.py:46
  482.2 86.3 %reduce-scatter.17.cloned.1.call-done = f32[256,2048]{1,0:T(8,128)} async-done(((f32[1024,2048]{1,0:T(8,128)}), f32[256,2048]{1,0:T(8,128)}) %reduce-scatter.17.cloned.1.call-update) | async-done | bytes 2097168 | tf_op jit(solution)/shard_map/reduce_scatter | solution.py:188
  574.4 52.1 %all-gather.17.cloned.1.call-done = bf16[1024,2048]{1,0:T(8,128)(2,1)} async-done(((bf16[256,2048]{1,0:T(8,128)(2,1)}), bf16[1024,2048]{1,0:T(8,128)(2,1)}) %all-gather.17.cloned.1.call-update) | async-done | bytes 4194320 | tf_op jit(solution)/shard_map/all_gather | solution.py:162
  626.4 15.5 fusion.190
  655.1 26.0 %all-gather.23.cloned.1.call-done = bf16[1024,2048]{1,0:T(8,128)(2,1)} async-done(((bf16[256,2048]{1,0:T(8,128)(2,1)}), bf16[1024,2048]{1,0:T(8,128)(2,1)}) %all-gather.23.cloned.1.call-update) | async-done | bytes 4194320 | tf_op jit(solution)/shard_map/all_gather | solution.py:175
  681.2 22.3 %multiply_convert_fusion = (bf16[1024,2048]{1,0:T(8,128)(2,1)}, bf16[1024,2048]{1,0:T(8,128)(2,1)}, bf16[1024,2048]{1,0:T(8,128)(2,1)}) fusion(f32[1024,2048]{1,0:T(8,128)} %fusion.189, f32[1024,2048]{1,0:T(8,128)} %fusion.190, bf16[1024,2048]{1,0:T(8,128)(2,1)} %all-gather.23.cloned.1.call-done, bf16[2048,2048]{1,0:T(8,128)(2,1)} %param.22), kind=kOutput, calls=%fused_computation.54 | convolution fusion | flops 8623489024 | bytes 41943040 | tf_op jit(solution)/shard_map/dot_general | solution.py:46
  729.4 14.0 convolution_convert_fusion
  743.5 72.4 %reduce-scatter.21.cloned.1.call-done = f32[256,2048]{1,0:T(8,128)} async-done(((f32[1024,2048]{1,0:T(8,128)}), f32[256,2048]{1,0:T(8,128)}) %reduce-scatter.21.cloned.1.call-update) | async-done | bytes 2097168 | tf_op jit(solution)/shard_map/reduce_scatter | solution.py:188
  819.4 52.2 %reduce-scatter.15.cloned.1.call-done = bf16[256,2048]{1,0:T(8,128)(2,1)} async-done(((bf16[1024,2048]{1,0:T(8,128)(2,1)}), bf16[256,2048]{1,0:T(8,128)(2,1)}) %reduce-scatter.15.cloned.1.call-update) | async-done | bytes 1048592 | tf_op jit(solution)/shard_map/reduce_scatter | solution.py:166
  878.8 52.0 %all-gather.21.cloned.1.call-done = bf16[1024,2048]{1,0:T(8,128)(2,1)} async-done(((bf16[256,2048]{1,0:T(8,128)(2,1)}), bf16[1024,2048]{1,0:T(8,128)(2,1)}) %all-gather.21.cloned.1.call-update) | async-done | bytes 4194320 | tf_op jit(solution)/shard_map/all_gather | solution.py:198
  1030.9 15.0 fusion
  1135.3 14.2 convolution_convert_fusion.1
  1149.6 15.8 fusion.202
  1188.9 16.2 add_convert_fusion
  1205.1 16.1 add_convert_fusion.1
  1221.2 16.3 add_convert_fusion.2
  1261.2 15.1 all-reduce.2
  1276.4 14.6 all-reduce.3
  1302.7 547.4 %all-reduce.7.cloned.1.call-done = (bf16[512,2048]{1,0:T(8,128)(2,1)}, bf16[128,2048]{1,0:T(8,128)(2,1)}, bf16[128,2048]{1,0:T(8,128)(2,1)}, bf16[512,2048]{1,0:...) async-done(((bf16[512,2048]{1,0:T(8,128)(2,1)}, bf16[128,2048]{1,0:T(8,128)(2,1)}, bf16[128,2048]{1,0:T(8,128)(2,1)}, ...) | async-done | bytes 30408720 | tf_op jit(solution)/shard_map/psum | solution.py:275
  (520 shorter events, 586.0 us)
Async XLA Ops:
  7.2 129.6 %copy-start = (bf16[512,2048]{1,0:T(8,128)(2,1)S(1)}, bf16[512,2048]{1,0:T(8,128)(2,1)}, u32[]{:S(2)}) copy-start(bf16[512,2048]{1,0:T(8,128)(2,1)} %param.18) | copy-start | bytes 6291460
  7.2 69.6 %all-gather.15.cloned.1.call-start = ((), (), s32[]{:S(2)}) async-start(), calls=%async_computation.12 | async-start | bytes 5242880 | tf_op jit(solution)/shard_map/all_gather | solution.py:113
  23.7 131.5 %all-gather.11.cloned.1.call-start = ((), (), s32[]{:S(2)}) async-start(), calls=%async_computation.8 | async-start | bytes 5242880 | tf_op jit(solution)/shard_map/all_gather | solution.py:113
  24.4 204.7 %reduce-scatter.13.cloned.1.call-start = ((), (), s32[]{:S(2)}) async-start(), calls=%async_computation.13 | async-start | bytes 10485760 | tf_op jit(solution)/shard_map/reduce_scatter | solution.py:153
  142.5 176.3 %reduce-scatter.9.cloned.1.call-start = ((), (), s32[]{:S(2)}) async-start(), calls=%async_computation.9 | async-start | bytes 10485760 | tf_op jit(solution)/shard_map/reduce_scatter | solution.py:153
  217.2 161.8 %all-gather.13.cloned.1.call-start = ((), (), s32[]{:S(2)}) async-start(), calls=%async_computation.10 | async-start | bytes 5242880 | tf_op jit(solution)/shard_map/all_gather | solution.py:162
  225.9 645.8 %copy-start.68 = (f32[4,1,512]{2,1,0:T(1,128)}, f32[4,1,512]{2,1,0:T(1,128)S(1)}, u32[]{:S(2)}) copy-start(f32[4,1,512]{2,1,0:T(1,128)S(1)} %convert_element_type.369) | copy-start | bytes 24580
  323.7 548.0 %copy-start.91 = (f32[256]{0:T(256)}, f32[256]{0:T(256)S(1)}, u32[]{:S(2)}) copy-start(f32[256]{0:T(256)S(1)} %add_rsqrt_fusion.2) | copy-start | bytes 3076
  326.2 107.8 %all-gather.19.cloned.1.call-start = ((), (), s32[]{:S(2)}) async-start(), calls=%async_computation.16 | async-start | bytes 5242880 | tf_op jit(solution)/shard_map/all_gather | solution.py:175
  329.7 238.8 %reduce-scatter.17.cloned.1.call-start = ((), (), s32[]{:S(2)}) async-start(), calls=%async_computation.17 | async-start | bytes 10485760 | tf_op jit(solution)/shard_map/reduce_scatter | solution.py:188
  481.9 144.6 %all-gather.17.cloned.1.call-start = ((), (), s32[]{:S(2)}) async-start(), calls=%async_computation.14 | async-start | bytes 5242880 | tf_op jit(solution)/shard_map/all_gather | solution.py:162
  482.2 389.5 %copy-start.89 = (f32[256]{0:T(256)}, f32[256]{0:T(256)S(1)}, u32[]{:S(2)}) copy-start(f32[256]{0:T(256)S(1)} %add_rsqrt_fusion) | copy-start | bytes 3076
  573.6 107.6 %all-gather.23.cloned.1.call-start = ((), (), s32[]{:S(2)}) async-start(), calls=%async_computation.20 | async-start | bytes 5242880 | tf_op jit(solution)/shard_map/all_gather | solution.py:175
  574.3 241.6 %reduce-scatter.21.cloned.1.call-start = ((), (), s32[]{:S(2)}) async-start(), calls=%async_computation.21 | async-start | bytes 10485760 | tf_op jit(solution)/shard_map/reduce_scatter | solution.py:188
  729.4 142.2 %reduce-scatter.15.cloned.1.call-start = ((), (), s32[]{:S(2)}) async-start(), calls=%async_computation.15 | async-start | bytes 5242880 | tf_op jit(solution)/shard_map/reduce_scatter | solution.py:166
  743.5 187.4 %all-gather.21.cloned.1.call-start = ((), (), s32[]{:S(2)}) async-start(), calls=%async_computation.18 | async-start | bytes 5242880 | tf_op jit(solution)/shard_map/all_gather | solution.py:198
  743.5 134.4 %copy-start.99 = (f32[256]{0:T(256)}, f32[256]{0:T(256)S(1)}, u32[]{:S(2)}) copy-start(f32[256]{0:T(256)S(1)} %broadcast_multiply_fusion.9) | copy-start | bytes 3076
  819.4 58.7 %copy-start.79 = (f32[2,4,512]{2,1,0:T(4,128)S(1)}, f32[2,4,512]{2,1,0:T(4,128)}, u32[]{:S(2)}) copy-start(f32[2,4,512]{2,1,0:T(4,128)} %copy-done.78) | copy-start | bytes 49156
  819.4 58.7 %copy-start.84 = (f32[2,4,512]{2,1,0:T(4,128)S(1)}, f32[2,4,512]{2,1,0:T(4,128)}, u32[]{:S(2)}) copy-start(f32[2,4,512]{2,1,0:T(4,128)} %copy-done.83) | copy-start | bytes 49156
  878.0 108.2 %all-gather.25.cloned.1.call-start = ((), (), s32[]{:S(2)}) async-start(), calls=%async_computation.22 | async-start | bytes 5242880 | tf_op jit(solution)/shard_map/all_gather | solution.py:198
  878.7 379.5 %reduce-scatter.19.cloned.1.call-start = ((), (), s32[]{:S(2)}) async-start(), calls=%async_computation.19 | async-start | bytes 5242880 | tf_op jit(solution)/shard_map/reduce_scatter | solution.py:253
  1029.9 228.3 %reduce-scatter.23.cloned.1.call-start = ((), (), s32[]{:S(2)}) async-start(), calls=%async_computation.23 | async-start | bytes 5242880 | tf_op jit(solution)/shard_map/reduce_scatter | solution.py:253
  1135.2 156.9 %reduce-scatter.11.cloned.1.call-start = ((), (), s32[]{:S(2)}) async-start(), calls=%async_computation.11 | async-start | bytes 5242880 | tf_op jit(solution)/shard_map/reduce_scatter | solution.py:166
  1149.5 700.6 %all-reduce.7.cloned.1.call-start = ((), (), s32[]{:S(2)}) async-start(), calls=%async_computation.24 | async-start | bytes 60817408 | tf_op jit(solution)/shard_map/psum | solution.py:275
  (149 other events, 1669.5 us)
Sparse Core Ops, SparseCore 0:
  23.8 52.9 all-gather.14
  79.2 52.6 all-gather.10
  142.6 86.4 reduce-scatter.12
  232.4 86.3 reduce-scatter.8
  326.3 52.6 all-gather.12
  381.3 52.6 all-gather.18
  482.0 86.4 reduce-scatter.16
  573.7 52.6 all-gather.16
  628.4 52.6 all-gather.22
  729.5 86.4 reduce-scatter.20
  818.9 52.6 reduce-scatter.14
  878.1 52.6 all-gather.20
  933.4 52.6 all-gather.24
  1030.1 52.6 reduce-scatter.18
  1135.4 52.6 reduce-scatter.22
  1191.2 52.6 reduce-scatter.10
  1256.5 593.6 all-reduce.6
where the time goes:
time: 1910 us; the launch traced here: 1900 us
  waiting for transfers between devices  1100 us (58%)
  matrix products  510 us (27%)
  other arithmetic  179 us (9%)
  blocking collectives  55.1 us (3%)
  local copies, waits for them, and re-layouts  39.5 us (2%)
    psum x1, waiting for transfers between devices, body(): lax.psum(sums[1].astype(jnp.bfloat16), 'replica').astype(jnp.float32)  547 us
    reduce_scatter x2, waiting for transfers between devices, body(): lax.psum_scatter(jnp.dot(gate_grad, w_gate, preferred_element_type=jnp.fl...  159 us
    dot_general x14, matrix products, contract_last(): lax.dot_general(left, right, (((1,), (1,)), ((), ())), preferred_element_...  129 us
    dot_general x14, matrix products, contract_first(): lax.dot_general(left, right, (((0,), (0,)), ((), ())), preferred_element_...  104 us
    all_gather x2, waiting for transfers between devices, body(): rows_all = lax.all_gather(normed_ff, 'shard', axis=0, tiled=True)  101 us
    reduce_scatter x2, waiting for transfers between devices, body(): lax.psum_scatter(jnp.dot(attended_h, w_out, preferred_element_type=jnp.fl...  92.9 us
    all_gather x2, waiting for transfers between devices, body(): out_all = lax.all_gather(out_grad, 'shard', axis=0, tiled=True)  61 us
    reduce_scatter x2, waiting for transfers between devices, body(): lax.psum_scatter(jnp.dot(hidden, w_down, preferred_element_type=jnp.float...  52.2 us
  transfers between devices with their start and end apart: 17, of which 13 were waited for; matrix products, arithmetic and copies ran while one was open for 26% of the time, Pallas kernels for 0%

commit v1 on v0

v1 whole, which is shorter than its diff:
```python
import functools
import math

import jax
import jax.numpy as jnp
from jax import lax
from jax.experimental import pallas as pl
from jax.experimental.pallas import tpu as pltpu
from jax.sharding import PartitionSpec as P

HEADS = 32
KV_HEADS = 8
HEAD_DIM = 64
PAIR = 2 * HEAD_DIM
GROUP = HEADS // KV_HEADS

EPSILON = 1e-05
RESIDUAL = 0.22
ATTN_SCALE = 0.015625
ROPE_BASE = 10000000.0
NEGATIVE = -1e30
BF16 = jnp.bfloat16
F32 = jnp.float32


def dot_nt(left, right):
    return lax.dot_general(left, right, (((1,), (1,)), ((), ())), preferred_element_type=F32)


def dot_nn(left, right):
    return lax.dot_general(left, right, (((1,), (0,)), ((), ())), preferred_element_type=F32)


def dot_tn(left, right):
    return lax.dot_general(left, right, (((0,), (0,)), ((), ())), preferred_element_type=F32)


def tree_layout(segment_row, parent_row):
    seg_numbers = jnp.arange(parent_row.shape[0], dtype=jnp.int32)
    member = (segment_row[:, None] == seg_numbers[None, :]).astype(jnp.int32)
    lengths = jnp.sum(member, axis=0)
    earlier = seg_numbers[None, :] < seg_numbers[:, None]
    starts = jnp.sum(jnp.where(earlier, lengths[None, :], 0), axis=1)
    parent_hit = parent_row[:, None] == seg_numbers[None, :]
    grandparent = jnp.sum(jnp.where(parent_hit, parent_row[None, :], 0), axis=1)
    itself = seg_numbers[:, None] == seg_numbers[None, :]
    related = itself | parent_hit | (grandparent[:, None] == seg_numbers[None, :])
    before = jnp.sum(jnp.where(related & jnp.logical_not(itself), lengths[None, :], 0), axis=1)
    shift = jnp.sum(member * (before - starts)[None, :], axis=1)
    position = jnp.arange(segment_row.shape[0], dtype=jnp.int32) + shift
    pad = ((0, 0), (0, PAIR - parent_row.shape[0]))
    sees = dot_nn(member.astype(BF16), related.astype(BF16)).astype(BF16)
    return position, jnp.pad(member.astype(BF16), pad), jnp.pad(sees, pad)


def rope_tables(position):
    lane = jnp.arange(PAIR, dtype=jnp.int32) % HEAD_DIM
    half = HEAD_DIM // 2
    fraction = (lane % half).astype(F32) * (2.0 / HEAD_DIM)
    freq = jnp.exp(-math.log(ROPE_BASE) * fraction)
    angle = position.astype(F32)[:, None] * freq[None, :]
    return jnp.cos(angle), jnp.sin(angle) * jnp.where(lane < half, -1.0, 1.0)[None, :]


def swap_halves(block):
    lane = lax.broadcasted_iota(jnp.int32, block.shape, 1)
    half = HEAD_DIM // 2
    up = pltpu.roll(block, PAIR - half, 1)
    down = pltpu.roll(block, half, 1)
    return jnp.where(lane % HEAD_DIM < half, up, down)


def turn(block, cosine, sine):
    return block * cosine + swap_halves(block) * sine


def place_heads(wide, kv_heads, fill):
    placed = []
    for g in range(kv_heads):
        base = wide[:, (g // 2) * PAIR : (g // 2) * PAIR + PAIR] if wide.shape[1] >= PAIR else wide
        lane = lax.broadcasted_iota(jnp.int32, base.shape, 1)
        moved = pltpu.roll(base, HEAD_DIM, 1)
        for p in range(2):
            source = base if g % 2 == p else moved
            inside = (lane // HEAD_DIM) == p
            placed.append(jnp.where(inside, source, jnp.full_like(source, fill)))
    return placed


def attention_forward_kernel(
    kv_heads,
    blocks,
    order_ref,
    q_ref,
    kv_ref,
    cos_ref,
    sin_ref,
    member_ref,
    sees_ref,
    out_ref,
    q_out_ref,
    kv_out_ref,
    lse_ref,
    keys,
    values,
    bias,
):
    step = pl.program_id(0)
    rows = q_ref.shape[0]
    tree = rows * blocks
    kv_width = kv_heads * HEAD_DIM

    @pl.when(step == 0)
    def _():
        for b in range(blocks):
            here = pl.ds(b * rows, rows)
            raw = kv_ref[pl.ds(pl.multiple_of(order_ref[b] * rows, rows), rows), :]
            cosine, sine = cos_ref[here, :], sin_ref[here, :]
            if kv_width >= PAIR:
                turned = jnp.concatenate(
                    [
                        turn(raw[:, c : c + PAIR], cosine, sine)
                        for c in range(0, kv_width, PAIR)
                    ],
                    axis=1,
                )
                plain = raw[:, kv_width:]
            else:
                lane = lax.broadcasted_iota(jnp.int32, raw.shape, 1)
                turned = turn(raw, cosine, sine)
                plain = pltpu.roll(raw, HEAD_DIM, 1)
                both = jnp.where(lane < HEAD_DIM, turned, raw)
            if kv_width >= PAIR:
                both = jnp.concatenate([turned, plain], axis=1)
            kv_out_ref[here, :] = both.astype(BF16)
            for index, placed in enumerate(place_heads(turned, kv_heads, 0.0)):
                keys[index, here, :] = placed.astype(BF16)
            for index, placed in enumerate(place_heads(plain, kv_heads, 1.0)):
                values[index, here, :] = placed.astype(BF16)

    here = pl.ds(pl.multiple_of(step * rows, rows), rows)
    cosine, sine = cos_ref[here, :], sin_ref[here, :]
    for j in range(q_ref.shape[1] // PAIR):
        lanes = slice(j * PAIR, j * PAIR + PAIR)
        q_out_ref[:, lanes] = (turn(q_ref[:, lanes], cosine, sine).astype(BF16)) * BF16(ATTN_SCALE)

    link = dot_nt(sees_ref[here, :], member_ref[...])
    row_index = lax.broadcasted_iota(jnp.int32, (rows, tree), 0) + step * rows
    col_index = lax.broadcasted_iota(jnp.int32, (rows, tree), 1)
    bias[...] = jnp.where((link > 0.5) & (col_index <= row_index), 0.0, NEGATIVE)

    lane = lax.broadcasted_iota(jnp.int32, (rows, PAIR), 1)
    for block in range(blocks):
        width = (block + 1) * rows

        @pl.when(step == block)
        def _(width=width):
            lse = jnp.zeros((rows, PAIR), F32)
            for j in range(q_ref.shape[1] // PAIR):
                lanes = slice(j * PAIR, j * PAIR + PAIR)
                group = 2 * j // GROUP
                mixed, tops = [], []
                for p in range(2):
                    scores = dot_nt(q_out_ref[:, lanes], keys[group * 2 + p, :width, :])
                    scores = scores + bias[:, :width]
                    top = jnp.max(scores, axis=1, keepdims=True)
                    expo = jnp.exp(scores - top).astype(BF16)
                    mixed.append(dot_nn(expo, values[group * 2 + p, :width, :]))
                    tops.append(top)
                upper = lane >= HEAD_DIM
                total = pltpu.roll(jnp.where(upper, mixed[0], mixed[1]), HEAD_DIM, 1)
                out_ref[:, lanes] = (jnp.where(upper, mixed[1], mixed[0]) / total).astype(BF16)
                logs = jnp.log(total)
                lse = jnp.where(lane == 2 * j, tops[0] + logs[:, :1], lse)
                lse = jnp.where(lane == 2 * j + 1, tops[1] + logs[:, HEAD_DIM : HEAD_DIM + 1], lse)
            lse_ref[...] = lse


def attention_forward(order, qkv, cosine, sine, member, sees, q_width, blocks):
    tree = qkv.shape[0]
    rows = tree // blocks
    kv_width = (qkv.shape[1] - q_width) // 2
    kv_heads = kv_width // HEAD_DIM
    whole = lambda width: pl.BlockSpec((tree, width), lambda i, order: (0, 0))
    natural = lambda width: pl.BlockSpec((rows, width), lambda i, order: (i, 0))
    return pl.pallas_call(
        functools.partial(attention_forward_kernel, kv_heads, blocks),
        grid_spec=pltpu.PrefetchScalarGridSpec(
            num_scalar_prefetch=1,
            grid=(blocks,),
            in_specs=[
                pl.BlockSpec((rows, q_width), lambda i, order: (order[i], 0)),
                pl.BlockSpec((tree, 2 * kv_width), lambda i, order: (0, q_width // (2 * kv_width))),
                whole(PAIR),
                whole(PAIR),
                whole(PAIR),
                whole(PAIR),
            ],
            out_specs=[
                pl.BlockSpec((rows, q_width), lambda i, order: (order[i], 0)),
                natural(q_width),
                whole(2 * kv_width),
                natural(PAIR),
            ],
            scratch_shapes=[
                pltpu.VMEM((2 * kv_heads, tree, PAIR), BF16),
                pltpu.VMEM((2 * kv_heads, tree, PAIR), BF16),
                pltpu.VMEM((rows, tree), F32),
            ],
        ),
        out_shape=[
            jax.ShapeDtypeStruct((tree, q_width), BF16),
            jax.ShapeDtypeStruct((tree, q_width), BF16),
            jax.ShapeDtypeStruct((tree, 2 * kv_width), BF16),
            jax.ShapeDtypeStruct((tree, PAIR), F32),
        ],
        compiler_params=pltpu.CompilerParams(vmem_limit_bytes=40 << 20),
        cost_estimate=pl.CostEstimate(
            flops=10_000_000_000, bytes_accessed=12_000_000, transcendentals=5_000_000
        ),
        name="attention_forward",
    )(order, qkv, qkv, cosine, sine, member, sees)


def attention_backward_kernel(
    kv_heads,
    blocks,
    order_ref,
    grad_ref,
    q_ref,
    kv_ref,
    lse_ref,
    cos_ref,
    sin_ref,
    member_ref,
    sees_ref,
    dq_ref,
    dkv_ref,
    keys,
    values,
    bias,
    key_sum,
    value_sum,
):
    step = pl.program_id(0)
    rows = q_ref.shape[0]
    tree = rows * blocks
    kv_width = kv_heads * HEAD_DIM

    @pl.when(step == 0)
    def _():
        for b in range(blocks):
            here = pl.ds(b * rows, rows)
            both = kv_ref[here, :].astype(F32)
            if kv_width >= PAIR:
                turned, plain = both[:, :kv_width], both[:, kv_width:]
            else:
                turned, plain = both, pltpu.roll(both, HEAD_DIM, 1)
            for index, placed in enumerate(place_heads(turned, kv_heads, 0.0)):
                keys[index, here, :] = placed.astype(BF16)
            for index, placed in enumerate(place_heads(plain, kv_heads, 0.0)):
                values[index, here, :] = placed.astype(BF16)
        key_sum[...] = jnp.zeros_like(key_sum)
        value_sum[...] = jnp.zeros_like(value_sum)

    here = pl.ds(pl.multiple_of(step * rows, rows), rows)
    link = dot_nt(member_ref[...], sees_ref[here, :])
    key_index = lax.broadcasted_iota(jnp.int32, (tree, rows), 0)
    query_index = lax.broadcasted_iota(jnp.int32, (tree, rows), 1) + step * rows
    bias[...] = jnp.where((link > 0.5) & (key_index <= query_index), 0.0, NEGATIVE)
    lse_rows = jnp.transpose(lse_ref[...])

    for block in range(blocks):
        width = (block + 1) * rows

        @pl.when(step == block)
        def _(width=width):
            cosine, sine = cos_ref[here, :], sin_ref[here, :]
            for j in range(q_ref.shape[1] // PAIR):
                lanes = slice(j * PAIR, j * PAIR + PAIR)
                group = 2 * j // GROUP
                query, grad = q_ref[:, lanes], grad_ref[:, lanes]
                dq = jnp.zeros((rows, PAIR), F32)
                for p in range(2):
                    index, head = group * 2 + p, 2 * j + p
                    scores = dot_nt(keys[index, :width, :], query) + bias[:width, :]
                    probs = jnp.exp(scores - lse_rows[head : head + 1, :])
                    probs_grad = dot_nt(values[index, :width, :], grad)
                    value_sum[index, :width, :] += dot_nn(probs.astype(BF16), grad)
                    weighted = probs * probs_grad
                    delta = jnp.sum(weighted, axis=0, keepdims=True)
                    score_grad = (weighted - probs * delta).astype(BF16)
                    key_sum[index, :width, :] += dot_nn(score_grad, query)
                    dq = dq + dot_tn(score_grad, keys[index, :width, :])
                dq_ref[:, lanes] = turn(dq * ATTN_SCALE, cosine, -sine).astype(BF16)

    @pl.when(step == blocks - 1)
    def _():
        for b in range(blocks):
            here = pl.ds(b * rows, rows)
            there = pl.ds(pl.multiple_of(order_ref[b] * rows, rows), rows)
            cosine, sine = cos_ref[here, :], sin_ref[here, :]
            lane = lax.broadcasted_iota(jnp.int32, (rows, PAIR), 1)
            lower = lane < HEAD_DIM
            for c in range(0, kv_heads, 2):
                halves = []
                for acc in (key_sum, value_sum):
                    own, other = [], []
                    for g in range(c, min(c + 2, kv_heads)):
                        low, high = acc[g * 2, here, :], acc[g * 2 + 1, here, :]
                        own.append(low)
                        other.append(high)
                    first = own[0] + pltpu.roll(other[0], HEAD_DIM, 1)
                    if len(own) == 2:
                        second = other[1] + pltpu.roll(own[1], HEAD_DIM, 1)
                    else:
                        second = first
                    halves.append(jnp.where(lower, first, second))
                turned = turn(halves[0], cosine, -sine)
                if kv_width >= PAIR:
                    lanes = slice(c * HEAD_DIM, c * HEAD_DIM + PAIR)
                    dkv_ref[there, lanes] = turned.astype(BF16)
                    lanes = slice(kv_width + c * HEAD_DIM, kv_width + c * HEAD_DIM + PAIR)
                    dkv_ref[there, lanes] = halves[1].astype(BF16)
                else:
                    moved = pltpu.roll(halves[1], HEAD_DIM, 1)
                    dkv_ref[there, :] = jnp.where(lower, turned, moved).astype(BF16)


def attention_backward(order, grad, query, kv, lse, cosine, sine, member, sees, blocks):
    tree, q_width = query.shape
    rows = tree // blocks
    kv_width = kv.shape[1] // 2
    kv_heads = kv_width // HEAD_DIM
    whole = lambda width: pl.BlockSpec((tree, width), lambda i, order: (0, 0))
    natural = lambda width: pl.BlockSpec((rows, width), lambda i, order: (i, 0))
    ordered = lambda width: pl.BlockSpec((rows, width), lambda i, order: (order[i], 0))
    return pl.pallas_call(
        functools.partial(attention_backward_kernel, kv_heads, blocks),
        grid_spec=pltpu.PrefetchScalarGridSpec(
            num_scalar_prefetch=1,
            grid=(blocks,),
            in_specs=[
                ordered(q_width),
                natural(q_width),
                whole(2 * kv_width),
                natural(PAIR),
                whole(PAIR),
                whole(PAIR),
                whole(PAIR),
                whole(PAIR),
            ],
            out_specs=[ordered(q_width), whole(2 * kv_width)],
            scratch_shapes=[
                pltpu.VMEM((2 * kv_heads, tree, PAIR), BF16),
                pltpu.VMEM((2 * kv_heads, tree, PAIR), BF16),
                pltpu.VMEM((tree, rows), F32),
                pltpu.VMEM((2 * kv_heads, tree, PAIR), F32),
                pltpu.VMEM((2 * kv_heads, tree, PAIR), F32),
            ],
        ),
        out_shape=[
            jax.ShapeDtypeStruct((tree, q_width), BF16),
            jax.ShapeDtypeStruct((tree, 2 * kv_width), BF16),
        ],
        compiler_params=pltpu.CompilerParams(vmem_limit_bytes=48 << 20),
        cost_estimate=pl.CostEstimate(
            flops=20_000_000_000, bytes_accessed=12_000_000, transcendentals=5_000_000
        ),
        name="attention_backward",
    )(order, grad, query, kv, lse, cosine, sine, member, sees)


def sync(*values):
    return lax.optimization_barrier(values)


class Square:
    def __init__(self, shard, replica):
        self.shard, self.replica = shard, replica
        self.x = [(i, i ^ 1) for i in range(shard)]
        self.y = [(i, i ^ 2) for i in range(shard)]
        self.d = [(i, i ^ 3) for i in range(shard)]
        self.core = [(i, i ^ 1) for i in range(replica)]
        both = lambda pairs: [(2 * a + c, 2 * b + c) for a, b in pairs for c in range(2)]
        self.outer = both([(0, 1), (1, 0), (2, 3), (3, 2)])
        self.middle = both([(1, 2), (2, 1)])

    def order(self):
        return jnp.arange(self.shard, dtype=jnp.int32) ^ lax.axis_index("shard")

    def reorder(self, blocks, axis):
        me = lax.axis_index("shard")
        return jnp.concatenate(
            [lax.dynamic_slice_in_dim(blocks, n ^ me, 1, axis) for n in range(self.shard)], axis=axis
        )

    def gather_small(self, own):
        parts = [
            own,
            lax.ppermute(own, "shard", self.x),
            lax.ppermute(own, "shard", self.y),
            lax.ppermute(own, "shard", self.d),
        ]
        return self.reorder(jnp.stack(parts), 0)

    def gather_first(self, own):
        return lax.ppermute(own, "shard", self.x), lax.ppermute(own, "shard", self.y)

    def gather_second(self, own, got):
        from_x, from_y = got
        half = own.shape[0] // 2
        first = lax.ppermute(from_y[:half], "shard", self.x)
        second = lax.ppermute(from_x[half:], "shard", self.y)
        return [own, from_x, from_y, first, second]

    def split(self, part):
        trees, width = part.shape[0] // self.rows // 4, part.shape[1]
        return part.reshape(trees, 4, 2, self.rows // 2, width)

    def sum_first(self, part):
        pieces = self.split(part)
        send_x = jnp.stack([pieces[:, 1, 0], pieces[:, 3, 0]])
        send_y = jnp.stack([pieces[:, 2, 1], pieces[:, 3, 1]])
        return lax.ppermute(send_x, "shard", self.x), lax.ppermute(send_y, "shard", self.y)

    def sum_second(self, part, got):
        pieces = self.split(part)
        got_x, got_y = got
        next_y = (pieces[:, 2, 0].astype(F32) + got_x[1].astype(F32)).astype(BF16)
        next_x = (pieces[:, 1, 1].astype(F32) + got_y[1].astype(F32)).astype(BF16)
        return lax.ppermute(next_y, "shard", self.y), lax.ppermute(next_x, "shard", self.x)

    def sum_last(self, part, got, last):
        pieces = self.split(part)
        wide = lambda v: v.astype(F32)
        first = wide(pieces[:, 0, 0]) + wide(got[0][0]) + wide(last[0])
        second = wide(pieces[:, 0, 1]) + wide(got[1][0]) + wide(last[1])
        both = jnp.concatenate([first, second], axis=1)
        return [both[t] for t in range(both.shape[0])]

    def sum_small(self, values):
        share = values.shape[1] // self.shard
        blocks = values.reshape(values.shape[0], self.shard, share)
        blocks = self.reorder(blocks, 1)
        total = blocks[:, 0]
        for k, perm in ((1, self.x), (2, self.y), (3, self.d)):
            total = total + lax.ppermute(blocks[:, k], "shard", perm)
        for step in (1, 2, 4):
            perm = [(i, i ^ step) for i in range(self.replica)]
            total = total + lax.ppermute(total, "replica", perm)
        return total

    def start_line(self):
        self.entering = []
        self.waiting = []
        self.outer_flight = None
        self.middle_flight = None
        self.wholes = None
        self.finals = {}

    def feed(self, name, grad, chunks):
        half = grad.shape[0] // 2
        core = lax.axis_index("replica") % 2
        send = lax.dynamic_slice_in_dim(grad, (1 - core) * half, half, 0)
        got = lax.ppermute(send, "replica", self.core)
        rows = half // chunks
        self.finals[name] = [None] * chunks
        for c in range(chunks):
            keep = lax.dynamic_slice_in_dim(grad, core * half + c * rows, rows, 0)
            mine = keep.astype(F32) + got[c * rows : (c + 1) * rows].astype(F32)
            self.waiting.append((name, c, mine.astype(BF16)))

    def busy(self):
        return any(v is not None for v in (self.outer_flight, self.middle_flight, self.wholes)) or bool(
            self.waiting
        )

    def tick(self, *values):
        place = lax.axis_index("replica") // 2
        inner = (place == 1) | (place == 2)
        outer, middle = self.outer_flight, self.middle_flight
        flights = (outer and outer[2], middle and middle[2])
        chunk = self.waiting.pop(0) if self.waiting else None
        flights, mine, values = sync(flights, chunk and chunk[2], values)
        add = lambda a, b: (a.astype(F32) + b.astype(F32)).astype(BF16)
        whole = None
        if middle is not None:
            whole = (middle[0], add(middle[1], flights[1]))
        self.middle_flight = None
        if outer is not None:
            entered, left, _ = outer
            if left is not None:
                (name, c), value = left
                final = jnp.where(inner, value, flights[0][: value.shape[0]])
                self.finals[name][c] = (final, lax.ppermute(final, "replica", self.core))
            if entered is not None:
                key, own = entered
                pair = add(own, flights[0][: own.shape[0]])
                self.middle_flight = (key, pair, lax.ppermute(pair, "replica", self.middle))
        self.outer_flight = None
        if chunk is not None or whole is not None:
            entering = None if chunk is None else ((chunk[0], chunk[1]), mine)
            if entering is None:
                send = whole[1]
            elif whole is None:
                send = mine
            else:
                rows = max(mine.shape[0], whole[1].shape[0])
                pad = lambda v: jnp.pad(v, ((0, rows - v.shape[0]), (0, 0)))
                send = jnp.where(inner, pad(whole[1]), pad(mine))
            self.outer_flight = (entering, whole, lax.ppermute(send, "replica", self.outer))
        return values

    def finish(self, name):
        mine = jnp.concatenate([f for f, _ in self.finals[name]], axis=0)
        other = jnp.concatenate([o for _, o in self.finals[name]], axis=0)
        first = lax.axis_index("replica") % 2 == 0
        return jnp.concatenate(
            [jnp.where(first, mine, other), jnp.where(first, other, mine)], axis=0
        ).astype(F32)

    def drain(self):
        while self.waiting or self.outer_flight is not None or self.middle_flight is not None:
            self.tick()


class General:
    def __init__(self, shard, replica):
        self.shard, self.replica = shard, replica

    def order(self):
        return jnp.arange(self.shard, dtype=jnp.int32)

    def gather_small(self, own):
        return lax.all_gather(own, "shard", axis=0, tiled=False)

    def gather_first(self, own):
        return lax.all_gather(own, "shard", axis=0, tiled=True)

    def gather_second(self, own, got):
        return [got]

    def sum_first(self, part):
        return lax.psum_scatter(
            part.reshape(-1, self.shard * self.rows, part.shape[1]),
            "shard",
            scatter_dimension=1,
            tiled=True,
        )

    def sum_second(self, part, got):
        return ()

    def sum_last(self, part, got, last):
        return [got[t].astype(F32) for t in range(got.shape[0])]

    def sum_small(self, values):
        share = lax.psum_scatter(values, "shard", scatter_dimension=1, tiled=True)
        return lax.psum(share, "replica")

    def start_line(self):
        self.finals = {}

    def feed(self, name, grad, chunks):
        self.finals[name] = lax.psum(grad, "replica").astype(F32)

    def tick(self, *values):
        return values

    def drain(self):
        pass

    def finish(self, name):
        return self.finals[name]


def rms_scale(values):
    return lax.rsqrt(jnp.mean(values * values, axis=-1, keepdims=True) + EPSILON)


def normalized(piece, gain):
    values = piece.astype(F32)
    return (values * rms_scale(values) * gain).astype(BF16)


def norm_back(values, scale, gain, grad_in):
    scaled = values * scale
    weighted = grad_in * gain
    back = scale * (weighted - scaled * jnp.mean(weighted * scaled, axis=-1, keepdims=True))
    return back, jnp.sum(grad_in * scaled, axis=0)


def body(
    links,
    tokens,
    gain_attn,
    w_query,
    w_key,
    w_value,
    w_out,
    gain_ff,
    w_gate,
    w_up,
    w_down,
    cotangent,
    segment_ids,
    parents,
):
    trees, _, own_rows, width = tokens.shape
    shard = links.shard
    q_width, kv_width = w_query.shape[0], w_key.shape[0]
    tree_rows = own_rows * shard
    links.rows = own_rows
    links.start_line()
    order = links.order()
    share = gain_attn.shape[0]
    w_qkv = jnp.concatenate([w_query, w_key, w_value], axis=0)
    token_rows = [tokens[t, 0] for t in range(trees)]
    cot_rows = [cotangent[t, 0] for t in range(trees)]

    small = jnp.concatenate(
        [gain_attn, gain_ff] + [segment_ids[t, 0].astype(BF16) for t in range(trees)]
    )
    smalls = links.gather_small(small)
    got = links.gather_first(token_rows[0])
    got, smalls, token_rows = sync(got, smalls, token_rows)
    gain_first = smalls[:, :share].reshape(width).astype(F32)
    gain_second = smalls[:, share : 2 * share].reshape(width).astype(F32)
    masks, tables = [], []
    for t in range(trees):
        begin = 2 * share + t * own_rows
        segments = smalls[:, begin : begin + own_rows].reshape(tree_rows).astype(jnp.int32)
        position, member, sees = tree_layout(segments, parents[t, 0])
        masks.append((member, sees))
        tables.append(rope_tables(position))

    normed_all, saved = [], []

    def attention(t, pieces):
        normed = jnp.concatenate([normalized(piece, gain_first) for piece in pieces], axis=0)
        normed_all.append(normed)
        attended, query, kv, lse = attention_forward(
            order, dot_nt(normed, w_qkv), *tables[t], *masks[t], q_width, shard
        )
        saved.append((attended, query, kv, lse))
        return dot_nn(attended, w_out).astype(BF16)

    def after_attention(t, branch):
        value = token_rows[t].astype(F32) + RESIDUAL * branch
        scale = rms_scale(value)
        return value, scale, (value * scale * gain_second).astype(BF16)

    pieces_0 = links.gather_second(token_rows[0], got)
    got = links.gather_first(token_rows[1])
    pieces_0, got, cot_rows = sync(pieces_0, got, cot_rows)

    pieces_1 = links.gather_second(token_rows[1], got)
    cot_got = links.gather_first(cot_rows[0])
    part_0 = attention(0, pieces_0)
    part_0, pieces_1, cot_got = sync(part_0, pieces_1, cot_got)

    got_0 = links.sum_first(part_0)
    cot_pieces_0 = links.gather_second(cot_rows[0], cot_got)
    part_1 = attention(1, pieces_1)
    got_0, cot_pieces_0, part_1 = sync(got_0, cot_pieces_0, part_1)

    last_0 = links.sum_second(part_0, got_0)
    got_1 = links.sum_first(part_1)
    last_0, got_1 = sync(last_0, got_1)

    middle_0, scale_0, own_0 = after_attention(0, links.sum_last(part_0, got_0, last_0)[0])
    last_1 = links.sum_second(part_1, got_1)
    ff_got_0 = links.gather_first(own_0)
    ff_got_0, last_1 = sync(ff_got_0, last_1)

    middle_1, scale_1, own_1 = after_attention(1, links.sum_last(part_1, got_1, last_1)[0])
    ff_pieces_0 = links.gather_second(own_0, ff_got_0)
    ff_got_1 = links.gather_first(own_1)
    ff_pieces_0, ff_got_1 = sync(ff_pieces_0, ff_got_1)
    ff_pieces_1 = links.gather_second(own_1, ff_got_1)
    ff_pieces_0, ff_pieces_1, cot_rows, cot_pieces_0 = sync(
        ff_pieces_0, ff_pieces_1, cot_rows, cot_pieces_0
    )

    rows_all = jnp.concatenate(ff_pieces_0 + ff_pieces_1, axis=0)
    cot_got = links.gather_first(cot_rows[1])
    gate = dot_nt(rows_all, w_gate).astype(BF16)
    gate, cot_got, rows_all = sync(gate, cot_got, rows_all)
    cot_pieces_1 = links.gather_second(cot_rows[1], cot_got)
    upper = dot_nt(rows_all, w_up)
    wide = gate.astype(F32)
    hidden = (wide * jax.nn.sigmoid(wide) * upper).astype(BF16)
    upper = upper.astype(BF16)
    hidden, upper, gate, cot_pieces_1 = sync(hidden, upper, gate, cot_pieces_1)
    cot_all = jnp.concatenate(
        [(RESIDUAL * piece.astype(F32)).astype(BF16) for piece in cot_pieces_0 + cot_pieces_1], axis=0
    )
    hidden_grad = dot_nt(cot_all, w_down)
    wide = gate.astype(F32)
    sigma = jax.nn.sigmoid(wide)
    gate_grad = (
        hidden_grad * upper.astype(F32) * sigma * (1.0 + wide * (1.0 - sigma))
    ).astype(BF16)
    up_grad = (hidden_grad * wide * sigma).astype(BF16)
    gate_grad, up_grad, hidden, cot_all = sync(gate_grad, up_grad, hidden, cot_all)

    grad_down = dot_tn(hidden, cot_all).astype(BF16)
    grad_down, gate_grad, up_grad = sync(grad_down, gate_grad, up_grad)
    links.feed("down", grad_down, 2)
    ff_part = (dot_nn(gate_grad, w_gate) + dot_nn(up_grad, w_up)).astype(BF16)
    ff_part, gate_grad, up_grad, hidden = links.tick(ff_part, gate_grad, up_grad, hidden)

    ff_sum = links.sum_first(ff_part)
    grad_gate = dot_tn(gate_grad, rows_all).astype(BF16)
    grad_gate, up_grad, ff_sum = links.tick(grad_gate, up_grad, ff_sum)
    links.feed("gate", grad_gate, 2)
    ff_last = links.sum_second(ff_part, ff_sum)
    grad_up = dot_tn(up_grad, rows_all).astype(BF16)
    grad_up, hidden, ff_last = links.tick(grad_up, hidden, ff_last)
    links.feed("up", grad_up, 2)

    ff_grad = links.sum_last(ff_part, ff_sum, ff_last)
    out_own, middle_grads = [], []
    gain_ff_sum = jnp.zeros((width,), F32)
    for t, (middle, scale) in enumerate(((middle_0, scale_0), (middle_1, scale_1))):
        middle_back, term = norm_back(middle, scale, gain_second, ff_grad[t])
        gain_ff_sum = gain_ff_sum + term
        middle_grads.append(cot_rows[t].astype(F32) + middle_back)
        out_own.append((RESIDUAL * middle_grads[t]).astype(BF16))
    out_got_0 = links.gather_first(out_own[0])
    down_part = dot_nn(hidden, w_down).astype(BF16)
    down_part, out_got_0, out_own = links.tick(down_part, out_got_0, out_own)

    out_pieces_0 = links.gather_second(out_own[0], out_got_0)
    out_got_1 = links.gather_first(out_own[1])
    out_pieces_0, out_got_1, down_part = links.tick(out_pieces_0, out_got_1, down_part)

    def attention_back(t, out_all):
        attended, query, kv, lse = saved[t]
        attended_grad = dot_nt(out_all, w_out).astype(BF16)
        dq, dkv = attention_backward(
            order, attended_grad, query, kv, lse, *tables[t], *masks[t], shard
        )
        qkv_grad = jnp.concatenate([dq, dkv], axis=1)
        return qkv_grad, dot_nn(qkv_grad, w_qkv).astype(BF16)

    out_pieces_1 = links.gather_second(out_own[1], out_got_1)
    down_sum = links.sum_first(down_part)
    out_all_0 = jnp.concatenate(out_pieces_0, axis=0)
    qkv_grad_0, normed_part_0 = attention_back(0, out_all_0)
    qkv_grad_0, normed_part_0, out_pieces_1, down_sum = links.tick(
        qkv_grad_0, normed_part_0, out_pieces_1, down_sum
    )

    normed_sum_0 = links.sum_first(normed_part_0)
    down_last = links.sum_second(down_part, down_sum)
    out_all_1 = jnp.concatenate(out_pieces_1, axis=0)
    qkv_grad_1, normed_part_1 = attention_back(1, out_all_1)
    qkv_grad_1, normed_part_1, normed_sum_0, down_last = links.tick(
        qkv_grad_1, normed_part_1, normed_sum_0, down_last
    )

    normed_last_0 = links.sum_second(normed_part_0, normed_sum_0)
    normed_sum_1 = links.sum_first(normed_part_1)
    attended_all = jnp.concatenate([saved[t][0] for t in range(trees)], axis=0)
    grad_out = dot_tn(attended_all, jnp.concatenate([out_all_0, out_all_1], axis=0)).astype(BF16)
    grad_qkv = dot_tn(
        jnp.concatenate([qkv_grad_0, qkv_grad_1], axis=0), jnp.concatenate(normed_all, axis=0)
    ).astype(BF16)
    grad_out, grad_qkv, normed_last_0, normed_sum_1 = links.tick(
        grad_out, grad_qkv, normed_last_0, normed_sum_1
    )
    links.feed("out", grad_out, 1)
    links.feed("qkv", grad_qkv, 1)

    normed_last_1 = links.sum_second(normed_part_1, normed_sum_1)
    down = links.sum_last(down_part, down_sum, down_last)
    results = [
        (middle + RESIDUAL * down[t]).astype(BF16) for t, middle in enumerate((middle_0, middle_1))
    ]
    results, normed_last_1 = links.tick(results, normed_last_1)
    normed_grads = links.sum_last(normed_part_0, normed_sum_0, normed_last_0)
    normed_grads += links.sum_last(normed_part_1, normed_sum_1, normed_last_1)
    input_grads = []
    gain_attn_sum = jnp.zeros((width,), F32)
    for t in range(trees):
        inputs = token_rows[t].astype(F32)
        input_back, term = norm_back(inputs, rms_scale(inputs), gain_first, normed_grads[t])
        gain_attn_sum = gain_attn_sum + term
        input_grads.append(middle_grads[t] + input_back)
    gains = links.sum_small(jnp.stack([gain_attn_sum, gain_ff_sum]))
    links.drain()
    grad_qkv = links.finish("qkv")
    return (
        jnp.stack(results)[:, None],
        jnp.stack(input_grads)[:, None],
        gains[0],
        grad_qkv[:q_width],
        grad_qkv[q_width : q_width + kv_width],
        grad_qkv[q_width + kv_width :],
        links.finish("out"),
        gains[1],
        links.finish("gate"),
        links.finish("up"),
        links.finish("down"),
    )


def solution(mesh):
    shard, replica = mesh.shape["shard"], mesh.shape["replica"]
    links = (Square if (shard, replica) == (4, 8) else General)(shard, replica)
    in_specs = (
        P(None, "replica", "shard", None),
        P("shard"),
        P("shard", None),
        P("shard", None),
        P("shard", None),
        P("shard", None),
        P("shard"),
        P("shard", None),
        P("shard", None),
        P("shard", None),
        P(None, "replica", "shard", None),
        P(None, "replica", "shard"),
        P(None, "replica", None),
    )
    out_specs = (
        P(None, "replica", "shard", None),
        P(None, "replica", "shard", None),
        P("shard"),
        P("shard", None),
        P("shard", None),
        P("shard", None),
        P("shard", None),
        P("shard"),
        P("shard", None),
        P("shard", None),
        P("shard", None),
    )
    return jax.shard_map(
        functools.partial(body, links),
        mesh=mesh,
        in_specs=in_specs,
        out_specs=out_specs,
        check_vma=False,
    )
```

time: 1910 us -> 1150 us (0.60)
  waiting for transfers between devices: 1100 us -> 329 us
  matrix products: 510 us -> 278 us
  starting transfers between devices: 0.91 us -> 118 us
  Pallas kernels: 0 us -> 82.7 us
  other arithmetic: 179 us -> 242 us
  blocking collectives: 55.1 us -> 0 us
  local copies, waits for them, and re-layouts: 39.5 us -> 85.8 us
    psum x1 -> x0, waiting for transfers between devices: 547 us -> none  [body(): lax.psum(sums[1].astype(jnp.bfloat16), 'replica').astype(jnp.float32)]
    ppermute x0 -> x98, waiting for transfers between devices: none -> 329 us  [the longest x12 97.6 us: tick(): lax.ppermute(send, 'replica', self.outer)]
    reduce_scatter x8 -> x0, waiting for transfers between devices: 304 us -> none  [the longest x2 159 us: body(): lax.psum_scatter(jnp.dot(gate_grad, w_gate, preferred_element_type=jnp.fl...]
    all_gather x8 -> x0, waiting for transfers between devices: 247 us -> none  [the longest x2 101 us: body(): rows_all = lax.all_gather(normed_ff, 'shard', axis=0, tiled=True)]
    dot_general x72 -> x21, matrix products: 510 us -> 278 us  [the longest x7 101 us: dot_nt(): lax.dot_general(left, right, (((1,), (1,)), ((), ())), preferred_element_...]
    ppermute x0 -> x98, starting transfers between devices: none -> 118 us  [the longest x12 28.1 us: tick(): lax.ppermute(send, 'replica', self.outer)]
    pallas_call x0 -> x4, Pallas kernels: none -> 82.7 us  [the longest x2 47.5 us: attention_backward(): pl.pallas_call(functools.partial(attention_backward_kernel, kv_heads, blo...]
    select_n x0 -> x18, other arithmetic: none -> 52.3 us  [the longest x5 19.1 us: finish(): jnp.where(first, mine, other)]
  transfers between devices with their start and end apart: 17 -> 98, of which waited for: 13 -> 28; matrix products, arithmetic and copies ran while one was open for 26% -> 42% of each run, Pallas kernels for 0% -> 7%
where the time goes in v1:
time: 1150 us; the launch traced here: 1140 us
  waiting for transfers between devices  329 us (29%)
  matrix products  278 us (24%)
  other arithmetic  242 us (21%)
  starting transfers between devices  118 us (10%)
  local copies, waits for them, and re-layouts  85.8 us (7%)
  Pallas kernels  82.7 us (7%)
    dot_general x7, matrix products, dot_nt(): lax.dot_general(left, right, (((1,), (1,)), ((), ())), preferred_element_...  101 us
    ppermute x12, waiting for transfers between devices, tick(): lax.ppermute(send, 'replica', self.outer)  97.6 us
    dot_general x9, matrix products, dot_nn(): lax.dot_general(left, right, (((1,), (0,)), ((), ())), preferred_element_...  89.2 us
    dot_general x5, matrix products, dot_tn(): lax.dot_general(left, right, (((0,), (0,)), ((), ())), preferred_element_...  88.3 us
    ppermute x8, waiting for transfers between devices, gather_second(): first = lax.ppermute(from_y[:half], 'shard', self.x)  66.4 us
    ppermute x6, waiting for transfers between devices, sum_second(): lax.ppermute(next_y, 'shard', self.y)  54.7 us
    pallas_call x2, Pallas kernels, attention_backward(): pl.pallas_call(functools.partial(attention_backward_kernel, kv_heads, blo...  47.5 us
    ppermute x8, waiting for transfers between devices, gather_second(): second = lax.ppermute(from_x[half:], 'shard', self.y)  47.1 us
  transfers between devices with their start and end apart: 98, of which 28 were waited for; matrix products, arithmetic and copies ran while one was open for 42% of the time, Pallas kernels for 7%

profile of v1, /device:TPU:0, one launch (start us, length us, event | category | flops | bytes accessed | tf_op | source)
XLA Modules:
  0.0 1139.9 jit_solution(338920087766767261)
XLA Ops:
  49.8 17.0 %collective-permute-done.5 = bf16[128,2048]{1,0:T(8,128)(2,1)} collective-permute-done((bf16[128,2048]{1,0:T(8,128)(2,1)}, bf16[128,2048]{1,0:T(8,128)(2,1)}, u32[]{:S(2)}, u32[]{:S(2)}) %collective-permute-start.5) | collective-permute-done | bytes 524320 | tf_op jit(solution)/shard_map/ppermute | solution.py:413
  92.2 17.7 %attention_forward.2 = (bf16[1024,512]{1,0:T(8,128)(2,1)S(1)}, bf16[1024,512]{1,0:T(8,128)(2,1)S(1)}, bf16[1024,256]{1,0:T(8,128)(2,1)S(1)}, f32[1024,128]{1,0:T(8,128)S(1)}) custom-call(s32[4]{0:T(128)S(1)} %iota_xor_fusion.order_ref, f32[1024,768]{1,0:T(8,128)S(1)} %fusion.151.q_ref.kv_ref, f32[1024,768]{1,0:T(8,128)S(1)} %fusion.151.q_ref.kv_ref, ...), custom_call_target="tpu_custom_call" | custom-call | flops 10000000000 | bytes 12000000 | tf_op jit(solution)/shard_map/attention_forward/pallas_call | solution.py:186
  137.8 17.4 %attention_forward.3 = (bf16[1024,512]{1,0:T(8,128)(2,1)S(1)}, bf16[1024,512]{1,0:T(8,128)(2,1)S(1)}, bf16[1024,256]{1,0:T(8,128)(2,1)S(1)}, f32[1024,128]{1,0:T(8,128)S(1)}) custom-call(s32[4]{0:T(128)S(1)} %iota_xor_fusion.order_ref, f32[1024,768]{1,0:T(8,128)S(1)} %fusion.152.q_ref.kv_ref, f32[1024,768]{1,0:T(8,128)S(1)} %fusion.152.q_ref.kv_ref, ...), custom_call_target="tpu_custom_call" | custom-call | flops 10000000000 | bytes 12000000 | tf_op jit(solution)/shard_map/attention_forward/pallas_call | solution.py:186
  163.4 28.0 %collective-permute-done.17 = bf16[1,128,2048]{2,1,0:T(8,128)(2,1)S(1)} collective-permute-done((bf16[1,128,2048]{2,1,0:T(8,128)(2,1)S(1)}, bf16[1,128,2048]{2,1,0:T(8,128)(2,1)S(1)}, u32[]{:S(2)}, u32[]{:S(2)}) %collective-permute-start.17) | collective-permute-done | bytes 524320 | tf_op jit(solution)/shard_map/ppermute | solution.py:432
  197.9 26.8 %collective-permute-done.23 = bf16[1,128,2048]{2,1,0:T(8,128)(2,1)S(1)} collective-permute-done((bf16[1,128,2048]{2,1,0:T(8,128)(2,1)S(1)}, bf16[1,128,2048]{2,1,0:T(8,128)(2,1)S(1)}, u32[]{:S(2)}, u32[]{:S(2)}) %collective-permute-start.23) | collective-permute-done | bytes 524320 | tf_op jit(solution)/shard_map/ppermute | solution.py:432
  233.0 27.4 %collective-permute-done.25 = bf16[128,2048]{1,0:T(8,128)(2,1)S(1)} collective-permute-done((bf16[128,2048]{1,0:T(8,128)(2,1)S(1)}, bf16[128,2048]{1,0:T(8,128)(2,1)S(1)}, u32[]{:S(2)}, u32[]{:S(2)}) %collective-permute-start.25) | collective-permute-done | bytes 524320 | tf_op jit(solution)/shard_map/ppermute | solution.py:413
  290.0 25.8 %convolution_convert_fusion.4 = bf16[2048,2048]{1,0:T(8,128)(2,1)} fusion(bf16[2048,2048]{1,0:T(8,128)(2,1)S(1)} %constant_dynamic-update-slice_fusion.7, bf16[2048,2048]{1,0:T(8,128)(2,1)} %param.20), kind=kOutput, calls=%fused_computation.26 | convolution fusion | flops 17184063488 | bytes 25165824 | tf_op jit(solution)/shard_map/dot_general | solution.py:27
  321.5 27.4 %fusion.149 = (bf16[2048,2048]{1,0:T(8,128)(2,1)}, bf16[2048,2048]{1,0:T(8,128)(2,1)}) fusion(bf16[2048,2048]{1,0:T(8,128)(2,1)} %convolution_convert_fusion.4, bf16[2048,2048]{1,0:T(8,128)(2,1)} %copy-done.119, bf16[2048,2048]{1,0:T(8,128)(2,1)} %param.21), kind=kOutput, calls=%fused_computation.502 | convolution fusion | flops 17213423616 | bytes 41943040 | tf_op jit(solution)/shard_map/dot_general | solution.py:27
  358.9 32.1 %fusion.11 = (bf16[2048,2048]{1,0:T(8,128)(2,1)}, bf16[2048,2048]{1,0:T(8,128)(2,1)}) fusion(bf16[2048,2048]{1,0:T(8,128)(2,1)} %convolution_convert_fusion.4, bf16[2048,2048]{1,0:T(8,128)(2,1)} %get-tuple-element.253, bf16[2048,2048]{1,0:T(8,128)(2,1)} %fusion.118, bf16[2048,2048]{1,0:T(8,128)(2,1)} %param.22), kind=kOutput, calls=%fused_computation.16 | convolution fusion | flops 17242783744 | bytes 50331648 | tf_op jit(solution)/shard_map/dot_general | solution.py:27
  391.0 22.4 %convolution_convert_fusion.3 = bf16[2048,2048]{1,0:T(8,128)(2,1)S(1)} fusion(bf16[2048,2048]{1,0:T(8,128)(2,1)} %get-tuple-element.277, bf16[2048,2048]{1,0:T(8,128)(2,1)} %fusion.118), kind=kOutput, calls=%fused_computation.25 | convolution fusion | flops 17184063488 | bytes 25165824 | tf_op jit(solution)/shard_map/dot_general | solution.py:35
  421.2 22.1 %fusion.153 = f32[2048,2048]{1,0:T(8,128)} fusion(bf16[2048,2048]{1,0:T(8,128)(2,1)S(1)} %copy-done.135, bf16[2048,2048]{1,0:T(8,128)(2,1)} %param.20), kind=kOutput, calls=%fused_computation.506 | convolution fusion | flops 17179869184 | bytes 33554432 | tf_op jit(solution)/shard_map/dot_general | solution.py:31
  443.2 23.8 %add_convert_fusion = bf16[2048,2048]{1,0:T(8,128)(2,1)S(1)} fusion(f32[2048,2048]{1,0:T(8,128)} %fusion.153, bf16[2048,2048]{1,0:T(8,128)(2,1)} %get-tuple-element.270, bf16[2048,2048]{1,0:T(8,128)(2,1)} %param.21), kind=kOutput, calls=%fused_computation.17 | convolution fusion | flops 17188257792 | bytes 41943040 | tf_op jit(solution)/shard_map/dot_general | solution.py:31
  479.7 24.2 %convolution_convert_fusion.2 = bf16[2048,2048]{1,0:T(8,128)(2,1)} fusion(bf16[2048,2048]{1,0:T(8,128)(2,1)} %get-tuple-element.264, bf16[2048,2048]{1,0:T(8,128)(2,1)} %copy-done.119), kind=kOutput, calls=%fused_computation.24 | convolution fusion | flops 17184063488 | bytes 25165824 | tf_op jit(solution)/shard_map/dot_general | solution.py:35
  503.8 17.0 %collective-permute-done.36 = bf16[512,2048]{1,0:T(8,128)(2,1)S(1)} collective-permute-done((bf16[512,2048]{1,0:T(8,128)(2,1)S(1)}, bf16[512,2048]{1,0:T(8,128)(2,1)S(1)}, u32[]{:S(2)}, u32[]{:S(2)}) %collective-permute-start.36) | collective-permute-done | bytes 2097184 | tf_op jit(solution)/shard_map/ppermute | solution.py:512
  533.8 22.5 %convolution_convert_fusion.1 = bf16[2048,2048]{1,0:T(8,128)(2,1)S(1)} fusion(bf16[2048,2048]{1,0:T(8,128)(2,1)} %get-tuple-element.270, bf16[2048,2048]{1,0:T(8,128)(2,1)} %copy-done.119), kind=kOutput, calls=%fused_computation.23 | convolution fusion | flops 17184063488 | bytes 25165824 | tf_op jit(solution)/shard_map/dot_general | solution.py:35
  593.9 23.5 %convolution_convert_fusion = bf16[2048,2048]{1,0:T(8,128)(2,1)} fusion(bf16[2048,2048]{1,0:T(8,128)(2,1)} %get-tuple-element.277, bf16[2048,2048]{1,0:T(8,128)(2,1)} %param.22), kind=kOutput, calls=%fused_computation.22 | convolution fusion | flops 17184063488 | bytes 25165824 | tf_op jit(solution)/shard_map/dot_general | solution.py:31
  617.4 14.0 %collective-permute-done.44 = bf16[512,2048]{1,0:T(8,128)(2,1)S(1)} collective-permute-done((bf16[512,2048]{1,0:T(8,128)(2,1)}, bf16[512,2048]{1,0:T(8,128)(2,1)S(1)}, u32[]{:S(2)}, u32[]{:S(2)}) %collective-permute-start.44) | collective-permute-done | bytes 2097184 | tf_op jit(solution)/shard_map/ppermute | solution.py:512
  675.5 22.4 %collective-permute-done.52 = bf16[128,2048]{1,0:T(8,128)(2,1)S(1)} collective-permute-done((bf16[128,2048]{1,0:T(8,128)(2,1)S(1)}, bf16[128,2048]{1,0:T(8,128)(2,1)S(1)}, u32[]{:S(2)}, u32[]{:S(2)}) %collective-permute-start.52) | collective-permute-done | bytes 524320 | tf_op jit(solution)/shard_map/ppermute | solution.py:414
  724.7 23.8 %attention_backward.2 = (bf16[1024,512]{1,0:T(8,128)(2,1)S(1)}, bf16[1024,256]{1,0:T(8,128)(2,1)S(1)}) custom-call(s32[4]{0:T(128)S(1)} %iota_xor_fusion.order_ref, bf16[1024,512]{1,0:T(8,128)(2,1)S(1)} %convolution_convert_fusion.12.grad_ref, bf16[1024,512]{1,0:T(8,128)(2,1)} %copy-done.14, bf16[1024,256]{1,0:T(8,128)(2,1)S(1)} %get-tuple-element.299.kv_ref, ...), custom_call_target="tpu_custom_call" | custom-call | flops 20000000000 | bytes 12000000 | tf_op jit(solution)/shard_map/attention_backward/pallas_call | solution.py:338
  761.7 19.0 %collective-permute-done.58 = bf16[128,2048]{1,0:T(8,128)(2,1)S(1)} collective-permute-done((bf16[128,2048]{1,0:T(8,128)(2,1)S(1)}, bf16[128,2048]{1,0:T(8,128)(2,1)S(1)}, u32[]{:S(2)}, u32[]{:S(2)}) %collective-permute-start.58) | collective-permute-done | bytes 524320 | tf_op jit(solution)/shard_map/ppermute | solution.py:414
  801.2 23.8 %attention_backward.3 = (bf16[1024,512]{1,0:T(8,128)(2,1)S(1)}, bf16[1024,256]{1,0:T(8,128)(2,1)S(1)}) custom-call(s32[4]{0:T(128)S(1)} %iota_xor_fusion.order_ref, bf16[1024,512]{1,0:T(8,128)(2,1)S(1)} %convolution_convert_fusion.11.grad_ref, bf16[1024,512]{1,0:T(8,128)(2,1)} %copy-done.15, bf16[1024,256]{1,0:T(8,128)(2,1)S(1)} %copy-done.19, ...), custom_call_target="tpu_custom_call" | custom-call | flops 20000000000 | bytes 12000000 | tf_op jit(solution)/shard_map/attention_backward/pallas_call | solution.py:338
  1028.2 21.3 %collective-permute-done.85 = bf16[384,2048]{1,0:T(8,128)(2,1)S(1)} collective-permute-done((bf16[384,2048]{1,0:T(8,128)(2,1)}, bf16[384,2048]{1,0:T(8,128)(2,1)S(1)}, u32[]{:S(2)}, u32[]{:S(2)}) %collective-permute-start.85) | collective-permute-done | bytes 1572896 | tf_op jit(solution)/shard_map/ppermute | solution.py:512
  1058.7 13.8 %collective-permute-done.81 = f32[2,512]{1,0:T(2,128)S(1)} collective-permute-done((f32[2,512]{1,0:T(2,128)S(1)}, f32[2,512]{1,0:T(2,128)S(1)}, u32[]{:S(2)}, u32[]{:S(2)}) %collective-permute-start.81) | collective-permute-done | bytes 4128 | tf_op jit(solution)/shard_map/ppermute | solution.py:451
  1092.3 23.0 %collective-permute-done.89 = bf16[384,2048]{1,0:T(8,128)(2,1)S(1)} collective-permute-done((bf16[384,2048]{1,0:T(8,128)(2,1)S(1)}, bf16[384,2048]{1,0:T(8,128)(2,1)S(1)}, u32[]{:S(2)}, u32[]{:S(2)}) %collective-permute-start.89) | collective-permute-done | bytes 1572896 | tf_op jit(solution)/shard_map/ppermute | solution.py:512
  (714 shorter events, 600.1 us)
Async XLA Ops:
  67.6 44.7 %collective-permute-start.11 = (bf16[256,2048]{1,0:T(8,128)(2,1)}, bf16[256,2048]{1,0:T(8,128)(2,1)S(1)}, u32[]{:S(2)}, u32[]{:S(2)}) collective-permute-start(bf16[256,2048]{1,0:T(8,128)(2,1)} %get-tuple-element.278), channel_id=1, source_target_pairs={{0,8},{8,0},{16,24},{24,16},{1,9},{9,1},{17,25},{25,17},{2,10},{10... | collective-permute-start | bytes 3145736 | tf_op jit(solution)/shard_map/ppermute | solution.py:408
  112.7 45.0 %collective-permute-start.13 = (bf16[2,1,128,2048]{3,2,1,0:T(8,128)(2,1)S(1)}, bf16[2,1,128,2048]{3,2,1,0:T(8,128)(2,1)S(1)}, u32[]{:S(2)}, u32[]{:S(2)}) collective-permute-start(bf16[2,1,128,2048]{3,2,1,0:T(8,128)(2,1)S(1)} %pad_maximum_fusion.9), channel_id=1, source_target_pairs={{0,8},{8,0},{16,24},{24,16},{1,9},{9,1},{17,25},{25,17},{2,10},{10... | collective-permute-start | bytes 3145736 | tf_op jit(solution)/shard_map/ppermute | solution.py:425
  113.7 44.0 %collective-permute-start.14 = (bf16[2,1,128,2048]{3,2,1,0:T(8,128)(2,1)S(1)}, bf16[2,1,128,2048]{3,2,1,0:T(8,128)(2,1)S(1)}, u32[]{:S(2)}, u32[]{:S(2)}) collective-permute-start(bf16[2,1,128,2048]{3,2,1,0:T(8,128)(2,1)S(1)} %pad_maximum_fusion.10), channel_id=1, source_target_pairs={{0,16},{8,24},{16,0},{24,8},{1,17},{9,25},{17,1},{25,9},{2,18},{10... | collective-permute-start | bytes 3145736 | tf_op jit(solution)/shard_map/ppermute | solution.py:425
  419.6 47.5 %collective-permute-start.35 = (bf16[1024,2048]{1,0:T(8,128)(2,1)}, bf16[1024,2048]{1,0:T(8,128)(2,1)S(1)}, u32[]{:S(2)}, u32[]{:S(2)}) collective-permute-start(bf16[1024,2048]{1,0:T(8,128)(2,1)} %constant_dynamic-slice_fusion.7), channel_id=1, source_target_pairs={{0,1},{1,0},{2,3},{3,2},{4,5},{5,4},{6,7},{7,6},{8,9},{9,8},{10,11... | collective-permute-start | bytes 12582920 | tf_op jit(solution)/shard_map/ppermute | solution.py:466
  474.3 46.5 %collective-permute-start.36 = (bf16[512,2048]{1,0:T(8,128)(2,1)S(1)}, bf16[512,2048]{1,0:T(8,128)(2,1)S(1)}, u32[]{:S(2)}, u32[]{:S(2)}) collective-permute-start(bf16[512,2048]{1,0:T(8,128)(2,1)S(1)} %get-tuple-element.263), channel_id=1, source_target_pairs={{0,2},{1,3},{2,0},{3,1},{4,6},{5,7},{6,4},{7,5},{8,10},{9,11},{10,... | collective-permute-start | bytes 6291464 | tf_op jit(solution)/shard_map/ppermute | solution.py:512
  476.5 46.3 %collective-permute-start.37 = (bf16[2,2,128,2048]{3,2,1,0:T(8,128)(2,1)S(1)}, bf16[2,2,128,2048]{3,2,1,0:T(8,128)(2,1)S(1)}, u32[]{:S(2)}, u32[]{:S(2)}) collective-permute-start(bf16[2,2,128,2048]{3,2,1,0:T(8,128)(2,1)S(1)} %pad_maximum_fusion.5), channel_id=1, source_target_pairs={{0,8},{8,0},{16,24},{24,16},{1,9},{9,1},{17,25},{25,17},{2,10},{10... | collective-permute-start | bytes 6291464 | tf_op jit(solution)/shard_map/ppermute | solution.py:425
  477.8 46.1 %collective-permute-start.38 = (bf16[2,2,128,2048]{3,2,1,0:T(8,128)(2,1)S(1)}, bf16[2,2,128,2048]{3,2,1,0:T(8,128)(2,1)S(1)}, u32[]{:S(2)}, u32[]{:S(2)}) collective-permute-start(bf16[2,2,128,2048]{3,2,1,0:T(8,128)(2,1)S(1)} %pad_maximum_fusion.6), channel_id=1, source_target_pairs={{0,16},{8,24},{16,0},{24,8},{1,17},{9,25},{17,1},{25,9},{2,18},{10... | collective-permute-start | bytes 6291464 | tf_op jit(solution)/shard_map/ppermute | solution.py:425
  523.8 45.1 %collective-permute-start.39 = (bf16[512,2048]{1,0:T(8,128)(2,1)S(1)}, bf16[512,2048]{1,0:T(8,128)(2,1)S(1)}, u32[]{:S(2)}, u32[]{:S(2)}) collective-permute-start(bf16[512,2048]{1,0:T(8,128)(2,1)S(1)} %get-tuple-element.267), channel_id=1, source_target_pairs={{0,2},{1,3},{2,0},{3,1},{4,6},{5,7},{6,4},{7,5},{8,10},{9,11},{10,... | collective-permute-start | bytes 6291464 | tf_op jit(solution)/shard_map/ppermute | solution.py:512
  585.7 45.7 %collective-permute-start.44 = (bf16[512,2048]{1,0:T(8,128)(2,1)}, bf16[512,2048]{1,0:T(8,128)(2,1)S(1)}, u32[]{:S(2)}, u32[]{:S(2)}) collective-permute-start(bf16[512,2048]{1,0:T(8,128)(2,1)} %broadcast_select_fusion.15), channel_id=1, source_target_pairs={{0,2},{1,3},{2,0},{3,1},{4,6},{5,7},{6,4},{7,5},{8,10},{9,11},{10,... | collective-permute-start | bytes 6291464 | tf_op jit(solution)/shard_map/ppermute | solution.py:512
  593.9 74.2 %collective-permute-start.50 = (bf16[1024,2048]{1,0:T(8,128)(2,1)}, bf16[1024,2048]{1,0:T(8,128)(2,1)}, u32[]{:S(2)}, u32[]{:S(2)}) collective-permute-start(bf16[1024,2048]{1,0:T(8,128)(2,1)} %constant_dynamic-slice_fusion.5), channel_id=1, source_target_pairs={{0,1},{1,0},{2,3},{3,2},{4,5},{5,4},{6,7},{7,6},{8,9},{9,8},{10,11... | collective-permute-start | bytes 12582920 | tf_op jit(solution)/shard_map/ppermute | solution.py:466
  638.6 59.3 %collective-permute-start.48 = (bf16[512,2048]{1,0:T(8,128)(2,1)}, bf16[512,2048]{1,0:T(8,128)(2,1)}, u32[]{:S(2)}, u32[]{:S(2)}) collective-permute-start(bf16[512,2048]{1,0:T(8,128)(2,1)} %broadcast_select_fusion.14), channel_id=1, source_target_pairs={{0,2},{1,3},{2,0},{3,1},{4,6},{5,7},{6,4},{7,5},{8,10},{9,11},{10,... | collective-permute-start | bytes 6291464 | tf_op jit(solution)/shard_map/ppermute | solution.py:512
  643.0 54.9 %collective-permute-start.49 = (bf16[512,2048]{1,0:T(8,128)(2,1)}, bf16[512,2048]{1,0:T(8,128)(2,1)}, u32[]{:S(2)}, u32[]{:S(2)}) collective-permute-start(bf16[512,2048]{1,0:T(8,128)(2,1)} %add_convert_fusion.11), channel_id=1, source_target_pairs={{2,4},{3,5},{4,2},{5,3},{10,12},{11,13},{12,10},{13,11},{18,20},{1... | collective-permute-start | bytes 6291464 | tf_op jit(solution)/shard_map/ppermute | solution.py:500
  703.1 77.6 %collective-permute-start.55 = (bf16[512,2048]{1,0:T(8,128)(2,1)}, bf16[512,2048]{1,0:T(8,128)(2,1)S(1)}, u32[]{:S(2)}, u32[]{:S(2)}) collective-permute-start(bf16[512,2048]{1,0:T(8,128)(2,1)} %broadcast_select_fusion.13), channel_id=1, source_target_pairs={{0,2},{1,3},{2,0},{3,1},{4,6},{5,7},{6,4},{7,5},{8,10},{9,11},{10,... | collective-permute-start | bytes 6291464 | tf_op jit(solution)/shard_map/ppermute | solution.py:512
  707.2 73.5 %collective-permute-start.56 = (bf16[512,2048]{1,0:T(8,128)(2,1)S(1)}, bf16[512,2048]{1,0:T(8,128)(2,1)}, u32[]{:S(2)}, u32[]{:S(2)}) collective-permute-start(bf16[512,2048]{1,0:T(8,128)(2,1)S(1)} %add_convert_fusion.7), channel_id=1, source_target_pairs={{2,4},{3,5},{4,2},{5,3},{10,12},{11,13},{12,10},{13,11},{18,20},{1... | collective-permute-start | bytes 6291464 | tf_op jit(solution)/shard_map/ppermute | solution.py:500
  721.3 59.5 %collective-permute-start.59 = (bf16[2,2,128,2048]{3,2,1,0:T(8,128)(2,1)}, bf16[2,2,128,2048]{3,2,1,0:T(8,128)(2,1)}, u32[]{:S(2)}, u32[]{:S(2)}) collective-permute-start(bf16[2,2,128,2048]{3,2,1,0:T(8,128)(2,1)} %pad_maximum_fusion.7), channel_id=1, source_target_pairs={{0,8},{8,0},{16,24},{24,16},{1,9},{9,1},{17,25},{25,17},{2,10},{10... | collective-permute-start | bytes 6291464 | tf_op jit(solution)/shard_map/ppermute | solution.py:425
  724.4 56.4 %collective-permute-start.60 = (bf16[2,2,128,2048]{3,2,1,0:T(8,128)(2,1)}, bf16[2,2,128,2048]{3,2,1,0:T(8,128)(2,1)}, u32[]{:S(2)}, u32[]{:S(2)}) collective-permute-start(bf16[2,2,128,2048]{3,2,1,0:T(8,128)(2,1)} %pad_maximum_fusion.8), channel_id=1, source_target_pairs={{0,16},{8,24},{16,0},{24,8},{1,17},{9,25},{17,1},{25,9},{2,18},{10... | collective-permute-start | bytes 6291464 | tf_op jit(solution)/shard_map/ppermute | solution.py:425
  780.7 66.0 %collective-permute-start.97 = (bf16[512,2048]{1,0:T(8,128)(2,1)S(1)}, bf16[512,2048]{1,0:T(8,128)(2,1)S(1)}, u32[]{:S(2)}, u32[]{:S(2)}) collective-permute-start(bf16[512,2048]{1,0:T(8,128)(2,1)S(1)} %broadcast_select_fusion.6), channel_id=1, source_target_pairs={{0,1},{1,0},{2,3},{3,2},{4,5},{5,4},{6,7},{7,6},{8,9},{9,8},{10,11... | collective-permute-start | bytes 6291464 | tf_op jit(solution)/shard_map/ppermute | solution.py:496
  785.1 105.8 %collective-permute-start.61 = (bf16[512,2048]{1,0:T(8,128)(2,1)}, bf16[512,2048]{1,0:T(8,128)(2,1)}, u32[]{:S(2)}, u32[]{:S(2)}) collective-permute-start(bf16[512,2048]{1,0:T(8,128)(2,1)} %broadcast_select_fusion.12), channel_id=1, source_target_pairs={{0,2},{1,3},{2,0},{3,1},{4,6},{5,7},{6,4},{7,5},{8,10},{9,11},{10,... | collective-permute-start | bytes 6291464 | tf_op jit(solution)/shard_map/ppermute | solution.py:512
  788.9 102.0 %collective-permute-start.62 = (bf16[512,2048]{1,0:T(8,128)(2,1)}, bf16[512,2048]{1,0:T(8,128)(2,1)}, u32[]{:S(2)}, u32[]{:S(2)}) collective-permute-start(bf16[512,2048]{1,0:T(8,128)(2,1)} %add_convert_fusion.4), channel_id=1, source_target_pairs={{2,4},{3,5},{4,2},{5,3},{10,12},{11,13},{12,10},{13,11},{18,20},{1... | collective-permute-start | bytes 6291464 | tf_op jit(solution)/shard_map/ppermute | solution.py:500
  829.3 48.2 %collective-permute-start.64 = (bf16[2,1,128,2048]{3,2,1,0:T(8,128)(2,1)}, bf16[2,1,128,2048]{3,2,1,0:T(8,128)(2,1)}, u32[]{:S(2)}, u32[]{:S(2)}) collective-permute-start(bf16[2,1,128,2048]{3,2,1,0:T(8,128)(2,1)} %pad_maximum_fusion.14), channel_id=1, source_target_pairs={{0,16},{8,24},{16,0},{24,8},{1,17},{9,25},{17,1},{25,9},{2,18},{10... | collective-permute-start | bytes 3145736 | tf_op jit(solution)/shard_map/ppermute | solution.py:425
  893.9 46.1 %collective-permute-start.67 = (bf16[512,2048]{1,0:T(8,128)(2,1)S(1)}, bf16[512,2048]{1,0:T(8,128)(2,1)S(1)}, u32[]{:S(2)}, u32[]{:S(2)}) collective-permute-start(bf16[512,2048]{1,0:T(8,128)(2,1)S(1)} %add_convert_fusion.2), channel_id=1, source_target_pairs={{0,2},{1,3},{2,0},{3,1},{4,6},{5,7},{6,4},{7,5},{8,10},{9,11},{10,... | collective-permute-start | bytes 6291464 | tf_op jit(solution)/shard_map/ppermute | solution.py:512
  943.8 50.0 %collective-permute-start.73 = (bf16[512,2048]{1,0:T(8,128)(2,1)}, bf16[512,2048]{1,0:T(8,128)(2,1)}, u32[]{:S(2)}, u32[]{:S(2)}) collective-permute-start(bf16[512,2048]{1,0:T(8,128)(2,1)} %add_convert_fusion.1), channel_id=1, source_target_pairs={{0,2},{1,3},{2,0},{3,1},{4,6},{5,7},{6,4},{7,5},{8,10},{9,11},{10,... | collective-permute-start | bytes 6291464 | tf_op jit(solution)/shard_map/ppermute | solution.py:512
  982.9 92.3 %collective-permute-start.94 = (bf16[512,2048]{1,0:T(8,128)(2,1)}, bf16[512,2048]{1,0:T(8,128)(2,1)}, u32[]{:S(2)}, u32[]{:S(2)}) collective-permute-start(bf16[512,2048]{1,0:T(8,128)(2,1)} %broadcast_select_fusion.9), channel_id=1, source_target_pairs={{0,1},{1,0},{2,3},{3,2},{4,5},{5,4},{6,7},{7,6},{8,9},{9,8},{10,11... | collective-permute-start | bytes 6291464 | tf_op jit(solution)/shard_map/ppermute | solution.py:496
  1027.5 58.3 %collective-permute-start.95 = (bf16[512,2048]{1,0:T(8,128)(2,1)S(1)}, bf16[512,2048]{1,0:T(8,128)(2,1)S(1)}, u32[]{:S(2)}, u32[]{:S(2)}) collective-permute-start(bf16[512,2048]{1,0:T(8,128)(2,1)S(1)} %broadcast_select_fusion.8), channel_id=1, source_target_pairs={{0,1},{1,0},{2,3},{3,2},{4,5},{5,4},{6,7},{7,6},{8,9},{9,8},{10,11... | collective-permute-start | bytes 6291464 | tf_op jit(solution)/shard_map/ppermute | solution.py:496
  (212 other events, 4107.3 us)

commit v2 on v1

--- a/solution.py
+++ b/solution.py
@@ -375,6 +375,56 @@
     return lax.optimization_barrier(values)
 
 
+def assemble(where, chunks):
+    rows, width = chunks[0][0].shape
+    block = math.gcd(rows, 128)
+    each = rows // block
+    half = each * len(chunks)
+
+    def source(c, k):
+        def index(i, where):
+            local = jnp.clip(i - (k // 2) * half - c * each, 0, each - 1)
+            chosen = where[1] == (1 if k % 2 == 0 else 0)
+            return (jnp.where(chosen, local, 0), 0)
+
+        return pl.BlockSpec((block, width), index)
+
+    def target(i, where):
+        own = i < half
+        return (jnp.where(own, where[0] * half + i, (1 - where[0]) * half + i - half), 0)
+
+    def kernel(where_ref, *refs):
+        i = pl.program_id(0)
+        out = refs[-1]
+        for c in range(len(chunks)):
+            for k in range(4):
+                begin = (k // 2) * half + c * each
+
+                @pl.when(
+                    (i >= begin)
+                    & (i < begin + each)
+                    & (where_ref[1] == (1 if k % 2 == 0 else 0))
+                )
+                def _(ref=refs[4 * c + k]):
+                    out[...] = ref[...].astype(F32)
+
+    return pl.pallas_call(
+        kernel,
+        grid_spec=pltpu.PrefetchScalarGridSpec(
+            num_scalar_prefetch=1,
+            grid=(2 * half,),
+            in_specs=[source(c, k) for c in range(len(chunks)) for k in range(4)],
+            out_specs=pl.BlockSpec((block, width), target),
+        ),
+        out_shape=jax.ShapeDtypeStruct((2 * half * block, width), F32),
+        compiler_params=pltpu.CompilerParams(vmem_limit_bytes=40 << 20),
+        cost_estimate=pl.CostEstimate(
+            flops=0, bytes_accessed=12 * half * block * width, transcendentals=0
+        ),
+        name="assemble",
+    )(where, *[array for chunk in chunks for array in chunk])
+
+
 class Square:
     def __init__(self, shard, replica):
         self.shard, self.replica = shard, replica
@@ -383,7 +433,8 @@
         self.d = [(i, i ^ 3) for i in range(shard)]
         self.core = [(i, i ^ 1) for i in range(replica)]
         both = lambda pairs: [(2 * a + c, 2 * b + c) for a, b in pairs for c in range(2)]
-        self.outer = both([(0, 1), (1, 0), (2, 3), (3, 2)])
+        self.inward = both([(0, 1), (3, 2)])
+        self.outward = both([(1, 0), (2, 3)])
         self.middle = both([(1, 2), (2, 1)])
 
     def order(self):
@@ -452,11 +503,10 @@
         return total
 
     def start_line(self):
-        self.entering = []
         self.waiting = []
-        self.outer_flight = None
+        self.inward_flight = None
         self.middle_flight = None
-        self.wholes = None
+        self.outward_flight = None
         self.finals = {}
 
     def feed(self, name, grad, chunks):
@@ -469,59 +519,43 @@
         for c in range(chunks):
             keep = lax.dynamic_slice_in_dim(grad, core * half + c * rows, rows, 0)
             mine = keep.astype(F32) + got[c * rows : (c + 1) * rows].astype(F32)
-            self.waiting.append((name, c, mine.astype(BF16)))
-
-    def busy(self):
-        return any(v is not None for v in (self.outer_flight, self.middle_flight, self.wholes)) or bool(
-            self.waiting
+            self.waiting.append(((name, c), mine.astype(BF16)))
+
+    def tick(self, *values):
+        flying = (self.inward_flight, self.middle_flight, self.outward_flight)
+        chunk = self.waiting.pop(0) if self.waiting else None
+        landed, mine, values = sync(
+            tuple(f and f[-1] for f in flying), None if chunk is None else chunk[1], values
         )
-
-    def tick(self, *values):
-        place = lax.axis_index("replica") // 2
-        inner = (place == 1) | (place == 2)
-        outer, middle = self.outer_flight, self.middle_flight
-        flights = (outer and outer[2], middle and middle[2])
-        chunk = self.waiting.pop(0) if self.waiting else None
-        flights, mine, values = sync(flights, chunk and chunk[2], values)
         add = lambda a, b: (a.astype(F32) + b.astype(F32)).astype(BF16)
-        whole = None
-        if middle is not None:
-            whole = (middle[0], add(middle[1], flights[1]))
-        self.middle_flight = None
-        if outer is not None:
-            entered, left, _ = outer
-            if left is not None:
-                (name, c), value = left
-                final = jnp.where(inner, value, flights[0][: value.shape[0]])
-                self.finals[name][c] = (final, lax.ppermute(final, "replica", self.core))
-            if entered is not None:
-                key, own = entered
-                pair = add(own, flights[0][: own.shape[0]])
-                self.middle_flight = (key, pair, lax.ppermute(pair, "replica", self.middle))
-        self.outer_flight = None
-        if chunk is not None or whole is not None:
-            entering = None if chunk is None else ((chunk[0], chunk[1]), mine)
-            if entering is None:
-                send = whole[1]
-            elif whole is None:
-                send = mine
-            else:
-                rows = max(mine.shape[0], whole[1].shape[0])
-                pad = lambda v: jnp.pad(v, ((0, rows - v.shape[0]), (0, 0)))
-                send = jnp.where(inner, pad(whole[1]), pad(mine))
-            self.outer_flight = (entering, whole, lax.ppermute(send, "replica", self.outer))
+        move = lambda v, perm: lax.ppermute(v, "replica", perm)
+        self.inward_flight = self.middle_flight = self.outward_flight = None
+        if flying[0] is not None:
+            pair = add(flying[0][1], landed[0])
+            self.middle_flight = (flying[0][0], pair, move(pair, self.middle))
+        if flying[1] is not None:
+            whole = add(flying[1][1], landed[1])
+            self.outward_flight = (flying[1][0], whole, move(whole, self.outward))
+        if flying[2] is not None:
+            (name, c), whole, _ = flying[2]
+            self.finals[name][c] = (
+                whole,
+                landed[2],
+                move(whole, self.core),
+                move(landed[2], self.core),
+            )
+        if chunk is not None:
+            self.inward_flight = (chunk[0], mine, move(mine, self.inward))
         return values
 
     def finish(self, name):
-        mine = jnp.concatenate([f for f, _ in self.finals[name]], axis=0)
-        other = jnp.concatenate([o for _, o in self.finals[name]], axis=0)
-        first = lax.axis_index("replica") % 2 == 0
-        return jnp.concatenate(
-            [jnp.where(first, mine, other), jnp.where(first, other, mine)], axis=0
-        ).astype(F32)
+        place = lax.axis_index("replica")
+        z = place // 2
+        inner = ((z == 1) | (z == 2)).astype(jnp.int32)
+        return assemble(jnp.stack([place % 2, inner]), self.finals[name])
 
     def drain(self):
-        while self.waiting or self.outer_flight is not None or self.middle_flight is not None:
+        while self.waiting or self.inward_flight or self.middle_flight or self.outward_flight:
             self.tick()
 
 
@@ -637,11 +671,14 @@
 
     normed_all, saved = [], []
 
-    def attention(t, pieces):
+    def project(pieces):
         normed = jnp.concatenate([normalized(piece, gain_first) for piece in pieces], axis=0)
         normed_all.append(normed)
+        return dot_nt(normed, w_qkv)
+
+    def attention(t, qkv):
         attended, query, kv, lse = attention_forward(
-            order, dot_nt(normed, w_qkv), *tables[t], *masks[t], q_width, shard
+            order, qkv, *tables[t], *masks[t], q_width, shard
         )
         saved.append((attended, query, kv, lse))
         return dot_nn(attended, w_out).astype(BF16)
@@ -657,27 +694,30 @@
 
     pieces_1 = links.gather_second(token_rows[1], got)
     cot_got = links.gather_first(cot_rows[0])
-    part_0 = attention(0, pieces_0)
+    part_0 = attention(0, project(pieces_0))
     part_0, pieces_1, cot_got = sync(part_0, pieces_1, cot_got)
 
     got_0 = links.sum_first(part_0)
+    qkv_1 = project(pieces_1)
+    got_0, qkv_1, cot_got = sync(got_0, qkv_1, cot_got)
+
+    last_0 = links.sum_second(part_0, got_0)
     cot_pieces_0 = links.gather_second(cot_rows[0], cot_got)
-    part_1 = attention(1, pieces_1)
-    got_0, cot_pieces_0, part_1 = sync(got_0, cot_pieces_0, part_1)
-
-    last_0 = links.sum_second(part_0, got_0)
+    part_1 = attention(1, qkv_1)
+    last_0, part_1 = sync(last_0, part_1)
+
     got_1 = links.sum_first(part_1)
-    last_0, got_1 = sync(last_0, got_1)
-
     middle_0, scale_0, own_0 = after_attention(0, links.sum_last(part_0, got_0, last_0)[0])
+    ff_got_0 = links.gather_first(own_0)
+    got_1, own_0 = sync(got_1, own_0)
+
     last_1 = links.sum_second(part_1, got_1)
-    ff_got_0 = links.gather_first(own_0)
-    ff_got_0, last_1 = sync(ff_got_0, last_1)
-
+    last_1, ff_got_0 = sync(last_1, ff_got_0)
+
+    ff_pieces_0 = links.gather_second(own_0, ff_got_0)
     middle_1, scale_1, own_1 = after_attention(1, links.sum_last(part_1, got_1, last_1)[0])
-    ff_pieces_0 = links.gather_second(own_0, ff_got_0)
     ff_got_1 = links.gather_first(own_1)
-    ff_pieces_0, ff_got_1 = sync(ff_pieces_0, ff_got_1)
+    ff_pieces_0, ff_got_1, own_1, cot_pieces_0 = sync(ff_pieces_0, ff_got_1, own_1, cot_pieces_0)
     ff_pieces_1 = links.gather_second(own_1, ff_got_1)
     ff_pieces_0, ff_pieces_1, cot_rows, cot_pieces_0 = sync(
         ff_pieces_0, ff_pieces_1, cot_rows, cot_pieces_0
@@ -696,6 +736,9 @@
     cot_all = jnp.concatenate(
         [(RESIDUAL * piece.astype(F32)).astype(BF16) for piece in cot_pieces_0 + cot_pieces_1], axis=0
     )
+    grad_down = dot_tn(hidden, cot_all).astype(BF16)
+    grad_down, hidden, cot_all, gate, upper = sync(grad_down, hidden, cot_all, gate, upper)
+    links.feed("down", grad_down, 4)
     hidden_grad = dot_nt(cot_all, w_down)
     wide = gate.astype(F32)
     sigma = jax.nn.sigmoid(wide)
@@ -703,22 +746,21 @@
         hidden_grad * upper.astype(F32) * sigma * (1.0 + wide * (1.0 - sigma))
     ).astype(BF16)
     up_grad = (hidden_grad * wide * sigma).astype(BF16)
-    gate_grad, up_grad, hidden, cot_all = sync(gate_grad, up_grad, hidden, cot_all)
-
-    grad_down = dot_tn(hidden, cot_all).astype(BF16)
-    grad_down, gate_grad, up_grad = sync(grad_down, gate_grad, up_grad)
-    links.feed("down", grad_down, 2)
-    ff_part = (dot_nn(gate_grad, w_gate) + dot_nn(up_grad, w_up)).astype(BF16)
+    gate_grad, up_grad, hidden = links.tick(gate_grad, up_grad, hidden)
+
+    half_part = dot_nn(gate_grad, w_gate)
+    half_part, gate_grad, up_grad = links.tick(half_part, gate_grad, up_grad)
+    ff_part = (half_part + dot_nn(up_grad, w_up)).astype(BF16)
     ff_part, gate_grad, up_grad, hidden = links.tick(ff_part, gate_grad, up_grad, hidden)
 
     ff_sum = links.sum_first(ff_part)
     grad_gate = dot_tn(gate_grad, rows_all).astype(BF16)
     grad_gate, up_grad, ff_sum = links.tick(grad_gate, up_grad, ff_sum)
-    links.feed("gate", grad_gate, 2)
+    links.feed("gate", grad_gate, 4)
     ff_last = links.sum_second(ff_part, ff_sum)
     grad_up = dot_tn(up_grad, rows_all).astype(BF16)
     grad_up, hidden, ff_last = links.tick(grad_up, hidden, ff_last)
-    links.feed("up", grad_up, 2)
+    links.feed("up", grad_up, 4)
 
     ff_grad = links.sum_last(ff_part, ff_sum, ff_last)
     out_own, middle_grads = [], []
@@ -728,6 +770,7 @@
         gain_ff_sum = gain_ff_sum + term
         middle_grads.append(cot_rows[t].astype(F32) + middle_back)
         out_own.append((RESIDUAL * middle_grads[t]).astype(BF16))
+    out_own, hidden = links.tick(out_own, hidden)
     out_got_0 = links.gather_first(out_own[0])
     down_part = dot_nn(hidden, w_down).astype(BF16)
     down_part, out_got_0, out_own = links.tick(down_part, out_got_0, out_own)
@@ -743,6 +786,7 @@
             order, attended_grad, query, kv, lse, *tables[t], *masks[t], shard
         )
         qkv_grad = jnp.concatenate([dq, dkv], axis=1)
+        (qkv_grad,) = links.tick(qkv_grad)
         return qkv_grad, dot_nn(qkv_grad, w_qkv).astype(BF16)
 
     out_pieces_1 = links.gather_second(out_own[1], out_got_1)
@@ -765,14 +809,13 @@
     normed_sum_1 = links.sum_first(normed_part_1)
     attended_all = jnp.concatenate([saved[t][0] for t in range(trees)], axis=0)
     grad_out = dot_tn(attended_all, jnp.concatenate([out_all_0, out_all_1], axis=0)).astype(BF16)
+    grad_out, qkv_grad_0, qkv_grad_1 = links.tick(grad_out, qkv_grad_0, qkv_grad_1)
+    links.feed("out", grad_out, 1)
     grad_qkv = dot_tn(
         jnp.concatenate([qkv_grad_0, qkv_grad_1], axis=0), jnp.concatenate(normed_all, axis=0)
     ).astype(BF16)
-    grad_out, grad_qkv, normed_last_0, normed_sum_1 = links.tick(
-        grad_out, grad_qkv, normed_last_0, normed_sum_1
-    )
-    links.feed("out", grad_out, 1)
-    links.feed("qkv", grad_qkv, 1)
+    grad_qkv, normed_last_0, normed_sum_1 = links.tick(grad_qkv, normed_last_0, normed_sum_1)
+    links.feed("qkv", grad_qkv, 2)
 
     normed_last_1 = links.sum_second(normed_part_1, normed_sum_1)
     down = links.sum_last(down_part, down_sum, down_last)

time: 1150 us -> 1240 us (1.078)
  starting transfers between devices: 118 us -> 215 us
  other arithmetic: 242 us -> 172 us
  Pallas kernels: 82.7 us -> 137 us
    ppermute x28 -> x75, starting transfers between devices: 40.8 us -> 146 us  [tick(): move = lambda v, perm: lax.ppermute(v, 'replica', perm)]
    pallas_call x0 -> x5, Pallas kernels: none -> 54.3 us  [assemble(): pl.pallas_call(kernel, grid_spec=pltpu.PrefetchScalarGridSpec(num_scalar_...]
    select_n x17 -> x0, other arithmetic: 52.3 us -> none  [the longest x5 19.1 us: finish(): jnp.where(first, mine, other)]
    ppermute x6, waiting for transfers between devices: 54.7 us -> 6.17 us  [sum_second(): lax.ppermute(next_y, 'shard', self.y)]
    ppermute x8, waiting for transfers between devices: 0.02 us -> 38.8 us  [gather_first(): lax.ppermute(own, 'shard', self.x)]
    ppermute x6, waiting for transfers between devices: 1.7 us -> 35.3 us  [sum_first(): lax.ppermute(send_y, 'shard', self.y)]
    convert_element_type x10 -> x6, other arithmetic: 67 us -> 35.2 us  [the longest x5 23.3 us: feed(): self.waiting.append(((name, c), mine.astype(BF16)))]
    ppermute x8, waiting for transfers between devices: 47.1 us -> 18.5 us  [gather_second(): second = lax.ppermute(from_x[half:], 'shard', self.y)]
  transfers between devices with their start and end apart: 98 -> 145, of which waited for: 28 -> 41; matrix products, arithmetic and copies ran while one was open for 42% -> 32% of each run, Pallas kernels for 7% -> 11%
where the time goes in v2:
time: 1240 us; the launch traced here: 1230 us
  waiting for transfers between devices  335 us (27%)
  matrix products  269 us (22%)
  starting transfers between devices  215 us (17%)
  other arithmetic  172 us (14%)
  Pallas kernels  137 us (11%)
  local copies, waits for them, and re-layouts  93.5 us (8%)
    ppermute x75, starting transfers between devices, tick(): move = lambda v, perm: lax.ppermute(v, 'replica', perm)  146 us
    ppermute x75, waiting for transfers between devices, tick(): move = lambda v, perm: lax.ppermute(v, 'replica', perm)  113 us
    dot_general x7, matrix products, dot_nt(): lax.dot_general(left, right, (((1,), (1,)), ((), ())), preferred_element_...  99.9 us
    dot_general x5, matrix products, dot_tn(): lax.dot_general(left, right, (((0,), (0,)), ((), ())), preferred_element_...  84.9 us
    dot_general x9, matrix products, dot_nn(): lax.dot_general(left, right, (((1,), (0,)), ((), ())), preferred_element_...  84.4 us
    ppermute x8, waiting for transfers between devices, gather_second(): first = lax.ppermute(from_y[:half], 'shard', self.x)  83.7 us
    unnamed x460, local copies, waits for them, and re-layouts  58 us
    pallas_call x5, Pallas kernels, assemble(): pl.pallas_call(kernel, grid_spec=pltpu.PrefetchScalarGridSpec(num_scalar_...  54.3 us
  transfers between devices with their start and end apart: 145, of which 41 were waited for; matrix products, arithmetic and copies ran while one was open for 32% of the time, Pallas kernels for 11%

profile of v2, /device:TPU:0, one launch (start us, length us, event | category | flops | bytes accessed | tf_op | source)
XLA Modules:
  0.0 1226.2 jit_solution(15677909883224090841)
XLA Ops:
  18.6 16.0 %collective-permute-done = bf16[256,2048]{1,0:T(8,128)(2,1)} collective-permute-done((bf16[256,2048]{1,0:T(8,128)(2,1)}, bf16[256,2048]{1,0:T(8,128)(2,1)}, u32[]{:S(2)}, u32[]{:S(2)}) %collective-permute-start) | collective-permute-done | bytes 1048608 | tf_op jit(solution)/shard_map/ppermute | solution.py:459
  52.6 17.7 %collective-permute-done.5 = bf16[128,2048]{1,0:T(8,128)(2,1)} collective-permute-done((bf16[128,2048]{1,0:T(8,128)(2,1)}, bf16[128,2048]{1,0:T(8,128)(2,1)}, u32[]{:S(2)}, u32[]{:S(2)}) %collective-permute-start.5) | collective-permute-done | bytes 524320 | tf_op jit(solution)/shard_map/ppermute | solution.py:464
  96.8 17.7 %attention_forward.2 = (bf16[1024,512]{1,0:T(8,128)(2,1)S(1)}, bf16[1024,512]{1,0:T(8,128)(2,1)S(1)}, bf16[1024,256]{1,0:T(8,128)(2,1)S(1)}, f32[1024,128]{1,0:T(8,128)S(1)}) custom-call(s32[4]{0:T(128)S(1)} %iota_xor_fusion.order_ref, f32[1024,768]{1,0:T(8,128)S(1)} %fusion.160.q_ref.kv_ref, f32[1024,768]{1,0:T(8,128)S(1)} %fusion.160.q_ref.kv_ref, ...), custom_call_target="tpu_custom_call" | custom-call | flops 10000000000 | bytes 12000000 | tf_op jit(solution)/shard_map/attention_forward/pallas_call | solution.py:186
  147.9 17.6 %attention_forward.3 = (bf16[1024,512]{1,0:T(8,128)(2,1)S(1)}, bf16[1024,512]{1,0:T(8,128)(2,1)S(1)}, bf16[1024,256]{1,0:T(8,128)(2,1)S(1)}, f32[1024,128]{1,0:T(8,128)S(1)}) custom-call(s32[4]{0:T(128)S(1)} %iota_xor_fusion.order_ref, f32[1024,768]{1,0:T(8,128)S(1)} %fusion.161.q_ref.kv_ref, f32[1024,768]{1,0:T(8,128)S(1)} %fusion.161.q_ref.kv_ref, ...), custom_call_target="tpu_custom_call" | custom-call | flops 10000000000 | bytes 12000000 | tf_op jit(solution)/shard_map/attention_forward/pallas_call | solution.py:186
  177.1 18.6 %collective-permute-done.18 = bf16[2,1,128,2048]{3,2,1,0:T(8,128)(2,1)S(1)} collective-permute-done((bf16[2,1,128,2048]{3,2,1,0:T(8,128)(2,1)S(1)}, bf16[2,1,128,2048]{3,2,1,0:T(8,128)(2,1)S(1)}, u32[]{:S(2)}, u32[]{:S(2)}) %collective-permute-start.18) | collective-permute-done | bytes 1048608 | tf_op jit(solution)/shard_map/ppermute | solution.py:476
  200.5 19.8 %collective-permute-done.21 = bf16[256,2048]{1,0:T(8,128)(2,1)S(1)} collective-permute-done((bf16[256,2048]{1,0:T(8,128)(2,1)S(1)}, bf16[256,2048]{1,0:T(8,128)(2,1)S(1)}, u32[]{:S(2)}, u32[]{:S(2)}) %collective-permute-start.21) | collective-permute-done | bytes 1048608 | tf_op jit(solution)/shard_map/ppermute | solution.py:459
  242.9 16.7 %collective-permute-done.28 = bf16[128,2048]{1,0:T(8,128)(2,1)S(1)} collective-permute-done((bf16[128,2048]{1,0:T(8,128)(2,1)S(1)}, bf16[128,2048]{1,0:T(8,128)(2,1)S(1)}, u32[]{:S(2)}, u32[]{:S(2)}) %collective-permute-start.28) | collective-permute-done | bytes 524320 | tf_op jit(solution)/shard_map/ppermute | solution.py:465
  299.8 24.8 %convolution_convert_fusion.4 = bf16[2048,2048]{1,0:T(8,128)(2,1)} fusion(bf16[2048,2048]{1,0:T(8,128)(2,1)S(1)} %constant_dynamic-update-slice_fusion.3, bf16[2048,2048]{1,0:T(8,128)(2,1)} %param.20), kind=kOutput, calls=%fused_computation.23 | convolution fusion | flops 17184063488 | bytes 25165824 | tf_op jit(solution)/shard_map/dot_general | solution.py:27
  331.7 27.5 %fusion.157 = (bf16[2048,2048]{1,0:T(8,128)(2,1)}, bf16[2048,2048]{1,0:T(8,128)(2,1)}) fusion(bf16[2048,2048]{1,0:T(8,128)(2,1)} %convolution_convert_fusion.4, bf16[2048,2048]{1,0:T(8,128)(2,1)} %copy-done.198, bf16[2048,2048]{1,0:T(8,128)(2,1)} %param.21), kind=kOutput, calls=%fused_computation.484 | convolution fusion | flops 17213423616 | bytes 41943040 | tf_op jit(solution)/shard_map/dot_general | solution.py:27
  368.2 22.5 %convolution_convert_fusion.3 = bf16[2048,2048]{1,0:T(8,128)(2,1)S(1)} fusion(bf16[2048,2048]{1,0:T(8,128)(2,1)} %get-tuple-element.347, bf16[2048,2048]{1,0:T(8,128)(2,1)} %fusion.118), kind=kOutput, calls=%fused_computation.22 | convolution fusion | flops 17184063488 | bytes 25165824 | tf_op jit(solution)/shard_map/dot_general | solution.py:35
  395.3 32.1 %fusion.11 = (bf16[2048,2048]{1,0:T(8,128)(2,1)}, bf16[2048,2048]{1,0:T(8,128)(2,1)}) fusion(bf16[2048,2048]{1,0:T(8,128)(2,1)} %convolution_convert_fusion.4, bf16[2048,2048]{1,0:T(8,128)(2,1)} %get-tuple-element.311, bf16[2048,2048]{1,0:T(8,128)(2,1)} %fusion.118, bf16[2048,2048]{1,0:T(8,128)(2,1)} %param.22), kind=kOutput, calls=%fused_computation.16 | convolution fusion | flops 17242783744 | bytes 50331648 | tf_op jit(solution)/shard_map/dot_general | solution.py:27
  436.8 24.9 %fusion.162 = f32[2048,2048]{1,0:T(8,128)} fusion(bf16[2048,2048]{1,0:T(8,128)(2,1)} %get-tuple-element.326, bf16[2048,2048]{1,0:T(8,128)(2,1)} %param.20), kind=kOutput, calls=%fused_computation.489 | convolution fusion | flops 17179869184 | bytes 33554432 | tf_op jit(solution)/shard_map/dot_general | solution.py:31
  461.7 20.6 %fusion.163 = f32[2048,2048]{1,0:T(8,128)} fusion(bf16[2048,2048]{1,0:T(8,128)(2,1)S(1)} %bitcast.473, bf16[2048,2048]{1,0:T(8,128)(2,1)S(1)} %bitcast.471), kind=kOutput, calls=%fused_computation.490 | convolution fusion | flops 17179869184 | bytes 33554432 | tf_op jit(solution)/shard_map/dot_general | solution.py:31
  524.8 22.4 %convolution_convert_fusion.2 = bf16[2048,2048]{1,0:T(8,128)(2,1)S(1)} fusion(bf16[2048,2048]{1,0:T(8,128)(2,1)} %get-tuple-element.326, bf16[2048,2048]{1,0:T(8,128)(2,1)} %copy-done.198), kind=kOutput, calls=%fused_computation.21 | convolution fusion | flops 17184063488 | bytes 25165824 | tf_op jit(solution)/shard_map/dot_general | solution.py:35
  580.2 22.5 %convolution_convert_fusion.1 = bf16[2048,2048]{1,0:T(8,128)(2,1)S(1)} fusion(bf16[2048,2048]{1,0:T(8,128)(2,1)} %get-tuple-element.333, bf16[2048,2048]{1,0:T(8,128)(2,1)} %copy-done.198), kind=kOutput, calls=%fused_computation.20 | convolution fusion | flops 17184063488 | bytes 25165824 | tf_op jit(solution)/shard_map/dot_general | solution.py:35
  664.3 22.2 %convolution_convert_fusion = bf16[2048,2048]{1,0:T(8,128)(2,1)S(1)} fusion(bf16[2048,2048]{1,0:T(8,128)(2,1)} %get-tuple-element.347, bf16[2048,2048]{1,0:T(8,128)(2,1)} %param.22), kind=kOutput, calls=%fused_computation.19 | convolution fusion | flops 17184063488 | bytes 25165824 | tf_op jit(solution)/shard_map/dot_general | solution.py:31
  750.0 23.8 %attention_backward.2 = (bf16[1024,512]{1,0:T(8,128)(2,1)S(1)}, bf16[1024,256]{1,0:T(8,128)(2,1)S(1)}) custom-call(s32[4]{0:T(128)S(1)} %iota_xor_fusion.order_ref, bf16[1024,512]{1,0:T(8,128)(2,1)S(1)} %convolution_convert_fusion.12.grad_ref, bf16[1024,512]{1,0:T(8,128)(2,1)} %copy-done.74, bf16[1024,256]{1,0:T(8,128)(2,1)S(1)} %copy-done.78, ...), custom_call_target="tpu_custom_call" | custom-call | flops 20000000000 | bytes 12000000 | tf_op jit(solution)/shard_map/attention_backward/pallas_call | solution.py:338
  793.2 35.7 %collective-permute-done.72 = bf16[128,2048]{1,0:T(8,128)(2,1)S(1)} collective-permute-done((bf16[128,2048]{1,0:T(8,128)(2,1)S(1)}, bf16[128,2048]{1,0:T(8,128)(2,1)S(1)}, u32[]{:S(2)}, u32[]{:S(2)}) %collective-permute-start.72) | collective-permute-done | bytes 524320 | tf_op jit(solution)/shard_map/ppermute | solution.py:464
  878.8 23.8 %attention_backward.3 = (bf16[1024,512]{1,0:T(8,128)(2,1)S(1)}, bf16[1024,256]{1,0:T(8,128)(2,1)S(1)}) custom-call(s32[4]{0:T(128)S(1)} %iota_xor_fusion.order_ref, bf16[1024,512]{1,0:T(8,128)(2,1)S(1)} %convolution_convert_fusion.11.grad_ref, bf16[1024,512]{1,0:T(8,128)(2,1)} %copy-done.73, bf16[1024,256]{1,0:T(8,128)(2,1)S(1)} %get-tuple-element.388.kv_ref, ...), custom_call_target="tpu_custom_call" | custom-call | flops 20000000000 | bytes 12000000 | tf_op jit(solution)/shard_map/attention_backward/pallas_call | solution.py:338
  1034.6 15.5 %collective-permute-done.107 = bf16[192,2048]{1,0:T(8,128)(2,1)S(1)} collective-permute-done((bf16[192,2048]{1,0:T(8,128)(2,1)S(1)}, bf16[192,2048]{1,0:T(8,128)(2,1)S(1)}, u32[]{:S(2)}, u32[]{:S(2)}) %collective-permute-start.107) | collective-permute-done | bytes 786464 | tf_op jit(solution)/shard_map/ppermute | solution.py:531
  1069.1 14.3 %collective-permute-done.109 = bf16[192,2048]{1,0:T(8,128)(2,1)S(1)} collective-permute-done((bf16[192,2048]{1,0:T(8,128)(2,1)S(1)}, bf16[192,2048]{1,0:T(8,128)(2,1)S(1)}, u32[]{:S(2)}, u32[]{:S(2)}) %collective-permute-start.109) | collective-permute-done | bytes 786464 | tf_op jit(solution)/shard_map/ppermute | solution.py:531
  1126.6 13.8 %collective-permute-done.105 = f32[2,512]{1,0:T(2,128)S(1)} collective-permute-done((f32[2,512]{1,0:T(2,128)S(1)}, f32[2,512]{1,0:T(2,128)S(1)}, u32[]{:S(2)}, u32[]{:S(2)}) %collective-permute-start.105) | collective-permute-done | bytes 4128 | tf_op jit(solution)/shard_map/ppermute | solution.py:502
  1168.2 17.4 %assemble.7 = f32[2048,2048]{1,0:T(8,128)} custom-call(s32[2]{0:T(128)S(1)} %pad_add_fusion.where_ref, bf16[256,2048]{1,0:T(8,128)(2,1)S(1)} %copy-done.14, bf16[256,2048]{1,0:T(8,128)(2,1)} %collective-permute-done.60.refs_1_, bf16[256,2048]{1,0:T(8,128)(2,1)S(1)} %copy-done.48, bf16[256,2048]{1,0:T(8,128)(2,1)} %collective-permute-done.122.refs_3_, ...), custom_call_target="tpu_custom_call" | custom-call | bytes 25165824 | tf_op jit(solution)/shard_map/assemble/pallas_call | solution.py:411
  1197.7 14.6 %assemble.8 = f32[2048,2048]{1,0:T(8,128)} custom-call(s32[2]{0:T(128)S(1)} %pad_add_fusion.where_ref, bf16[256,2048]{1,0:T(8,128)(2,1)} %add_convert_fusion.10.refs_0_, bf16[256,2048]{1,0:T(8,128)(2,1)S(1)} %copy-done.32, bf16[256,2048]{1,0:T(8,128)(2,1)} %collective-permute-done.129.refs_2_, bf16[256,2048]{1,0:T(8,128)(2,1)S(1)} %copy-done.52, ...), custom_call_target="tpu_custom_call" | custom-call | bytes 25165824 | tf_op jit(solution)/shard_map/assemble/pallas_call | solution.py:411
  (960 shorter events, 719.1 us)
Async XLA Ops:
  70.6 46.4 %collective-permute-start.11 = (bf16[256,2048]{1,0:T(8,128)(2,1)S(1)}, bf16[256,2048]{1,0:T(8,128)(2,1)S(1)}, u32[]{:S(2)}, u32[]{:S(2)}) collective-permute-start(bf16[256,2048]{1,0:T(8,128)(2,1)S(1)} %copy-done.92), channel_id=1, source_target_pairs={{0,8},{8,0},{16,24},{24,16},{1,9},{9,1},{17,25},{25,17},{2,10},{10... | collective-permute-start | bytes 3145736 | tf_op jit(solution)/shard_map/ppermute | solution.py:459
  72.0 45.0 %collective-permute-start.12 = (bf16[256,2048]{1,0:T(8,128)(2,1)S(1)}, bf16[256,2048]{1,0:T(8,128)(2,1)S(1)}, u32[]{:S(2)}, u32[]{:S(2)}) collective-permute-start(bf16[256,2048]{1,0:T(8,128)(2,1)S(1)} %copy-done.92), channel_id=1, source_target_pairs={{0,16},{8,24},{16,0},{24,8},{1,17},{9,25},{17,1},{25,9},{2,18},{10... | collective-permute-start | bytes 3145736 | tf_op jit(solution)/shard_map/ppermute | solution.py:459
  175.0 45.4 %collective-permute-start.21 = (bf16[256,2048]{1,0:T(8,128)(2,1)S(1)}, bf16[256,2048]{1,0:T(8,128)(2,1)S(1)}, u32[]{:S(2)}, u32[]{:S(2)}) collective-permute-start(bf16[256,2048]{1,0:T(8,128)(2,1)S(1)} %multiply_convert_fusion.9), channel_id=1, source_target_pairs={{0,8},{8,0},{16,24},{24,16},{1,9},{9,1},{17,25},{25,17},{2,10},{10... | collective-permute-start | bytes 3145736 | tf_op jit(solution)/shard_map/ppermute | solution.py:459
  512.9 46.3 %collective-permute-start.43 = (bf16[2,2,128,2048]{3,2,1,0:T(8,128)(2,1)}, bf16[2,2,128,2048]{3,2,1,0:T(8,128)(2,1)S(1)}, u32[]{:S(2)}, u32[]{:S(2)}) collective-permute-start(bf16[2,2,128,2048]{3,2,1,0:T(8,128)(2,1)} %pad_maximum_fusion.3), channel_id=1, source_target_pairs={{0,16},{8,24},{16,0},{24,8},{1,17},{9,25},{17,1},{25,9},{2,18},{10... | collective-permute-start | bytes 6291464 | tf_op jit(solution)/shard_map/ppermute | solution.py:476
  514.8 45.9 %collective-permute-start.42 = (bf16[2,2,128,2048]{3,2,1,0:T(8,128)(2,1)}, bf16[2,2,128,2048]{3,2,1,0:T(8,128)(2,1)S(1)}, u32[]{:S(2)}, u32[]{:S(2)}) collective-permute-start(bf16[2,2,128,2048]{3,2,1,0:T(8,128)(2,1)} %pad_maximum_fusion.2), channel_id=1, source_target_pairs={{0,8},{8,0},{16,24},{24,16},{1,9},{9,1},{17,25},{25,17},{2,10},{10... | collective-permute-start | bytes 6291464 | tf_op jit(solution)/shard_map/ppermute | solution.py:476
  565.6 47.0 %collective-permute-start.48 = (bf16[2,128,2048]{2,1,0:T(8,128)(2,1)}, bf16[2,128,2048]{2,1,0:T(8,128)(2,1)S(1)}, u32[]{:S(2)}, u32[]{:S(2)}) collective-permute-start(bf16[2,128,2048]{2,1,0:T(8,128)(2,1)} %get-tuple-element.495), channel_id=1, source_target_pairs={{0,16},{8,24},{16,0},{24,8},{1,17},{9,25},{17,1},{25,9},{2,18},{10... | collective-permute-start | bytes 3145736 | tf_op jit(solution)/shard_map/ppermute | solution.py:483
  567.3 45.2 %collective-permute-start.49 = (bf16[2,128,2048]{2,1,0:T(8,128)(2,1)}, bf16[2,128,2048]{2,1,0:T(8,128)(2,1)S(1)}, u32[]{:S(2)}, u32[]{:S(2)}) collective-permute-start(bf16[2,128,2048]{2,1,0:T(8,128)(2,1)} %get-tuple-element.494), channel_id=1, source_target_pairs={{0,8},{8,0},{16,24},{24,16},{1,9},{9,1},{17,25},{25,17},{2,10},{10... | collective-permute-start | bytes 3145736 | tf_op jit(solution)/shard_map/ppermute | solution.py:483
  568.5 44.1 %collective-permute-start.46 = (bf16[256,2048]{1,0:T(8,128)(2,1)S(1)}, bf16[256,2048]{1,0:T(8,128)(2,1)S(1)}, u32[]{:S(2)}, u32[]{:S(2)}) collective-permute-start(bf16[256,2048]{1,0:T(8,128)(2,1)S(1)} %add_convert_fusion.31.refs_4_), channel_id=1, source_target_pairs={{2,0},{3,1},{4,6},{5,7},{10,8},{11,9},{12,14},{13,15},{18,16},{19,... | collective-permute-start | bytes 3145736 | tf_op jit(solution)/shard_map/ppermute | solution.py:531
  713.7 63.3 %collective-permute-start.68 = (bf16[1024,2048]{1,0:T(8,128)(2,1)}, bf16[1024,2048]{1,0:T(8,128)(2,1)}, u32[]{:S(2)}, u32[]{:S(2)}) collective-permute-start(bf16[1024,2048]{1,0:T(8,128)(2,1)} %constant_dynamic-slice_fusion.6), channel_id=1, source_target_pairs={{0,1},{1,0},{2,3},{3,2},{4,5},{5,4},{6,7},{7,6},{8,9},{9,8},{10,11... | collective-permute-start | bytes 12582920 | tf_op jit(solution)/shard_map/ppermute | solution.py:516
  727.7 111.0 %collective-permute-start.75 = (bf16[2,2,128,2048]{3,2,1,0:T(8,128)(2,1)}, bf16[2,2,128,2048]{3,2,1,0:T(8,128)(2,1)}, u32[]{:S(2)}, u32[]{:S(2)}) collective-permute-start(bf16[2,2,128,2048]{3,2,1,0:T(8,128)(2,1)} %pad_maximum_fusion.5), channel_id=1, source_target_pairs={{0,16},{8,24},{16,0},{24,8},{1,17},{9,25},{17,1},{25,9},{2,18},{10... | collective-permute-start | bytes 6291464 | tf_op jit(solution)/shard_map/ppermute | solution.py:476
  730.9 54.3 %collective-permute-start.67 = (bf16[256,2048]{1,0:T(8,128)(2,1)S(1)}, bf16[256,2048]{1,0:T(8,128)(2,1)}, u32[]{:S(2)}, u32[]{:S(2)}) collective-permute-start(bf16[256,2048]{1,0:T(8,128)(2,1)S(1)} %add_convert_fusion.19.refs_4_), channel_id=1, source_target_pairs={{2,0},{3,1},{4,6},{5,7},{10,8},{11,9},{12,14},{13,15},{18,16},{19,... | collective-permute-start | bytes 3145736 | tf_op jit(solution)/shard_map/ppermute | solution.py:531
  732.6 53.4 %collective-permute-start.66 = (bf16[256,2048]{1,0:T(8,128)(2,1)S(1)}, bf16[256,2048]{1,0:T(8,128)(2,1)}, u32[]{:S(2)}, u32[]{:S(2)}) collective-permute-start(bf16[256,2048]{1,0:T(8,128)(2,1)S(1)} %add_convert_fusion.20), channel_id=1, source_target_pairs={{2,4},{3,5},{4,2},{5,3},{10,12},{11,13},{12,10},{13,11},{18,20},{1... | collective-permute-start | bytes 3145736 | tf_op jit(solution)/shard_map/ppermute | solution.py:531
  734.3 52.2 %collective-permute-start.65 = (bf16[256,2048]{1,0:T(8,128)(2,1)S(1)}, bf16[256,2048]{1,0:T(8,128)(2,1)}, u32[]{:S(2)}, u32[]{:S(2)}) collective-permute-start(bf16[256,2048]{1,0:T(8,128)(2,1)S(1)} %get-tuple-element.358), channel_id=1, source_target_pairs={{0,2},{1,3},{6,4},{7,5},{8,10},{9,11},{14,12},{15,13},{16,18},{17,... | collective-permute-start | bytes 3145736 | tf_op jit(solution)/shard_map/ppermute | solution.py:531
  777.0 61.8 %collective-permute-start.74 = (bf16[2,2,128,2048]{3,2,1,0:T(8,128)(2,1)}, bf16[2,2,128,2048]{3,2,1,0:T(8,128)(2,1)}, u32[]{:S(2)}, u32[]{:S(2)}) collective-permute-start(bf16[2,2,128,2048]{3,2,1,0:T(8,128)(2,1)} %pad_maximum_fusion.4), channel_id=1, source_target_pairs={{0,8},{8,0},{16,24},{24,16},{1,9},{9,1},{17,25},{25,17},{2,10},{10... | collective-permute-start | bytes 6291464 | tf_op jit(solution)/shard_map/ppermute | solution.py:476
  785.2 43.7 %collective-permute-start.72 = (bf16[128,2048]{1,0:T(8,128)(2,1)S(1)}, bf16[128,2048]{1,0:T(8,128)(2,1)S(1)}, u32[]{:S(2)}, u32[]{:S(2)}) collective-permute-start(bf16[128,2048]{1,0:T(8,128)(2,1)S(1)} %slice.445), channel_id=1, source_target_pairs={{0,8},{8,0},{16,24},{24,16},{1,9},{9,1},{17,25},{25,17},{2,10},{10... | collective-permute-start | bytes 1572872 | tf_op jit(solution)/shard_map/ppermute | solution.py:464
  786.1 44.5 %collective-permute-start.73 = (bf16[128,2048]{1,0:T(8,128)(2,1)S(1)}, bf16[128,2048]{1,0:T(8,128)(2,1)}, u32[]{:S(2)}, u32[]{:S(2)}) collective-permute-start(bf16[128,2048]{1,0:T(8,128)(2,1)S(1)} %slice.446), channel_id=1, source_target_pairs={{0,16},{8,24},{16,0},{24,8},{1,17},{9,25},{17,1},{25,9},{2,18},{10... | collective-permute-start | bytes 1572872 | tf_op jit(solution)/shard_map/ppermute | solution.py:465
  789.1 49.6 %collective-permute-start.71 = (bf16[256,2048]{1,0:T(8,128)(2,1)}, bf16[256,2048]{1,0:T(8,128)(2,1)}, u32[]{:S(2)}, u32[]{:S(2)}) collective-permute-start(bf16[256,2048]{1,0:T(8,128)(2,1)} %add_convert_fusion.16.refs_8_), channel_id=1, source_target_pairs={{2,0},{3,1},{4,6},{5,7},{10,8},{11,9},{12,14},{13,15},{18,16},{19,... | collective-permute-start | bytes 3145736 | tf_op jit(solution)/shard_map/ppermute | solution.py:531
  851.7 59.4 %collective-permute-start.84 = (bf16[2,128,2048]{2,1,0:T(8,128)(2,1)}, bf16[2,128,2048]{2,1,0:T(8,128)(2,1)}, u32[]{:S(2)}, u32[]{:S(2)}) collective-permute-start(bf16[2,128,2048]{2,1,0:T(8,128)(2,1)} %get-tuple-element.487), channel_id=1, source_target_pairs={{0,16},{8,24},{16,0},{24,8},{1,17},{9,25},{17,1},{25,9},{2,18},{10... | collective-permute-start | bytes 3145736 | tf_op jit(solution)/shard_map/ppermute | solution.py:483
  852.2 59.6 %collective-permute-start.85 = (bf16[2,128,2048]{2,1,0:T(8,128)(2,1)}, bf16[2,128,2048]{2,1,0:T(8,128)(2,1)}, u32[]{:S(2)}, u32[]{:S(2)}) collective-permute-start(bf16[2,128,2048]{2,1,0:T(8,128)(2,1)} %get-tuple-element.486), channel_id=1, source_target_pairs={{0,8},{8,0},{16,24},{24,16},{1,9},{9,1},{17,25},{25,17},{2,10},{10... | collective-permute-start | bytes 3145736 | tf_op jit(solution)/shard_map/ppermute | solution.py:483
  1115.1 70.5 %collective-permute-start.135 = (bf16[256,2048]{1,0:T(8,128)(2,1)}, bf16[256,2048]{1,0:T(8,128)(2,1)}, u32[]{:S(2)}, u32[]{:S(2)}) collective-permute-start(bf16[256,2048]{1,0:T(8,128)(2,1)} %copy-done.20), channel_id=1, source_target_pairs={{0,1},{1,0},{2,3},{3,2},{4,5},{5,4},{6,7},{7,6},{8,9},{9,8},{10,11... | collective-permute-start | bytes 3145736 | tf_op jit(solution)/shard_map/ppermute | solution.py:531
  1118.3 67.3 %collective-permute-start.116 = (bf16[192,2048]{1,0:T(8,128)(2,1)}, bf16[192,2048]{1,0:T(8,128)(2,1)}, u32[]{:S(2)}, u32[]{:S(2)}) collective-permute-start(bf16[192,2048]{1,0:T(8,128)(2,1)} %add_convert_fusion.40.refs_4_), channel_id=1, source_target_pairs={{2,0},{3,1},{4,6},{5,7},{10,8},{11,9},{12,14},{13,15},{18,16},{19,... | collective-permute-start | bytes 2359304 | tf_op jit(solution)/shard_map/ppermute | solution.py:531
  1125.2 61.7 %collective-permute-start.134 = (bf16[256,2048]{1,0:T(8,128)(2,1)}, bf16[256,2048]{1,0:T(8,128)(2,1)}, u32[]{:S(2)}, u32[]{:S(2)}) collective-permute-start(bf16[256,2048]{1,0:T(8,128)(2,1)} %collective-permute-done.90.refs_9_), channel_id=1, source_target_pairs={{0,1},{1,0},{2,3},{3,2},{4,5},{5,4},{6,7},{7,6},{8,9},{9,8},{10,11... | collective-permute-start | bytes 3145736 | tf_op jit(solution)/shard_map/ppermute | solution.py:531
  1126.1 64.0 %collective-permute-start.136 = (bf16[256,2048]{1,0:T(8,128)(2,1)}, bf16[256,2048]{1,0:T(8,128)(2,1)}, u32[]{:S(2)}, u32[]{:S(2)}) collective-permute-start(bf16[256,2048]{1,0:T(8,128)(2,1)} %collective-permute-done.97.refs_13_), channel_id=1, source_target_pairs={{0,1},{1,0},{2,3},{3,2},{4,5},{5,4},{6,7},{7,6},{8,9},{9,8},{10,11... | collective-permute-start | bytes 3145736 | tf_op jit(solution)/shard_map/ppermute | solution.py:531
  1140.5 50.2 %collective-permute-start.119 = (bf16[256,2048]{1,0:T(8,128)(2,1)}, bf16[256,2048]{1,0:T(8,128)(2,1)}, u32[]{:S(2)}, u32[]{:S(2)}) collective-permute-start(bf16[256,2048]{1,0:T(8,128)(2,1)} %add_convert_fusion.1.refs_0_), channel_id=1, source_target_pairs={{0,1},{1,0},{2,3},{3,2},{4,5},{5,4},{6,7},{7,6},{8,9},{9,8},{10,11... | collective-permute-start | bytes 3145736 | tf_op jit(solution)/shard_map/ppermute | solution.py:531
  (337 other events, 5889.1 us)

commit v3 on v2

--- a/solution.py
+++ b/solution.py
@@ -62,6 +62,303 @@
     return jnp.cos(angle), jnp.sin(angle) * jnp.where(lane < half, -1.0, 1.0)[None, :]
 
 
+MESH = pl.DeviceIdType.MESH
+CHUNK = 64
+
+
+def remote(source, target, sems, index, device):
+    return pltpu.make_async_remote_copy(
+        source, target, sems.at[0, index], sems.at[1, index], device_id=device, device_id_type=MESH
+    )
+
+
+class GatherJob:
+    def __init__(self, own):
+        self.operand = own
+        self.rows, self.width = own.shape
+        self.chunks = self.rows // CHUNK
+        self.out_shape = jax.ShapeDtypeStruct((4 * self.rows, self.width), own.dtype)
+        self.out_spec = pl.BlockSpec(memory_space=pl.ANY)
+
+    def scratch(self):
+        return [pltpu.SemaphoreType.DMA((2, 3 * self.chunks)), pltpu.SemaphoreType.DMA(())]
+
+    def bind(self, operand, out, scratch, x, y):
+        sems, local = scratch
+        n, rows = self.chunks, self.rows
+        at = lambda block, j: out.at[pl.ds(block * rows + j * CHUNK, CHUNK), :]
+        own = lambda j: operand.at[pl.ds(j * CHUNK, CHUNK), :]
+        self.local = pltpu.make_async_copy(operand, out.at[pl.ds(0, rows), :], local)
+        self.to_x = [remote(own(j), at(1, j), sems, j, x) for j in range(n)]
+        self.to_y = [remote(own(j), at(2, j), sems, n + j, y) for j in range(n)]
+        self.on_x = [remote(at(2, j), at(3, j), sems, 2 * n + j, x) for j in range(n // 2)]
+        self.on_y = [remote(at(1, j), at(3, j), sems, 2 * n + j, y) for j in range(n // 2, n)]
+
+    def begin(self):
+        n = self.chunks
+        half = n // 2
+        for k in range(n):
+            self.to_x[(k + half) % n].start()
+            self.to_y[k].start()
+        self.local.start()
+
+    def stages(self):
+        def stage(k):
+            half = self.chunks // 2
+            self.to_y[k].wait_recv()
+            self.on_x[k].start()
+            self.to_x[half + k].wait_recv()
+            self.on_y[k].start()
+
+        return [functools.partial(stage, k) for k in range(self.chunks // 2)]
+
+    def finish(self):
+        half = self.chunks // 2
+        for copy in self.to_x[:half] + self.to_y[half:] + self.on_x + self.on_y:
+            copy.wait_recv()
+        for copy in self.to_x + self.to_y + self.on_x + self.on_y:
+            copy.wait_send()
+        self.local.wait()
+
+
+class SumJob:
+    def __init__(self, part):
+        self.operand = part
+        self.rows, self.width = part.shape[0] // 4, part.shape[1]
+        self.half = self.rows // 2
+        self.chunks = self.half // CHUNK
+        self.out_shape = jax.ShapeDtypeStruct((self.rows, self.width), F32)
+        self.out_spec = pl.BlockSpec((self.rows, self.width), lambda *_: (0, 0))
+
+    def scratch(self):
+        return [
+            pltpu.VMEM((4, self.half, self.width), BF16),
+            pltpu.VMEM((6, self.half, self.width), BF16),
+            pltpu.SemaphoreType.DMA((2, 6 * self.chunks)),
+            pltpu.SemaphoreType.DMA((4,)),
+        ]
+
+    def bind(self, part, out, scratch, x, y):
+        self.out = out
+        self.mine, self.got, sems, local = scratch
+        n, half = self.chunks, self.half
+        rows = lambda block, second: pl.ds(block * self.rows + second * half, half)
+        piece = lambda block, second, j: part.at[
+            pl.ds(block * self.rows + second * half + j * CHUNK, CHUNK), :
+        ]
+        here = lambda ref, k, j: ref.at[k, pl.ds(j * CHUNK, CHUNK), :]
+        self.loads = [
+            pltpu.make_async_copy(part.at[rows(block, second), :], self.mine.at[k], local.at[k])
+            for k, (block, second) in enumerate(((0, 0), (0, 1), (2, 0), (1, 1)))
+        ]
+        send = lambda k, source, device: [
+            remote(source(j), here(self.got, k, j), sems, k * n + j, device) for j in range(n)
+        ]
+        self.sends = [
+            send(0, lambda j: piece(1, 0, j), x),
+            send(1, lambda j: piece(3, 0, j), x),
+            send(2, lambda j: here(self.mine, 2, j), y),
+            send(3, lambda j: piece(2, 1, j), y),
+            send(4, lambda j: piece(3, 1, j), y),
+            send(5, lambda j: here(self.mine, 3, j), x),
+        ]
+
+    def begin(self):
+        for j in range(self.chunks):
+            self.sends[1][j].start()
+            self.sends[4][j].start()
+        for load in self.loads:
+            load.start()
+        for j in range(self.chunks):
+            self.sends[0][j].start()
+            self.sends[3][j].start()
+
+    def stages(self):
+        def stage(j):
+            if j == 0:
+                for load in self.loads:
+                    load.wait()
+            rows = pl.ds(j * CHUNK, CHUNK)
+            for first, second, own in ((1, 2, 2), (4, 5, 3)):
+                self.sends[first][j].wait_recv()
+                total = self.mine[own, rows, :].astype(F32) + self.got[first, rows, :].astype(F32)
+                self.mine[own, rows, :] = total.astype(BF16)
+                self.sends[second][j].start()
+
+        return [functools.partial(stage, j) for j in range(self.chunks)]
+
+    def finish(self):
+        for j in range(self.chunks):
+            rows = pl.ds(j * CHUNK, CHUNK)
+            for own, one, two in ((0, 0, 2), (1, 3, 5)):
+                self.sends[one][j].wait_recv()
+                self.sends[two][j].wait_recv()
+                self.out[pl.ds(own * self.half + j * CHUNK, CHUNK), :] = (
+                    self.mine[own, rows, :].astype(F32)
+                    + self.got[one, rows, :].astype(F32)
+                    + self.got[two, rows, :].astype(F32)
+                )
+        for copies in self.sends:
+            for copy in copies:
+                copy.wait_send()
+
+
+class Comm:
+    def __init__(self, jobs, number):
+        self.jobs, self.number = jobs, number
+        self.operands = [job.operand for job in jobs]
+        self.in_specs = [pl.BlockSpec(memory_space=pl.ANY) for _ in jobs]
+        self.out_specs = [job.out_spec for job in jobs]
+        self.out_shapes = [job.out_shape for job in jobs]
+        self.scratch = [entry for job in jobs for entry in job.scratch()]
+
+    def enter(self, operands, outs, scratch, now):
+        shard, replica = lax.axis_index("shard"), lax.axis_index("replica")
+        x = (shard + 1 - 2 * (shard % 2), replica)
+        y = ((shard + 2) % 4, replica)
+        scratch = list(scratch)
+        for job, operand, out in zip(self.jobs, operands, outs):
+            count = len(job.scratch())
+            job.bind(operand, out, scratch[:count], x, y)
+            scratch = scratch[count:]
+
+        @pl.when(now)
+        def _():
+            barrier = pltpu.get_barrier_semaphore()
+            for device in (x, y):
+                pl.semaphore_signal(barrier, inc=1, device_id=device, device_id_type=MESH)
+            pl.semaphore_wait(barrier, 2)
+            for job in self.jobs:
+                job.begin()
+
+    def stages(self):
+        return [stage for job in self.jobs for stage in job.stages()]
+
+    def advance(self, step, steps):
+        stages = self.stages()
+        for index, stage in enumerate(stages):
+            due = min(steps - 1, steps // 2 + index * (steps - steps // 2) // len(stages))
+            pl.when(step == due)(stage)
+
+    def finish(self, now):
+        @pl.when(now)
+        def _():
+            for job in self.jobs:
+                job.finish()
+
+
+class NoComm:
+    operands = in_specs = out_specs = out_shapes = scratch = ()
+    number = None
+
+    def enter(self, *_):
+        pass
+
+    def advance(self, *_):
+        pass
+
+    def finish(self, *_):
+        pass
+
+
+def comm_params(comm, vmem):
+    if comm.number is None:
+        return pltpu.CompilerParams(vmem_limit_bytes=vmem << 20)
+    return pltpu.CompilerParams(
+        vmem_limit_bytes=vmem << 20, collective_id=comm.number, has_side_effects=True
+    )
+
+
+def split_refs(refs, *counts):
+    parts, begin = [], 0
+    for count in counts:
+        parts.append(refs[begin : begin + count])
+        begin += count
+    return parts
+
+
+def transfer(comm):
+    count = len(comm.operands)
+
+    def kernel(*refs):
+        operands, outs, scratch = split_refs(refs, count, count, len(comm.scratch))
+        now = pl.program_id(0) == 0
+        comm.enter(operands, outs, scratch, now)
+        for stage in comm.stages():
+            stage()
+        comm.finish(now)
+
+    return pl.pallas_call(
+        kernel,
+        grid=(1,),
+        in_specs=comm.in_specs,
+        out_specs=comm.out_specs,
+        out_shape=comm.out_shapes,
+        scratch_shapes=comm.scratch,
+        compiler_params=comm_params(comm, 40),
+        name="transfer",
+    )(*comm.operands)
+
+
+def products(items, block, comm):
+    specs, shapes, out_specs, steps, rights = [], [], [], [], []
+    total = sum((l.shape[1] if t else l.shape[0]) // block for l, _, t in items)
+    begin = 0
+    for left, right, transposed in items:
+        size = left.shape[1] if transposed else left.shape[0]
+        count = size // block
+
+        def place(i, begin=begin, count=count):
+            return jnp.clip(i - begin, 0, count - 1)
+
+        if transposed:
+            specs.append(pl.BlockSpec((left.shape[0], block), lambda i, p=place: (0, p(i))))
+        else:
+            specs.append(pl.BlockSpec((block, left.shape[1]), lambda i, p=place: (p(i), 0)))
+        out_specs.append(pl.BlockSpec((block, right.shape[1]), lambda i, p=place: (p(i), 0)))
+        shapes.append(jax.ShapeDtypeStruct((size, right.shape[1]), BF16))
+        if not any(right is r for r in rights):
+            rights.append(right)
+        steps.append((begin, count))
+        begin += count
+    right_specs = [
+        pl.BlockSpec(r.shape, lambda i: (0, 0), pipeline_mode=pl.Buffered(1)) for r in rights
+    ]
+    which = [next(k for k, r in enumerate(rights) if r is right) for _, right, _ in items]
+    n = len(items)
+
+    def kernel(*refs):
+        lefts, held, operands, outs, comm_outs, scratch = split_refs(
+            refs, n, len(rights), len(comm.operands), n, len(comm.operands), len(comm.scratch)
+        )
+        step = pl.program_id(0)
+        comm.enter(operands, comm_outs, scratch, step == 0)
+        comm.advance(step, total)
+        for k, (_, _, transposed) in enumerate(items):
+            begin, count = steps[k]
+
+            @pl.when((step >= begin) & (step < begin + count))
+            def _(k=k, transposed=transposed):
+                dot = dot_tn if transposed else dot_nn
+                outs[k][...] = dot(lefts[k][...], held[which[k]][...]).astype(BF16)
+
+        comm.finish(step == total - 1)
+
+    flops = 2 * sum(math.prod(l.shape) * r.shape[1] for l, r, _ in items)
+    out = pl.pallas_call(
+        kernel,
+        grid=(total,),
+        in_specs=specs + right_specs + list(comm.in_specs),
+        out_specs=out_specs + list(comm.out_specs),
+        out_shape=shapes + list(comm.out_shapes),
+        scratch_shapes=list(comm.scratch),
+        compiler_params=comm_params(comm, 58),
+        cost_estimate=pl.CostEstimate(flops=flops, bytes_accessed=30_000_000, transcendentals=0),
+        name="products",
+    )(*[l for l, _, _ in items], *rights, *comm.operands)
+    return out[:n], out[n:]
+
+
 def swap_halves(block):
     lane = lax.broadcasted_iota(jnp.int32, block.shape, 1)
     half = HEAD_DIM // 2
@@ -87,34 +384,26 @@
     return placed
 
 
-def attention_forward_kernel(
-    kv_heads,
-    blocks,
-    order_ref,
-    q_ref,
-    kv_ref,
-    cos_ref,
-    sin_ref,
-    member_ref,
-    sees_ref,
-    out_ref,
-    q_out_ref,
-    kv_out_ref,
-    lse_ref,
-    keys,
-    values,
-    bias,
-):
+def attention_forward_kernel(kv_heads, blocks, place, comm, *refs):
+    jobs = len(comm.operands)
+    inputs, operands, outs, comm_outs, own, scratch = split_refs(
+        refs, 6, jobs, 4, jobs, 3, len(comm.scratch)
+    )
+    q_ref, kv_ref, cos_ref, sin_ref, member_ref, sees_ref = inputs
+    out_ref, q_out_ref, kv_out_ref, lse_ref = outs
+    keys, values, bias = own
     step = pl.program_id(0)
-    rows = q_ref.shape[0]
-    tree = rows * blocks
+    comm.enter(operands, comm_outs, scratch, step == 0)
+    comm.advance(step, blocks)
+    tree = q_ref.shape[0]
+    rows = tree // blocks
     kv_width = kv_heads * HEAD_DIM
 
     @pl.when(step == 0)
     def _():
         for b in range(blocks):
             here = pl.ds(b * rows, rows)
-            raw = kv_ref[pl.ds(pl.multiple_of(order_ref[b] * rows, rows), rows), :]
+            raw = kv_ref[pl.ds(pl.multiple_of(place(b) * rows, rows), rows), :]
             cosine, sine = cos_ref[here, :], sin_ref[here, :]
             if kv_width >= PAIR:
                 turned = jnp.concatenate(
@@ -139,10 +428,12 @@
                 values[index, here, :] = placed.astype(BF16)
 
     here = pl.ds(pl.multiple_of(step * rows, rows), rows)
+    there = pl.ds(pl.multiple_of(place(step) * rows, rows), rows)
     cosine, sine = cos_ref[here, :], sin_ref[here, :]
     for j in range(q_ref.shape[1] // PAIR):
         lanes = slice(j * PAIR, j * PAIR + PAIR)
-        q_out_ref[:, lanes] = (turn(q_ref[:, lanes], cosine, sine).astype(BF16)) * BF16(ATTN_SCALE)
+        turned = turn(q_ref[there, lanes], cosine, sine).astype(BF16)
+        q_out_ref[:, lanes] = turned * BF16(ATTN_SCALE)
 
     link = dot_nt(sees_ref[here, :], member_ref[...])
     row_index = lax.broadcasted_iota(jnp.int32, (rows, tree), 0) + step * rows
@@ -169,43 +460,47 @@
                     tops.append(top)
                 upper = lane >= HEAD_DIM
                 total = pltpu.roll(jnp.where(upper, mixed[0], mixed[1]), HEAD_DIM, 1)
-                out_ref[:, lanes] = (jnp.where(upper, mixed[1], mixed[0]) / total).astype(BF16)
+                out_ref[there, lanes] = (jnp.where(upper, mixed[1], mixed[0]) / total).astype(BF16)
                 logs = jnp.log(total)
                 lse = jnp.where(lane == 2 * j, tops[0] + logs[:, :1], lse)
                 lse = jnp.where(lane == 2 * j + 1, tops[1] + logs[:, HEAD_DIM : HEAD_DIM + 1], lse)
             lse_ref[...] = lse
 
-
-def attention_forward(order, qkv, cosine, sine, member, sees, q_width, blocks):
+    comm.finish(step == blocks - 1)
+
+
+def attention_forward(place, qkv, cosine, sine, member, sees, q_width, blocks, comm):
     tree = qkv.shape[0]
     rows = tree // blocks
     kv_width = (qkv.shape[1] - q_width) // 2
     kv_heads = kv_width // HEAD_DIM
-    whole = lambda width: pl.BlockSpec((tree, width), lambda i, order: (0, 0))
-    natural = lambda width: pl.BlockSpec((rows, width), lambda i, order: (i, 0))
-    return pl.pallas_call(
-        functools.partial(attention_forward_kernel, kv_heads, blocks),
-        grid_spec=pltpu.PrefetchScalarGridSpec(
-            num_scalar_prefetch=1,
+    whole = lambda width: pl.BlockSpec((tree, width), lambda i: (0, 0))
+    natural = lambda width: pl.BlockSpec((rows, width), lambda i: (i, 0))
+    out = pl.pallas_call(
+        functools.partial(attention_forward_kernel, kv_heads, blocks, place, comm),
+        grid_spec=pl.GridSpec(
             grid=(blocks,),
             in_specs=[
-                pl.BlockSpec((rows, q_width), lambda i, order: (order[i], 0)),
-                pl.BlockSpec((tree, 2 * kv_width), lambda i, order: (0, q_width // (2 * kv_width))),
+                whole(q_width),
+                pl.BlockSpec((tree, 2 * kv_width), lambda i: (0, q_width // (2 * kv_width))),
                 whole(PAIR),
                 whole(PAIR),
                 whole(PAIR),
                 whole(PAIR),
+                *comm.in_specs,
             ],
             out_specs=[
-                pl.BlockSpec((rows, q_width), lambda i, order: (order[i], 0)),
+                whole(q_width),
                 natural(q_width),
                 whole(2 * kv_width),
                 natural(PAIR),
+                *comm.out_specs,
             ],
             scratch_shapes=[
                 pltpu.VMEM((2 * kv_heads, tree, PAIR), BF16),
                 pltpu.VMEM((2 * kv_heads, tree, PAIR), BF16),
                 pltpu.VMEM((rows, tree), F32),
+                *comm.scratch,
             ],
         ),
         out_shape=[
@@ -213,38 +508,29 @@
             jax.ShapeDtypeStruct((tree, q_width), BF16),
             jax.ShapeDtypeStruct((tree, 2 * kv_width), BF16),
             jax.ShapeDtypeStruct((tree, PAIR), F32),
+            *comm.out_shapes,
         ],
-        compiler_params=pltpu.CompilerParams(vmem_limit_bytes=40 << 20),
+        compiler_params=comm_params(comm, 40),
         cost_estimate=pl.CostEstimate(
             flops=10_000_000_000, bytes_accessed=12_000_000, transcendentals=5_000_000
         ),
         name="attention_forward",
-    )(order, qkv, qkv, cosine, sine, member, sees)
-
-
-def attention_backward_kernel(
-    kv_heads,
-    blocks,
-    order_ref,
-    grad_ref,
-    q_ref,
-    kv_ref,
-    lse_ref,
-    cos_ref,
-    sin_ref,
-    member_ref,
-    sees_ref,
-    dq_ref,
-    dkv_ref,
-    keys,
-    values,
-    bias,
-    key_sum,
-    value_sum,
-):
+    )(qkv, qkv, cosine, sine, member, sees, *comm.operands)
+    return out[:4], out[4:]
+
+
+def attention_backward_kernel(kv_heads, blocks, place, comm, *refs):
+    jobs = len(comm.operands)
+    inputs, operands, outs, comm_outs, own, scratch = split_refs(
+        refs, 8, jobs, 2, jobs, 5, len(comm.scratch)
+    )
+    grad_ref, q_ref, kv_ref, lse_ref, cos_ref, sin_ref, member_ref, sees_ref = inputs
+    dq_ref, dkv_ref = outs
+    keys, values, bias, key_sum, value_sum = own
     step = pl.program_id(0)
-    rows = q_ref.shape[0]
-    tree = rows * blocks
+    comm.enter(operands, comm_outs, scratch, step == 0)
+    comm.advance(step, blocks)
+    tree, rows = grad_ref.shape[0], q_ref.shape[0]
     kv_width = kv_heads * HEAD_DIM
 
     @pl.when(step == 0)
@@ -264,6 +550,7 @@
         value_sum[...] = jnp.zeros_like(value_sum)
 
     here = pl.ds(pl.multiple_of(step * rows, rows), rows)
+    there = pl.ds(pl.multiple_of(place(step) * rows, rows), rows)
     link = dot_nt(member_ref[...], sees_ref[here, :])
     key_index = lax.broadcasted_iota(jnp.int32, (tree, rows), 0)
     query_index = lax.broadcasted_iota(jnp.int32, (tree, rows), 1) + step * rows
@@ -279,7 +566,7 @@
             for j in range(q_ref.shape[1] // PAIR):
                 lanes = slice(j * PAIR, j * PAIR + PAIR)
                 group = 2 * j // GROUP
-                query, grad = q_ref[:, lanes], grad_ref[:, lanes]
+                query, grad = q_ref[:, lanes], grad_ref[there, lanes]
                 dq = jnp.zeros((rows, PAIR), F32)
                 for p in range(2):
                     index, head = group * 2 + p, 2 * j + p
@@ -292,13 +579,13 @@
                     score_grad = (weighted - probs * delta).astype(BF16)
                     key_sum[index, :width, :] += dot_nn(score_grad, query)
                     dq = dq + dot_tn(score_grad, keys[index, :width, :])
-                dq_ref[:, lanes] = turn(dq * ATTN_SCALE, cosine, -sine).astype(BF16)
+                dq_ref[there, lanes] = turn(dq * ATTN_SCALE, cosine, -sine).astype(BF16)
 
     @pl.when(step == blocks - 1)
     def _():
         for b in range(blocks):
             here = pl.ds(b * rows, rows)
-            there = pl.ds(pl.multiple_of(order_ref[b] * rows, rows), rows)
+            there = pl.ds(pl.multiple_of(place(b) * rows, rows), rows)
             cosine, sine = cos_ref[here, :], sin_ref[here, :]
             lane = lax.broadcasted_iota(jnp.int32, (rows, PAIR), 1)
             lower = lane < HEAD_DIM
@@ -326,22 +613,22 @@
                     moved = pltpu.roll(halves[1], HEAD_DIM, 1)
                     dkv_ref[there, :] = jnp.where(lower, turned, moved).astype(BF16)
 
-
-def attention_backward(order, grad, query, kv, lse, cosine, sine, member, sees, blocks):
+    comm.finish(step == blocks - 1)
+
+
+def attention_backward(place, grad, query, kv, lse, cosine, sine, member, sees, blocks, comm):
     tree, q_width = query.shape
     rows = tree // blocks
     kv_width = kv.shape[1] // 2
     kv_heads = kv_width // HEAD_DIM
-    whole = lambda width: pl.BlockSpec((tree, width), lambda i, order: (0, 0))
-    natural = lambda width: pl.BlockSpec((rows, width), lambda i, order: (i, 0))
-    ordered = lambda width: pl.BlockSpec((rows, width), lambda i, order: (order[i], 0))
-    return pl.pallas_call(
-        functools.partial(attention_backward_kernel, kv_heads, blocks),
-        grid_spec=pltpu.PrefetchScalarGridSpec(
-            num_scalar_prefetch=1,
+    whole = lambda width: pl.BlockSpec((tree, width), lambda i: (0, 0))
+    natural = lambda width: pl.BlockSpec((rows, width), lambda i: (i, 0))
+    out = pl.pallas_call(
+        functools.partial(attention_backward_kernel, kv_heads, blocks, place, comm),
+        grid_spec=pl.GridSpec(
             grid=(blocks,),
             in_specs=[
-                ordered(q_width),
+                whole(q_width),
                 natural(q_width),
                 whole(2 * kv_width),
                 natural(PAIR),
@@ -349,26 +636,30 @@
                 whole(PAIR),
                 whole(PAIR),
                 whole(PAIR),
+                *comm.in_specs,
             ],
-            out_specs=[ordered(q_width), whole(2 * kv_width)],
+            out_specs=[whole(q_width), whole(2 * kv_width), *comm.out_specs],
             scratch_shapes=[
                 pltpu.VMEM((2 * kv_heads, tree, PAIR), BF16),
                 pltpu.VMEM((2 * kv_heads, tree, PAIR), BF16),
                 pltpu.VMEM((tree, rows), F32),
                 pltpu.VMEM((2 * kv_heads, tree, PAIR), F32),
                 pltpu.VMEM((2 * kv_heads, tree, PAIR), F32),
+                *comm.scratch,
             ],
         ),
         out_shape=[
             jax.ShapeDtypeStruct((tree, q_width), BF16),
             jax.ShapeDtypeStruct((tree, 2 * kv_width), BF16),
+            *comm.out_shapes,
         ],
-        compiler_params=pltpu.CompilerParams(vmem_limit_bytes=48 << 20),
+        compiler_params=comm_params(comm, 56),
         cost_estimate=pl.CostEstimate(
             flops=20_000_000_000, bytes_accessed=12_000_000, transcendentals=5_000_000
         ),
         name="attention_backward",
-    )(order, grad, query, kv, lse, cosine, sine, member, sees)
+    )(grad, query, kv, lse, cosine, sine, member, sees, *comm.operands)
+    return out[:2], out[2:]
 
 
 def sync(*values):
@@ -437,8 +728,9 @@
         self.outward = both([(1, 0), (2, 3)])
         self.middle = both([(1, 2), (2, 1)])
 
-    def order(self):
-        return jnp.arange(self.shard, dtype=jnp.int32) ^ lax.axis_index("shard")
+    def place(self, block):
+        shard = lax.axis_index("shard")
+        return (block + shard) % 2 + 2 * ((block // 2 + shard // 2) % 2)
 
     def reorder(self, blocks, axis):
         me = lax.axis_index("shard")
@@ -454,41 +746,6 @@
             lax.ppermute(own, "shard", self.d),
         ]
         return self.reorder(jnp.stack(parts), 0)
-
-    def gather_first(self, own):
-        return lax.ppermute(own, "shard", self.x), lax.ppermute(own, "shard", self.y)
-
-    def gather_second(self, own, got):
-        from_x, from_y = got
-        half = own.shape[0] // 2
-        first = lax.ppermute(from_y[:half], "shard", self.x)
-        second = lax.ppermute(from_x[half:], "shard", self.y)
-        return [own, from_x, from_y, first, second]
-
-    def split(self, part):
-        trees, width = part.shape[0] // self.rows // 4, part.shape[1]
-        return part.reshape(trees, 4, 2, self.rows // 2, width)
-
-    def sum_first(self, part):
-        pieces = self.split(part)
-        send_x = jnp.stack([pieces[:, 1, 0], pieces[:, 3, 0]])
-        send_y = jnp.stack([pieces[:, 2, 1], pieces[:, 3, 1]])
-        return lax.ppermute(send_x, "shard", self.x), lax.ppermute(send_y, "shard", self.y)
-
-    def sum_second(self, part, got):
-        pieces = self.split(part)
-        got_x, got_y = got
-        next_y = (pieces[:, 2, 0].astype(F32) + got_x[1].astype(F32)).astype(BF16)
-        next_x = (pieces[:, 1, 1].astype(F32) + got_y[1].astype(F32)).astype(BF16)
-        return lax.ppermute(next_y, "shard", self.y), lax.ppermute(next_x, "shard", self.x)
-
-    def sum_last(self, part, got, last):
-        pieces = self.split(part)
-        wide = lambda v: v.astype(F32)
-        first = wide(pieces[:, 0, 0]) + wide(got[0][0]) + wide(last[0])
-        second = wide(pieces[:, 0, 1]) + wide(got[1][0]) + wide(last[1])
-        both = jnp.concatenate([first, second], axis=1)
-        return [both[t] for t in range(both.shape[0])]
 
     def sum_small(self, values):
         share = values.shape[1] // self.shard
@@ -502,7 +759,28 @@
             total = total + lax.ppermute(total, "replica", perm)
         return total
 
+    def gather_start(self, own):
+        return lax.ppermute(own, "shard", self.x), lax.ppermute(own, "shard", self.y)
+
+    def gather_more(self, own, got):
+        from_x, from_y = got
+        half = own.shape[0] // 2
+        first = lax.ppermute(from_y[:half], "shard", self.x)
+        second = lax.ppermute(from_x[half:], "shard", self.y)
+        return [own, from_x, from_y, first, second]
+
+    def carry(self, compute, gathers=(), sums=()):
+        jobs = [GatherJob(own) for own in gathers] + [SumJob(part) for part in sums]
+        self.kernels += 1
+        comm = Comm(jobs, self.kernels)
+        if compute is None:
+            results, moved = None, transfer(comm)
+        else:
+            results, moved = compute(comm)
+        return results, list(moved[: len(gathers)]), list(moved[len(gathers) :])
+
     def start_line(self):
+        self.kernels = 0
         self.waiting = []
         self.inward_flight = None
         self.middle_flight = None
@@ -563,31 +841,26 @@
     def __init__(self, shard, replica):
         self.shard, self.replica = shard, replica
 
-    def order(self):
-        return jnp.arange(self.shard, dtype=jnp.int32)
+    def place(self, block):
+        return block
 
     def gather_small(self, own):
         return lax.all_gather(own, "shard", axis=0, tiled=False)
 
-    def gather_first(self, own):
+    def carry(self, compute, gathers=(), sums=()):
+        results = None if compute is None else compute(NoComm())[0]
+        gathered = [lax.all_gather(own, "shard", axis=0, tiled=True) for own in gathers]
+        summed = [
+            lax.psum_scatter(part, "shard", scatter_dimension=0, tiled=True).astype(F32)
+            for part in sums
+        ]
+        return results, gathered, summed
+
+    def gather_start(self, own):
         return lax.all_gather(own, "shard", axis=0, tiled=True)
 
-    def gather_second(self, own, got):
+    def gather_more(self, own, got):
         return [got]
-
-    def sum_first(self, part):
-        return lax.psum_scatter(
-            part.reshape(-1, self.shard * self.rows, part.shape[1]),
-            "shard",
-            scatter_dimension=1,
-            tiled=True,
-        )
-
-    def sum_second(self, part, got):
-        return ()
-
-    def sum_last(self, part, got, last):
-        return [got[t].astype(F32) for t in range(got.shape[0])]
 
     def sum_small(self, values):
         share = lax.psum_scatter(values, "shard", scatter_dimension=1, tiled=True)
@@ -645,9 +918,7 @@
     shard = links.shard
     q_width, kv_width = w_query.shape[0], w_key.shape[0]
     tree_rows = own_rows * shard
-    links.rows = own_rows
     links.start_line()
-    order = links.order()
     share = gain_attn.shape[0]
     w_qkv = jnp.concatenate([w_query, w_key, w_value], axis=0)
     token_rows = [tokens[t, 0] for t in range(trees)]
@@ -657,8 +928,7 @@
         [gain_attn, gain_ff] + [segment_ids[t, 0].astype(BF16) for t in range(trees)]
     )
     smalls = links.gather_small(small)
-    got = links.gather_first(token_rows[0])
-    got, smalls, token_rows = sync(got, smalls, token_rows)
+    _, (rows_0,), _ = links.carry(None, gathers=[token_rows[0]])
     gain_first = smalls[:, :share].reshape(width).astype(F32)
     gain_second = smalls[:, share : 2 * share].reshape(width).astype(F32)
     masks, tables = [], []
@@ -669,76 +939,48 @@
         masks.append((member, sees))
         tables.append(rope_tables(position))
 
-    normed_all, saved = [], []
-
-    def project(pieces):
-        normed = jnp.concatenate([normalized(piece, gain_first) for piece in pieces], axis=0)
-        normed_all.append(normed)
-        return dot_nt(normed, w_qkv)
-
     def attention(t, qkv):
-        attended, query, kv, lse = attention_forward(
-            order, qkv, *tables[t], *masks[t], q_width, shard
+        return lambda comm: attention_forward(
+            links.place, qkv, *tables[t], *masks[t], q_width, shard, comm
         )
-        saved.append((attended, query, kv, lse))
-        return dot_nn(attended, w_out).astype(BF16)
 
     def after_attention(t, branch):
         value = token_rows[t].astype(F32) + RESIDUAL * branch
         scale = rms_scale(value)
         return value, scale, (value * scale * gain_second).astype(BF16)
 
-    pieces_0 = links.gather_second(token_rows[0], got)
-    got = links.gather_first(token_rows[1])
-    pieces_0, got, cot_rows = sync(pieces_0, got, cot_rows)
-
-    pieces_1 = links.gather_second(token_rows[1], got)
-    cot_got = links.gather_first(cot_rows[0])
-    part_0 = attention(0, project(pieces_0))
-    part_0, pieces_1, cot_got = sync(part_0, pieces_1, cot_got)
-
-    got_0 = links.sum_first(part_0)
-    qkv_1 = project(pieces_1)
-    got_0, qkv_1, cot_got = sync(got_0, qkv_1, cot_got)
-
-    last_0 = links.sum_second(part_0, got_0)
-    cot_pieces_0 = links.gather_second(cot_rows[0], cot_got)
-    part_1 = attention(1, qkv_1)
-    last_0, part_1 = sync(last_0, part_1)
-
-    got_1 = links.sum_first(part_1)
-    middle_0, scale_0, own_0 = after_attention(0, links.sum_last(part_0, got_0, last_0)[0])
-    ff_got_0 = links.gather_first(own_0)
-    got_1, own_0 = sync(got_1, own_0)
-
-    last_1 = links.sum_second(part_1, got_1)
-    last_1, ff_got_0 = sync(last_1, ff_got_0)
-
-    ff_pieces_0 = links.gather_second(own_0, ff_got_0)
-    middle_1, scale_1, own_1 = after_attention(1, links.sum_last(part_1, got_1, last_1)[0])
-    ff_got_1 = links.gather_first(own_1)
-    ff_pieces_0, ff_got_1, own_1, cot_pieces_0 = sync(ff_pieces_0, ff_got_1, own_1, cot_pieces_0)
-    ff_pieces_1 = links.gather_second(own_1, ff_got_1)
-    ff_pieces_0, ff_pieces_1, cot_rows, cot_pieces_0 = sync(
-        ff_pieces_0, ff_pieces_1, cot_rows, cot_pieces_0
-    )
-
-    rows_all = jnp.concatenate(ff_pieces_0 + ff_pieces_1, axis=0)
-    cot_got = links.gather_first(cot_rows[1])
+    normed_0 = normalized(rows_0, gain_first)
+    saved_0, (rows_1,), _ = links.carry(
+        attention(0, dot_nt(normed_0, w_qkv)), gathers=[token_rows[1]]
+    )
+    part_0 = dot_nn(saved_0[0], w_out).astype(BF16)
+    normed_1 = normalized(rows_1, gain_first)
+    saved_1, _, (branch_0,) = links.carry(attention(1, dot_nt(normed_1, w_qkv)), sums=[part_0])
+    part_1 = dot_nn(saved_1[0], w_out).astype(BF16)
+    middle_0, scale_0, own_0 = after_attention(0, branch_0)
+    _, (ff_rows_0,), (branch_1,) = links.carry(None, gathers=[own_0], sums=[part_1])
+    middle_1, scale_1, own_1 = after_attention(1, branch_1)
+    _, (ff_rows_1,), _ = links.carry(None, gathers=[own_1])
+    ff_rows_0, ff_rows_1, cot_rows = sync(ff_rows_0, ff_rows_1, cot_rows)
+
+    cot_got = [links.gather_start(cot) for cot in cot_rows]
+    rows_all = jnp.concatenate([ff_rows_0, ff_rows_1], axis=0)
     gate = dot_nt(rows_all, w_gate).astype(BF16)
     gate, cot_got, rows_all = sync(gate, cot_got, rows_all)
-    cot_pieces_1 = links.gather_second(cot_rows[1], cot_got)
+    cot_pieces = [links.gather_more(cot, got) for cot, got in zip(cot_rows, cot_got)]
     upper = dot_nt(rows_all, w_up)
     wide = gate.astype(F32)
     hidden = (wide * jax.nn.sigmoid(wide) * upper).astype(BF16)
     upper = upper.astype(BF16)
-    hidden, upper, gate, cot_pieces_1 = sync(hidden, upper, gate, cot_pieces_1)
+    hidden, upper, gate, cot_pieces = sync(hidden, upper, gate, cot_pieces)
     cot_all = jnp.concatenate(
-        [(RESIDUAL * piece.astype(F32)).astype(BF16) for piece in cot_pieces_0 + cot_pieces_1], axis=0
+        [(RESIDUAL * piece.astype(F32)).astype(BF16) for pieces in cot_pieces for piece in pieces],
+        axis=0,
     )
     grad_down = dot_tn(hidden, cot_all).astype(BF16)
     grad_down, hidden, cot_all, gate, upper = sync(grad_down, hidden, cot_all, gate, upper)
-    links.feed("down", grad_down, 4)
+    links.feed("down", grad_down, 1)
+    cot_all, gate, upper, hidden = links.tick(cot_all, gate, upper, hidden)
     hidden_grad = dot_nt(cot_all, w_down)
     wide = gate.astype(F32)
     sigma = jax.nn.sigmoid(wide)
@@ -746,23 +988,17 @@
         hidden_grad * upper.astype(F32) * sigma * (1.0 + wide * (1.0 - sigma))
     ).astype(BF16)
     up_grad = (hidden_grad * wide * sigma).astype(BF16)
-    gate_grad, up_grad, hidden = links.tick(gate_grad, up_grad, hidden)
-
-    half_part = dot_nn(gate_grad, w_gate)
-    half_part, gate_grad, up_grad = links.tick(half_part, gate_grad, up_grad)
-    ff_part = (half_part + dot_nn(up_grad, w_up)).astype(BF16)
+    ff_part = (dot_nn(gate_grad, w_gate) + dot_nn(up_grad, w_up)).astype(BF16)
     ff_part, gate_grad, up_grad, hidden = links.tick(ff_part, gate_grad, up_grad, hidden)
 
-    ff_sum = links.sum_first(ff_part)
-    grad_gate = dot_tn(gate_grad, rows_all).astype(BF16)
-    grad_gate, up_grad, ff_sum = links.tick(grad_gate, up_grad, ff_sum)
-    links.feed("gate", grad_gate, 4)
-    ff_last = links.sum_second(ff_part, ff_sum)
-    grad_up = dot_tn(up_grad, rows_all).astype(BF16)
-    grad_up, hidden, ff_last = links.tick(grad_up, hidden, ff_last)
-    links.feed("up", grad_up, 4)
-
-    ff_grad = links.sum_last(ff_part, ff_sum, ff_last)
+    parts = lambda whole: [whole[t * tree_rows : (t + 1) * tree_rows] for t in range(trees)]
+    (grad_gate, grad_up), _, ff_grad = links.carry(
+        lambda comm: products([(gate_grad, rows_all, True), (up_grad, rows_all, True)], 512, comm),
+        sums=parts(ff_part),
+    )
+    links.feed("gate", grad_gate, 1)
+    links.feed("up", grad_up, 1)
+    (hidden, ff_grad) = links.tick(hidden, ff_grad)
     out_own, middle_grads = [], []
     gain_ff_sum = jnp.zeros((width,), F32)
     for t, (middle, scale) in enumerate(((middle_0, scale_0), (middle_1, scale_1))):
@@ -770,61 +1006,42 @@
         gain_ff_sum = gain_ff_sum + term
         middle_grads.append(cot_rows[t].astype(F32) + middle_back)
         out_own.append((RESIDUAL * middle_grads[t]).astype(BF16))
-    out_own, hidden = links.tick(out_own, hidden)
-    out_got_0 = links.gather_first(out_own[0])
-    down_part = dot_nn(hidden, w_down).astype(BF16)
-    down_part, out_got_0, out_own = links.tick(down_part, out_got_0, out_own)
-
-    out_pieces_0 = links.gather_second(out_own[0], out_got_0)
-    out_got_1 = links.gather_first(out_own[1])
-    out_pieces_0, out_got_1, down_part = links.tick(out_pieces_0, out_got_1, down_part)
-
-    def attention_back(t, out_all):
-        attended, query, kv, lse = saved[t]
-        attended_grad = dot_nt(out_all, w_out).astype(BF16)
-        dq, dkv = attention_backward(
-            order, attended_grad, query, kv, lse, *tables[t], *masks[t], shard
+    (down_part,), out_alls, _ = links.carry(
+        lambda comm: products([(hidden, w_down, False)], 512, comm), gathers=out_own
+    )
+    down_part, out_alls = links.tick(down_part, out_alls)
+
+    def attention_back(t, saved):
+        _, query, kv, lse = saved
+        attended_grad = dot_nt(out_alls[t], w_out).astype(BF16)
+        return lambda comm: attention_backward(
+            links.place, attended_grad, query, kv, lse, *tables[t], *masks[t], shard, comm
         )
-        qkv_grad = jnp.concatenate([dq, dkv], axis=1)
-        (qkv_grad,) = links.tick(qkv_grad)
-        return qkv_grad, dot_nn(qkv_grad, w_qkv).astype(BF16)
-
-    out_pieces_1 = links.gather_second(out_own[1], out_got_1)
-    down_sum = links.sum_first(down_part)
-    out_all_0 = jnp.concatenate(out_pieces_0, axis=0)
-    qkv_grad_0, normed_part_0 = attention_back(0, out_all_0)
-    qkv_grad_0, normed_part_0, out_pieces_1, down_sum = links.tick(
-        qkv_grad_0, normed_part_0, out_pieces_1, down_sum
-    )
-
-    normed_sum_0 = links.sum_first(normed_part_0)
-    down_last = links.sum_second(down_part, down_sum)
-    out_all_1 = jnp.concatenate(out_pieces_1, axis=0)
-    qkv_grad_1, normed_part_1 = attention_back(1, out_all_1)
-    qkv_grad_1, normed_part_1, normed_sum_0, down_last = links.tick(
-        qkv_grad_1, normed_part_1, normed_sum_0, down_last
-    )
-
-    normed_last_0 = links.sum_second(normed_part_0, normed_sum_0)
-    normed_sum_1 = links.sum_first(normed_part_1)
-    attended_all = jnp.concatenate([saved[t][0] for t in range(trees)], axis=0)
-    grad_out = dot_tn(attended_all, jnp.concatenate([out_all_0, out_all_1], axis=0)).astype(BF16)
-    grad_out, qkv_grad_0, qkv_grad_1 = links.tick(grad_out, qkv_grad_0, qkv_grad_1)
+
+    down_parts = parts(down_part)
+    back_0, _, (down_0,) = links.carry(attention_back(0, saved_0), sums=[down_parts[0]])
+    back_1, _, (down_1,) = links.carry(attention_back(1, saved_1), sums=[down_parts[1]])
+    results = [
+        (middle + RESIDUAL * down).astype(BF16)
+        for middle, down in ((middle_0, down_0), (middle_1, down_1))
+    ]
+    qkv_grad = jnp.concatenate(
+        [jnp.concatenate(back_0, axis=1), jnp.concatenate(back_1, axis=1)], axis=0
+    )
+    normed_part = dot_nn(qkv_grad, w_qkv).astype(BF16)
+    qkv_grad, normed_part, results = links.tick(qkv_grad, normed_part, results)
+    attended_all = jnp.concatenate([saved_0[0], saved_1[0]], axis=0)
+    out_all = jnp.concatenate(out_alls, axis=0)
+    normed_all = jnp.concatenate([normed_0, normed_1], axis=0)
+    (grad_out, grad_qkv), _, normed_grads = links.carry(
+        lambda comm: products(
+            [(attended_all, out_all, True), (qkv_grad, normed_all, True)], 128 if shard > 4 else 256, comm
+        ),
+        sums=parts(normed_part),
+    )
+    grad_out, grad_qkv, normed_grads = links.tick(grad_out, grad_qkv, normed_grads)
     links.feed("out", grad_out, 1)
-    grad_qkv = dot_tn(
-        jnp.concatenate([qkv_grad_0, qkv_grad_1], axis=0), jnp.concatenate(normed_all, axis=0)
-    ).astype(BF16)
-    grad_qkv, normed_last_0, normed_sum_1 = links.tick(grad_qkv, normed_last_0, normed_sum_1)
-    links.feed("qkv", grad_qkv, 2)
-
-    normed_last_1 = links.sum_second(normed_part_1, normed_sum_1)
-    down = links.sum_last(down_part, down_sum, down_last)
-    results = [
-        (middle + RESIDUAL * down[t]).astype(BF16) for t, middle in enumerate((middle_0, middle_1))
-    ]
-    results, normed_last_1 = links.tick(results, normed_last_1)
-    normed_grads = links.sum_last(normed_part_0, normed_sum_0, normed_last_0)
-    normed_grads += links.sum_last(normed_part_1, normed_sum_1, normed_last_1)
+    links.feed("qkv", grad_qkv, 1)
     input_grads = []
     gain_attn_sum = jnp.zeros((width,), F32)
     for t in range(trees):

time: 1240 us -> 1340 us (1.081)
  Pallas kernels: 137 us -> 583 us
  waiting for transfers between devices: 335 us -> 189 us
  matrix products: 269 us -> 196 us
  starting transfers between devices: 215 us -> 155 us
  local copies, waits for them, and re-layouts: 93.5 us -> 60.2 us
  other arithmetic: 172 us -> 149 us
    pallas_call x0 -> x6, Pallas kernels: none -> 369 us  [the longest x3 230 us: products(): pl.pallas_call(kernel, grid=(total,), in_specs=specs + right_specs + list...]
    ppermute x56 -> x8, waiting for transfers between devices: 197 us -> 15.6 us  [the longest x2 14.5 us: gather_start(): lax.ppermute(own, 'shard', self.x)]
    dot_general x5 -> x1, matrix products: 84.9 us -> 19.7 us  [dot_tn(): lax.dot_general(left, right, (((0,), (0,)), ((), ())), preferred_element_...]
    ppermute x56 -> x8, starting transfers between devices: 57.1 us -> 8.17 us  [the longest x2 2.99 us: gather_more(): first = lax.ppermute(from_y[:half], 'shard', self.x)]
    ppermute x75 -> x25, waiting for transfers between devices: 113 us -> 161 us  [tick(): move = lambda v, perm: lax.ppermute(v, 'replica', perm)]
    pallas_call x2, Pallas kernels: 47.5 us -> 91.8 us  [attention_backward(): pl.pallas_call(functools.partial(attention_backward_kernel, kv_heads, blo...]
    unnamed x460 -> x199, local copies, waits for them, and re-layouts: 58 us -> 13.9 us
    pallas_call x2, Pallas kernels: 35.2 us -> 69.9 us  [attention_forward(): pl.pallas_call(functools.partial(attention_forward_kernel, kv_heads, bloc...]
  transfers between devices with their start and end apart: 145 -> 47, of which waited for: 41 -> 12; matrix products, arithmetic and copies ran while one was open for 32% -> 20% of each run, Pallas kernels for 11% -> 25%
where the time goes in v3:
time: 1340 us
  Pallas kernels  583 us (44%)
  matrix products  196 us (15%)
  waiting for transfers between devices  189 us (14%)
  starting transfers between devices  155 us (12%)
  other arithmetic  149 us (11%)
  local copies, waits for them, and re-layouts  60.2 us (4%)
    pallas_call x3, Pallas kernels, products(): pl.pallas_call(kernel, grid=(total,), in_specs=specs + right_specs + list...  230 us
    ppermute x25, waiting for transfers between devices, tick(): move = lambda v, perm: lax.ppermute(v, 'replica', perm)  161 us
    pallas_call x3, Pallas kernels, transfer(): pl.pallas_call(kernel, grid=(1,), in_specs=comm.in_specs, out_specs=comm....  139 us
    ppermute x25, starting transfers between devices, tick(): move = lambda v, perm: lax.ppermute(v, 'replica', perm)  130 us
    dot_general x7, matrix products, dot_nt(): lax.dot_general(left, right, (((1,), (1,)), ((), ())), preferred_element_...  103 us
    pallas_call x2, Pallas kernels, attention_backward(): pl.pallas_call(functools.partial(attention_backward_kernel, kv_heads, blo...  91.8 us
    dot_general x7, matrix products, dot_nn(): lax.dot_general(left, right, (((1,), (0,)), ((), ())), preferred_element_...  73.5 us
    pallas_call x2, Pallas kernels, attention_forward(): pl.pallas_call(functools.partial(attention_forward_kernel, kv_heads, bloc...  69.9 us
  transfers between devices with their start and end apart: 47, of which 12 were waited for; matrix products, arithmetic and copies ran while one was open for 20% of the time, Pallas kernels for 25%

profile of v3, /device:TPU:0, one launch (start us, length us, event | category | flops | bytes accessed | tf_op | source)
XLA Modules:
  0.0 1335.5 jit_solution(1098210630637864837)
XLA Ops:
  10.6 37.0 %transfer.3 = bf16[1024,2048]{1,0:T(8,128)(2,1)S(1)} custom-call(bf16[256,2048]{1,0:T(8,128)(2,1)S(1)} %get-tuple-element.279.refs_0_), custom_call_target="tpu_custom_call" | custom-call | tf_op jit(solution)/shard_map/transfer/pallas_call | solution.py:291
  73.0 35.5 %attention_forward.2 = (bf16[1024,512]{1,0:T(8,128)(2,1)S(1)}, bf16[1024,512]{1,0:T(8,128)(2,1)S(1)}, bf16[1024,256]{1,0:T(8,128)(2,1)S(1)}, f32[1024,128]{1,0:T(8,128)S(1)}, bf16[1024,2048]{1,0:T(8,128)(2,1)S(1)}) custom-call(f32[1024,768]{1,0:T(8,128)S(1)} %fusion.72.refs_0_.refs_1_, f32[1024,768]{1,0:T(8,128)S(1)} %fusion.72.refs_0_.refs_1_, ...), custom_call_target="tpu_custom_call" | custom-call | flops 10000000000 | bytes 12000000 | tf_op jit(solution)/shard_map/attention_forward/pallas_call | solution.py:479
  123.4 34.4 %attention_forward.3 = (bf16[1024,512]{1,0:T(8,128)(2,1)S(1)}, bf16[1024,512]{1,0:T(8,128)(2,1)S(1)}, bf16[1024,256]{1,0:T(8,128)(2,1)S(1)}, f32[1024,128]{1,0:T(8,128)S(1)}, f32[256,2048]{1,0:T(8,128)S(1)}) custom-call(f32[1024,768]{1,0:T(8,128)S(1)} %copy-done.17, f32[1024,768]{1,0:T(8,128)S(1)} %copy-done.17, f32[1024,128]{1,0:T(8,128)S(1)} %copy-done.12, ...), custom_call_target="tpu_custom_call" | custom-call | flops 10000000000 | bytes 12000000 | tf_op jit(solution)/shard_map/attention_forward/pallas_call | solution.py:479
  163.4 67.4 %transfer.4 = (bf16[1024,2048]{1,0:T(8,128)(2,1)S(1)}, f32[256,2048]{1,0:T(8,128)S(1)}) custom-call(bf16[256,2048]{1,0:T(8,128)(2,1)S(1)} %multiply_convert_fusion.9.refs_0_, bf16[1024,2048]{1,0:T(8,128)(2,1)S(1)} %convolution_convert_fusion.3.refs_1_), custom_call_target="tpu_custom_call" | custom-call | tf_op jit(solution)/shard_map/transfer/pallas_call | solution.py:291
  231.6 34.5 %transfer.5 = bf16[1024,2048]{1,0:T(8,128)(2,1)S(1)} custom-call(bf16[256,2048]{1,0:T(8,128)(2,1)S(1)} %multiply_convert_fusion.8.refs_0_), custom_call_target="tpu_custom_call" | custom-call | tf_op jit(solution)/shard_map/transfer/pallas_call | solution.py:291
  271.5 22.8 %convolution_convert_fusion.2 = bf16[2048,2048]{1,0:T(8,128)(2,1)} fusion(bf16[2048,2048]{1,0:T(8,128)(2,1)S(1)} %constant_dynamic-update-slice_fusion.3.refs_2_, bf16[2048,2048]{1,0:T(8,128)(2,1)} %param.20), kind=kOutput, calls=%fused_computation.42 | convolution fusion | flops 17184063488 | bytes 25165824 | tf_op jit(solution)/shard_map/dot_general | solution.py:27
  317.5 27.6 %fusion.66 = (bf16[2048,2048]{1,0:T(8,128)(2,1)}, bf16[2048,2048]{1,0:T(8,128)(2,1)}) fusion(bf16[2048,2048]{1,0:T(8,128)(2,1)} %convolution_convert_fusion.2, bf16[2048,2048]{1,0:T(8,128)(2,1)} %copy-done.62, bf16[2048,2048]{1,0:T(8,128)(2,1)} %param.21), kind=kOutput, calls=%fused_computation.215 | convolution fusion | flops 17213423616 | bytes 41943040 | tf_op jit(solution)/shard_map/dot_general | solution.py:27
  354.5 19.7 %convolution_convert_fusion.1 = bf16[2048,2048]{1,0:T(8,128)(2,1)S(1)} fusion(bf16[2048,2048]{1,0:T(8,128)(2,1)S(1)} %copy-done.91, bf16[2048,2048]{1,0:T(8,128)(2,1)S(1)} %fusion.50), kind=kOutput, calls=%fused_computation.41 | convolution fusion | flops 17184063488 | bytes 25165824 | tf_op jit(solution)/shard_map/dot_general | solution.py:35
  399.5 31.8 %fusion.11 = (bf16[2048,2048]{1,0:T(8,128)(2,1)}, bf16[2048,2048]{1,0:T(8,128)(2,1)}) fusion(bf16[2048,2048]{1,0:T(8,128)(2,1)} %convolution_convert_fusion.2, bf16[2048,2048]{1,0:T(8,128)(2,1)} %get-tuple-element.145, bf16[2048,2048]{1,0:T(8,128)(2,1)} %copy-done.78, bf16[2048,2048]{1,0:T(8,128)(2,1)} %refs_1_.1), kind=kOutput, calls=%fused_computation.16 | convolution fusion | flops 17242783744 | bytes 50331648 | tf_op jit(solution)/shard_map/dot_general | solution.py:27
  431.3 24.2 %fusion.74 = f32[2048,2048]{1,0:T(8,128)} fusion(bf16[2048,2048]{1,0:T(8,128)(2,1)} %get-tuple-element.149.refs_0_, bf16[2048,2048]{1,0:T(8,128)(2,1)} %param.20), kind=kOutput, calls=%fused_computation.223 | convolution fusion | flops 17179869184 | bytes 33554432 | tf_op jit(solution)/shard_map/dot_general | solution.py:31
  455.5 24.0 %add_convert_fusion = bf16[2048,2048]{1,0:T(8,128)(2,1)S(1)} fusion(f32[2048,2048]{1,0:T(8,128)} %fusion.74, bf16[2048,2048]{1,0:T(8,128)(2,1)} %get-tuple-element.150.refs_1_, bf16[2048,2048]{1,0:T(8,128)(2,1)} %param.21), kind=kOutput, calls=%fused_computation.17 | convolution fusion | flops 17188257792 | bytes 41943040 | tf_op jit(solution)/shard_map/dot_general | solution.py:31
  491.5 78.4 %products.3 = (bf16[2048,2048]{1,0:T(8,128)(2,1)}, bf16[2048,2048]{1,0:T(8,128)(2,1)}, f32[256,2048]{1,0:T(8,128)}, f32[256,2048]{1,0:T(8,128)}) custom-call(bf16[2048,2048]{1,0:T(8,128)(2,1)} %get-tuple-element.149.refs_0_, bf16[2048,2048]{1,0:T(8,128)(2,1)} %get-tuple-element.150.refs_1_, bf16[2048,2048]{1,0:T(8,128)(2,1)} %copy-done.62, ...), custom_call_target="tpu_custom_call" | custom-call | flops 34359738368 | bytes 30000000 | tf_op jit(solution)/shard_map/products/pallas_call | solution.py:348
  601.7 91.8 %collective-permute-start.15 = (bf16[1024,2048]{1,0:T(8,128)(2,1)}, bf16[1024,2048]{1,0:T(8,128)(2,1)}, u32[]{:S(2)}, u32[]{:S(2)}) collective-permute-start(bf16[1024,2048]{1,0:T(8,128)(2,1)} %add_convert_fusion.7), channel_id=1, source_target_pairs={{0,2},{1,3},{6,4},{7,5},{8,10},{9,11},{14,12},{15,13},{16,18},{17,... | collective-permute-start | bytes 12582920 | tf_op jit(solution)/shard_map/ppermute | solution.py:809
  704.4 75.9 %products.4 = (bf16[2048,2048]{1,0:T(8,128)(2,1)}, bf16[1024,2048]{1,0:T(8,128)(2,1)}, bf16[1024,2048]{1,0:T(8,128)(2,1)}) custom-call(bf16[2048,2048]{1,0:T(8,128)(2,1)} %get-tuple-element.159.refs_0_, bf16[2048,2048]{1,0:T(8,128)(2,1)} %refs_1_.1, bf16[256,2048]{1,0:T(8,128)(2,1)} %multiply_convert_fusion.1.refs_2_, ...), custom_call_target="tpu_custom_call" | custom-call | flops 17179869184 | bytes 30000000 | tf_op jit(solution)/shard_map/products/pallas_call | solution.py:348
  812.1 39.1 %attention_backward.3 = (bf16[1024,512]{1,0:T(8,128)(2,1)}, bf16[1024,256]{1,0:T(8,128)(2,1)}, f32[256,2048]{1,0:T(8,128)}) custom-call(bf16[1024,512]{1,0:T(8,128)(2,1)} %convolution_convert_fusion.5.refs_0_, bf16[1024,512]{1,0:T(8,128)(2,1)} %copy-done.18, bf16[1024,256]{1,0:T(8,128)(2,1)} %copy-done.20, f32[1024,128]{1,0:T(8,128)} %copy-done.21, ...), custom_call_target="tpu_custom_call" | custom-call | flops 20000000000 | bytes 12000000 | tf_op jit(solution)/shard_map/attention_backward/pallas_call | solution.py:626
  851.2 52.7 %attention_backward.2 = (bf16[1024,512]{1,0:T(8,128)(2,1)}, bf16[1024,256]{1,0:T(8,128)(2,1)}, f32[256,2048]{1,0:T(8,128)}) custom-call(bf16[1024,512]{1,0:T(8,128)(2,1)} %convolution_convert_fusion.6.refs_0_, bf16[1024,512]{1,0:T(8,128)(2,1)} %copy-done.19, bf16[1024,256]{1,0:T(8,128)(2,1)} %copy-done.22, f32[1024,128]{1,0:T(8,128)} %copy-done.23, ...), custom_call_target="tpu_custom_call" | custom-call | flops 20000000000 | bytes 12000000 | tf_op jit(solution)/shard_map/attention_backward/pallas_call | solution.py:626
  915.8 19.9 %convolution_convert_fusion = bf16[2048,2048]{1,0:T(8,128)(2,1)} fusion(bf16[768,2048]{1,0:T(8,128)(2,1)} %constant_dynamic-update-slice_fusion, bf16[1024,256]{1,0:T(8,128)(2,1)S(1)} %copy-done.72, bf16[1024,512]{1,0:T(8,128)(2,1)S(1)} %copy-done.67, bf16[1024,256]{1,0:T(8,128)(2,1)S(1)} %copy-done.73, bf16[1024,512]{1,0:T(8,128)(2,1)S(1)} %copy-done.68), kind=kOutput, calls=%fused_computation.40 | convolution fusion | flops 6459228160 | bytes 14680064 | tf_op jit(solution)/shard_map/dot_general | solution.py:31
  980.1 76.2 %products.5 = (bf16[512,2048]{1,0:T(8,128)(2,1)}, bf16[768,2048]{1,0:T(8,128)(2,1)}, f32[256,2048]{1,0:T(8,128)}, f32[256,2048]{1,0:T(8,128)}) custom-call(bf16[2048,512]{1,0:T(8,128)(2,1)} %pad_maximum_fusion.2.refs_0_, bf16[2048,768]{1,0:T(8,128)(2,1)} %maximum_maximum_fusion.refs_1_, bf16[2048,2048]{1,0:T(8,128)(2,1)} %pad_maximum_fusion.refs_2_, ...), custom_call_target="tpu_custom_call" | custom-call | flops 10737418240 | bytes 30000000 | tf_op jit(solution)/shard_map/products/pallas_call | solution.py:348
  1071.9 82.9 %collective-permute-done.28.refs_1_ = bf16[1024,2048]{1,0:T(8,128)(2,1)} collective-permute-done((bf16[1024,2048]{1,0:T(8,128)(2,1)}, bf16[1024,2048]{1,0:T(8,128)(2,1)}, u32[]{:S(2)}, u32[]{:S(2)}) %collective-permute-start.28) | collective-permute-done | bytes 4194336 | tf_op jit(solution)/shard_map/ppermute | solution.py:809
  1190.4 16.4 %collective-permute-done.32 = bf16[384,2048]{1,0:T(8,128)(2,1)} collective-permute-done((bf16[384,2048]{1,0:T(8,128)(2,1)}, bf16[384,2048]{1,0:T(8,128)(2,1)}, u32[]{:S(2)}, u32[]{:S(2)}) %collective-permute-start.32) | collective-permute-done | bytes 1572896 | tf_op jit(solution)/shard_map/ppermute | solution.py:809
  1216.5 19.0 %collective-permute-done.35.refs_1_ = bf16[256,2048]{1,0:T(8,128)(2,1)S(1)} collective-permute-done((bf16[256,2048]{1,0:T(8,128)(2,1)S(1)}, bf16[256,2048]{1,0:T(8,128)(2,1)S(1)}, u32[]{:S(2)}, u32[]{:S(2)}) %collective-permute-start.35) | collective-permute-done | bytes 1048608 | tf_op jit(solution)/shard_map/ppermute | solution.py:809
  1247.1 15.9 %assemble.9 = f32[2048,2048]{1,0:T(8,128)} custom-call(s32[2]{0:T(128)S(1)} %pad_add_fusion.where_ref, bf16[1024,2048]{1,0:T(8,128)(2,1)} %add_convert_fusion.6.refs_0_, bf16[1024,2048]{1,0:T(8,128)(2,1)} %collective-permute-done.16.refs_1_, bf16[1024,2048]{1,0:T(8,128)(2,1)} %collective-permute-done.45.refs_2_, ...), custom_call_target="tpu_custom_call" | custom-call | bytes 25165824 | tf_op jit(solution)/shard_map/assemble/pallas_call | solution.py:702
  1264.5 19.9 %collective-permute-done.36.refs_1_ = bf16[384,2048]{1,0:T(8,128)(2,1)} collective-permute-done((bf16[384,2048]{1,0:T(8,128)(2,1)}, bf16[384,2048]{1,0:T(8,128)(2,1)}, u32[]{:S(2)}, u32[]{:S(2)}) %collective-permute-start.36) | collective-permute-done | bytes 1572896 | tf_op jit(solution)/shard_map/ppermute | solution.py:809
  1309.9 14.8 %assemble.8 = f32[2048,2048]{1,0:T(8,128)} custom-call(s32[2]{0:T(128)S(1)} %pad_add_fusion.where_ref, bf16[1024,2048]{1,0:T(8,128)(2,1)} %add_convert_fusion.1.refs_0_, bf16[1024,2048]{1,0:T(8,128)(2,1)} %collective-permute-done.28.refs_1_, bf16[1024,2048]{1,0:T(8,128)(2,1)} %collective-permute-done.43.refs_2_, ...), custom_call_target="tpu_custom_call" | custom-call | bytes 25165824 | tf_op jit(solution)/shard_map/assemble/pallas_call | solution.py:702
  (422 shorter events, 371.0 us)
Async XLA Ops:
  2.2 51.7 %collective-permute-start = (bf16[1536]{0:T(1024)(128)(2,1)S(1)}, bf16[1536]{0:T(1024)(128)(2,1)S(1)}, u32[]{:S(2)}, u32[]{:S(2)}) collective-permute-start(bf16[1536]{0:T(1024)(128)(2,1)S(1)} %pad_maximum_fusion.5), channel_id=1, source_target_pairs={{0,8},{8,0},{16,24},{24,16},{1,9},{9,1},{17,25},{25,17},{2,10},{10... | collective-permute-start | bytes 9224 | tf_op jit(solution)/shard_map/ppermute | solution.py:744
  5.2 48.7 %collective-permute-start.1 = (bf16[1536]{0:T(1024)(128)(2,1)S(1)}, bf16[1536]{0:T(1024)(128)(2,1)S(1)}, u32[]{:S(2)}, u32[]{:S(2)}) collective-permute-start(bf16[1536]{0:T(1024)(128)(2,1)S(1)} %pad_maximum_fusion.5), channel_id=1, source_target_pairs={{0,16},{8,24},{16,0},{24,8},{1,17},{9,25},{17,1},{25,9},{2,18},{10... | collective-permute-start | bytes 9224 | tf_op jit(solution)/shard_map/ppermute | solution.py:745
  6.7 47.2 %collective-permute-start.2 = (bf16[1536]{0:T(1024)(128)(2,1)S(1)}, bf16[1536]{0:T(1024)(128)(2,1)S(1)}, u32[]{:S(2)}, u32[]{:S(2)}) collective-permute-start(bf16[1536]{0:T(1024)(128)(2,1)S(1)} %pad_maximum_fusion.5), channel_id=1, source_target_pairs={{0,24},{8,16},{16,8},{24,0},{1,25},{9,17},{17,9},{25,1},{2,26},{10... | collective-permute-start | bytes 9224 | tf_op jit(solution)/shard_map/ppermute | solution.py:746
  268.3 40.6 %collective-permute-start.5 = (bf16[256,2048]{1,0:T(8,128)(2,1)S(1)}, bf16[256,2048]{1,0:T(8,128)(2,1)S(1)}, u32[]{:S(2)}, u32[]{:S(2)}) collective-permute-start(bf16[256,2048]{1,0:T(8,128)(2,1)S(1)} %copy-done.37), channel_id=1, source_target_pairs={{0,8},{8,0},{16,24},{24,16},{1,9},{9,1},{17,25},{25,17},{2,10},{10... | collective-permute-start | bytes 3145736 | tf_op jit(solution)/shard_map/ppermute | solution.py:763
  268.8 41.2 %collective-permute-start.6 = (bf16[256,2048]{1,0:T(8,128)(2,1)S(1)}, bf16[256,2048]{1,0:T(8,128)(2,1)S(1)}, u32[]{:S(2)}, u32[]{:S(2)}) collective-permute-start(bf16[256,2048]{1,0:T(8,128)(2,1)S(1)} %copy-done.37), channel_id=1, source_target_pairs={{0,16},{8,24},{16,0},{24,8},{1,17},{9,25},{17,1},{25,9},{2,18},{10... | collective-permute-start | bytes 3145736 | tf_op jit(solution)/shard_map/ppermute | solution.py:763
  394.0 93.9 %collective-permute-start.12 = (bf16[1024,2048]{1,0:T(8,128)(2,1)}, bf16[1024,2048]{1,0:T(8,128)(2,1)}, u32[]{:S(2)}, u32[]{:S(2)}) collective-permute-start(bf16[1024,2048]{1,0:T(8,128)(2,1)} %add_convert_fusion.9), channel_id=1, source_target_pairs={{0,2},{1,3},{6,4},{7,5},{8,10},{9,11},{14,12},{15,13},{16,18},{17,... | collective-permute-start | bytes 12582920 | tf_op jit(solution)/shard_map/ppermute | solution.py:809
  583.7 114.5 %collective-permute-start.17 = (bf16[1024,2048]{1,0:T(8,128)(2,1)}, bf16[1024,2048]{1,0:T(8,128)(2,1)S(1)}, u32[]{:S(2)}, u32[]{:S(2)}) collective-permute-start(bf16[1024,2048]{1,0:T(8,128)(2,1)} %constant_dynamic-slice_fusion.6), channel_id=1, source_target_pairs={{0,1},{1,0},{2,3},{3,2},{4,5},{5,4},{6,7},{7,6},{8,9},{9,8},{10,11... | collective-permute-start | bytes 12582920 | tf_op jit(solution)/shard_map/ppermute | solution.py:794
  600.1 180.1 %collective-permute-start.16 = (bf16[1024,2048]{1,0:T(8,128)(2,1)}, bf16[1024,2048]{1,0:T(8,128)(2,1)}, u32[]{:S(2)}, u32[]{:S(2)}) collective-permute-start(bf16[1024,2048]{1,0:T(8,128)(2,1)} %add_convert_fusion.6.refs_0_), channel_id=1, source_target_pairs={{2,0},{3,1},{4,6},{5,7},{10,8},{11,9},{12,14},{13,15},{18,16},{19,... | collective-permute-start | bytes 12582920 | tf_op jit(solution)/shard_map/ppermute | solution.py:809
  601.7 179.5 %collective-permute-start.15 = (bf16[1024,2048]{1,0:T(8,128)(2,1)}, bf16[1024,2048]{1,0:T(8,128)(2,1)}, u32[]{:S(2)}, u32[]{:S(2)}) collective-permute-start(bf16[1024,2048]{1,0:T(8,128)(2,1)} %add_convert_fusion.7), channel_id=1, source_target_pairs={{0,2},{1,3},{6,4},{7,5},{8,10},{9,11},{14,12},{15,13},{16,18},{17,... | collective-permute-start | bytes 12582920 | tf_op jit(solution)/shard_map/ppermute | solution.py:809
  802.2 133.4 %collective-permute-start.19 = (bf16[1024,2048]{1,0:T(8,128)(2,1)}, bf16[1024,2048]{1,0:T(8,128)(2,1)}, u32[]{:S(2)}, u32[]{:S(2)}) collective-permute-start(bf16[1024,2048]{1,0:T(8,128)(2,1)} %add_convert_fusion.4), channel_id=1, source_target_pairs={{2,4},{3,5},{4,2},{5,3},{10,12},{11,13},{12,10},{13,11},{18,20},{1... | collective-permute-start | bytes 12582920 | tf_op jit(solution)/shard_map/ppermute | solution.py:809
  804.8 130.9 %collective-permute-start.18 = (bf16[1024,2048]{1,0:T(8,128)(2,1)}, bf16[1024,2048]{1,0:T(8,128)(2,1)}, u32[]{:S(2)}, u32[]{:S(2)}) collective-permute-start(bf16[1024,2048]{1,0:T(8,128)(2,1)} %add_convert_fusion.5), channel_id=1, source_target_pairs={{0,2},{1,3},{6,4},{7,5},{8,10},{9,11},{14,12},{15,13},{16,18},{17,... | collective-permute-start | bytes 12582920 | tf_op jit(solution)/shard_map/ppermute | solution.py:809
  943.5 112.7 %collective-permute-start.21 = (bf16[1024,2048]{1,0:T(8,128)(2,1)}, bf16[1024,2048]{1,0:T(8,128)(2,1)}, u32[]{:S(2)}, u32[]{:S(2)}) collective-permute-start(bf16[1024,2048]{1,0:T(8,128)(2,1)} %add_convert_fusion.2.refs_0_), channel_id=1, source_target_pairs={{2,0},{3,1},{4,6},{5,7},{10,8},{11,9},{12,14},{13,15},{18,16},{19,... | collective-permute-start | bytes 12582920 | tf_op jit(solution)/shard_map/ppermute | solution.py:809
  952.7 103.5 %collective-permute-start.20 = (bf16[1024,2048]{1,0:T(8,128)(2,1)}, bf16[1024,2048]{1,0:T(8,128)(2,1)}, u32[]{:S(2)}, u32[]{:S(2)}) collective-permute-start(bf16[1024,2048]{1,0:T(8,128)(2,1)} %add_convert_fusion.3), channel_id=1, source_target_pairs={{2,4},{3,5},{4,2},{5,3},{10,12},{11,13},{12,10},{13,11},{18,20},{1... | collective-permute-start | bytes 12582920 | tf_op jit(solution)/shard_map/ppermute | solution.py:809
  1064.0 90.7 %collective-permute-start.28 = (bf16[1024,2048]{1,0:T(8,128)(2,1)}, bf16[1024,2048]{1,0:T(8,128)(2,1)}, u32[]{:S(2)}, u32[]{:S(2)}) collective-permute-start(bf16[1024,2048]{1,0:T(8,128)(2,1)} %add_convert_fusion.1.refs_0_), channel_id=1, source_target_pairs={{2,0},{3,1},{4,6},{5,7},{10,8},{11,9},{12,14},{13,15},{18,16},{19,... | collective-permute-start | bytes 12582920 | tf_op jit(solution)/shard_map/ppermute | solution.py:809
  1069.5 88.3 %collective-permute-start.31 = (bf16[384,2048]{1,0:T(8,128)(2,1)}, bf16[384,2048]{1,0:T(8,128)(2,1)}, u32[]{:S(2)}, u32[]{:S(2)}) collective-permute-start(bf16[384,2048]{1,0:T(8,128)(2,1)} %constant_dynamic-slice_fusion), channel_id=1, source_target_pairs={{0,1},{1,0},{2,3},{3,2},{4,5},{5,4},{6,7},{7,6},{8,9},{9,8},{10,11... | collective-permute-start | bytes 4718600 | tf_op jit(solution)/shard_map/ppermute | solution.py:794
  1157.2 79.7 %collective-permute-start.45 = (bf16[1024,2048]{1,0:T(8,128)(2,1)}, bf16[1024,2048]{1,0:T(8,128)(2,1)}, u32[]{:S(2)}, u32[]{:S(2)}) collective-permute-start(bf16[1024,2048]{1,0:T(8,128)(2,1)} %add_convert_fusion.6.refs_0_), channel_id=1, source_target_pairs={{0,1},{1,0},{2,3},{3,2},{4,5},{5,4},{6,7},{7,6},{8,9},{9,8},{10,11... | collective-permute-start | bytes 12582920 | tf_op jit(solution)/shard_map/ppermute | solution.py:809
  1157.2 86.5 %collective-permute-start.46 = (bf16[1024,2048]{1,0:T(8,128)(2,1)}, bf16[1024,2048]{1,0:T(8,128)(2,1)}, u32[]{:S(2)}, u32[]{:S(2)}) collective-permute-start(bf16[1024,2048]{1,0:T(8,128)(2,1)} %collective-permute-done.16.refs_1_), channel_id=1, source_target_pairs={{0,1},{1,0},{2,3},{3,2},{4,5},{5,4},{6,7},{7,6},{8,9},{9,8},{10,11... | collective-permute-start | bytes 12582920 | tf_op jit(solution)/shard_map/ppermute | solution.py:809
  1216.3 68.8 %collective-permute-start.41 = (bf16[1024,2048]{1,0:T(8,128)(2,1)}, bf16[1024,2048]{1,0:T(8,128)(2,1)}, u32[]{:S(2)}, u32[]{:S(2)}) collective-permute-start(bf16[1024,2048]{1,0:T(8,128)(2,1)} %add_convert_fusion.2.refs_0_), channel_id=1, source_target_pairs={{0,1},{1,0},{2,3},{3,2},{4,5},{5,4},{6,7},{7,6},{8,9},{9,8},{10,11... | collective-permute-start | bytes 12582920 | tf_op jit(solution)/shard_map/ppermute | solution.py:809
  1236.4 53.9 %collective-permute-start.43 = (bf16[1024,2048]{1,0:T(8,128)(2,1)}, bf16[1024,2048]{1,0:T(8,128)(2,1)}, u32[]{:S(2)}, u32[]{:S(2)}) collective-permute-start(bf16[1024,2048]{1,0:T(8,128)(2,1)} %add_convert_fusion.1.refs_0_), channel_id=1, source_target_pairs={{0,1},{1,0},{2,3},{3,2},{4,5},{5,4},{6,7},{7,6},{8,9},{9,8},{10,11... | collective-permute-start | bytes 12582920 | tf_op jit(solution)/shard_map/ppermute | solution.py:809
  1236.4 54.4 %collective-permute-start.42 = (bf16[1024,2048]{1,0:T(8,128)(2,1)}, bf16[1024,2048]{1,0:T(8,128)(2,1)}, u32[]{:S(2)}, u32[]{:S(2)}) collective-permute-start(bf16[1024,2048]{1,0:T(8,128)(2,1)} %collective-permute-done.21.refs_1_), channel_id=1, source_target_pairs={{0,1},{1,0},{2,3},{3,2},{4,5},{5,4},{6,7},{7,6},{8,9},{9,8},{10,11... | collective-permute-start | bytes 12582920 | tf_op jit(solution)/shard_map/ppermute | solution.py:809
  1243.7 66.2 %collective-permute-start.44 = (bf16[1024,2048]{1,0:T(8,128)(2,1)}, bf16[1024,2048]{1,0:T(8,128)(2,1)}, u32[]{:S(2)}, u32[]{:S(2)}) collective-permute-start(bf16[1024,2048]{1,0:T(8,128)(2,1)} %collective-permute-done.28.refs_1_), channel_id=1, source_target_pairs={{0,1},{1,0},{2,3},{3,2},{4,5},{5,4},{6,7},{7,6},{8,9},{9,8},{10,11... | collective-permute-start | bytes 12582920 | tf_op jit(solution)/shard_map/ppermute | solution.py:809
  1245.7 38.8 %collective-permute-start.36 = (bf16[384,2048]{1,0:T(8,128)(2,1)}, bf16[384,2048]{1,0:T(8,128)(2,1)}, u32[]{:S(2)}, u32[]{:S(2)}) collective-permute-start(bf16[384,2048]{1,0:T(8,128)(2,1)} %add_convert_fusion.10.refs_0_), channel_id=1, source_target_pairs={{2,0},{3,1},{4,6},{5,7},{10,8},{11,9},{12,14},{13,15},{18,16},{19,... | collective-permute-start | bytes 4718600 | tf_op jit(solution)/shard_map/ppermute | solution.py:809
  1285.1 42.6 %collective-permute-start.37 = (bf16[384,2048]{1,0:T(8,128)(2,1)}, bf16[384,2048]{1,0:T(8,128)(2,1)S(1)}, u32[]{:S(2)}, u32[]{:S(2)}) collective-permute-start(bf16[384,2048]{1,0:T(8,128)(2,1)} %add_convert_fusion.10.refs_0_), channel_id=1, source_target_pairs={{0,1},{1,0},{2,3},{3,2},{4,5},{5,4},{6,7},{7,6},{8,9},{9,8},{10,11... | collective-permute-start | bytes 4718600 | tf_op jit(solution)/shard_map/ppermute | solution.py:809
  1289.0 38.7 %collective-permute-start.38 = (bf16[384,2048]{1,0:T(8,128)(2,1)}, bf16[384,2048]{1,0:T(8,128)(2,1)S(1)}, u32[]{:S(2)}, u32[]{:S(2)}) collective-permute-start(bf16[384,2048]{1,0:T(8,128)(2,1)} %collective-permute-done.36.refs_1_), channel_id=1, source_target_pairs={{0,1},{1,0},{2,3},{3,2},{4,5},{5,4},{6,7},{7,6},{8,9},{9,8},{10,11... | collective-permute-start | bytes 4718600 | tf_op jit(solution)/shard_map/ppermute | solution.py:809
  (117 other events, 2945.3 us)

commit v4 on v3

--- a/solution.py
+++ b/solution.py
@@ -203,6 +203,145 @@
                 copy.wait_send()
 
 
+class LineJob:
+    LINE_ROWS = 32
+    LAG = 2
+
+    def __init__(self, grad):
+        self.operand = grad
+        self.half, self.width = grad.shape[0] // 2, grad.shape[1]
+        self.chunks = self.half // self.LINE_ROWS
+        self.steps = self.chunks + 1 + 3 * self.LAG
+        self.out_shape = jax.ShapeDtypeStruct(grad.shape, BF16)
+        self.out_spec = pl.BlockSpec(memory_space=pl.ANY)
+
+    def scratch(self):
+        place = lambda: pltpu.VMEM((self.half, self.width), BF16)
+        return [place(), place(), place(), place(), pltpu.SemaphoreType.DMA((9, self.chunks))]
+
+    def bind(self, grad, out, scratch, x, y):
+        self.grad, self.out = grad, out
+        self.from_core, self.own, self.from_line, self.from_inner, self.sems = scratch
+        shard, place = lax.axis_index("shard"), lax.axis_index("replica")
+        self.core, z = place % 2, place // 2
+        self.inner = (z == 1) | (z == 2)
+        self.outer = (z == 0) | (z == 3)
+        self.twin = (shard, z * 2 + 1 - self.core)
+        self.pair = (shard, (z + 1 - 2 * (z % 2)) * 2 + self.core)
+        self.across = (shard, (3 - z) * 2 + self.core)
+
+    def chunk(self, c):
+        return pl.ds(pl.multiple_of(c * self.LINE_ROWS, self.LINE_ROWS), self.LINE_ROWS)
+
+    def at(self, core, c):
+        return pl.ds(
+            pl.multiple_of(core * self.half + c * self.LINE_ROWS, self.LINE_ROWS), self.LINE_ROWS
+        )
+
+    def send(self, source, target, index, arrival, device, c):
+        return pltpu.make_async_remote_copy(
+            source,
+            target,
+            self.sems.at[index, c],
+            self.sems.at[arrival, c],
+            device_id=device,
+            device_id_type=MESH,
+        )
+
+    def to_twin(self, c):
+        source = self.grad.at[self.at(1 - self.core, c), :]
+        return self.send(source, self.from_core.at[self.chunk(c), :], 0, 1, self.twin, c)
+
+    def load(self, c):
+        source = self.grad.at[self.at(self.core, c), :]
+        return pltpu.make_async_copy(source, self.own.at[self.chunk(c), :], self.sems.at[2, c])
+
+    def inward(self, c):
+        rows = self.chunk(c)
+        return self.send(self.own.at[rows, :], self.from_line.at[rows, :], 3, 4, self.pair, c)
+
+    def between(self, c):
+        rows = self.chunk(c)
+        return self.send(self.own.at[rows, :], self.from_inner.at[rows, :], 3, 5, self.across, c)
+
+    def outward(self, c):
+        rows = self.chunk(c)
+        return self.send(self.from_core.at[rows, :], self.from_line.at[rows, :], 6, 4, self.pair, c)
+
+    def store(self, source, c):
+        target = self.out.at[self.at(self.core, c), :]
+        return pltpu.make_async_copy(source.at[self.chunk(c), :], target, self.sems.at[2, c])
+
+    def give(self, source, c):
+        target = self.out.at[self.at(self.core, c), :]
+        return self.send(source.at[self.chunk(c), :], target, 7, 8, self.twin, c)
+
+    def begin(self):
+        pass
+
+    def stages(self):
+        return []
+
+    def step(self, s):
+        n, lag = self.chunks, self.LAG
+        live = lambda begin: (s >= begin) & (s < n + begin)
+        add = lambda a, b: (a.astype(F32) + b.astype(F32)).astype(BF16)
+
+        @pl.when(live(0))
+        def _():
+            self.to_twin(s).start()
+            self.load(s).start()
+
+        @pl.when(live(1))
+        def _():
+            c = s - 1
+            rows = self.chunk(c)
+            self.to_twin(c).wait()
+            self.load(c).wait()
+            self.own[rows, :] = add(self.own[rows, :], self.from_core[rows, :])
+            pl.when(self.outer)(lambda: self.inward(c).start())
+
+        @pl.when(live(1 + lag) & self.inner)
+        def _():
+            c = s - 1 - lag
+            rows = self.chunk(c)
+            self.inward(c).wait_recv()
+            self.own[rows, :] = add(self.own[rows, :], self.from_line[rows, :])
+            self.between(c).start()
+
+        @pl.when(live(1 + 2 * lag) & self.inner)
+        def _():
+            c = s - 1 - 2 * lag
+            rows = self.chunk(c)
+            self.between(c).wait_recv()
+            self.from_core[rows, :] = add(self.own[rows, :], self.from_inner[rows, :])
+            self.outward(c).start()
+            self.store(self.from_core, c).start()
+            self.give(self.from_core, c).start()
+
+        @pl.when(live(1 + 3 * lag) & self.outer)
+        def _():
+            c = s - 1 - 3 * lag
+            self.outward(c).wait_recv()
+            self.store(self.from_line, c).start()
+            self.give(self.from_line, c).start()
+
+    def finish(self):
+        def body(c, carry):
+            self.store(self.from_line, c).wait()
+            self.give(self.from_line, c).wait()
+
+            @pl.when(self.inner)
+            def _():
+                self.between(c).wait_send()
+                self.outward(c).wait_send()
+
+            pl.when(self.outer)(lambda: self.inward(c).wait_send())
+            return carry
+
+        lax.fori_loop(0, self.chunks, body, 0)
+
+
 class Comm:
     def __init__(self, jobs, number):
         self.jobs, self.number = jobs, number
@@ -222,12 +361,32 @@
             job.bind(operand, out, scratch[:count], x, y)
             scratch = scratch[count:]
 
+        lines = [job for job in self.jobs if isinstance(job, LineJob)]
+        square = len(lines) < len(self.jobs)
+
         @pl.when(now)
         def _():
             barrier = pltpu.get_barrier_semaphore()
-            for device in (x, y):
+
+            def greet(device):
                 pl.semaphore_signal(barrier, inc=1, device_id=device, device_id_type=MESH)
-            pl.semaphore_wait(barrier, 2)
+
+            near = ([x, y] if square else []) + ([lines[0].twin, lines[0].pair] if lines else [])
+            for device in near:
+                greet(device)
+            if lines:
+
+                @pl.when(lines[0].inner)
+                def _():
+                    greet(lines[0].across)
+                    pl.semaphore_wait(barrier, len(near) + 1)
+
+                @pl.when(lines[0].outer)
+                def _():
+                    pl.semaphore_wait(barrier, len(near))
+
+            else:
+                pl.semaphore_wait(barrier, len(near))
             for job in self.jobs:
                 job.begin()
 
@@ -236,8 +395,20 @@
 
     def advance(self, step, steps):
         stages = self.stages()
+        for job in self.jobs:
+            if isinstance(job, LineJob):
+                each = -(-job.steps // steps)
+
+                def body(k, carry, job=job, each=each):
+                    job.step(step * each + k)
+                    return carry
+
+                lax.fori_loop(0, each, body, 0)
         for index, stage in enumerate(stages):
-            due = min(steps - 1, steps // 2 + index * (steps - steps // 2) // len(stages))
+            if steps <= 4:
+                due = min(steps - 1, steps // 2 + index * (steps - steps // 2) // len(stages))
+            else:
+                due = min(steps - 1, max(1, int(steps * (0.25 + 0.5 * index / len(stages)))))
             pl.when(step == due)(stage)
 
     def finish(self, now):
@@ -279,28 +450,32 @@
 
 def transfer(comm):
     count = len(comm.operands)
+    steps = 9 if any(isinstance(job, LineJob) for job in comm.jobs) else 1
 
     def kernel(*refs):
         operands, outs, scratch = split_refs(refs, count, count, len(comm.scratch))
-        now = pl.program_id(0) == 0
-        comm.enter(operands, outs, scratch, now)
-        for stage in comm.stages():
-            stage()
-        comm.finish(now)
+        step = pl.program_id(0)
+        comm.enter(operands, outs, scratch, step == 0)
+        if steps == 1:
+            for stage in comm.stages():
+                stage()
+        else:
+            comm.advance(step, steps)
+        comm.finish(step == steps - 1)
 
     return pl.pallas_call(
         kernel,
-        grid=(1,),
+        grid=(steps,),
         in_specs=comm.in_specs,
         out_specs=comm.out_specs,
         out_shape=comm.out_shapes,
         scratch_shapes=comm.scratch,
-        compiler_params=comm_params(comm, 40),
+        compiler_params=comm_params(comm, 48),
         name="transfer",
     )(*comm.operands)
 
 
-def products(items, block, comm):
+def products(items, block, comm, joined=False):
     specs, shapes, out_specs, steps, rights = [], [], [], [], []
     total = sum((l.shape[1] if t else l.shape[0]) // block for l, _, t in items)
     begin = 0
@@ -315,8 +490,9 @@
             specs.append(pl.BlockSpec((left.shape[0], block), lambda i, p=place: (0, p(i))))
         else:
             specs.append(pl.BlockSpec((block, left.shape[1]), lambda i, p=place: (p(i), 0)))
-        out_specs.append(pl.BlockSpec((block, right.shape[1]), lambda i, p=place: (p(i), 0)))
-        shapes.append(jax.ShapeDtypeStruct((size, right.shape[1]), BF16))
+        if not joined:
+            out_specs.append(pl.BlockSpec((block, right.shape[1]), lambda i, p=place: (p(i), 0)))
+            shapes.append(jax.ShapeDtypeStruct((size, right.shape[1]), BF16))
         if not any(right is r for r in rights):
             rights.append(right)
         steps.append((begin, count))
@@ -326,10 +502,15 @@
     ]
     which = [next(k for k, r in enumerate(rights) if r is right) for _, right, _ in items]
     n = len(items)
+    if joined:
+        width = items[0][1].shape[1]
+        out_specs = [pl.BlockSpec((block, width), lambda i: (i, 0))]
+        shapes = [jax.ShapeDtypeStruct((total * block, width), BF16)]
+    made = len(shapes)
 
     def kernel(*refs):
         lefts, held, operands, outs, comm_outs, scratch = split_refs(
-            refs, n, len(rights), len(comm.operands), n, len(comm.operands), len(comm.scratch)
+            refs, n, len(rights), len(comm.operands), made, len(comm.operands), len(comm.scratch)
         )
         step = pl.program_id(0)
         comm.enter(operands, comm_outs, scratch, step == 0)
@@ -340,7 +521,7 @@
             @pl.when((step >= begin) & (step < begin + count))
             def _(k=k, transposed=transposed):
                 dot = dot_tn if transposed else dot_nn
-                outs[k][...] = dot(lefts[k][...], held[which[k]][...]).astype(BF16)
+                outs[0 if joined else k][...] = dot(lefts[k][...], held[which[k]][...]).astype(BF16)
 
         comm.finish(step == total - 1)
 
@@ -356,7 +537,7 @@
         cost_estimate=pl.CostEstimate(flops=flops, bytes_accessed=30_000_000, transcendentals=0),
         name="products",
     )(*[l for l, _, _ in items], *rights, *comm.operands)
-    return out[:n], out[n:]
+    return out[:made], out[made:]
 
 
 def swap_halves(block):
@@ -519,17 +700,35 @@
     return out[:4], out[4:]
 
 
-def attention_backward_kernel(kv_heads, blocks, place, comm, *refs):
+def attention_backward_kernel(kv_heads, blocks, trees, place, comm, *refs):
     jobs = len(comm.operands)
     inputs, operands, outs, comm_outs, own, scratch = split_refs(
-        refs, 8, jobs, 2, jobs, 5, len(comm.scratch)
-    )
+        refs, 8 * trees, jobs, 2 * trees, jobs, 5, len(comm.scratch)
+    )
+    step = pl.program_id(0)
+    comm.enter(operands, comm_outs, scratch, step == 0)
+    comm.advance(step, blocks * trees)
+    for t in range(trees):
+
+        @pl.when((step >= t * blocks) & (step < (t + 1) * blocks))
+        def _(t=t):
+            attention_backward_step(
+                kv_heads,
+                blocks,
+                place,
+                step - t * blocks,
+                inputs[8 * t : 8 * t + 8],
+                outs[2 * t : 2 * t + 2],
+                own,
+            )
+
+    comm.finish(step == blocks * trees - 1)
+
+
+def attention_backward_step(kv_heads, blocks, place, step, inputs, outs, own):
     grad_ref, q_ref, kv_ref, lse_ref, cos_ref, sin_ref, member_ref, sees_ref = inputs
     dq_ref, dkv_ref = outs
     keys, values, bias, key_sum, value_sum = own
-    step = pl.program_id(0)
-    comm.enter(operands, comm_outs, scratch, step == 0)
-    comm.advance(step, blocks)
     tree, rows = grad_ref.shape[0], q_ref.shape[0]
     kv_width = kv_heads * HEAD_DIM
 
@@ -613,107 +812,52 @@
                     moved = pltpu.roll(halves[1], HEAD_DIM, 1)
                     dkv_ref[there, :] = jnp.where(lower, turned, moved).astype(BF16)
 
-    comm.finish(step == blocks - 1)
-
-
-def attention_backward(place, grad, query, kv, lse, cosine, sine, member, sees, blocks, comm):
-    tree, q_width = query.shape
+
+def attention_backward(place, arrays, blocks, comm):
+    trees = len(arrays)
+    tree, q_width = arrays[0][1].shape
     rows = tree // blocks
-    kv_width = kv.shape[1] // 2
+    kv_width = arrays[0][2].shape[1] // 2
     kv_heads = kv_width // HEAD_DIM
     whole = lambda width: pl.BlockSpec((tree, width), lambda i: (0, 0))
-    natural = lambda width: pl.BlockSpec((rows, width), lambda i: (i, 0))
-    out = pl.pallas_call(
-        functools.partial(attention_backward_kernel, kv_heads, blocks, place, comm),
-        grid_spec=pl.GridSpec(
-            grid=(blocks,),
-            in_specs=[
-                whole(q_width),
-                natural(q_width),
-                whole(2 * kv_width),
-                natural(PAIR),
-                whole(PAIR),
-                whole(PAIR),
-                whole(PAIR),
-                whole(PAIR),
-                *comm.in_specs,
-            ],
-            out_specs=[whole(q_width), whole(2 * kv_width), *comm.out_specs],
-            scratch_shapes=[
-                pltpu.VMEM((2 * kv_heads, tree, PAIR), BF16),
-                pltpu.VMEM((2 * kv_heads, tree, PAIR), BF16),
-                pltpu.VMEM((tree, rows), F32),
-                pltpu.VMEM((2 * kv_heads, tree, PAIR), F32),
-                pltpu.VMEM((2 * kv_heads, tree, PAIR), F32),
-                *comm.scratch,
-            ],
-        ),
-        out_shape=[
+
+    def natural(width, t):
+        return pl.BlockSpec((rows, width), lambda i: (jnp.clip(i - t * blocks, 0, blocks - 1), 0))
+
+    in_specs, out_specs, out_shapes = [], [], []
+    for t in range(trees):
+        in_specs += [whole(q_width), natural(q_width, t), whole(2 * kv_width), natural(PAIR, t)]
+        in_specs += [whole(PAIR)] * 4
+        out_specs += [whole(q_width), whole(2 * kv_width)]
+        out_shapes += [
             jax.ShapeDtypeStruct((tree, q_width), BF16),
             jax.ShapeDtypeStruct((tree, 2 * kv_width), BF16),
-            *comm.out_shapes,
+        ]
+    out = pl.pallas_call(
+        functools.partial(attention_backward_kernel, kv_heads, blocks, trees, place, comm),
+        grid=(blocks * trees,),
+        in_specs=in_specs + list(comm.in_specs),
+        out_specs=out_specs + list(comm.out_specs),
+        out_shape=out_shapes + list(comm.out_shapes),
+        scratch_shapes=[
+            pltpu.VMEM((2 * kv_heads, tree, PAIR), BF16),
+            pltpu.VMEM((2 * kv_heads, tree, PAIR), BF16),
+            pltpu.VMEM((tree, rows), F32),
+            pltpu.VMEM((2 * kv_heads, tree, PAIR), F32),
+            pltpu.VMEM((2 * kv_heads, tree, PAIR), F32),
+            *comm.scratch,
         ],
-        compiler_params=comm_params(comm, 56),
+        compiler_params=comm_params(comm, 60),
         cost_estimate=pl.CostEstimate(
-            flops=20_000_000_000, bytes_accessed=12_000_000, transcendentals=5_000_000
+            flops=40_000_000_000, bytes_accessed=24_000_000, transcendentals=10_000_000
         ),
         name="attention_backward",
-    )(grad, query, kv, lse, cosine, sine, member, sees, *comm.operands)
-    return out[:2], out[2:]
+    )(*[array for per_tree in arrays for array in per_tree], *comm.operands)
+    return out[: 2 * trees], out[2 * trees :]
 
 
 def sync(*values):
     return lax.optimization_barrier(values)
-
-
-def assemble(where, chunks):
-    rows, width = chunks[0][0].shape
-    block = math.gcd(rows, 128)
-    each = rows // block
-    half = each * len(chunks)
-
-    def source(c, k):
-        def index(i, where):
-            local = jnp.clip(i - (k // 2) * half - c * each, 0, each - 1)
-            chosen = where[1] == (1 if k % 2 == 0 else 0)
-            return (jnp.where(chosen, local, 0), 0)
-
-        return pl.BlockSpec((block, width), index)
-
-    def target(i, where):
-        own = i < half
-        return (jnp.where(own, where[0] * half + i, (1 - where[0]) * half + i - half), 0)
-
-    def kernel(where_ref, *refs):
-        i = pl.program_id(0)
-        out = refs[-1]
-        for c in range(len(chunks)):
-            for k in range(4):
-                begin = (k // 2) * half + c * each
-
-                @pl.when(
-                    (i >= begin)
-                    & (i < begin + each)
-                    & (where_ref[1] == (1 if k % 2 == 0 else 0))
-                )
-                def _(ref=refs[4 * c + k]):
-                    out[...] = ref[...].astype(F32)
-
-    return pl.pallas_call(
-        kernel,
-        grid_spec=pltpu.PrefetchScalarGridSpec(
-            num_scalar_prefetch=1,
-            grid=(2 * half,),
-            in_specs=[source(c, k) for c in range(len(chunks)) for k in range(4)],
-            out_specs=pl.BlockSpec((block, width), target),
-        ),
-        out_shape=jax.ShapeDtypeStruct((2 * half * block, width), F32),
-        compiler_params=pltpu.CompilerParams(vmem_limit_bytes=40 << 20),
-        cost_estimate=pl.CostEstimate(
-            flops=0, bytes_accessed=12 * half * block * width, transcendentals=0
-        ),
-        name="assemble",
-    )(where, *[array for chunk in chunks for array in chunk])
 
 
 class Square:
@@ -722,11 +866,6 @@
         self.x = [(i, i ^ 1) for i in range(shard)]
         self.y = [(i, i ^ 2) for i in range(shard)]
         self.d = [(i, i ^ 3) for i in range(shard)]
-        self.core = [(i, i ^ 1) for i in range(replica)]
-        both = lambda pairs: [(2 * a + c, 2 * b + c) for a, b in pairs for c in range(2)]
-        self.inward = both([(0, 1), (3, 2)])
-        self.outward = both([(1, 0), (2, 3)])
-        self.middle = both([(1, 2), (2, 1)])
 
     def place(self, block):
         shard = lax.axis_index("shard")
@@ -769,72 +908,19 @@
         second = lax.ppermute(from_x[half:], "shard", self.y)
         return [own, from_x, from_y, first, second]
 
-    def carry(self, compute, gathers=(), sums=()):
+    def carry(self, compute, gathers=(), sums=(), totals=()):
         jobs = [GatherJob(own) for own in gathers] + [SumJob(part) for part in sums]
+        jobs += [LineJob(grad) for grad in totals]
         self.kernels += 1
         comm = Comm(jobs, self.kernels)
         if compute is None:
             results, moved = None, transfer(comm)
         else:
             results, moved = compute(comm)
-        return results, list(moved[: len(gathers)]), list(moved[len(gathers) :])
-
-    def start_line(self):
+        return (results, *map(list, split_refs(moved, len(gathers), len(sums), len(totals))))
+
+    def start(self):
         self.kernels = 0
-        self.waiting = []
-        self.inward_flight = None
-        self.middle_flight = None
-        self.outward_flight = None
-        self.finals = {}
-
-    def feed(self, name, grad, chunks):
-        half = grad.shape[0] // 2
-        core = lax.axis_index("replica") % 2
-        send = lax.dynamic_slice_in_dim(grad, (1 - core) * half, half, 0)
-        got = lax.ppermute(send, "replica", self.core)
-        rows = half // chunks
-        self.finals[name] = [None] * chunks
-        for c in range(chunks):
-            keep = lax.dynamic_slice_in_dim(grad, core * half + c * rows, rows, 0)
-            mine = keep.astype(F32) + got[c * rows : (c + 1) * rows].astype(F32)
-            self.waiting.append(((name, c), mine.astype(BF16)))
-
-    def tick(self, *values):
-        flying = (self.inward_flight, self.middle_flight, self.outward_flight)
-        chunk = self.waiting.pop(0) if self.waiting else None
-        landed, mine, values = sync(
-            tuple(f and f[-1] for f in flying), None if chunk is None else chunk[1], values
-        )
-        add = lambda a, b: (a.astype(F32) + b.astype(F32)).astype(BF16)
-        move = lambda v, perm: lax.ppermute(v, "replica", perm)
-        self.inward_flight = self.middle_flight = self.outward_flight = None
-        if flying[0] is not None:
-            pair = add(flying[0][1], landed[0])
-            self.middle_flight = (flying[0][0], pair, move(pair, self.middle))
-        if flying[1] is not None:
-            whole = add(flying[1][1], landed[1])
-            self.outward_flight = (flying[1][0], whole, move(whole, self.outward))
-        if flying[2] is not None:
-            (name, c), whole, _ = flying[2]
-            self.finals[name][c] = (
-                whole,
-                landed[2],
-                move(whole, self.core),
-                move(landed[2], self.core),
-            )
-        if chunk is not None:
-            self.inward_flight = (chunk[0], mine, move(mine, self.inward))
-        return values
-
-    def finish(self, name):
-        place = lax.axis_index("replica")
-        z = place // 2
-        inner = ((z == 1) | (z == 2)).astype(jnp.int32)
-        return assemble(jnp.stack([place % 2, inner]), self.finals[name])
-
-    def drain(self):
-        while self.waiting or self.inward_flight or self.middle_flight or self.outward_flight:
-            self.tick()
 
 
 class General:
@@ -847,14 +933,14 @@
     def gather_small(self, own):
         return lax.all_gather(own, "shard", axis=0, tiled=False)
 
-    def carry(self, compute, gathers=(), sums=()):
+    def carry(self, compute, gathers=(), sums=(), totals=()):
         results = None if compute is None else compute(NoComm())[0]
         gathered = [lax.all_gather(own, "shard", axis=0, tiled=True) for own in gathers]
         summed = [
             lax.psum_scatter(part, "shard", scatter_dimension=0, tiled=True).astype(F32)
             for part in sums
         ]
-        return results, gathered, summed
+        return results, gathered, summed, [lax.psum(grad, "replica") for grad in totals]
 
     def gather_start(self, own):
         return lax.all_gather(own, "shard", axis=0, tiled=True)
@@ -866,20 +952,8 @@
         share = lax.psum_scatter(values, "shard", scatter_dimension=1, tiled=True)
         return lax.psum(share, "replica")
 
-    def start_line(self):
-        self.finals = {}
-
-    def feed(self, name, grad, chunks):
-        self.finals[name] = lax.psum(grad, "replica").astype(F32)
-
-    def tick(self, *values):
-        return values
-
-    def drain(self):
+    def start(self):
         pass
-
-    def finish(self, name):
-        return self.finals[name]
 
 
 def rms_scale(values):
@@ -918,7 +992,7 @@
     shard = links.shard
     q_width, kv_width = w_query.shape[0], w_key.shape[0]
     tree_rows = own_rows * shard
-    links.start_line()
+    links.start()
     share = gain_attn.shape[0]
     w_qkv = jnp.concatenate([w_query, w_key, w_value], axis=0)
     token_rows = [tokens[t, 0] for t in range(trees)]
@@ -928,7 +1002,7 @@
         [gain_attn, gain_ff] + [segment_ids[t, 0].astype(BF16) for t in range(trees)]
     )
     smalls = links.gather_small(small)
-    _, (rows_0,), _ = links.carry(None, gathers=[token_rows[0]])
+    _, (rows_0,), _, _ = links.carry(None, gathers=[token_rows[0]])
     gain_first = smalls[:, :share].reshape(width).astype(F32)
     gain_second = smalls[:, share : 2 * share].reshape(width).astype(F32)
     masks, tables = [], []
@@ -950,17 +1024,17 @@
         return value, scale, (value * scale * gain_second).astype(BF16)
 
     normed_0 = normalized(rows_0, gain_first)
-    saved_0, (rows_1,), _ = links.carry(
+    saved_0, (rows_1,), _, _ = links.carry(
         attention(0, dot_nt(normed_0, w_qkv)), gathers=[token_rows[1]]
     )
     part_0 = dot_nn(saved_0[0], w_out).astype(BF16)
     normed_1 = normalized(rows_1, gain_first)
-    saved_1, _, (branch_0,) = links.carry(attention(1, dot_nt(normed_1, w_qkv)), sums=[part_0])
+    saved_1, _, (branch_0,), _ = links.carry(attention(1, dot_nt(normed_1, w_qkv)), sums=[part_0])
     part_1 = dot_nn(saved_1[0], w_out).astype(BF16)
     middle_0, scale_0, own_0 = after_attention(0, branch_0)
-    _, (ff_rows_0,), (branch_1,) = links.carry(None, gathers=[own_0], sums=[part_1])
+    _, (ff_rows_0,), (branch_1,), _ = links.carry(None, gathers=[own_0], sums=[part_1])
     middle_1, scale_1, own_1 = after_attention(1, branch_1)
-    _, (ff_rows_1,), _ = links.carry(None, gathers=[own_1])
+    _, (ff_rows_1,), _, _ = links.carry(None, gathers=[own_1])
     ff_rows_0, ff_rows_1, cot_rows = sync(ff_rows_0, ff_rows_1, cot_rows)
 
     cot_got = [links.gather_start(cot) for cot in cot_rows]
@@ -978,9 +1052,6 @@
         axis=0,
     )
     grad_down = dot_tn(hidden, cot_all).astype(BF16)
-    grad_down, hidden, cot_all, gate, upper = sync(grad_down, hidden, cot_all, gate, upper)
-    links.feed("down", grad_down, 1)
-    cot_all, gate, upper, hidden = links.tick(cot_all, gate, upper, hidden)
     hidden_grad = dot_nt(cot_all, w_down)
     wide = gate.astype(F32)
     sigma = jax.nn.sigmoid(wide)
@@ -989,16 +1060,12 @@
     ).astype(BF16)
     up_grad = (hidden_grad * wide * sigma).astype(BF16)
     ff_part = (dot_nn(gate_grad, w_gate) + dot_nn(up_grad, w_up)).astype(BF16)
-    ff_part, gate_grad, up_grad, hidden = links.tick(ff_part, gate_grad, up_grad, hidden)
-
     parts = lambda whole: [whole[t * tree_rows : (t + 1) * tree_rows] for t in range(trees)]
-    (grad_gate, grad_up), _, ff_grad = links.carry(
-        lambda comm: products([(gate_grad, rows_all, True), (up_grad, rows_all, True)], 512, comm),
+    (grad_gate, grad_up), _, ff_grad, (total_down,) = links.carry(
+        lambda comm: products([(gate_grad, rows_all, True), (up_grad, rows_all, True)], 256, comm),
         sums=parts(ff_part),
-    )
-    links.feed("gate", grad_gate, 1)
-    links.feed("up", grad_up, 1)
-    (hidden, ff_grad) = links.tick(hidden, ff_grad)
+        totals=[grad_down],
+    )
     out_own, middle_grads = [], []
     gain_ff_sum = jnp.zeros((width,), F32)
     for t, (middle, scale) in enumerate(((middle_0, scale_0), (middle_1, scale_1))):
@@ -1006,42 +1073,39 @@
         gain_ff_sum = gain_ff_sum + term
         middle_grads.append(cot_rows[t].astype(F32) + middle_back)
         out_own.append((RESIDUAL * middle_grads[t]).astype(BF16))
-    (down_part,), out_alls, _ = links.carry(
-        lambda comm: products([(hidden, w_down, False)], 512, comm), gathers=out_own
-    )
-    down_part, out_alls = links.tick(down_part, out_alls)
-
-    def attention_back(t, saved):
-        _, query, kv, lse = saved
+    (down_part,), out_alls, _, (total_gate,) = links.carry(
+        lambda comm: products([(hidden, w_down, False)], 256, comm),
+        gathers=out_own,
+        totals=[grad_gate],
+    )
+    arrays = []
+    for t, (_, query, kv, lse) in enumerate((saved_0, saved_1)):
         attended_grad = dot_nt(out_alls[t], w_out).astype(BF16)
-        return lambda comm: attention_backward(
-            links.place, attended_grad, query, kv, lse, *tables[t], *masks[t], shard, comm
-        )
-
-    down_parts = parts(down_part)
-    back_0, _, (down_0,) = links.carry(attention_back(0, saved_0), sums=[down_parts[0]])
-    back_1, _, (down_1,) = links.carry(attention_back(1, saved_1), sums=[down_parts[1]])
+        arrays.append((attended_grad, query, kv, lse, *tables[t], *masks[t]))
+    back, _, downs, (total_up,) = links.carry(
+        lambda comm: attention_backward(links.place, arrays, shard, comm),
+        sums=parts(down_part),
+        totals=[grad_up],
+    )
     results = [
-        (middle + RESIDUAL * down).astype(BF16)
-        for middle, down in ((middle_0, down_0), (middle_1, down_1))
+        (middle + RESIDUAL * down).astype(BF16) for middle, down in zip((middle_0, middle_1), downs)
     ]
     qkv_grad = jnp.concatenate(
-        [jnp.concatenate(back_0, axis=1), jnp.concatenate(back_1, axis=1)], axis=0
+        [jnp.concatenate(back[2 * t : 2 * t + 2], axis=1) for t in range(trees)], axis=0
     )
     normed_part = dot_nn(qkv_grad, w_qkv).astype(BF16)
-    qkv_grad, normed_part, results = links.tick(qkv_grad, normed_part, results)
     attended_all = jnp.concatenate([saved_0[0], saved_1[0]], axis=0)
     out_all = jnp.concatenate(out_alls, axis=0)
     normed_all = jnp.concatenate([normed_0, normed_1], axis=0)
-    (grad_out, grad_qkv), _, normed_grads = links.carry(
-        lambda comm: products(
-            [(attended_all, out_all, True), (qkv_grad, normed_all, True)], 128 if shard > 4 else 256, comm
-        ),
-        sums=parts(normed_part),
-    )
-    grad_out, grad_qkv, normed_grads = links.tick(grad_out, grad_qkv, normed_grads)
-    links.feed("out", grad_out, 1)
-    links.feed("qkv", grad_qkv, 1)
+    (grad_attn,), _ = products(
+        [(attended_all, out_all, True), (qkv_grad, normed_all, True)],
+        128 if shard > 4 else 256,
+        NoComm(),
+        joined=True,
+    )
+    _, _, normed_grads, (total_attn,) = links.carry(
+        None, sums=parts(normed_part), totals=[grad_attn]
+    )
     input_grads = []
     gain_attn_sum = jnp.zeros((width,), F32)
     for t in range(trees):
@@ -1050,20 +1114,19 @@
         gain_attn_sum = gain_attn_sum + term
         input_grads.append(middle_grads[t] + input_back)
     gains = links.sum_small(jnp.stack([gain_attn_sum, gain_ff_sum]))
-    links.drain()
-    grad_qkv = links.finish("qkv")
+    rows = lambda begin, count: total_attn[begin : begin + count].astype(F32)
     return (
         jnp.stack(results)[:, None],
         jnp.stack(input_grads)[:, None],
         gains[0],
-        grad_qkv[:q_width],
-        grad_qkv[q_width : q_width + kv_width],
-        grad_qkv[q_width + kv_width :],
-        links.finish("out"),
+        rows(q_width, q_width),
+        rows(2 * q_width, kv_width),
+        rows(2 * q_width + kv_width, kv_width),
+        rows(0, q_width),
         gains[1],
-        links.finish("gate"),
-        links.finish("up"),
-        links.finish("down"),
+        total_gate.astype(F32),
+        total_up.astype(F32),
+        total_down.astype(F32),
     )
 
 

time: 1340 us -> 1160 us (0.87)
  waiting for transfers between devices: 189 us -> 4.2 us
  Pallas kernels: 583 us -> 758 us
  starting transfers between devices: 155 us -> 17.9 us
  other arithmetic: 149 us -> 116 us
  local copies, waits for them, and re-layouts: 60.2 us -> 46.2 us
    ppermute x30 -> x0, waiting for transfers between devices: 168 us -> none  [the longest x25 161 us: tick(): move = lambda v, perm: lax.ppermute(v, 'replica', perm)]
    ppermute x30 -> x0, starting transfers between devices: 131 us -> none  [the longest x25 130 us: tick(): move = lambda v, perm: lax.ppermute(v, 'replica', perm)]
    pallas_call x2 -> x1, Pallas kernels: 91.8 us -> 202 us  [attention_backward(): pl.pallas_call(functools.partial(attention_backward_kernel, kv_heads, blo...]
    convert_element_type x17 -> x5, other arithmetic: 81.1 us -> 41 us  [the longest x1 11.7 us: body(): total_down.astype(F32)]
    pallas_call x3, Pallas kernels: 230 us -> 263 us  [products(): pl.pallas_call(kernel, grid=(total,), in_specs=specs + right_specs + list...]
    pallas_call x8 -> x4, Pallas kernels: 191 us -> 213 us  [transfer(): pl.pallas_call(kernel, grid=(steps,), in_specs=comm.in_specs, out_specs=c...]
    ppermute x2, waiting for transfers between devices: 14.5 us -> 0.01 us  [gather_start(): lax.ppermute(own, 'shard', self.x)]
    dynamic_slice x5 -> x0, local copies, waits for them, and re-layouts: 13.8 us -> none  [feed(): send = lax.dynamic_slice_in_dim(grad, (1 - core) * half, half, 0)]
  transfers between devices with their start and end apart: 47 -> 17, of which waited for: 12 -> 2; matrix products, arithmetic and copies ran while one was open for 20% -> 11% of each run, Pallas kernels for 25% -> 3%
where the time goes in v4:
time: 1160 us; the launch traced here: 1150 us
  Pallas kernels  758 us (65%)
  matrix products  203 us (18%)
  other arithmetic  116 us (10%)
  local copies, waits for them, and re-layouts  46.2 us (4%)
  starting transfers between devices  17.9 us (2%)
    pallas_call x3, Pallas kernels, products(): pl.pallas_call(kernel, grid=(total,), in_specs=specs + right_specs + list...  263 us
    pallas_call x4, Pallas kernels, transfer(): pl.pallas_call(kernel, grid=(steps,), in_specs=comm.in_specs, out_specs=c...  213 us
    pallas_call x1, Pallas kernels, attention_backward(): pl.pallas_call(functools.partial(attention_backward_kernel, kv_heads, blo...  202 us
    dot_general x7, matrix products, dot_nt(): lax.dot_general(left, right, (((1,), (1,)), ((), ())), preferred_element_...  106 us
    pallas_call x2, Pallas kernels, attention_forward(): pl.pallas_call(functools.partial(attention_forward_kernel, kv_heads, bloc...  79.5 us
    dot_general x7, matrix products, dot_nn(): lax.dot_general(left, right, (((1,), (0,)), ((), ())), preferred_element_...  75.6 us
  transfers between devices with their start and end apart: 17, of which 2 were waited for; matrix products, arithmetic and copies ran while one was open for 11% of the time, Pallas kernels for 3%

profile of v4, /device:TPU:0, one launch (start us, length us, event | category | flops | bytes accessed | tf_op | source)
XLA Modules:
  0.0 1147.4 jit_solution(16134853883933875896)
XLA Ops:
  13.1 36.9 %transfer.4 = bf16[1024,2048]{1,0:T(8,128)(2,1)S(1)} custom-call(bf16[256,2048]{1,0:T(8,128)(2,1)S(1)} %get-tuple-element.197.refs_0_), custom_call_target="tpu_custom_call" | custom-call | tf_op jit(solution)/shard_map/transfer/pallas_call | solution.py:466
  66.7 6.9 fusion.73.refs_0_.refs_1_
  77.4 35.2 %attention_forward.2 = (bf16[1024,512]{1,0:T(8,128)(2,1)S(1)}, bf16[1024,512]{1,0:T(8,128)(2,1)S(1)}, bf16[1024,256]{1,0:T(8,128)(2,1)S(1)}, f32[1024,128]{1,0:T(8,128)S(1)}, bf16[1024,2048]{1,0:T(8,128)(2,1)S(1)}) custom-call(f32[1024,768]{1,0:T(8,128)S(1)} %fusion.73.refs_0_.refs_1_, f32[1024,768]{1,0:T(8,128)S(1)} %fusion.73.refs_0_.refs_1_, ...), custom_call_target="tpu_custom_call" | custom-call | flops 10000000000 | bytes 12000000 | tf_op jit(solution)/shard_map/attention_forward/pallas_call | solution.py:660
  114.7 6.9 fusion.74.refs_0_.refs_1_
  124.0 44.3 %attention_forward.3 = (bf16[1024,512]{1,0:T(8,128)(2,1)S(1)}, bf16[1024,512]{1,0:T(8,128)(2,1)S(1)}, bf16[1024,256]{1,0:T(8,128)(2,1)S(1)}, f32[1024,128]{1,0:T(8,128)S(1)}, f32[256,2048]{1,0:T(8,128)S(1)}) custom-call(f32[1024,768]{1,0:T(8,128)S(1)} %fusion.74.refs_0_.refs_1_, f32[1024,768]{1,0:T(8,128)S(1)} %fusion.74.refs_0_.refs_1_, ...), custom_call_target="tpu_custom_call" | custom-call | flops 10000000000 | bytes 12000000 | tf_op jit(solution)/shard_map/attention_forward/pallas_call | solution.py:660
  173.8 66.9 %transfer.5 = (bf16[1024,2048]{1,0:T(8,128)(2,1)}, f32[256,2048]{1,0:T(8,128)S(1)}) custom-call(bf16[256,2048]{1,0:T(8,128)(2,1)S(1)} %multiply_convert_fusion.9.refs_0_, bf16[1024,2048]{1,0:T(8,128)(2,1)} %convolution_convert_fusion.3.refs_1_), custom_call_target="tpu_custom_call" | custom-call | tf_op jit(solution)/shard_map/transfer/pallas_call | solution.py:466
  242.9 34.3 %transfer.6 = bf16[1024,2048]{1,0:T(8,128)(2,1)S(1)} custom-call(bf16[256,2048]{1,0:T(8,128)(2,1)S(1)} %multiply_convert_fusion.8.refs_0_), custom_call_target="tpu_custom_call" | custom-call | tf_op jit(solution)/shard_map/transfer/pallas_call | solution.py:466
  282.5 23.7 %convolution_convert_fusion.2 = bf16[2048,2048]{1,0:T(8,128)(2,1)} fusion(bf16[2048,2048]{1,0:T(8,128)(2,1)S(1)} %constant_dynamic-update-slice_fusion.3.refs_2_, bf16[2048,2048]{1,0:T(8,128)(2,1)} %param.20), kind=kOutput, calls=%fused_computation.33 | convolution fusion | flops 17184063488 | bytes 25165824 | tf_op jit(solution)/shard_map/dot_general | solution.py:27
  308.3 8.4 pad_maximum_fusion.1.refs_3_
  331.2 27.6 %fusion.68 = (bf16[2048,2048]{1,0:T(8,128)(2,1)}, bf16[2048,2048]{1,0:T(8,128)(2,1)}) fusion(bf16[2048,2048]{1,0:T(8,128)(2,1)} %convolution_convert_fusion.2, bf16[2048,2048]{1,0:T(8,128)(2,1)} %copy-done.36, bf16[2048,2048]{1,0:T(8,128)(2,1)} %param.21), kind=kOutput, calls=%fused_computation.200 | convolution fusion | flops 17213423616 | bytes 41943040 | tf_op jit(solution)/shard_map/dot_general | solution.py:27
  374.3 20.7 %convolution_convert_fusion.1.refs_5_ = bf16[2048,2048]{1,0:T(8,128)(2,1)} fusion(bf16[2048,2048]{1,0:T(8,128)(2,1)S(1)} %bitcast.132, bf16[2048,2048]{1,0:T(8,128)(2,1)S(1)} %fusion.52), kind=kOutput, calls=%fused_computation.32 | convolution fusion | flops 17184063488 | bytes 25165824 | tf_op jit(solution)/shard_map/dot_general | solution.py:35
  395.0 32.1 %fusion.11 = (bf16[2048,2048]{1,0:T(8,128)(2,1)}, bf16[2048,2048]{1,0:T(8,128)(2,1)}) fusion(bf16[2048,2048]{1,0:T(8,128)(2,1)} %convolution_convert_fusion.2, bf16[2048,2048]{1,0:T(8,128)(2,1)} %get-tuple-element.92, bf16[2048,2048]{1,0:T(8,128)(2,1)} %copy-done.48, bf16[2048,2048]{1,0:T(8,128)(2,1)} %refs_1_.1), kind=kOutput, calls=%fused_computation.16 | convolution fusion | flops 17242783744 | bytes 50331648 | tf_op jit(solution)/shard_map/dot_general | solution.py:27
  427.1 24.2 %fusion.75 = f32[2048,2048]{1,0:T(8,128)} fusion(bf16[2048,2048]{1,0:T(8,128)(2,1)} %get-tuple-element.174.refs_1_, bf16[2048,2048]{1,0:T(8,128)(2,1)} %param.21), kind=kOutput, calls=%fused_computation.207 | convolution fusion | flops 17179869184 | bytes 33554432 | tf_op jit(solution)/shard_map/dot_general | solution.py:31
  451.3 24.2 %add_convert_fusion = bf16[2048,2048]{1,0:T(8,128)(2,1)S(1)} fusion(f32[2048,2048]{1,0:T(8,128)} %fusion.75, bf16[2048,2048]{1,0:T(8,128)(2,1)} %get-tuple-element.175.refs_0_, bf16[2048,2048]{1,0:T(8,128)(2,1)} %param.20), kind=kOutput, calls=%fused_computation.17 | convolution fusion | flops 17188257792 | bytes 41943040 | tf_op jit(solution)/shard_map/dot_general | solution.py:31
  479.2 127.6 %products.3 = (bf16[2048,2048]{1,0:T(8,128)(2,1)}, bf16[2048,2048]{1,0:T(8,128)(2,1)}, f32[256,2048]{1,0:T(8,128)}, f32[256,2048]{1,0:T(8,128)}, bf16[2048,2048]{1,0:T(8,128)(2,1)}) custom-call(bf16[2048,2048]{1,0:T(8,128)(2,1)} %get-tuple-element.175.refs_0_, bf16[2048,2048]{1,0:T(8,128)(2,1)} %get-tuple-element.174.refs_1_, bf16[2048,2048]{1,0:T(8,128)(2,1)} %copy-done.36, ...), custom_call_target="tpu_custom_call" | custom-call | flops 34359738368 | bytes 30000000 | tf_op jit(solution)/shard_map/products/pallas_call | solution.py:529
  616.4 116.1 %products.4 = (bf16[2048,2048]{1,0:T(8,128)(2,1)}, bf16[1024,2048]{1,0:T(8,128)(2,1)}, bf16[1024,2048]{1,0:T(8,128)(2,1)}, bf16[2048,2048]{1,0:T(8,128)(2,1)}) custom-call(bf16[2048,2048]{1,0:T(8,128)(2,1)} %get-tuple-element.81.refs_0_, bf16[2048,2048]{1,0:T(8,128)(2,1)} %refs_1_.1, bf16[256,2048]{1,0:T(8,128)(2,1)} %multiply_convert_fusion.1.refs_2_, ...), custom_call_target="tpu_custom_call" | custom-call | flops 17179869184 | bytes 30000000 | tf_op jit(solution)/shard_map/products/pallas_call | solution.py:529
  741.6 8.5 pad_maximum_fusion.refs_2_
  756.3 202.0 %attention_backward.1 = (bf16[1024,512]{1,0:T(8,128)(2,1)}, bf16[1024,256]{1,0:T(8,128)(2,1)}, bf16[1024,512]{1,0:T(8,128)(2,1)}, bf16[1024,256]{1,0:T(8,128)(2,...) custom-call(bf16[1024,512]{1,0:T(8,128)(2,1)} %convolution_convert_fusion.6.refs_0_, ...), custom_call_target="tpu_custom_call" | custom-call | flops 40000000000 | bytes 24000000 | tf_op jit(solution)/shard_map/attention_backward/pallas_call | solution.py:836
  962.3 19.8 %convolution_convert_fusion = bf16[2048,2048]{1,0:T(8,128)(2,1)} fusion(bf16[768,2048]{1,0:T(8,128)(2,1)} %constant_dynamic-update-slice_fusion, bf16[1024,256]{1,0:T(8,128)(2,1)S(1)} %copy-done.43, bf16[1024,512]{1,0:T(8,128)(2,1)S(1)} %copy-done.39, bf16[1024,256]{1,0:T(8,128)(2,1)S(1)} %copy-done.42, bf16[1024,512]{1,0:T(8,128)(2,1)S(1)} %copy-done.38), kind=kOutput, calls=%fused_computation.31 | convolution fusion | flops 6459228160 | bytes 14680064 | tf_op jit(solution)/shard_map/dot_general | solution.py:31
  988.2 19.4 %products.5.refs_2_ = bf16[1280,2048]{1,0:T(8,128)(2,1)} custom-call(bf16[2048,512]{1,0:T(8,128)(2,1)} %pad_maximum_fusion.2.refs_0_, bf16[2048,768]{1,0:T(8,128)(2,1)} %maximum_maximum_fusion.refs_1_, bf16[2048,2048]{1,0:T(8,128)(2,1)} %pad_maximum_fusion.refs_2_, bf16[2048,2048]{1,0:T(8,128)(2,1)} %pad_maximum_fusion.1.refs_3_), custom_call_target="tpu_custom_call" | custom-call | flops 10737418240 | bytes 30000000 | tf_op jit(solution)/shard_map/products/pallas_call | solution.py:529
  1007.6 75.0 %transfer.7 = (f32[256,2048]{1,0:T(8,128)S(1)}, f32[256,2048]{1,0:T(8,128)S(1)}, bf16[1280,2048]{1,0:T(8,128)(2,1)}) custom-call(bf16[1024,2048]{1,0:T(8,128)(2,1)} %get-tuple-element.179.refs_0_, bf16[1024,2048]{1,0:T(8,128)(2,1)} %get-tuple-element.178.refs_1_, bf16[1280,2048]{1,0:T(8,128)(2,1)} %products.5.refs_2_), custom_call_target="tpu_custom_call" | custom-call | tf_op jit(solution)/shard_map/transfer/pallas_call | solution.py:466
  1111.4 11.7 %convert_element_type.342 = f32[2048,2048]{1,0:T(8,128)} convert(bf16[2048,2048]{1,0:T(8,128)(2,1)} %get-tuple-element.117) | non-fusion elementwise | flops 4194304 | bytes 25165824 | tf_op jit(solution)/shard_map/convert_element_type | solution.py:1128
  1123.1 11.7 %convert_element_type.341 = f32[2048,2048]{1,0:T(8,128)} convert(bf16[2048,2048]{1,0:T(8,128)(2,1)} %get-tuple-element.116) | non-fusion elementwise | flops 4194304 | bytes 25165824 | tf_op jit(solution)/shard_map/convert_element_type | solution.py:1127
  1134.7 11.7 %convert_element_type.343 = f32[2048,2048]{1,0:T(8,128)} convert(bf16[2048,2048]{1,0:T(8,128)(2,1)} %get-tuple-element.118) | non-fusion elementwise | flops 4194304 | bytes 25165824 | tf_op jit(solution)/shard_map/convert_element_type | solution.py:1129
  (268 shorter events, 149.3 us)
Async XLA Ops:
  0.6 121.0 %copy-start = (bf16[512,2048]{1,0:T(8,128)(2,1)S(1)}, bf16[512,2048]{1,0:T(8,128)(2,1)}, u32[]{:S(2)}) copy-start(bf16[512,2048]{1,0:T(8,128)(2,1)} %param.18) | copy-start | bytes 6291460
  2.3 52.3 %collective-permute-start.2 = (bf16[1536]{0:T(1024)(128)(2,1)S(1)}, bf16[1536]{0:T(1024)(128)(2,1)S(1)}, u32[]{:S(2)}, u32[]{:S(2)}) collective-permute-start(bf16[1536]{0:T(1024)(128)(2,1)S(1)} %pad_maximum_fusion.5), channel_id=1, source_target_pairs={{0,24},{8,16},{16,8},{24,0},{1,25},{9,17},{17,9},{25,1},{2,26},{10... | collective-permute-start | bytes 9224 | tf_op jit(solution)/shard_map/ppermute | solution.py:885
  6.3 48.4 %collective-permute-start.1 = (bf16[1536]{0:T(1024)(128)(2,1)S(1)}, bf16[1536]{0:T(1024)(128)(2,1)S(1)}, u32[]{:S(2)}, u32[]{:S(2)}) collective-permute-start(bf16[1536]{0:T(1024)(128)(2,1)S(1)} %pad_maximum_fusion.5), channel_id=1, source_target_pairs={{0,16},{8,24},{16,0},{24,8},{1,17},{9,25},{17,1},{25,9},{2,18},{10... | collective-permute-start | bytes 9224 | tf_op jit(solution)/shard_map/ppermute | solution.py:884
  6.8 47.9 %collective-permute-start = (bf16[1536]{0:T(1024)(128)(2,1)S(1)}, bf16[1536]{0:T(1024)(128)(2,1)S(1)}, u32[]{:S(2)}, u32[]{:S(2)}) collective-permute-start(bf16[1536]{0:T(1024)(128)(2,1)S(1)} %pad_maximum_fusion.5), channel_id=1, source_target_pairs={{0,8},{8,0},{16,24},{24,16},{1,9},{9,1},{17,25},{25,17},{2,10},{10... | collective-permute-start | bytes 9224 | tf_op jit(solution)/shard_map/ppermute | solution.py:883
  57.2 184.1 %copy-start.40 = (f32[1,4,4,128]{3,1,2,0:T(4,128)}, f32[1,4,4,128]{3,1,2,0:T(4,128)S(1)}, u32[]{:S(2)}) copy-start(f32[1,4,4,128]{3,1,2,0:T(4,128)S(1)} %copy.43) | copy-start | bytes 24580
  277.2 39.5 %collective-permute-start.4 = (bf16[256,2048]{1,0:T(8,128)(2,1)}, bf16[256,2048]{1,0:T(8,128)(2,1)}, u32[]{:S(2)}, u32[]{:S(2)}) collective-permute-start(bf16[256,2048]{1,0:T(8,128)(2,1)} %get-tuple-element.82), channel_id=1, source_target_pairs={{0,16},{8,24},{16,0},{24,8},{1,17},{9,25},{17,1},{25,9},{2,18},{10... | collective-permute-start | bytes 3145736 | tf_op jit(solution)/shard_map/ppermute | solution.py:902
  277.8 38.9 %collective-permute-start.3 = (bf16[256,2048]{1,0:T(8,128)(2,1)}, bf16[256,2048]{1,0:T(8,128)(2,1)}, u32[]{:S(2)}, u32[]{:S(2)}) collective-permute-start(bf16[256,2048]{1,0:T(8,128)(2,1)} %get-tuple-element.82), channel_id=1, source_target_pairs={{0,8},{8,0},{16,24},{24,16},{1,9},{9,1},{17,25},{25,17},{2,10},{10... | collective-permute-start | bytes 3145736 | tf_op jit(solution)/shard_map/ppermute | solution.py:902
  279.3 40.3 %collective-permute-start.6 = (bf16[256,2048]{1,0:T(8,128)(2,1)S(1)}, bf16[256,2048]{1,0:T(8,128)(2,1)}, u32[]{:S(2)}, u32[]{:S(2)}) collective-permute-start(bf16[256,2048]{1,0:T(8,128)(2,1)S(1)} %copy-done.30), channel_id=1, source_target_pairs={{0,16},{8,24},{16,0},{24,8},{1,17},{9,25},{17,1},{25,9},{2,18},{10... | collective-permute-start | bytes 3145736 | tf_op jit(solution)/shard_map/ppermute | solution.py:902
  279.8 39.8 %collective-permute-start.5 = (bf16[256,2048]{1,0:T(8,128)(2,1)S(1)}, bf16[256,2048]{1,0:T(8,128)(2,1)}, u32[]{:S(2)}, u32[]{:S(2)}) collective-permute-start(bf16[256,2048]{1,0:T(8,128)(2,1)S(1)} %copy-done.30), channel_id=1, source_target_pairs={{0,8},{8,0},{16,24},{24,16},{1,9},{9,1},{17,25},{25,17},{2,10},{10... | collective-permute-start | bytes 3145736 | tf_op jit(solution)/shard_map/ppermute | solution.py:902
  327.1 31.6 %collective-permute-start.9 = (bf16[128,2048]{1,0:T(8,128)(2,1)}, bf16[128,2048]{1,0:T(8,128)(2,1)}, u32[]{:S(2)}, u32[]{:S(2)}) collective-permute-start(bf16[128,2048]{1,0:T(8,128)(2,1)} %slice.100), channel_id=1, source_target_pairs={{0,8},{8,0},{16,24},{24,16},{1,9},{9,1},{17,25},{25,17},{2,10},{10... | collective-permute-start | bytes 1572872 | tf_op jit(solution)/shard_map/ppermute | solution.py:907
  327.6 31.1 %collective-permute-start.10 = (bf16[128,2048]{1,0:T(8,128)(2,1)}, bf16[128,2048]{1,0:T(8,128)(2,1)}, u32[]{:S(2)}, u32[]{:S(2)}) collective-permute-start(bf16[128,2048]{1,0:T(8,128)(2,1)} %slice.101), channel_id=1, source_target_pairs={{0,16},{8,24},{16,0},{24,8},{1,17},{9,25},{17,1},{25,9},{2,18},{10... | collective-permute-start | bytes 1572872 | tf_op jit(solution)/shard_map/ppermute | solution.py:908
  329.1 29.6 %collective-permute-start.7 = (bf16[128,2048]{1,0:T(8,128)(2,1)}, bf16[128,2048]{1,0:T(8,128)(2,1)}, u32[]{:S(2)}, u32[]{:S(2)}) collective-permute-start(bf16[128,2048]{1,0:T(8,128)(2,1)} %slice.98), channel_id=1, source_target_pairs={{0,8},{8,0},{16,24},{24,16},{1,9},{9,1},{17,25},{25,17},{2,10},{10... | collective-permute-start | bytes 1572872 | tf_op jit(solution)/shard_map/ppermute | solution.py:907
  329.7 29.1 %collective-permute-start.8 = (bf16[128,2048]{1,0:T(8,128)(2,1)}, bf16[128,2048]{1,0:T(8,128)(2,1)}, u32[]{:S(2)}, u32[]{:S(2)}) collective-permute-start(bf16[128,2048]{1,0:T(8,128)(2,1)} %slice.99), channel_id=1, source_target_pairs={{0,16},{8,24},{16,0},{24,8},{1,17},{9,25},{17,1},{25,9},{2,18},{10... | collective-permute-start | bytes 1572872 | tf_op jit(solution)/shard_map/ppermute | solution.py:908
  479.2 127.6 %copy-start.22 = (f32[256,2048]{1,0:T(8,128)S(1)}, f32[256,2048]{1,0:T(8,128)}, u32[]{:S(2)}) copy-start(f32[256,2048]{1,0:T(8,128)} %copy-done.21) | copy-start | bytes 6291460
  479.2 127.6 %copy-start.41 = (f32[1,4,4,128]{3,1,2,0:T(4,128)S(1)}, f32[1,4,4,128]{3,1,2,0:T(4,128)}, u32[]{:S(2)}) copy-start(f32[1,4,4,128]{3,1,2,0:T(4,128)} %copy-done.40) | copy-start | bytes 24580
  479.2 127.7 %copy-start.52 = (f32[256]{0:T(256)S(1)}, f32[256]{0:T(256)}, u32[]{:S(2)}) copy-start(f32[256]{0:T(256)} %copy-done.51) | copy-start | bytes 3076
  479.2 130.0 %copy-start.31 = (bf16[256,2048]{1,0:T(8,128)(2,1)S(1)}, bf16[256,2048]{1,0:T(8,128)(2,1)}, u32[]{:S(2)}) copy-start(bf16[256,2048]{1,0:T(8,128)(2,1)} %get-tuple-element.87) | copy-start | bytes 3145732
  1007.6 76.3 %copy-start.53 = (f32[256]{0:T(256)S(1)}, f32[256]{0:T(256)}, u32[]{:S(2)}) copy-start(f32[256]{0:T(256)} %add_rsqrt_fusion.2) | copy-start | bytes 3076
  1085.3 17.9 %collective-permute-start.11 = (f32[2,512]{1,0:T(2,128)S(1)}, f32[2,512]{1,0:T(2,128)S(1)}, u32[]{:S(2)}, u32[]{:S(2)}) collective-permute-start(f32[2,512]{1,0:T(2,128)S(1)} %bitcast.128), channel_id=1, source_target_pairs={{0,8},{8,0},{16,24},{24,16},{1,9},{9,1},{17,25},{25,17},{2,10},{10... | collective-permute-start | bytes 12296 | tf_op jit(solution)/shard_map/ppermute | solution.py:895
  1086.5 16.7 %collective-permute-start.12 = (f32[2,512]{1,0:T(2,128)S(1)}, f32[2,512]{1,0:T(2,128)S(1)}, u32[]{:S(2)}, u32[]{:S(2)}) collective-permute-start(f32[2,512]{1,0:T(2,128)S(1)} %bitcast.127), channel_id=1, source_target_pairs={{0,16},{8,24},{16,0},{24,8},{1,17},{9,25},{17,1},{25,9},{2,18},{10... | collective-permute-start | bytes 12296 | tf_op jit(solution)/shard_map/ppermute | solution.py:895
  1087.4 15.8 %collective-permute-start.13 = (f32[2,512]{1,0:T(2,128)S(1)}, f32[2,512]{1,0:T(2,128)S(1)}, u32[]{:S(2)}, u32[]{:S(2)}) collective-permute-start(f32[2,512]{1,0:T(2,128)S(1)} %bitcast.126), channel_id=1, source_target_pairs={{0,24},{8,16},{16,8},{24,0},{1,25},{9,17},{17,9},{25,1},{2,26},{10... | collective-permute-start | bytes 12296 | tf_op jit(solution)/shard_map/ppermute | solution.py:895
  1103.1 1.6 collective-permute-start.14
  1104.8 3.7 collective-permute-start.15
  1108.5 37.9 %collective-permute-start.16 = (f32[2,512]{1,0:T(2,128)S(1)}, f32[2,512]{1,0:T(2,128)S(1)}, u32[]{:S(2)}, u32[]{:S(2)}) collective-permute-start(f32[2,512]{1,0:T(2,128)S(1)} %add.235), channel_id=1, source_target_pairs={{0,4},{1,5},{2,6},{3,7},{4,0},{5,1},{6,2},{7,3},{8,12},{9,13},{10,... | collective-permute-start | bytes 12296 | tf_op jit(solution)/shard_map/ppermute | solution.py:898
  (52 other events, 1024.6 us)

commit v5 on v4

--- a/solution.py
+++ b/solution.py
@@ -64,6 +64,7 @@
 
 MESH = pl.DeviceIdType.MESH
 CHUNK = 64
+SLOTS = 4
 
 
 def remote(source, target, sems, index, device):
@@ -73,58 +74,79 @@
 
 
 class GatherJob:
-    def __init__(self, own):
+    def __init__(self, own, trees):
         self.operand = own
-        self.rows, self.width = own.shape
+        self.trees = trees
+        self.rows, self.width = own.shape[0] // trees, own.shape[1]
         self.chunks = self.rows // CHUNK
-        self.out_shape = jax.ShapeDtypeStruct((4 * self.rows, self.width), own.dtype)
+        self.out_shape = jax.ShapeDtypeStruct((4 * own.shape[0], self.width), own.dtype)
         self.out_spec = pl.BlockSpec(memory_space=pl.ANY)
 
     def scratch(self):
-        return [pltpu.SemaphoreType.DMA((2, 3 * self.chunks)), pltpu.SemaphoreType.DMA(())]
+        return [
+            pltpu.SemaphoreType.DMA((2, 3 * self.chunks * self.trees)),
+            pltpu.SemaphoreType.DMA((self.trees,)),
+        ]
 
     def bind(self, operand, out, scratch, x, y):
         sems, local = scratch
         n, rows = self.chunks, self.rows
-        at = lambda block, j: out.at[pl.ds(block * rows + j * CHUNK, CHUNK), :]
-        own = lambda j: operand.at[pl.ds(j * CHUNK, CHUNK), :]
-        self.local = pltpu.make_async_copy(operand, out.at[pl.ds(0, rows), :], local)
-        self.to_x = [remote(own(j), at(1, j), sems, j, x) for j in range(n)]
-        self.to_y = [remote(own(j), at(2, j), sems, n + j, y) for j in range(n)]
-        self.on_x = [remote(at(2, j), at(3, j), sems, 2 * n + j, x) for j in range(n // 2)]
-        self.on_y = [remote(at(1, j), at(3, j), sems, 2 * n + j, y) for j in range(n // 2, n)]
+        self.local, self.to_x, self.to_y, self.on_x, self.on_y = [], [], [], [], []
+        for t in range(self.trees):
+            at = lambda block, j: out.at[pl.ds((4 * t + block) * rows + j * CHUNK, CHUNK), :]
+            own = lambda j: operand.at[pl.ds(t * rows + j * CHUNK, CHUNK), :]
+            sem = 3 * n * t
+            self.local.append(
+                pltpu.make_async_copy(
+                    operand.at[pl.ds(t * rows, rows), :],
+                    out.at[pl.ds(4 * t * rows, rows), :],
+                    local.at[t],
+                )
+            )
+            self.to_x.append([remote(own(j), at(1, j), sems, sem + j, x) for j in range(n)])
+            self.to_y.append([remote(own(j), at(2, j), sems, sem + n + j, y) for j in range(n)])
+            on = lambda block, j, to: remote(at(block, j), at(3, j), sems, sem + 2 * n + j, to)
+            self.on_x.append([on(2, j, x) for j in range(n // 2)])
+            self.on_y.append([on(1, j, y) for j in range(n // 2, n)])
 
     def begin(self):
         n = self.chunks
         half = n // 2
-        for k in range(n):
-            self.to_x[(k + half) % n].start()
-            self.to_y[k].start()
-        self.local.start()
+        for t in range(self.trees):
+            for k in range(n):
+                self.to_x[t][(k + half) % n].start()
+                self.to_y[t][k].start()
+            self.local[t].start()
 
     def stages(self):
-        def stage(k):
+        def stage(t, k):
             half = self.chunks // 2
-            self.to_y[k].wait_recv()
-            self.on_x[k].start()
-            self.to_x[half + k].wait_recv()
-            self.on_y[k].start()
-
-        return [functools.partial(stage, k) for k in range(self.chunks // 2)]
+            self.to_y[t][k].wait_recv()
+            self.on_x[t][k].start()
+            self.to_x[t][half + k].wait_recv()
+            self.on_y[t][k].start()
+
+        return [
+            functools.partial(stage, t, k)
+            for t in range(self.trees)
+            for k in range(self.chunks // 2)
+        ]
 
     def finish(self):
         half = self.chunks // 2
-        for copy in self.to_x[:half] + self.to_y[half:] + self.on_x + self.on_y:
-            copy.wait_recv()
-        for copy in self.to_x + self.to_y + self.on_x + self.on_y:
-            copy.wait_send()
-        self.local.wait()
+        for t in range(self.trees):
+            for copy in self.to_x[t][:half] + self.to_y[t][half:] + self.on_x[t] + self.on_y[t]:
+                copy.wait_recv()
+            for copy in self.to_x[t] + self.to_y[t] + self.on_x[t] + self.on_y[t]:
+                copy.wait_send()
+            self.local[t].wait()
 
 
 class SumJob:
-    def __init__(self, part):
+    def __init__(self, part, trees, tree):
         self.operand = part
-        self.rows, self.width = part.shape[0] // 4, part.shape[1]
+        self.rows, self.width = part.shape[0] // 4 // trees, part.shape[1]
+        self.base = 4 * self.rows * tree
         self.half = self.rows // 2
         self.chunks = self.half // CHUNK
         self.out_shape = jax.ShapeDtypeStruct((self.rows, self.width), F32)
@@ -142,9 +164,9 @@
         self.out = out
         self.mine, self.got, sems, local = scratch
         n, half = self.chunks, self.half
-        rows = lambda block, second: pl.ds(block * self.rows + second * half, half)
+        rows = lambda block, second: pl.ds(self.base + block * self.rows + second * half, half)
         piece = lambda block, second, j: part.at[
-            pl.ds(block * self.rows + second * half + j * CHUNK, CHUNK), :
+            pl.ds(self.base + block * self.rows + second * half + j * CHUNK, CHUNK), :
         ]
         here = lambda ref, k, j: ref.at[k, pl.ds(j * CHUNK, CHUNK), :]
         self.loads = [
@@ -393,23 +415,22 @@
     def stages(self):
         return [stage for job in self.jobs for stage in job.stages()]
 
-    def advance(self, step, steps):
+    def advance(self, slot, slots):
         stages = self.stages()
         for job in self.jobs:
             if isinstance(job, LineJob):
-                each = -(-job.steps // steps)
-
-                def body(k, carry, job=job, each=each):
-                    job.step(step * each + k)
+
+                def body(k, carry, job=job):
+                    job.step(k)
                     return carry
 
-                lax.fori_loop(0, each, body, 0)
+                lax.fori_loop(slot * job.steps // slots, (slot + 1) * job.steps // slots, body, 0)
         for index, stage in enumerate(stages):
-            if steps <= 4:
-                due = min(steps - 1, steps // 2 + index * (steps - steps // 2) // len(stages))
+            if slots <= 4:
+                due = min(slots - 1, slots // 2 + index * (slots - slots // 2) // len(stages))
             else:
-                due = min(steps - 1, max(1, int(steps * (0.25 + 0.5 * index / len(stages)))))
-            pl.when(step == due)(stage)
+                due = min(slots - 1, max(1, int(slots * (0.25 + 0.5 * index / len(stages)))))
+            pl.when(slot == due)(stage)
 
     def finish(self, now):
         @pl.when(now)
@@ -450,7 +471,7 @@
 
 def transfer(comm):
     count = len(comm.operands)
-    steps = 9 if any(isinstance(job, LineJob) for job in comm.jobs) else 1
+    steps = max([1] + [job.steps for job in comm.jobs if isinstance(job, LineJob)])
 
     def kernel(*refs):
         operands, outs, scratch = split_refs(refs, count, count, len(comm.scratch))
@@ -514,14 +535,23 @@
         )
         step = pl.program_id(0)
         comm.enter(operands, comm_outs, scratch, step == 0)
-        comm.advance(step, total)
-        for k, (_, _, transposed) in enumerate(items):
-            begin, count = steps[k]
-
-            @pl.when((step >= begin) & (step < begin + count))
-            def _(k=k, transposed=transposed):
-                dot = dot_tn if transposed else dot_nn
-                outs[0 if joined else k][...] = dot(lefts[k][...], held[which[k]][...]).astype(BF16)
+        width = items[0][1].shape[1] // SLOTS
+
+        def part(slot, carry):
+            comm.advance(step * SLOTS + slot, total * SLOTS)
+            columns = pl.ds(pl.multiple_of(slot * width, width), width)
+            for k, (_, _, transposed) in enumerate(items):
+                begin, count = steps[k]
+
+                @pl.when((step >= begin) & (step < begin + count))
+                def _(k=k, transposed=transposed):
+                    dot = dot_tn if transposed else dot_nn
+                    result = dot(lefts[k][...], held[which[k]][:, columns])
+                    outs[0 if joined else k][:, columns] = result.astype(BF16)
+
+            return carry
+
+        lax.fori_loop(0, SLOTS, part, 0)
 
         comm.finish(step == total - 1)
 
@@ -538,6 +568,51 @@
         name="products",
     )(*[l for l, _, _ in items], *rights, *comm.operands)
     return out[:made], out[made:]
+
+
+def feed_forward(rows_all, w_gate, w_up, block, comm):
+    rows, width = rows_all.shape
+    units = w_gate.shape[0]
+    steps = units // block
+    part = rows // SLOTS
+
+    def kernel(*refs):
+        inputs, operands, outs, comm_outs, scratch = split_refs(
+            refs, 3, len(comm.operands), 3, len(comm.operands), len(comm.scratch)
+        )
+        x_ref, gate_w, up_w = inputs
+        gate_ref, upper_ref, hidden_ref = outs
+        step = pl.program_id(0)
+        comm.enter(operands, comm_outs, scratch, step == 0)
+        comm.advance(step, steps)
+        for slot in range(SLOTS):
+            here = pl.ds(slot * part, part)
+            gate = dot_nt(x_ref[here, :], gate_w[...])
+            upper = dot_nt(x_ref[here, :], up_w[...])
+            gate_ref[here, :] = gate.astype(BF16)
+            upper_ref[here, :] = upper.astype(BF16)
+            hidden_ref[here, :] = (gate * jax.nn.sigmoid(gate) * upper).astype(BF16)
+        comm.finish(step == steps - 1)
+
+    out = pl.pallas_call(
+        kernel,
+        grid=(steps,),
+        in_specs=[
+            pl.BlockSpec((rows, width), lambda i: (0, 0), pipeline_mode=pl.Buffered(1)),
+            pl.BlockSpec((block, width), lambda i: (i, 0)),
+            pl.BlockSpec((block, width), lambda i: (i, 0)),
+            *comm.in_specs,
+        ],
+        out_specs=[pl.BlockSpec((rows, block), lambda i: (0, i))] * 3 + list(comm.out_specs),
+        out_shape=[jax.ShapeDtypeStruct((rows, units), BF16)] * 3 + list(comm.out_shapes),
+        scratch_shapes=list(comm.scratch),
+        compiler_params=comm_params(comm, 56),
+        cost_estimate=pl.CostEstimate(
+            flops=4 * rows * width * units, bytes_accessed=48_000_000, transcendentals=rows * units
+        ),
+        name="feed_forward",
+    )(rows_all, w_gate, w_up, *comm.operands)
+    return out[:3], out[3:]
 
 
 def swap_halves(block):
@@ -703,36 +778,43 @@
 def attention_backward_kernel(kv_heads, blocks, trees, place, comm, *refs):
     jobs = len(comm.operands)
     inputs, operands, outs, comm_outs, own, scratch = split_refs(
-        refs, 8 * trees, jobs, 2 * trees, jobs, 5, len(comm.scratch)
-    )
+        refs, 8 * trees, jobs, 1, jobs, 6, len(comm.scratch)
+    )
+    pairs = inputs[1].shape[1] // PAIR
+    each = blocks * pairs
     step = pl.program_id(0)
     comm.enter(operands, comm_outs, scratch, step == 0)
-    comm.advance(step, blocks * trees)
+    comm.advance(step, each * trees)
     for t in range(trees):
 
-        @pl.when((step >= t * blocks) & (step < (t + 1) * blocks))
+        @pl.when((step >= t * each) & (step < (t + 1) * each))
         def _(t=t):
+            local = step - t * each
             attention_backward_step(
                 kv_heads,
                 blocks,
+                pairs,
                 place,
-                step - t * blocks,
+                local // pairs,
+                local % pairs,
+                t,
                 inputs[8 * t : 8 * t + 8],
-                outs[2 * t : 2 * t + 2],
+                outs[0],
                 own,
             )
 
-    comm.finish(step == blocks * trees - 1)
-
-
-def attention_backward_step(kv_heads, blocks, place, step, inputs, outs, own):
+    comm.finish(step == each * trees - 1)
+
+
+def attention_backward_step(kv_heads, blocks, pairs, place, step, j, t, inputs, out_ref, own):
     grad_ref, q_ref, kv_ref, lse_ref, cos_ref, sin_ref, member_ref, sees_ref = inputs
-    dq_ref, dkv_ref = outs
-    keys, values, bias, key_sum, value_sum = own
+    keys, values, bias, lse_rows, key_sum, value_sum = own
     tree, rows = grad_ref.shape[0], q_ref.shape[0]
     kv_width = kv_heads * HEAD_DIM
-
-    @pl.when(step == 0)
+    q_width = q_ref.shape[1]
+    base = t * tree
+
+    @pl.when((step == 0) & (j == 0))
     def _():
         for b in range(blocks):
             here = pl.ds(b * rows, rows)
@@ -749,42 +831,45 @@
         value_sum[...] = jnp.zeros_like(value_sum)
 
     here = pl.ds(pl.multiple_of(step * rows, rows), rows)
+
+    @pl.when(j == 0)
+    def _():
+        link = dot_nt(member_ref[...], sees_ref[here, :])
+        key_index = lax.broadcasted_iota(jnp.int32, (tree, rows), 0)
+        query_index = lax.broadcasted_iota(jnp.int32, (tree, rows), 1) + step * rows
+        bias[...] = jnp.where((link > 0.5) & (key_index <= query_index), 0.0, NEGATIVE)
+        lse_rows[...] = jnp.transpose(lse_ref[...])
+
     there = pl.ds(pl.multiple_of(place(step) * rows, rows), rows)
-    link = dot_nt(member_ref[...], sees_ref[here, :])
-    key_index = lax.broadcasted_iota(jnp.int32, (tree, rows), 0)
-    query_index = lax.broadcasted_iota(jnp.int32, (tree, rows), 1) + step * rows
-    bias[...] = jnp.where((link > 0.5) & (key_index <= query_index), 0.0, NEGATIVE)
-    lse_rows = jnp.transpose(lse_ref[...])
-
+    out_rows = pl.ds(pl.multiple_of(base + place(step) * rows, rows), rows)
+    lanes = pl.ds(pl.multiple_of(j * PAIR, PAIR), PAIR)
+    group = 2 * j // GROUP
     for block in range(blocks):
         width = (block + 1) * rows
 
         @pl.when(step == block)
         def _(width=width):
             cosine, sine = cos_ref[here, :], sin_ref[here, :]
-            for j in range(q_ref.shape[1] // PAIR):
-                lanes = slice(j * PAIR, j * PAIR + PAIR)
-                group = 2 * j // GROUP
-                query, grad = q_ref[:, lanes], grad_ref[there, lanes]
-                dq = jnp.zeros((rows, PAIR), F32)
-                for p in range(2):
-                    index, head = group * 2 + p, 2 * j + p
-                    scores = dot_nt(keys[index, :width, :], query) + bias[:width, :]
-                    probs = jnp.exp(scores - lse_rows[head : head + 1, :])
-                    probs_grad = dot_nt(values[index, :width, :], grad)
-                    value_sum[index, :width, :] += dot_nn(probs.astype(BF16), grad)
-                    weighted = probs * probs_grad
-                    delta = jnp.sum(weighted, axis=0, keepdims=True)
-                    score_grad = (weighted - probs * delta).astype(BF16)
-                    key_sum[index, :width, :] += dot_nn(score_grad, query)
-                    dq = dq + dot_tn(score_grad, keys[index, :width, :])
-                dq_ref[there, lanes] = turn(dq * ATTN_SCALE, cosine, -sine).astype(BF16)
-
-    @pl.when(step == blocks - 1)
+            query, grad = q_ref[:, lanes], grad_ref[there, lanes]
+            dq = jnp.zeros((rows, PAIR), F32)
+            for p in range(2):
+                index = group * 2 + p
+                scores = dot_nt(keys[index, :width, :], query) + bias[:width, :]
+                probs = jnp.exp(scores - lse_rows[pl.ds(2 * j + p, 1), :])
+                probs_grad = dot_nt(values[index, :width, :], grad)
+                value_sum[index, :width, :] += dot_nn(probs.astype(BF16), grad)
+                weighted = probs * probs_grad
+                delta = jnp.sum(weighted, axis=0, keepdims=True)
+                score_grad = (weighted - probs * delta).astype(BF16)
+                key_sum[index, :width, :] += dot_nn(score_grad, query)
+                dq = dq + dot_tn(score_grad, keys[index, :width, :])
+            out_ref[out_rows, lanes] = turn(dq * ATTN_SCALE, cosine, -sine).astype(BF16)
+
+    @pl.when((step == blocks - 1) & (j == pairs - 1))
     def _():
         for b in range(blocks):
             here = pl.ds(b * rows, rows)
-            there = pl.ds(pl.multiple_of(place(b) * rows, rows), rows)
+            there = pl.ds(pl.multiple_of(base + place(b) * rows, rows), rows)
             cosine, sine = cos_ref[here, :], sin_ref[here, :]
             lane = lax.broadcasted_iota(jnp.int32, (rows, PAIR), 1)
             lower = lane < HEAD_DIM
@@ -793,9 +878,8 @@
                 for acc in (key_sum, value_sum):
                     own, other = [], []
                     for g in range(c, min(c + 2, kv_heads)):
-                        low, high = acc[g * 2, here, :], acc[g * 2 + 1, here, :]
-                        own.append(low)
-                        other.append(high)
+                        own.append(acc[g * 2, here, :])
+                        other.append(acc[g * 2 + 1, here, :])
                     first = own[0] + pltpu.roll(other[0], HEAD_DIM, 1)
                     if len(own) == 2:
                         second = other[1] + pltpu.roll(own[1], HEAD_DIM, 1)
@@ -804,13 +888,14 @@
                     halves.append(jnp.where(lower, first, second))
                 turned = turn(halves[0], cosine, -sine)
                 if kv_width >= PAIR:
-                    lanes = slice(c * HEAD_DIM, c * HEAD_DIM + PAIR)
-                    dkv_ref[there, lanes] = turned.astype(BF16)
-                    lanes = slice(kv_width + c * HEAD_DIM, kv_width + c * HEAD_DIM + PAIR)
-                    dkv_ref[there, lanes] = halves[1].astype(BF16)
+                    begin = q_width + c * HEAD_DIM
+                    out_ref[there, begin : begin + PAIR] = turned.astype(BF16)
+                    begin += kv_width
+                    out_ref[there, begin : begin + PAIR] = halves[1].astype(BF16)
                 else:
                     moved = pltpu.roll(halves[1], HEAD_DIM, 1)
-                    dkv_ref[there, :] = jnp.where(lower, turned, moved).astype(BF16)
+                    both = jnp.where(lower, turned, moved)
+                    out_ref[there, q_width : q_width + PAIR] = both.astype(BF16)
 
 
 def attention_backward(place, arrays, blocks, comm):
@@ -819,30 +904,31 @@
     rows = tree // blocks
     kv_width = arrays[0][2].shape[1] // 2
     kv_heads = kv_width // HEAD_DIM
+    each = blocks * (q_width // PAIR)
     whole = lambda width: pl.BlockSpec((tree, width), lambda i: (0, 0))
 
     def natural(width, t):
-        return pl.BlockSpec((rows, width), lambda i: (jnp.clip(i - t * blocks, 0, blocks - 1), 0))
-
-    in_specs, out_specs, out_shapes = [], [], []
+        return pl.BlockSpec(
+            (rows, width),
+            lambda i: (jnp.clip((i - t * each) // (q_width // PAIR), 0, blocks - 1), 0),
+        )
+
+    in_specs = []
     for t in range(trees):
         in_specs += [whole(q_width), natural(q_width, t), whole(2 * kv_width), natural(PAIR, t)]
         in_specs += [whole(PAIR)] * 4
-        out_specs += [whole(q_width), whole(2 * kv_width)]
-        out_shapes += [
-            jax.ShapeDtypeStruct((tree, q_width), BF16),
-            jax.ShapeDtypeStruct((tree, 2 * kv_width), BF16),
-        ]
+    total = q_width + 2 * kv_width
     out = pl.pallas_call(
         functools.partial(attention_backward_kernel, kv_heads, blocks, trees, place, comm),
-        grid=(blocks * trees,),
+        grid=(each * trees,),
         in_specs=in_specs + list(comm.in_specs),
-        out_specs=out_specs + list(comm.out_specs),
-        out_shape=out_shapes + list(comm.out_shapes),
+        out_specs=[pl.BlockSpec((trees * tree, total), lambda i: (0, 0))] + list(comm.out_specs),
+        out_shape=[jax.ShapeDtypeStruct((trees * tree, total), BF16)] + list(comm.out_shapes),
         scratch_shapes=[
             pltpu.VMEM((2 * kv_heads, tree, PAIR), BF16),
             pltpu.VMEM((2 * kv_heads, tree, PAIR), BF16),
             pltpu.VMEM((tree, rows), F32),
+            pltpu.VMEM((PAIR, rows), F32),
             pltpu.VMEM((2 * kv_heads, tree, PAIR), F32),
             pltpu.VMEM((2 * kv_heads, tree, PAIR), F32),
             *comm.scratch,
@@ -853,7 +939,7 @@
         ),
         name="attention_backward",
     )(*[array for per_tree in arrays for array in per_tree], *comm.operands)
-    return out[: 2 * trees], out[2 * trees :]
+    return out[:1], out[1:]
 
 
 def sync(*values):
@@ -898,18 +984,8 @@
             total = total + lax.ppermute(total, "replica", perm)
         return total
 
-    def gather_start(self, own):
-        return lax.ppermute(own, "shard", self.x), lax.ppermute(own, "shard", self.y)
-
-    def gather_more(self, own, got):
-        from_x, from_y = got
-        half = own.shape[0] // 2
-        first = lax.ppermute(from_y[:half], "shard", self.x)
-        second = lax.ppermute(from_x[half:], "shard", self.y)
-        return [own, from_x, from_y, first, second]
-
     def carry(self, compute, gathers=(), sums=(), totals=()):
-        jobs = [GatherJob(own) for own in gathers] + [SumJob(part) for part in sums]
+        jobs = [GatherJob(*own) for own in gathers] + [SumJob(*part) for part in sums]
         jobs += [LineJob(grad) for grad in totals]
         self.kernels += 1
         comm = Comm(jobs, self.kernels)
@@ -935,18 +1011,18 @@
 
     def carry(self, compute, gathers=(), sums=(), totals=()):
         results = None if compute is None else compute(NoComm())[0]
-        gathered = [lax.all_gather(own, "shard", axis=0, tiled=True) for own in gathers]
+        rows = lambda array, trees: array.reshape(trees, -1, array.shape[1])
+        gathered = [
+            lax.all_gather(rows(own, trees), "shard", axis=1, tiled=True).reshape(-1, own.shape[1])
+            for own, trees in gathers
+        ]
         summed = [
-            lax.psum_scatter(part, "shard", scatter_dimension=0, tiled=True).astype(F32)
-            for part in sums
+            lax.psum_scatter(
+                rows(part, trees)[tree], "shard", scatter_dimension=0, tiled=True
+            ).astype(F32)
+            for part, trees, tree in sums
         ]
         return results, gathered, summed, [lax.psum(grad, "replica") for grad in totals]
-
-    def gather_start(self, own):
-        return lax.all_gather(own, "shard", axis=0, tiled=True)
-
-    def gather_more(self, own, got):
-        return [got]
 
     def sum_small(self, values):
         share = lax.psum_scatter(values, "shard", scatter_dimension=1, tiled=True)
@@ -1002,7 +1078,7 @@
         [gain_attn, gain_ff] + [segment_ids[t, 0].astype(BF16) for t in range(trees)]
     )
     smalls = links.gather_small(small)
-    _, (rows_0,), _, _ = links.carry(None, gathers=[token_rows[0]])
+    _, (rows_0,), _, _ = links.carry(None, gathers=[(token_rows[0], 1)])
     gain_first = smalls[:, :share].reshape(width).astype(F32)
     gain_second = smalls[:, share : 2 * share].reshape(width).astype(F32)
     masks, tables = [], []
@@ -1025,31 +1101,21 @@
 
     normed_0 = normalized(rows_0, gain_first)
     saved_0, (rows_1,), _, _ = links.carry(
-        attention(0, dot_nt(normed_0, w_qkv)), gathers=[token_rows[1]]
+        attention(0, dot_nt(normed_0, w_qkv)), gathers=[(token_rows[1], 1)]
     )
     part_0 = dot_nn(saved_0[0], w_out).astype(BF16)
     normed_1 = normalized(rows_1, gain_first)
-    saved_1, _, (branch_0,), _ = links.carry(attention(1, dot_nt(normed_1, w_qkv)), sums=[part_0])
+    saved_1, _, (branch_0,), _ = links.carry(attention(1, dot_nt(normed_1, w_qkv)), sums=[(part_0, 1, 0)])
     part_1 = dot_nn(saved_1[0], w_out).astype(BF16)
     middle_0, scale_0, own_0 = after_attention(0, branch_0)
-    _, (ff_rows_0,), (branch_1,), _ = links.carry(None, gathers=[own_0], sums=[part_1])
+    _, _, (branch_1,), _ = links.carry(None, sums=[(part_1, 1, 0)])
     middle_1, scale_1, own_1 = after_attention(1, branch_1)
-    _, (ff_rows_1,), _, _ = links.carry(None, gathers=[own_1])
-    ff_rows_0, ff_rows_1, cot_rows = sync(ff_rows_0, ff_rows_1, cot_rows)
-
-    cot_got = [links.gather_start(cot) for cot in cot_rows]
-    rows_all = jnp.concatenate([ff_rows_0, ff_rows_1], axis=0)
-    gate = dot_nt(rows_all, w_gate).astype(BF16)
-    gate, cot_got, rows_all = sync(gate, cot_got, rows_all)
-    cot_pieces = [links.gather_more(cot, got) for cot, got in zip(cot_rows, cot_got)]
-    upper = dot_nt(rows_all, w_up)
-    wide = gate.astype(F32)
-    hidden = (wide * jax.nn.sigmoid(wide) * upper).astype(BF16)
-    upper = upper.astype(BF16)
-    hidden, upper, gate, cot_pieces = sync(hidden, upper, gate, cot_pieces)
-    cot_all = jnp.concatenate(
-        [(RESIDUAL * piece.astype(F32)).astype(BF16) for pieces in cot_pieces for piece in pieces],
-        axis=0,
+    own_all = jnp.concatenate([own_0, own_1], axis=0)
+    _, (rows_all,), _, _ = links.carry(None, gathers=[(own_all, trees)])
+
+    cot_own = jnp.concatenate([(RESIDUAL * cot.astype(F32)).astype(BF16) for cot in cot_rows], axis=0)
+    (gate, upper, hidden), (cot_all,), _, _ = links.carry(
+        lambda comm: feed_forward(rows_all, w_gate, w_up, 256, comm), gathers=[(cot_own, trees)]
     )
     grad_down = dot_tn(hidden, cot_all).astype(BF16)
     hidden_grad = dot_nt(cot_all, w_down)
@@ -1060,7 +1126,7 @@
     ).astype(BF16)
     up_grad = (hidden_grad * wide * sigma).astype(BF16)
     ff_part = (dot_nn(gate_grad, w_gate) + dot_nn(up_grad, w_up)).astype(BF16)
-    parts = lambda whole: [whole[t * tree_rows : (t + 1) * tree_rows] for t in range(trees)]
+    parts = lambda whole: [(whole, trees, t) for t in range(trees)]
     (grad_gate, grad_up), _, ff_grad, (total_down,) = links.carry(
         lambda comm: products([(gate_grad, rows_all, True), (up_grad, rows_all, True)], 256, comm),
         sums=parts(ff_part),
@@ -1073,16 +1139,16 @@
         gain_ff_sum = gain_ff_sum + term
         middle_grads.append(cot_rows[t].astype(F32) + middle_back)
         out_own.append((RESIDUAL * middle_grads[t]).astype(BF16))
-    (down_part,), out_alls, _, (total_gate,) = links.carry(
+    (down_part,), (out_all,), _, (total_gate,) = links.carry(
         lambda comm: products([(hidden, w_down, False)], 256, comm),
-        gathers=out_own,
+        gathers=[(jnp.concatenate(out_own, axis=0), trees)],
         totals=[grad_gate],
     )
     arrays = []
     for t, (_, query, kv, lse) in enumerate((saved_0, saved_1)):
-        attended_grad = dot_nt(out_alls[t], w_out).astype(BF16)
+        attended_grad = dot_nt(out_all[t * tree_rows : (t + 1) * tree_rows], w_out).astype(BF16)
         arrays.append((attended_grad, query, kv, lse, *tables[t], *masks[t]))
-    back, _, downs, (total_up,) = links.carry(
+    (qkv_grad,), _, downs, (total_up,) = links.carry(
         lambda comm: attention_backward(links.place, arrays, shard, comm),
         sums=parts(down_part),
         totals=[grad_up],
@@ -1090,12 +1156,8 @@
     results = [
         (middle + RESIDUAL * down).astype(BF16) for middle, down in zip((middle_0, middle_1), downs)
     ]
-    qkv_grad = jnp.concatenate(
-        [jnp.concatenate(back[2 * t : 2 * t + 2], axis=1) for t in range(trees)], axis=0
-    )
     normed_part = dot_nn(qkv_grad, w_qkv).astype(BF16)
     attended_all = jnp.concatenate([saved_0[0], saved_1[0]], axis=0)
-    out_all = jnp.concatenate(out_alls, axis=0)
     normed_all = jnp.concatenate([normed_0, normed_1], axis=0)
     (grad_attn,), _ = products(
         [(attended_all, out_all, True), (qkv_grad, normed_all, True)],

time: 1160 us -> 1010 us (0.87)
  matrix products: 203 us -> 146 us
  Pallas kernels: 758 us -> 727 us
  local copies, waits for them, and re-layouts: 46.2 us -> 19.2 us
  other arithmetic: 116 us -> 93.7 us
    pallas_call x1, Pallas kernels: 202 us -> 120 us  [attention_backward(): pl.pallas_call(functools.partial(attention_backward_kernel, kv_heads, blo...]
    pallas_call x0 -> x1, Pallas kernels: none -> 71.5 us  [feed_forward(): pl.pallas_call(kernel, grid=(steps,), in_specs=[pl.BlockSpec((rows, width...]
    dot_general x7 -> x5, matrix products: 106 us -> 55 us  [dot_nt(): lax.dot_general(left, right, (((1,), (1,)), ((), ())), preferred_element_...]
    slice x7 -> x0, local copies, waits for them, and re-layouts: 23.5 us -> none  [the longest x3 15.9 us: body(): whole[t * tree_rows:(t + 1) * tree_rows]]
  transfers between devices with their start and end apart: 17 -> 9, of which waited for: 2 -> 1; matrix products, arithmetic and copies ran while one was open for 11% -> 6% of each run, Pallas kernels for 3% -> 4%
where the time goes in v5:
time: 1010 us; the launch traced here: 1000 us
  Pallas kernels  727 us (72%)
  matrix products  146 us (14%)
  other arithmetic  93.7 us (9%)
  local copies, waits for them, and re-layouts  19.2 us (2%)
  starting transfers between devices  10.2 us (1%)
    pallas_call x3, Pallas kernels, products(): pl.pallas_call(kernel, grid=(total,), in_specs=specs + right_specs + list...  255 us
    pallas_call x4, Pallas kernels, transfer(): pl.pallas_call(kernel, grid=(steps,), in_specs=comm.in_specs, out_specs=c...  211 us
    pallas_call x1, Pallas kernels, attention_backward(): pl.pallas_call(functools.partial(attention_backward_kernel, kv_heads, blo...  120 us
    pallas_call x1, Pallas kernels, feed_forward(): pl.pallas_call(kernel, grid=(steps,), in_specs=[pl.BlockSpec((rows, width...  71.5 us
    pallas_call x2, Pallas kernels, attention_forward(): pl.pallas_call(functools.partial(attention_forward_kernel, kv_heads, bloc...  70.4 us
    dot_general x7, matrix products, dot_nn(): lax.dot_general(left, right, (((1,), (0,)), ((), ())), preferred_element_...  67.6 us
    dot_general x5, matrix products, dot_nt(): lax.dot_general(left, right, (((1,), (1,)), ((), ())), preferred_element_...  55 us
    dot_general x1, matrix products, dot_tn(): lax.dot_general(left, right, (((0,), (0,)), ((), ())), preferred_element_...  23.9 us
  transfers between devices with their start and end apart: 9, of which 1 were waited for; matrix products, arithmetic and copies ran while one was open for 6% of the time, Pallas kernels for 4%

profile of v5, /device:TPU:0, one launch (start us, length us, event | category | flops | bytes accessed | tf_op | source)
XLA Modules:
  0.0 1000.2 jit_solution(1359609149473561077)
XLA Ops:
  13.3 36.9 %transfer.4 = bf16[1024,2048]{1,0:T(8,128)(2,1)S(1)} custom-call(bf16[256,2048]{1,0:T(8,128)(2,1)S(1)} %get-tuple-element.143.refs_0_), custom_call_target="tpu_custom_call" | custom-call | tf_op jit(solution)/shard_map/transfer/pallas_call | solution.py:487
  64.4 6.9 fusion.66.refs_0_.refs_1_
  76.3 35.6 %attention_forward.2 = (bf16[1024,512]{1,0:T(8,128)(2,1)S(1)}, bf16[1024,512]{1,0:T(8,128)(2,1)S(1)}, bf16[1024,256]{1,0:T(8,128)(2,1)S(1)}, f32[1024,128]{1,0:T(8,128)S(1)}, bf16[1024,2048]{1,0:T(8,128)(2,1)S(1)}) custom-call(f32[1024,768]{1,0:T(8,128)S(1)} %fusion.66.refs_0_.refs_1_, f32[1024,768]{1,0:T(8,128)S(1)} %fusion.66.refs_0_.refs_1_, ...), custom_call_target="tpu_custom_call" | custom-call | flops 10000000000 | bytes 12000000 | tf_op jit(solution)/shard_map/attention_forward/pallas_call | solution.py:735
  116.6 7.1 fusion.67.refs_0_.refs_1_
  123.7 8.4 pad_maximum_fusion.refs_3_
  135.9 34.8 %attention_forward.3 = (bf16[1024,512]{1,0:T(8,128)(2,1)S(1)}, bf16[1024,512]{1,0:T(8,128)(2,1)S(1)}, bf16[1024,256]{1,0:T(8,128)(2,1)S(1)}, f32[1024,128]{1,0:T(8,128)S(1)}, f32[256,2048]{1,0:T(8,128)S(1)}) custom-call(f32[1024,768]{1,0:T(8,128)S(1)} %copy-done.15, f32[1024,768]{1,0:T(8,128)S(1)} %copy-done.15, f32[1024,128]{1,0:T(8,128)S(1)} %copy-done.8, ...), custom_call_target="tpu_custom_call" | custom-call | flops 10000000000 | bytes 12000000 | tf_op jit(solution)/shard_map/attention_forward/pallas_call | solution.py:735
  177.1 33.2 %transfer.5 = f32[256,2048]{1,0:T(8,128)S(1)} custom-call(bf16[1024,2048]{1,0:T(8,128)(2,1)} %convolution_convert_fusion.2.refs_0_), custom_call_target="tpu_custom_call" | custom-call | tf_op jit(solution)/shard_map/transfer/pallas_call | solution.py:487
  214.1 65.9 %transfer.6.refs_0_.refs_2_ = bf16[2048,2048]{1,0:T(8,128)(2,1)} custom-call(bf16[512,2048]{1,0:T(8,128)(2,1)S(1)} %pad_maximum_fusion.1.refs_0_), custom_call_target="tpu_custom_call" | custom-call | tf_op jit(solution)/shard_map/transfer/pallas_call | solution.py:487
  280.0 71.5 %feed_forward.1 = (bf16[2048,2048]{1,0:T(8,128)(2,1)}, bf16[2048,2048]{1,0:T(8,128)(2,1)}, bf16[2048,2048]{1,0:T(8,128)(2,1)}, bf16[2048,2048]{1,0:T(8,128)(2,1)}) custom-call(bf16[2048,2048]{1,0:T(8,128)(2,1)} %transfer.6.refs_0_.refs_2_, bf16[2048,2048]{1,0:T(8,128)(2,1)} %refs_1_.2, bf16[2048,2048]{1,0:T(8,128)(2,1)} %refs_2_.1, ...), custom_call_target="tpu_custom_call" | custom-call | flops 34359738368 | bytes 48000000 | tf_op jit(solution)/shard_map/feed_forward/pallas_call | solution.py:597
  351.6 23.9 %convolution_convert_fusion.1.refs_5_ = bf16[2048,2048]{1,0:T(8,128)(2,1)} fusion(bf16[2048,2048]{1,0:T(8,128)(2,1)} %get-tuple-element.44.refs_0_, bf16[2048,2048]{1,0:T(8,128)(2,1)} %get-tuple-element.45), kind=kOutput, calls=%fused_computation.24 | convolution fusion | flops 17184063488 | bytes 25165824 | tf_op jit(solution)/shard_map/dot_general | solution.py:35
  375.5 31.9 %fusion.7 = (bf16[2048,2048]{1,0:T(8,128)(2,1)}, bf16[2048,2048]{1,0:T(8,128)(2,1)}) fusion(bf16[2048,2048]{1,0:T(8,128)(2,1)} %get-tuple-element.47, bf16[2048,2048]{1,0:T(8,128)(2,1)} %get-tuple-element.46, bf16[2048,2048]{1,0:T(8,128)(2,1)} %get-tuple-element.45, bf16[2048,2048]{1,0:T(8,128)(2,1)} %refs_1_.3), kind=kOutput, calls=%fused_computation.10 | convolution fusion | flops 17242783744 | bytes 50331648 | tf_op jit(solution)/shard_map/dot_general | solution.py:27
  407.5 24.6 %fusion.68 = f32[2048,2048]{1,0:T(8,128)} fusion(bf16[2048,2048]{1,0:T(8,128)(2,1)} %get-tuple-element.125.refs_0_, bf16[2048,2048]{1,0:T(8,128)(2,1)} %refs_1_.2), kind=kOutput, calls=%fused_computation.180 | convolution fusion | flops 17179869184 | bytes 33554432 | tf_op jit(solution)/shard_map/dot_general | solution.py:31
  432.0 24.4 %add_convert_fusion.refs_3_.refs_4_ = bf16[2048,2048]{1,0:T(8,128)(2,1)} fusion(f32[2048,2048]{1,0:T(8,128)} %fusion.68, bf16[2048,2048]{1,0:T(8,128)(2,1)} %get-tuple-element.124.refs_1_, bf16[2048,2048]{1,0:T(8,128)(2,1)S(1)} %copy-done.51), kind=kOutput, calls=%fused_computation.11 | convolution fusion | flops 17188257792 | bytes 41943040 | tf_op jit(solution)/shard_map/dot_general | solution.py:31
  456.4 119.2 %products.3 = (bf16[2048,2048]{1,0:T(8,128)(2,1)}, bf16[2048,2048]{1,0:T(8,128)(2,1)}, f32[256,2048]{1,0:T(8,128)}, f32[256,2048]{1,0:T(8,128)}, bf16[2048,2048]{1,0:T(8,128)(2,1)}) custom-call(bf16[2048,2048]{1,0:T(8,128)(2,1)} %get-tuple-element.125.refs_0_, bf16[2048,2048]{1,0:T(8,128)(2,1)} %get-tuple-element.124.refs_1_, ...), custom_call_target="tpu_custom_call" | custom-call | flops 34359738368 | bytes 30000000 | tf_op jit(solution)/shard_map/products/pallas_call | solution.py:559
  584.2 113.2 %products.4 = (bf16[2048,2048]{1,0:T(8,128)(2,1)}, bf16[2048,2048]{1,0:T(8,128)(2,1)}, bf16[2048,2048]{1,0:T(8,128)(2,1)}) custom-call(bf16[2048,2048]{1,0:T(8,128)(2,1)} %get-tuple-element.44.refs_0_, bf16[2048,2048]{1,0:T(8,128)(2,1)} %refs_1_.3, bf16[512,2048]{1,0:T(8,128)(2,1)} %pad_maximum_fusion.3.refs_2_, bf16[2048,2048]{1,0:T(8,128)(2,1)} %get-tuple-element.50.refs_3_), custom_call_target="tpu_custom_call" | custom-call | flops 17179869184 | bytes 30000000 | tf_op jit(solution)/shard_map/products/pallas_call | solution.py:559
  697.4 5.7 fusion.43.refs_8_
  706.5 119.7 %attention_backward.1 = (bf16[2048,768]{1,0:T(8,128)(2,1)}, f32[256,2048]{1,0:T(8,128)}, f32[256,2048]{1,0:T(8,128)}, bf16[2048,2048]{1,0:T(8,128)(2,1)}) custom-call(bf16[1024,512]{1,0:T(8,128)(2,1)} %fusion.40.refs_0_, bf16[1024,512]{1,0:T(8,128)(2,1)} %copy-done.17, bf16[1024,256]{1,0:T(8,128)(2,1)} %copy-done.20, f32[1024,128]{1,0:T(8,128)} %copy-done.21, ...), custom_call_target="tpu_custom_call" | custom-call | flops 40000000000 | bytes 24000000 | tf_op jit(solution)/shard_map/attention_backward/pallas_call | solution.py:921
  826.2 11.3 %convolution_convert_fusion.refs_0_.refs_1_ = bf16[2048,2048]{1,0:T(8,128)(2,1)} fusion(bf16[2048,768]{1,0:T(8,128)(2,1)} %get-tuple-element.62.refs_1_, bf16[768,2048]{1,0:T(8,128)(2,1)} %constant_dynamic-update-slice_fusion), kind=kOutput, calls=%fused_computation.23 | convolution fusion | flops 6446645248 | bytes 14680064 | tf_op jit(solution)/shard_map/dot_general | solution.py:31
  837.4 22.8 %products.5.refs_2_ = bf16[1280,2048]{1,0:T(8,128)(2,1)} custom-call(bf16[2048,512]{1,0:T(8,128)(2,1)} %pad_maximum_fusion.4.refs_0_, bf16[2048,768]{1,0:T(8,128)(2,1)} %get-tuple-element.62.refs_1_, bf16[2048,2048]{1,0:T(8,128)(2,1)} %get-tuple-element.51.refs_2_, bf16[2048,2048]{1,0:T(8,128)(2,1)} %pad_maximum_fusion.refs_3_), custom_call_target="tpu_custom_call" | custom-call | flops 10737418240 | bytes 30000000 | tf_op jit(solution)/shard_map/products/pallas_call | solution.py:559
  860.2 74.5 %transfer.7 = (f32[256,2048]{1,0:T(8,128)S(1)}, f32[256,2048]{1,0:T(8,128)S(1)}, bf16[1280,2048]{1,0:T(8,128)(2,1)}) custom-call(bf16[2048,2048]{1,0:T(8,128)(2,1)} %convolution_convert_fusion.refs_0_.refs_1_, bf16[2048,2048]{1,0:T(8,128)(2,1)} %convolution_convert_fusion.refs_0_.refs_1_, bf16[1280,2048]{1,0:T(8,128)(2,1)} %products.5.refs_2_), custom_call_target="tpu_custom_call" | custom-call | tf_op jit(solution)/shard_map/transfer/pallas_call | solution.py:487
  940.5 5.0 fusion.36
  964.2 11.7 %convert_element_type.264 = f32[2048,2048]{1,0:T(8,128)} convert(bf16[2048,2048]{1,0:T(8,128)(2,1)} %get-tuple-element.67) | non-fusion elementwise | flops 4194304 | bytes 25165824 | tf_op jit(solution)/shard_map/convert_element_type | solution.py:1190
  975.9 11.7 %convert_element_type.263 = f32[2048,2048]{1,0:T(8,128)} convert(bf16[2048,2048]{1,0:T(8,128)(2,1)} %get-tuple-element.66) | non-fusion elementwise | flops 4194304 | bytes 25165824 | tf_op jit(solution)/shard_map/convert_element_type | solution.py:1189
  987.5 11.7 %convert_element_type.265 = f32[2048,2048]{1,0:T(8,128)} convert(bf16[2048,2048]{1,0:T(8,128)(2,1)} %get-tuple-element.68) | non-fusion elementwise | flops 4194304 | bytes 25165824 | tf_op jit(solution)/shard_map/convert_element_type | solution.py:1191
  (221 shorter events, 86.7 us)
Async XLA Ops:
  0.6 132.8 %copy-start = (bf16[512,2048]{1,0:T(8,128)(2,1)S(1)}, bf16[512,2048]{1,0:T(8,128)(2,1)}, u32[]{:S(2)}) copy-start(bf16[512,2048]{1,0:T(8,128)(2,1)} %param.18) | copy-start | bytes 6291460
  2.2 53.3 %collective-permute-start.2 = (bf16[1536]{0:T(1024)(128)(2,1)S(1)}, bf16[1536]{0:T(1024)(128)(2,1)S(1)}, u32[]{:S(2)}, u32[]{:S(2)}) collective-permute-start(bf16[1536]{0:T(1024)(128)(2,1)S(1)} %pad_maximum_fusion.7), channel_id=1, source_target_pairs={{0,24},{8,16},{16,8},{24,0},{1,25},{9,17},{17,9},{25,1},{2,26},{10... | collective-permute-start | bytes 9224 | tf_op jit(solution)/shard_map/ppermute | solution.py:971
  6.2 49.4 %collective-permute-start.1 = (bf16[1536]{0:T(1024)(128)(2,1)S(1)}, bf16[1536]{0:T(1024)(128)(2,1)S(1)}, u32[]{:S(2)}, u32[]{:S(2)}) collective-permute-start(bf16[1536]{0:T(1024)(128)(2,1)S(1)} %pad_maximum_fusion.7), channel_id=1, source_target_pairs={{0,16},{8,24},{16,0},{24,8},{1,17},{9,25},{17,1},{25,9},{2,18},{10... | collective-permute-start | bytes 9224 | tf_op jit(solution)/shard_map/ppermute | solution.py:970
  6.7 48.9 %collective-permute-start = (bf16[1536]{0:T(1024)(128)(2,1)S(1)}, bf16[1536]{0:T(1024)(128)(2,1)S(1)}, u32[]{:S(2)}, u32[]{:S(2)}) collective-permute-start(bf16[1536]{0:T(1024)(128)(2,1)S(1)} %pad_maximum_fusion.7), channel_id=1, source_target_pairs={{0,8},{8,0},{16,24},{24,16},{1,9},{9,1},{17,25},{25,17},{2,10},{10... | collective-permute-start | bytes 9224 | tf_op jit(solution)/shard_map/ppermute | solution.py:969
  58.1 55.5 %copy-start.41 = (f32[1,4,4,128]{3,1,2,0:T(4,128)}, f32[1,4,4,128]{3,1,2,0:T(4,128)S(1)}, u32[]{:S(2)}) copy-start(f32[1,4,4,128]{3,1,2,0:T(4,128)S(1)} %copy.40) | copy-start | bytes 24580
  60.0 16.3 %copy-start.11 = (bf16[1024,128]{1,0:T(8,128)(2,1)}, bf16[1024,128]{1,0:T(8,128)(2,1)S(1)}, u32[]{:S(2)}) copy-start(bf16[1024,128]{1,0:T(8,128)(2,1)S(1)} %pad.14.refs_5_.refs_7_) | copy-start | bytes 786436
  61.1 15.1 %copy-start.12 = (bf16[1024,128]{1,0:T(8,128)(2,1)}, bf16[1024,128]{1,0:T(8,128)(2,1)S(1)}, u32[]{:S(2)}) copy-start(bf16[1024,128]{1,0:T(8,128)(2,1)S(1)} %pad.13.refs_4_.refs_6_) | copy-start | bytes 786436
  76.2 35.6 %copy-start.9 = (f32[1024,128]{1,0:T(8,128)}, f32[1024,128]{1,0:T(8,128)S(1)}, u32[]{:S(2)}) copy-start(f32[1024,128]{1,0:T(8,128)S(1)} %get-tuple-element.164.refs_2_.refs_4_) | copy-start | bytes 1572868
  76.3 35.6 %copy-start.10 = (f32[1024,128]{1,0:T(8,128)}, f32[1024,128]{1,0:T(8,128)S(1)}, u32[]{:S(2)}) copy-start(f32[1024,128]{1,0:T(8,128)S(1)} %get-tuple-element.165.refs_3_.refs_5_) | copy-start | bytes 1572868
  177.1 34.8 %copy-start.43 = (f32[1,4,4,128]{3,1,2,0:T(4,128)}, f32[1,4,4,128]{3,1,2,0:T(4,128)S(1)}, u32[]{:S(2)}) copy-start(f32[1,4,4,128]{3,1,2,0:T(4,128)S(1)} %copy.43) | copy-start | bytes 24580
  177.1 33.2 %copy-start.28 = (bf16[2,1,256,2048]{3,2,1,0:T(8,128)(2,1)S(1)}, bf16[2,1,256,2048]{3,2,1,0:T(8,128)(2,1)}, u32[]{:S(2)}) copy-start(bf16[2,1,256,2048]{3,2,1,0:T(8,128)(2,1)} %param.13) | copy-start | bytes 6291460
  407.4 24.6 %copy-start.51 = (bf16[2048,2048]{1,0:T(8,128)(2,1)S(1)}, bf16[2048,2048]{1,0:T(8,128)(2,1)}, u32[]{:S(2)}) copy-start(bf16[2048,2048]{1,0:T(8,128)(2,1)} %refs_2_.1) | copy-start | bytes 25165828
  456.4 119.3 %copy-start.23 = (f32[256,2048]{1,0:T(8,128)S(1)}, f32[256,2048]{1,0:T(8,128)}, u32[]{:S(2)}) copy-start(f32[256,2048]{1,0:T(8,128)} %copy-done.22) | copy-start | bytes 6291460
  456.4 119.3 %copy-start.44 = (f32[1,4,4,128]{3,1,2,0:T(4,128)S(1)}, f32[1,4,4,128]{3,1,2,0:T(4,128)}, u32[]{:S(2)}) copy-start(f32[1,4,4,128]{3,1,2,0:T(4,128)} %copy-done.43) | copy-start | bytes 24580
  456.4 119.3 %copy-start.46 = (f32[256]{0:T(256)S(1)}, f32[256]{0:T(256)}, u32[]{:S(2)}) copy-start(f32[256]{0:T(256)} %copy-done.45) | copy-start | bytes 3076
  456.4 119.3 %copy-start.48 = (f32[256]{0:T(256)S(1)}, f32[256]{0:T(256)}, u32[]{:S(2)}) copy-start(f32[256]{0:T(256)} %copy-done.47) | copy-start | bytes 3076
  860.2 74.5 %copy-start.29 = (bf16[2,1,256,2048]{3,2,1,0:T(8,128)(2,1)S(1)}, bf16[2,1,256,2048]{3,2,1,0:T(8,128)(2,1)}, u32[]{:S(2)}) copy-start(bf16[2,1,256,2048]{3,2,1,0:T(8,128)(2,1)} %param.13) | copy-start | bytes 6291460
  860.2 74.5 %copy-start.42 = (f32[1,4,4,128]{3,1,2,0:T(4,128)S(1)}, f32[1,4,4,128]{3,1,2,0:T(4,128)}, u32[]{:S(2)}) copy-start(f32[1,4,4,128]{3,1,2,0:T(4,128)} %copy-done.41) | copy-start | bytes 24580
  936.9 18.6 %collective-permute-start.3 = (f32[2,512]{1,0:T(2,128)S(1)}, f32[2,512]{1,0:T(2,128)S(1)}, u32[]{:S(2)}, u32[]{:S(2)}) collective-permute-start(f32[2,512]{1,0:T(2,128)S(1)} %bitcast.133), channel_id=1, source_target_pairs={{0,8},{8,0},{16,24},{24,16},{1,9},{9,1},{17,25},{25,17},{2,10},{10... | collective-permute-start | bytes 12296 | tf_op jit(solution)/shard_map/ppermute | solution.py:981
  938.0 17.4 %collective-permute-start.4 = (f32[2,512]{1,0:T(2,128)S(1)}, f32[2,512]{1,0:T(2,128)S(1)}, u32[]{:S(2)}, u32[]{:S(2)}) collective-permute-start(f32[2,512]{1,0:T(2,128)S(1)} %bitcast.132), channel_id=1, source_target_pairs={{0,16},{8,24},{16,0},{24,8},{1,17},{9,25},{17,1},{25,9},{2,18},{10... | collective-permute-start | bytes 12296 | tf_op jit(solution)/shard_map/ppermute | solution.py:981
  939.0 16.5 %collective-permute-start.5 = (f32[2,512]{1,0:T(2,128)S(1)}, f32[2,512]{1,0:T(2,128)S(1)}, u32[]{:S(2)}, u32[]{:S(2)}) collective-permute-start(f32[2,512]{1,0:T(2,128)S(1)} %bitcast.131), channel_id=1, source_target_pairs={{0,24},{8,16},{16,8},{24,0},{1,25},{9,17},{17,9},{25,1},{2,26},{10... | collective-permute-start | bytes 12296 | tf_op jit(solution)/shard_map/ppermute | solution.py:981
  955.5 1.6 collective-permute-start.6
  957.1 3.7 collective-permute-start.7
  960.8 38.4 %collective-permute-start.8 = (f32[2,512]{1,0:T(2,128)S(1)}, f32[2,512]{1,0:T(2,128)S(1)}, u32[]{:S(2)}, u32[]{:S(2)}) collective-permute-start(f32[2,512]{1,0:T(2,128)S(1)} %add.231), channel_id=1, source_target_pairs={{0,4},{1,5},{2,6},{3,7},{4,0},{5,1},{6,2},{7,3},{8,12},{9,13},{10,... | collective-permute-start | bytes 12296 | tf_op jit(solution)/shard_map/ppermute | solution.py:984
  (40 other events, 137.7 us)

commit v6 on v5

--- a/solution.py
+++ b/solution.py
@@ -140,6 +140,40 @@
             for copy in self.to_x[t] + self.to_y[t] + self.on_x[t] + self.on_y[t]:
                 copy.wait_send()
             self.local[t].wait()
+
+
+class SmallJob:
+    def __init__(self, own):
+        self.operand = own
+        self.rows, self.width = own.shape
+        self.out_shape = jax.ShapeDtypeStruct((4 * self.rows, self.width), own.dtype)
+        self.out_spec = pl.BlockSpec(memory_space=pl.ANY)
+
+    def scratch(self):
+        return [pltpu.SemaphoreType.DMA((2, 3)), pltpu.SemaphoreType.DMA(())]
+
+    def bind(self, operand, out, scratch, x, y):
+        sems, local = scratch
+        shard = lax.axis_index("shard")
+        mine = out.at[pl.ds(pl.multiple_of(shard * self.rows, self.rows), self.rows), :]
+        self.local = pltpu.make_async_copy(operand, mine, local)
+        self.sends = [
+            remote(operand, mine, sems, k, device)
+            for k, device in enumerate((x, y, (3 - shard, x[1])))
+        ]
+
+    def begin(self):
+        for send in self.sends:
+            send.start()
+        self.local.start()
+
+    def stages(self):
+        return []
+
+    def finish(self):
+        for send in self.sends:
+            send.wait()
+        self.local.wait()
 
 
 class SumJob:
@@ -394,6 +428,8 @@
                 pl.semaphore_signal(barrier, inc=1, device_id=device, device_id_type=MESH)
 
             near = ([x, y] if square else []) + ([lines[0].twin, lines[0].pair] if lines else [])
+            if any(isinstance(job, SmallJob) for job in self.jobs):
+                near.append((3 - shard, replica))
             for device in near:
                 greet(device)
             if lines:
@@ -498,33 +534,44 @@
 
 def products(items, block, comm, joined=False):
     specs, shapes, out_specs, steps, rights = [], [], [], [], []
-    total = sum((l.shape[1] if t else l.shape[0]) // block for l, _, t in items)
     begin = 0
+    items = [
+        (l if isinstance(l, tuple) else (l,), r if isinstance(r, tuple) else (r,), t)
+        for l, r, t in items
+    ]
+    total = sum((l[0].shape[1] if t else l[0].shape[0]) // block for l, _, t in items)
     for left, right, transposed in items:
-        size = left.shape[1] if transposed else left.shape[0]
+        size = left[0].shape[1] if transposed else left[0].shape[0]
         count = size // block
 
         def place(i, begin=begin, count=count):
             return jnp.clip(i - begin, 0, count - 1)
 
-        if transposed:
-            specs.append(pl.BlockSpec((left.shape[0], block), lambda i, p=place: (0, p(i))))
-        else:
-            specs.append(pl.BlockSpec((block, left.shape[1]), lambda i, p=place: (p(i), 0)))
+        for l in left:
+            if transposed:
+                specs.append(pl.BlockSpec((l.shape[0], block), lambda i, p=place: (0, p(i))))
+            else:
+                specs.append(pl.BlockSpec((block, l.shape[1]), lambda i, p=place: (p(i), 0)))
+        columns = right[0].shape[1]
         if not joined:
-            out_specs.append(pl.BlockSpec((block, right.shape[1]), lambda i, p=place: (p(i), 0)))
-            shapes.append(jax.ShapeDtypeStruct((size, right.shape[1]), BF16))
-        if not any(right is r for r in rights):
-            rights.append(right)
+            out_specs.append(pl.BlockSpec((block, columns), lambda i, p=place: (p(i), 0)))
+            shapes.append(jax.ShapeDtypeStruct((size, columns), BF16))
+        for r in right:
+            if not any(r is other for other in rights):
+                rights.append(r)
         steps.append((begin, count))
         begin += count
     right_specs = [
         pl.BlockSpec(r.shape, lambda i: (0, 0), pipeline_mode=pl.Buffered(1)) for r in rights
     ]
-    which = [next(k for k, r in enumerate(rights) if r is right) for _, right, _ in items]
-    n = len(items)
+    which = [
+        [next(k for k, other in enumerate(rights) if other is r) for r in right]
+        for _, right, _ in items
+    ]
+    firsts = [sum(len(l) for l, _, _ in items[:k]) for k in range(len(items))]
+    n = sum(len(l) for l, _, _ in items)
     if joined:
-        width = items[0][1].shape[1]
+        width = items[0][1][0].shape[1]
         out_specs = [pl.BlockSpec((block, width), lambda i: (i, 0))]
         shapes = [jax.ShapeDtypeStruct((total * block, width), BF16)]
     made = len(shapes)
@@ -535,18 +582,26 @@
         )
         step = pl.program_id(0)
         comm.enter(operands, comm_outs, scratch, step == 0)
-        width = items[0][1].shape[1] // SLOTS
+        width = items[0][1][0].shape[1] // SLOTS
 
         def part(slot, carry):
             comm.advance(step * SLOTS + slot, total * SLOTS)
             columns = pl.ds(pl.multiple_of(slot * width, width), width)
-            for k, (_, _, transposed) in enumerate(items):
+            for k, (left, right, transposed) in enumerate(items):
                 begin, count = steps[k]
 
                 @pl.when((step >= begin) & (step < begin + count))
-                def _(k=k, transposed=transposed):
+                def _(k=k, left=left, right=right, transposed=transposed):
                     dot = dot_tn if transposed else dot_nn
-                    result = dot(lefts[k][...], held[which[k]][:, columns])
+                    result, pieces = 0.0, max(len(left), len(right))
+                    for piece in range(pieces):
+                        l, r = lefts[firsts[k] + piece % len(left)], held[which[k][piece % len(right)]]
+                        share = pl.ds(piece * (r.shape[0] // pieces), r.shape[0] // pieces)
+                        ours = pl.ds(piece * (l.shape[0] // pieces), l.shape[0] // pieces)
+                        result += dot(
+                            l[ours, :] if len(left) < pieces else l[...],
+                            r[share, columns] if len(right) < pieces else r[:, columns],
+                        )
                     outs[0 if joined else k][:, columns] = result.astype(BF16)
 
             return carry
@@ -555,7 +610,7 @@
 
         comm.finish(step == total - 1)
 
-    flops = 2 * sum(math.prod(l.shape) * r.shape[1] for l, r, _ in items)
+    flops = 2 * sum(math.prod(l.shape) * right[0].shape[1] for left, right, _ in items for l in left)
     out = pl.pallas_call(
         kernel,
         grid=(total,),
@@ -566,7 +621,7 @@
         compiler_params=comm_params(comm, 58),
         cost_estimate=pl.CostEstimate(flops=flops, bytes_accessed=30_000_000, transcendentals=0),
         name="products",
-    )(*[l for l, _, _ in items], *rights, *comm.operands)
+    )(*[l for left, _, _ in items for l in left], *rights, *comm.operands)
     return out[:made], out[made:]
 
 
@@ -946,6 +1001,12 @@
     return lax.optimization_barrier(values)
 
 
+def sum_beside(part, trees):
+    return lax.psum_scatter(
+        part.reshape(trees, -1, part.shape[1]), "shard", scatter_dimension=1, tiled=True
+    )
+
+
 class Square:
     def __init__(self, shard, replica):
         self.shard, self.replica = shard, replica
@@ -953,6 +1014,10 @@
         self.y = [(i, i ^ 2) for i in range(shard)]
         self.d = [(i, i ^ 3) for i in range(shard)]
 
+    def natural(self, rows, trees):
+        blocks = rows.reshape(trees, self.shard, -1, rows.shape[1])
+        return self.reorder(blocks, 1).reshape(rows.shape)
+
     def place(self, block):
         shard = lax.axis_index("shard")
         return (block + shard) % 2 + 2 * ((block // 2 + shard // 2) % 2)
@@ -963,14 +1028,11 @@
             [lax.dynamic_slice_in_dim(blocks, n ^ me, 1, axis) for n in range(self.shard)], axis=axis
         )
 
-    def gather_small(self, own):
-        parts = [
-            own,
-            lax.ppermute(own, "shard", self.x),
-            lax.ppermute(own, "shard", self.y),
-            lax.ppermute(own, "shard", self.d),
-        ]
-        return self.reorder(jnp.stack(parts), 0)
+    def first(self, small, own):
+        padded = jnp.pad(small, (0, -small.shape[0] % 2048)).reshape(16, -1)
+        self.kernels += 1
+        smalls, rows = transfer(Comm([SmallJob(padded), GatherJob(own, 1)], self.kernels))
+        return smalls.reshape(self.shard, -1)[:, : small.shape[0]], rows
 
     def sum_small(self, values):
         share = values.shape[1] // self.shard
@@ -1006,8 +1068,12 @@
     def place(self, block):
         return block
 
-    def gather_small(self, own):
-        return lax.all_gather(own, "shard", axis=0, tiled=False)
+    def natural(self, rows, trees):
+        return rows
+
+    def first(self, small, own):
+        rows = lax.all_gather(own, "shard", axis=0, tiled=True)
+        return lax.all_gather(small, "shard", axis=0, tiled=False), rows
 
     def carry(self, compute, gathers=(), sums=(), totals=()):
         results = None if compute is None else compute(NoComm())[0]
@@ -1077,8 +1143,7 @@
     small = jnp.concatenate(
         [gain_attn, gain_ff] + [segment_ids[t, 0].astype(BF16) for t in range(trees)]
     )
-    smalls = links.gather_small(small)
-    _, (rows_0,), _, _ = links.carry(None, gathers=[(token_rows[0], 1)])
+    smalls, rows_0 = links.first(small, token_rows[0])
     gain_first = smalls[:, :share].reshape(width).astype(F32)
     gain_second = smalls[:, share : 2 * share].reshape(width).astype(F32)
     masks, tables = [], []
@@ -1156,18 +1221,19 @@
     results = [
         (middle + RESIDUAL * down).astype(BF16) for middle, down in zip((middle_0, middle_1), downs)
     ]
-    normed_part = dot_nn(qkv_grad, w_qkv).astype(BF16)
-    attended_all = jnp.concatenate([saved_0[0], saved_1[0]], axis=0)
-    normed_all = jnp.concatenate([normed_0, normed_1], axis=0)
+    normed_part = dot_nn(links.natural(qkv_grad, trees), w_qkv).astype(BF16)
+    normed_sums = sum_beside(normed_part, trees)
     (grad_attn,), _ = products(
-        [(attended_all, out_all, True), (qkv_grad, normed_all, True)],
+        [
+            ((saved_0[0], saved_1[0]), out_all, True),
+            (qkv_grad, (normed_0, normed_1), True),
+        ],
         128 if shard > 4 else 256,
         NoComm(),
         joined=True,
     )
-    _, _, normed_grads, (total_attn,) = links.carry(
-        None, sums=parts(normed_part), totals=[grad_attn]
-    )
+    _, _, _, (total_attn,) = links.carry(None, totals=[grad_attn])
+    normed_grads = [normed_sums[t].astype(F32) for t in range(trees)]
     input_grads = []
     gain_attn_sum = jnp.zeros((width,), F32)
     for t in range(trees):

time: 1010 us -> 1030 us (1.020)
  Pallas kernels: 727 us -> 746 us
  between operations: 2.05 us -> 15.4 us
    pallas_call x2, Pallas kernels: 70.4 us -> 85.7 us  [attention_forward(): pl.pallas_call(functools.partial(attention_forward_kernel, kv_heads, bloc...]
    concatenate x3 -> x0, other arithmetic: 10.7 us -> none  [the longest x1 8.43 us: body(): normed_all = jnp.concatenate([normed_0, normed_1], axis=0)]
  transfers between devices with their start and end apart: 9 -> 7, of which waited for: 1 -> 2; matrix products, arithmetic and copies ran while one was open for 6% -> 5% of each run, Pallas kernels for 4% -> 9%
where the time goes in v6:
time: 1030 us; the launch traced here: 1020 us
  Pallas kernels  746 us (72%)
  matrix products  139 us (13%)
  other arithmetic  87.8 us (9%)
  local copies, waits for them, and re-layouts  24.9 us (2%)
  between operations  15.4 us (1%)
    pallas_call x3, Pallas kernels, products(): pl.pallas_call(kernel, grid=(total,), in_specs=specs + right_specs + list...  256 us
    pallas_call x4, Pallas kernels, transfer(): pl.pallas_call(kernel, grid=(steps,), in_specs=comm.in_specs, out_specs=c...  213 us
    pallas_call x1, Pallas kernels, attention_backward(): pl.pallas_call(functools.partial(attention_backward_kernel, kv_heads, blo...  119 us
    pallas_call x2, Pallas kernels, attention_forward(): pl.pallas_call(functools.partial(attention_forward_kernel, kv_heads, bloc...  85.7 us
    pallas_call x1, Pallas kernels, feed_forward(): pl.pallas_call(kernel, grid=(steps,), in_specs=[pl.BlockSpec((rows, width...  72.3 us
    dot_general x7, matrix products, dot_nn(): lax.dot_general(left, right, (((1,), (0,)), ((), ())), preferred_element_...  65.5 us
    dot_general x5, matrix products, dot_nt(): lax.dot_general(left, right, (((1,), (1,)), ((), ())), preferred_element_...  49.5 us
    dot_general x1, matrix products, dot_tn(): lax.dot_general(left, right, (((0,), (0,)), ((), ())), preferred_element_...  23.9 us
  transfers between devices with their start and end apart: 7, of which 2 were waited for; matrix products, arithmetic and copies ran while one was open for 5% of the time, Pallas kernels for 9%

profile of v6, /device:TPU:0, one launch (start us, length us, event | category | flops | bytes accessed | tf_op | source)
XLA Modules:
  0.0 1021.0 jit_solution(5505269584178254394)
XLA Ops:
  9.9 39.1 %transfer.4 = (bf16[64,128]{1,0:T(8,128)(2,1)S(1)}, bf16[1024,2048]{1,0:T(8,128)(2,1)S(1)}) custom-call(bf16[16,128]{1,0:T(8,128)(2,1)S(1)} %fusion.64.refs_0_, bf16[256,2048]{1,0:T(8,128)(2,1)S(1)} %get-tuple-element.143.refs_1_), custom_call_target="tpu_custom_call" | custom-call | tf_op jit(solution)/shard_map/transfer/pallas_call | solution.py:523
  68.6 4.9 fusion.49
  73.5 50.1 %attention_forward.2 = (bf16[1024,512]{1,0:T(8,128)(2,1)S(1)}, bf16[1024,512]{1,0:T(8,128)(2,1)S(1)}, bf16[1024,256]{1,0:T(8,128)(2,1)S(1)}, f32[1024,128]{1,0:T(8,128)S(1)}, bf16[1024,2048]{1,0:T(8,128)(2,1)S(1)}) custom-call(f32[1024,768]{1,0:T(8,128)S(1)} %fusion.74.refs_0_.refs_1_, f32[1024,768]{1,0:T(8,128)S(1)} %fusion.74.refs_0_.refs_1_, ...), custom_call_target="tpu_custom_call" | custom-call | flops 10000000000 | bytes 12000000 | tf_op jit(solution)/shard_map/attention_forward/pallas_call | solution.py:790
  128.4 5.2 fusion.75.refs_0_.refs_1_
  137.4 35.5 %attention_forward.3 = (bf16[1024,512]{1,0:T(8,128)(2,1)S(1)}, bf16[1024,512]{1,0:T(8,128)(2,1)S(1)}, bf16[1024,256]{1,0:T(8,128)(2,1)S(1)}, f32[1024,128]{1,0:T(8,128)S(1)}, f32[256,2048]{1,0:T(8,128)S(1)}) custom-call(f32[1024,768]{1,0:T(8,128)S(1)} %copy-done.14, f32[1024,768]{1,0:T(8,128)S(1)} %copy-done.14, f32[1024,128]{1,0:T(8,128)S(1)} %copy-done.4, ...), custom_call_target="tpu_custom_call" | custom-call | flops 10000000000 | bytes 12000000 | tf_op jit(solution)/shard_map/attention_forward/pallas_call | solution.py:790
  179.3 34.1 %transfer.5 = f32[256,2048]{1,0:T(8,128)S(1)} custom-call(bf16[1024,2048]{1,0:T(8,128)(2,1)} %convolution_convert_fusion.2.refs_0_), custom_call_target="tpu_custom_call" | custom-call | tf_op jit(solution)/shard_map/transfer/pallas_call | solution.py:523
  217.2 66.9 %transfer.6.refs_0_.refs_2_ = bf16[2048,2048]{1,0:T(8,128)(2,1)} custom-call(bf16[512,2048]{1,0:T(8,128)(2,1)S(1)} %pad_maximum_fusion.1.refs_0_), custom_call_target="tpu_custom_call" | custom-call | tf_op jit(solution)/shard_map/transfer/pallas_call | solution.py:523
  286.3 72.3 %feed_forward.1 = (bf16[2048,2048]{1,0:T(8,128)(2,1)}, bf16[2048,2048]{1,0:T(8,128)(2,1)}, bf16[2048,2048]{1,0:T(8,128)(2,1)}, bf16[2048,2048]{1,0:T(8,128)(2,1)}) custom-call(bf16[2048,2048]{1,0:T(8,128)(2,1)} %transfer.6.refs_0_.refs_2_, bf16[2048,2048]{1,0:T(8,128)(2,1)} %refs_1_.2, bf16[2048,2048]{1,0:T(8,128)(2,1)} %refs_2_.1, ...), custom_call_target="tpu_custom_call" | custom-call | flops 34359738368 | bytes 48000000 | tf_op jit(solution)/shard_map/feed_forward/pallas_call | solution.py:652
  358.6 23.9 %convolution_convert_fusion.1.refs_5_ = bf16[2048,2048]{1,0:T(8,128)(2,1)} fusion(bf16[2048,2048]{1,0:T(8,128)(2,1)} %get-tuple-element.45.refs_0_, bf16[2048,2048]{1,0:T(8,128)(2,1)} %get-tuple-element.46), kind=kOutput, calls=%fused_computation.23 | convolution fusion | flops 17184063488 | bytes 25165824 | tf_op jit(solution)/shard_map/dot_general | solution.py:35
  382.5 31.9 %fusion.7 = (bf16[2048,2048]{1,0:T(8,128)(2,1)}, bf16[2048,2048]{1,0:T(8,128)(2,1)}) fusion(bf16[2048,2048]{1,0:T(8,128)(2,1)} %get-tuple-element.48, bf16[2048,2048]{1,0:T(8,128)(2,1)} %get-tuple-element.47, bf16[2048,2048]{1,0:T(8,128)(2,1)} %get-tuple-element.46, bf16[2048,2048]{1,0:T(8,128)(2,1)} %refs_1_.3), kind=kOutput, calls=%fused_computation.10 | convolution fusion | flops 17242783744 | bytes 50331648 | tf_op jit(solution)/shard_map/dot_general | solution.py:27
  414.4 24.6 %fusion.76 = f32[2048,2048]{1,0:T(8,128)} fusion(bf16[2048,2048]{1,0:T(8,128)(2,1)} %get-tuple-element.121.refs_0_, bf16[2048,2048]{1,0:T(8,128)(2,1)} %refs_1_.2), kind=kOutput, calls=%fused_computation.189 | convolution fusion | flops 17179869184 | bytes 33554432 | tf_op jit(solution)/shard_map/dot_general | solution.py:31
  438.9 24.4 %add_convert_fusion.refs_3_.refs_4_ = bf16[2048,2048]{1,0:T(8,128)(2,1)} fusion(f32[2048,2048]{1,0:T(8,128)} %fusion.76, bf16[2048,2048]{1,0:T(8,128)(2,1)} %get-tuple-element.120.refs_1_, bf16[2048,2048]{1,0:T(8,128)(2,1)S(1)} %copy-done.57), kind=kOutput, calls=%fused_computation.11 | convolution fusion | flops 17188257792 | bytes 41943040 | tf_op jit(solution)/shard_map/dot_general | solution.py:31
  463.4 118.8 %products.3 = (bf16[2048,2048]{1,0:T(8,128)(2,1)}, bf16[2048,2048]{1,0:T(8,128)(2,1)}, f32[256,2048]{1,0:T(8,128)}, f32[256,2048]{1,0:T(8,128)}, bf16[2048,2048]{1,0:T(8,128)(2,1)}) custom-call(bf16[2048,2048]{1,0:T(8,128)(2,1)} %get-tuple-element.121.refs_0_, bf16[2048,2048]{1,0:T(8,128)(2,1)} %get-tuple-element.120.refs_1_, ...), custom_call_target="tpu_custom_call" | custom-call | flops 34359738368 | bytes 30000000 | tf_op jit(solution)/shard_map/products/pallas_call | solution.py:614
  590.6 113.5 %products.4 = (bf16[2048,2048]{1,0:T(8,128)(2,1)}, bf16[2048,2048]{1,0:T(8,128)(2,1)}, bf16[2048,2048]{1,0:T(8,128)(2,1)}) custom-call(bf16[2048,2048]{1,0:T(8,128)(2,1)} %get-tuple-element.45.refs_0_, bf16[2048,2048]{1,0:T(8,128)(2,1)} %refs_1_.3, bf16[512,2048]{1,0:T(8,128)(2,1)} %pad_maximum_fusion.3.refs_2_, bf16[2048,2048]{1,0:T(8,128)(2,1)} %get-tuple-element.51.refs_3_), custom_call_target="tpu_custom_call" | custom-call | flops 17179869184 | bytes 30000000 | tf_op jit(solution)/shard_map/products/pallas_call | solution.py:614
  704.2 5.7 fusion.40.refs_0_
  713.2 119.3 %attention_backward.1 = (bf16[2048,768]{1,0:T(8,128)(2,1)}, f32[256,2048]{1,0:T(8,128)}, f32[256,2048]{1,0:T(8,128)}, bf16[2048,2048]{1,0:T(8,128)(2,1)}) custom-call(bf16[1024,512]{1,0:T(8,128)(2,1)} %fusion.40.refs_0_, bf16[1024,512]{1,0:T(8,128)(2,1)} %copy-done.16, bf16[1024,256]{1,0:T(8,128)(2,1)} %copy-done.19, f32[1024,128]{1,0:T(8,128)} %copy-done.20, ...), custom_call_target="tpu_custom_call" | custom-call | flops 40000000000 | bytes 24000000 | tf_op jit(solution)/shard_map/attention_backward/pallas_call | solution.py:976
  836.4 9.2 convolution_convert_fusion
  845.6 23.5 %products.5.refs_0_ = bf16[1280,2048]{1,0:T(8,128)(2,1)} custom-call(bf16[1024,512]{1,0:T(8,128)(2,1)} %copy-done.11, bf16[1024,512]{1,0:T(8,128)(2,1)} %copy-done.13, bf16[2048,768]{1,0:T(8,128)(2,1)} %get-tuple-element.63.refs_2_, bf16[2048,2048]{1,0:T(8,128)(2,1)} %get-tuple-element.52.refs_3_, bf16[1024,2048]{1,0:T(8,128)(2,1)} %copy-done.35, ...), custom_call_target="tpu_custom_call" | custom-call | flops 10737418240 | bytes 30000000 | tf_op jit(solution)/shard_map/products/pallas_call | solution.py:614
  869.2 72.6 %transfer.7 = bf16[1280,2048]{1,0:T(8,128)(2,1)S(1)} custom-call(bf16[1280,2048]{1,0:T(8,128)(2,1)} %products.5.refs_0_), custom_call_target="tpu_custom_call" | custom-call | tf_op jit(solution)/shard_map/transfer/pallas_call | solution.py:523
  944.2 11.7 %convert_element_type.282 = f32[2048,2048]{1,0:T(8,128)} convert(bf16[2048,2048]{1,0:T(8,128)(2,1)} %get-tuple-element.65) | non-fusion elementwise | flops 4194304 | bytes 25165824 | tf_op jit(solution)/shard_map/convert_element_type | solution.py:1256
  955.9 11.7 %convert_element_type.281 = f32[2048,2048]{1,0:T(8,128)} convert(bf16[2048,2048]{1,0:T(8,128)(2,1)} %get-tuple-element.64) | non-fusion elementwise | flops 4194304 | bytes 25165824 | tf_op jit(solution)/shard_map/convert_element_type | solution.py:1255
  967.6 11.7 %convert_element_type.283 = f32[2048,2048]{1,0:T(8,128)} convert(bf16[2048,2048]{1,0:T(8,128)(2,1)} %get-tuple-element.66) | non-fusion elementwise | flops 4194304 | bytes 25165824 | tf_op jit(solution)/shard_map/convert_element_type | solution.py:1257
  982.1 6.7 slice_convert_fusion
  995.9 4.7 fusion.31
  (218 shorter events, 83.7 us)
Async XLA Ops:
  7.2 127.8 %copy-start = (bf16[512,2048]{1,0:T(8,128)(2,1)S(1)}, bf16[512,2048]{1,0:T(8,128)(2,1)}, u32[]{:S(2)}) copy-start(bf16[512,2048]{1,0:T(8,128)(2,1)} %param.18) | copy-start | bytes 6291460
  7.2 981.6 %reduce-scatter.2.cloned.1.call-start = ((), (), s32[]{:S(2)}) async-start(), calls=%async_computation.1 | async-start | bytes 10485760 | tf_op jit(solution)/shard_map/reduce_scatter | solution.py:1005
  8.1 45.2 %copy-start.56 = (s32[2,1,13]{2,1,0:T(1,128)S(1)}, s32[2,1,13]{2,1,0:T(1,128)}, u32[]{:S(2)}) copy-start(s32[2,1,13]{2,1,0:T(1,128)} %param.25) | copy-start | bytes 316
  55.4 69.9 %copy-start.44 = (f32[1,4,4,128]{3,1,2,0:T(4,128)}, f32[1,4,4,128]{3,1,2,0:T(4,128)S(1)}, u32[]{:S(2)}) copy-start(f32[1,4,4,128]{3,1,2,0:T(4,128)S(1)} %copy.40) | copy-start | bytes 24580
  60.4 13.1 %copy-start.7 = (bf16[1024,128]{1,0:T(8,128)(2,1)}, bf16[1024,128]{1,0:T(8,128)(2,1)S(1)}, u32[]{:S(2)}) copy-start(bf16[1024,128]{1,0:T(8,128)(2,1)S(1)} %pad.19.refs_5_.refs_7_) | copy-start | bytes 786436
  61.5 12.0 %copy-start.8 = (bf16[1024,128]{1,0:T(8,128)(2,1)}, bf16[1024,128]{1,0:T(8,128)(2,1)S(1)}, u32[]{:S(2)}) copy-start(bf16[1024,128]{1,0:T(8,128)(2,1)S(1)} %pad.18.refs_4_.refs_6_) | copy-start | bytes 786436
  65.1 61.3 %copy-start.40 = (bf16[768,2048]{1,0:T(8,128)(2,1)}, bf16[768,2048]{1,0:T(8,128)(2,1)S(1)}, u32[]{:S(2)}) copy-start(bf16[768,2048]{1,0:T(8,128)(2,1)S(1)} %constant_dynamic-update-slice_fusion) | copy-start | bytes 9437188
  73.5 50.2 %copy-start.5 = (f32[1024,128]{1,0:T(8,128)}, f32[1024,128]{1,0:T(8,128)S(1)}, u32[]{:S(2)}) copy-start(f32[1024,128]{1,0:T(8,128)S(1)} %get-tuple-element.162.refs_2_.refs_4_) | copy-start | bytes 1572868
  73.5 50.2 %copy-start.6 = (f32[1024,128]{1,0:T(8,128)}, f32[1024,128]{1,0:T(8,128)S(1)}, u32[]{:S(2)}) copy-start(f32[1024,128]{1,0:T(8,128)S(1)} %get-tuple-element.163.refs_3_.refs_5_) | copy-start | bytes 1572868
  179.3 34.1 %copy-start.26 = (bf16[2,1,256,2048]{3,2,1,0:T(8,128)(2,1)S(1)}, bf16[2,1,256,2048]{3,2,1,0:T(8,128)(2,1)}, u32[]{:S(2)}) copy-start(bf16[2,1,256,2048]{3,2,1,0:T(8,128)(2,1)} %param.13) | copy-start | bytes 6291460
  217.2 66.9 %copy-start.28 = (bf16[2,1,256,2048]{3,2,1,0:T(8,128)(2,1)S(1)}, bf16[2,1,256,2048]{3,2,1,0:T(8,128)(2,1)}, u32[]{:S(2)}) copy-start(bf16[2,1,256,2048]{3,2,1,0:T(8,128)(2,1)} %param.23) | copy-start | bytes 6291460
  414.4 24.6 %copy-start.57 = (bf16[2048,2048]{1,0:T(8,128)(2,1)S(1)}, bf16[2048,2048]{1,0:T(8,128)(2,1)}, u32[]{:S(2)}) copy-start(bf16[2048,2048]{1,0:T(8,128)(2,1)} %refs_2_.1) | copy-start | bytes 25165828
  463.3 118.8 %copy-start.22 = (f32[256,2048]{1,0:T(8,128)S(1)}, f32[256,2048]{1,0:T(8,128)}, u32[]{:S(2)}) copy-start(f32[256,2048]{1,0:T(8,128)} %copy-done.21) | copy-start | bytes 6291460
  463.4 118.8 %copy-start.47 = (f32[1,4,4,128]{3,1,2,0:T(4,128)S(1)}, f32[1,4,4,128]{3,1,2,0:T(4,128)}, u32[]{:S(2)}) copy-start(f32[1,4,4,128]{3,1,2,0:T(4,128)} %copy-done.46) | copy-start | bytes 24580
  463.4 118.8 %copy-start.49 = (f32[256]{0:T(256)S(1)}, f32[256]{0:T(256)}, u32[]{:S(2)}) copy-start(f32[256]{0:T(256)} %copy-done.48) | copy-start | bytes 3076
  463.4 118.8 %copy-start.51 = (f32[256]{0:T(256)S(1)}, f32[256]{0:T(256)}, u32[]{:S(2)}) copy-start(f32[256]{0:T(256)} %copy-done.50) | copy-start | bytes 3076
  967.6 11.7 %copy-start.53 = (f32[256]{0:T(256)S(1)}, f32[256]{0:T(256)}, u32[]{:S(2)}) copy-start(f32[256]{0:T(256)} %get-tuple-element.109) | copy-start | bytes 3076
  967.6 11.7 %copy-start.52 = (f32[256]{0:T(256)S(1)}, f32[256]{0:T(256)}, u32[]{:S(2)}) copy-start(f32[256]{0:T(256)} %get-tuple-element.108) | copy-start | bytes 3076
  992.3 8.3 collective-permute-start
  992.9 7.8 collective-permute-start.1
  993.9 6.7 collective-permute-start.2
  1000.7 4.3 collective-permute-start.3
  1005.0 3.7 collective-permute-start.4
  1008.7 4.5 collective-permute-start.5
  (42 other events, 142.6 us)
Sparse Core Ops, SparseCore 0:
  845.8 85.7 reduce-scatter.1

commit v7 on v6

--- a/solution.py
+++ b/solution.py
@@ -260,11 +260,9 @@
 
 
 class LineJob:
-    LINE_ROWS = 32
-    LAG = 2
-
-    def __init__(self, grad):
+    def __init__(self, grad, rows, lag):
         self.operand = grad
+        self.LINE_ROWS, self.LAG = rows, lag
         self.half, self.width = grad.shape[0] // 2, grad.shape[1]
         self.chunks = self.half // self.LINE_ROWS
         self.steps = self.chunks + 1 + 3 * self.LAG
@@ -1034,21 +1032,27 @@
         smalls, rows = transfer(Comm([SmallJob(padded), GatherJob(own, 1)], self.kernels))
         return smalls.reshape(self.shard, -1)[:, : small.shape[0]], rows
 
-    def sum_small(self, values):
+    def sum_small(self, values, beside):
         share = values.shape[1] // self.shard
         blocks = values.reshape(values.shape[0], self.shard, share)
         blocks = self.reorder(blocks, 1)
-        total = blocks[:, 0]
-        for k, perm in ((1, self.x), (2, self.y), (3, self.d)):
-            total = total + lax.ppermute(blocks[:, k], "shard", perm)
-        for step in (1, 2, 4):
-            perm = [(i, i ^ step) for i in range(self.replica)]
-            total = total + lax.ppermute(total, "replica", perm)
-        return total
+        hops = [[("shard", perm) for perm in (self.x, self.y, self.d)]]
+        hops += [[("replica", [(i, i ^ k) for i in range(self.replica)])] for k in (1, 2, 4)]
+        total, done = blocks[:, 0], []
+        for number, hop in enumerate(hops):
+            got = [
+                lax.ppermute(blocks[:, k + 1] if number == 0 else total, axis, perm)
+                for k, (axis, perm) in enumerate(hop)
+            ]
+            if number < len(beside):
+                done.append(beside[number](total))
+                got, done[-1] = sync(got, done[-1])
+            total = total + sum(got)
+        return total, done + [f(total) for f in beside[len(hops) :]]
 
     def carry(self, compute, gathers=(), sums=(), totals=()):
         jobs = [GatherJob(*own) for own in gathers] + [SumJob(*part) for part in sums]
-        jobs += [LineJob(grad) for grad in totals]
+        jobs += [LineJob(grad, *((32, 2) if compute is None else (64, 1))) for grad in totals]
         self.kernels += 1
         comm = Comm(jobs, self.kernels)
         if compute is None:
@@ -1090,9 +1094,9 @@
         ]
         return results, gathered, summed, [lax.psum(grad, "replica") for grad in totals]
 
-    def sum_small(self, values):
+    def sum_small(self, values, beside):
         share = lax.psum_scatter(values, "shard", scatter_dimension=1, tiled=True)
-        return lax.psum(share, "replica")
+        return lax.psum(share, "replica"), [f(share) for f in beside]
 
     def start(self):
         pass
@@ -1233,6 +1237,7 @@
         joined=True,
     )
     _, _, _, (total_attn,) = links.carry(None, totals=[grad_attn])
+    normed_sums, total_attn = sync(normed_sums, total_attn)
     normed_grads = [normed_sums[t].astype(F32) for t in range(trees)]
     input_grads = []
     gain_attn_sum = jnp.zeros((width,), F32)
@@ -1241,7 +1246,14 @@
         input_back, term = norm_back(inputs, rms_scale(inputs), gain_first, normed_grads[t])
         gain_attn_sum = gain_attn_sum + term
         input_grads.append(middle_grads[t] + input_back)
-    gains = links.sum_small(jnp.stack([gain_attn_sum, gain_ff_sum]))
+    totals = (total_down, total_gate, total_up)
+
+    def convert(index):
+        return lambda after: sync(totals[index], after)[0].astype(F32)
+
+    gains, converted = links.sum_small(
+        jnp.stack([gain_attn_sum, gain_ff_sum]), [convert(0), convert(1), convert(2)]
+    )
     rows = lambda begin, count: total_attn[begin : begin + count].astype(F32)
     return (
         jnp.stack(results)[:, None],
@@ -1252,9 +1264,9 @@
         rows(2 * q_width + kv_width, kv_width),
         rows(0, q_width),
         gains[1],
-        total_gate.astype(F32),
-        total_up.astype(F32),
-        total_down.astype(F32),
+        converted[1],
+        converted[2],
+        converted[0],
     )
 
 

time: 1030 us -> 1050 us (1.019)
  Pallas kernels: 746 us -> 773 us
    pallas_call x3, Pallas kernels: 256 us -> 271 us  [products(): pl.pallas_call(kernel, grid=(total,), in_specs=specs + right_specs + list...]
    pallas_call x1, Pallas kernels: 119 us -> 131 us  [attention_backward(): pl.pallas_call(functools.partial(attention_backward_kernel, kv_heads, blo...]
  transfers between devices with their start and end apart: 7 -> 7, of which waited for: 2 -> 1; matrix products, arithmetic and copies ran while one was open for 5% -> 5% of each run, Pallas kernels for 9% -> 9%
where the time goes in v7:
time: 1050 us
  Pallas kernels  773 us (74%)
  matrix products  139 us (13%)
  other arithmetic  87.9 us (8%)
  local copies, waits for them, and re-layouts  23.7 us (2%)
  between operations  15.5 us (1%)
    pallas_call x3, Pallas kernels, products(): pl.pallas_call(kernel, grid=(total,), in_specs=specs + right_specs + list...  271 us
    pallas_call x4, Pallas kernels, transfer(): pl.pallas_call(kernel, grid=(steps,), in_specs=comm.in_specs, out_specs=c...  213 us
    pallas_call x1, Pallas kernels, attention_backward(): pl.pallas_call(functools.partial(attention_backward_kernel, kv_heads, blo...  131 us
    pallas_call x2, Pallas kernels, attention_forward(): pl.pallas_call(functools.partial(attention_forward_kernel, kv_heads, bloc...  85.7 us
    pallas_call x1, Pallas kernels, feed_forward(): pl.pallas_call(kernel, grid=(steps,), in_specs=[pl.BlockSpec((rows, width...  72.3 us
    dot_general x7, matrix products, dot_nn(): lax.dot_general(left, right, (((1,), (0,)), ((), ())), preferred_element_...  65.5 us
    dot_general x5, matrix products, dot_nt(): lax.dot_general(left, right, (((1,), (1,)), ((), ())), preferred_element_...  49.6 us
    convert_element_type x3, other arithmetic, convert(): return lambda after: sync(totals[index], after)[0].astype(F32)  35.2 us
  transfers between devices with their start and end apart: 7, of which 1 were waited for; matrix products, arithmetic and copies ran while one was open for 5% of the time, Pallas kernels for 9%

profile of v7, /device:TPU:0, one launch (start us, length us, event | category | flops | bytes accessed | tf_op | source)
XLA Modules:
  0.0 1046.7 jit_solution(4749055364983385570)
XLA Ops:
  9.9 39.1 %transfer.4 = (bf16[64,128]{1,0:T(8,128)(2,1)S(1)}, bf16[1024,2048]{1,0:T(8,128)(2,1)S(1)}) custom-call(bf16[16,128]{1,0:T(8,128)(2,1)S(1)} %fusion.64.refs_0_, bf16[256,2048]{1,0:T(8,128)(2,1)S(1)} %get-tuple-element.169.refs_1_), custom_call_target="tpu_custom_call" | custom-call | tf_op jit(solution)/shard_map/transfer/pallas_call | solution.py:521
  68.6 4.9 fusion.49
  73.5 50.1 %attention_forward.2 = (bf16[1024,512]{1,0:T(8,128)(2,1)S(1)}, bf16[1024,512]{1,0:T(8,128)(2,1)S(1)}, bf16[1024,256]{1,0:T(8,128)(2,1)S(1)}, f32[1024,128]{1,0:T(8,128)S(1)}, bf16[1024,2048]{1,0:T(8,128)(2,1)S(1)}) custom-call(f32[1024,768]{1,0:T(8,128)S(1)} %fusion.72.refs_0_.refs_1_, f32[1024,768]{1,0:T(8,128)S(1)} %fusion.72.refs_0_.refs_1_, ...), custom_call_target="tpu_custom_call" | custom-call | flops 10000000000 | bytes 12000000 | tf_op jit(solution)/shard_map/attention_forward/pallas_call | solution.py:788
  128.4 5.2 fusion.73.refs_0_.refs_1_
  137.4 35.5 %attention_forward.3 = (bf16[1024,512]{1,0:T(8,128)(2,1)S(1)}, bf16[1024,512]{1,0:T(8,128)(2,1)S(1)}, bf16[1024,256]{1,0:T(8,128)(2,1)S(1)}, f32[1024,128]{1,0:T(8,128)S(1)}, f32[256,2048]{1,0:T(8,128)S(1)}) custom-call(f32[1024,768]{1,0:T(8,128)S(1)} %copy-done.14, f32[1024,768]{1,0:T(8,128)S(1)} %copy-done.14, f32[1024,128]{1,0:T(8,128)S(1)} %copy-done.4, ...), custom_call_target="tpu_custom_call" | custom-call | flops 10000000000 | bytes 12000000 | tf_op jit(solution)/shard_map/attention_forward/pallas_call | solution.py:788
  179.3 34.1 %transfer.5 = f32[256,2048]{1,0:T(8,128)S(1)} custom-call(bf16[1024,2048]{1,0:T(8,128)(2,1)} %convolution_convert_fusion.2.refs_0_), custom_call_target="tpu_custom_call" | custom-call | tf_op jit(solution)/shard_map/transfer/pallas_call | solution.py:521
  217.3 66.9 %transfer.6.refs_0_.refs_2_ = bf16[2048,2048]{1,0:T(8,128)(2,1)} custom-call(bf16[512,2048]{1,0:T(8,128)(2,1)S(1)} %pad_maximum_fusion.1.refs_0_), custom_call_target="tpu_custom_call" | custom-call | tf_op jit(solution)/shard_map/transfer/pallas_call | solution.py:521
  286.3 72.3 %feed_forward.1 = (bf16[2048,2048]{1,0:T(8,128)(2,1)}, bf16[2048,2048]{1,0:T(8,128)(2,1)}, bf16[2048,2048]{1,0:T(8,128)(2,1)}, bf16[2048,2048]{1,0:T(8,128)(2,1)}) custom-call(bf16[2048,2048]{1,0:T(8,128)(2,1)} %transfer.6.refs_0_.refs_2_, bf16[2048,2048]{1,0:T(8,128)(2,1)} %refs_1_.2, bf16[2048,2048]{1,0:T(8,128)(2,1)} %refs_2_.1, ...), custom_call_target="tpu_custom_call" | custom-call | flops 34359738368 | bytes 48000000 | tf_op jit(solution)/shard_map/feed_forward/pallas_call | solution.py:650
  358.6 23.9 %convolution_convert_fusion.1.refs_5_ = bf16[2048,2048]{1,0:T(8,128)(2,1)} fusion(bf16[2048,2048]{1,0:T(8,128)(2,1)} %get-tuple-element.58.refs_0_, bf16[2048,2048]{1,0:T(8,128)(2,1)} %get-tuple-element.59), kind=kOutput, calls=%fused_computation.23 | convolution fusion | flops 17184063488 | bytes 25165824 | tf_op jit(solution)/shard_map/dot_general | solution.py:35
  382.5 31.9 %fusion.7 = (bf16[2048,2048]{1,0:T(8,128)(2,1)}, bf16[2048,2048]{1,0:T(8,128)(2,1)}) fusion(bf16[2048,2048]{1,0:T(8,128)(2,1)} %get-tuple-element.61, bf16[2048,2048]{1,0:T(8,128)(2,1)} %get-tuple-element.60, bf16[2048,2048]{1,0:T(8,128)(2,1)} %get-tuple-element.59, bf16[2048,2048]{1,0:T(8,128)(2,1)} %refs_1_.3), kind=kOutput, calls=%fused_computation.10 | convolution fusion | flops 17242783744 | bytes 50331648 | tf_op jit(solution)/shard_map/dot_general | solution.py:27
  414.4 24.6 %fusion.74 = f32[2048,2048]{1,0:T(8,128)} fusion(bf16[2048,2048]{1,0:T(8,128)(2,1)} %get-tuple-element.147.refs_0_, bf16[2048,2048]{1,0:T(8,128)(2,1)} %refs_1_.2), kind=kOutput, calls=%fused_computation.186 | convolution fusion | flops 17179869184 | bytes 33554432 | tf_op jit(solution)/shard_map/dot_general | solution.py:31
  439.0 24.4 %add_convert_fusion.refs_3_.refs_4_ = bf16[2048,2048]{1,0:T(8,128)(2,1)} fusion(f32[2048,2048]{1,0:T(8,128)} %fusion.74, bf16[2048,2048]{1,0:T(8,128)(2,1)} %get-tuple-element.146.refs_1_, bf16[2048,2048]{1,0:T(8,128)(2,1)S(1)} %copy-done.57), kind=kOutput, calls=%fused_computation.11 | convolution fusion | flops 17188257792 | bytes 41943040 | tf_op jit(solution)/shard_map/dot_general | solution.py:31
  463.4 131.6 %products.3 = (bf16[2048,2048]{1,0:T(8,128)(2,1)}, bf16[2048,2048]{1,0:T(8,128)(2,1)}, f32[256,2048]{1,0:T(8,128)}, f32[256,2048]{1,0:T(8,128)}, bf16[2048,2048]{1,0:T(8,128)(2,1)}) custom-call(bf16[2048,2048]{1,0:T(8,128)(2,1)} %get-tuple-element.147.refs_0_, bf16[2048,2048]{1,0:T(8,128)(2,1)} %get-tuple-element.146.refs_1_, ...), custom_call_target="tpu_custom_call" | custom-call | flops 34359738368 | bytes 30000000 | tf_op jit(solution)/shard_map/products/pallas_call | solution.py:612
  603.5 116.2 %products.4 = (bf16[2048,2048]{1,0:T(8,128)(2,1)}, bf16[2048,2048]{1,0:T(8,128)(2,1)}, bf16[2048,2048]{1,0:T(8,128)(2,1)}) custom-call(bf16[2048,2048]{1,0:T(8,128)(2,1)} %get-tuple-element.58.refs_0_, bf16[2048,2048]{1,0:T(8,128)(2,1)} %refs_1_.3, bf16[512,2048]{1,0:T(8,128)(2,1)} %pad_maximum_fusion.3.refs_2_, bf16[2048,2048]{1,0:T(8,128)(2,1)} %get-tuple-element.64.refs_3_), custom_call_target="tpu_custom_call" | custom-call | flops 17179869184 | bytes 30000000 | tf_op jit(solution)/shard_map/products/pallas_call | solution.py:612
  719.7 5.7 fusion.40.refs_0_
  728.7 130.9 %attention_backward.1 = (bf16[2048,768]{1,0:T(8,128)(2,1)}, f32[256,2048]{1,0:T(8,128)}, f32[256,2048]{1,0:T(8,128)}, bf16[2048,2048]{1,0:T(8,128)(2,1)}) custom-call(bf16[1024,512]{1,0:T(8,128)(2,1)} %fusion.40.refs_0_, bf16[1024,512]{1,0:T(8,128)(2,1)} %copy-done.16, bf16[1024,256]{1,0:T(8,128)(2,1)} %copy-done.19, f32[1024,128]{1,0:T(8,128)} %copy-done.20, ...), custom_call_target="tpu_custom_call" | custom-call | flops 40000000000 | bytes 24000000 | tf_op jit(solution)/shard_map/attention_backward/pallas_call | solution.py:974
  863.6 9.2 convolution_convert_fusion
  872.8 23.0 %products.5.refs_0_ = bf16[1280,2048]{1,0:T(8,128)(2,1)} custom-call(bf16[1024,512]{1,0:T(8,128)(2,1)} %copy-done.11, bf16[1024,512]{1,0:T(8,128)(2,1)} %copy-done.13, bf16[2048,768]{1,0:T(8,128)(2,1)} %get-tuple-element.76.refs_2_, bf16[2048,2048]{1,0:T(8,128)(2,1)} %get-tuple-element.65.refs_3_, bf16[1024,2048]{1,0:T(8,128)(2,1)} %copy-done.34, ...), custom_call_target="tpu_custom_call" | custom-call | flops 10737418240 | bytes 30000000 | tf_op jit(solution)/shard_map/products/pallas_call | solution.py:612
  895.8 72.9 %transfer.7 = bf16[1280,2048]{1,0:T(8,128)(2,1)S(1)} custom-call(bf16[1280,2048]{1,0:T(8,128)(2,1)} %products.5.refs_0_), custom_call_target="tpu_custom_call" | custom-call | tf_op jit(solution)/shard_map/transfer/pallas_call | solution.py:521
  971.1 11.7 %convert_element_type.277 = f32[2048,2048]{1,0:T(8,128)} convert(bf16[2048,2048]{1,0:T(8,128)(2,1)} %get-tuple-element.79) | non-fusion elementwise | flops 4194304 | bytes 25165824 | tf_op jit(solution)/shard_map/convert_element_type | solution.py:1252
  990.0 5.3 fusion.31
  996.6 4.5 fusion.28
  1007.2 11.7 %convert_element_type.278 = f32[2048,2048]{1,0:T(8,128)} convert(bf16[2048,2048]{1,0:T(8,128)(2,1)} %get-tuple-element.84) | non-fusion elementwise | flops 4194304 | bytes 25165824 | tf_op jit(solution)/shard_map/convert_element_type | solution.py:1252
  1021.3 11.8 %convert_element_type.279 = f32[2048,2048]{1,0:T(8,128)} convert(bf16[2048,2048]{1,0:T(8,128)(2,1)} %get-tuple-element.87) | non-fusion elementwise | flops 4194304 | bytes 25165824 | tf_op jit(solution)/shard_map/convert_element_type | solution.py:1252
  (223 shorter events, 84.0 us)
Async XLA Ops:
  7.2 127.8 %copy-start = (bf16[512,2048]{1,0:T(8,128)(2,1)S(1)}, bf16[512,2048]{1,0:T(8,128)(2,1)}, u32[]{:S(2)}) copy-start(bf16[512,2048]{1,0:T(8,128)(2,1)} %param.18) | copy-start | bytes 6291460
  7.2 975.6 %reduce-scatter.2.cloned.1.call-start = ((), (), s32[]{:S(2)}) async-start(), calls=%async_computation.1 | async-start | bytes 10485760 | tf_op jit(solution)/shard_map/reduce_scatter | solution.py:1003
  8.1 45.2 %copy-start.56 = (s32[2,1,13]{2,1,0:T(1,128)S(1)}, s32[2,1,13]{2,1,0:T(1,128)}, u32[]{:S(2)}) copy-start(s32[2,1,13]{2,1,0:T(1,128)} %param.25) | copy-start | bytes 316
  55.4 69.9 %copy-start.44 = (f32[1,4,4,128]{3,1,2,0:T(4,128)}, f32[1,4,4,128]{3,1,2,0:T(4,128)S(1)}, u32[]{:S(2)}) copy-start(f32[1,4,4,128]{3,1,2,0:T(4,128)S(1)} %copy.40) | copy-start | bytes 24580
  60.4 13.1 %copy-start.7 = (bf16[1024,128]{1,0:T(8,128)(2,1)}, bf16[1024,128]{1,0:T(8,128)(2,1)S(1)}, u32[]{:S(2)}) copy-start(bf16[1024,128]{1,0:T(8,128)(2,1)S(1)} %pad.19.refs_5_.refs_7_) | copy-start | bytes 786436
  61.5 12.0 %copy-start.8 = (bf16[1024,128]{1,0:T(8,128)(2,1)}, bf16[1024,128]{1,0:T(8,128)(2,1)S(1)}, u32[]{:S(2)}) copy-start(bf16[1024,128]{1,0:T(8,128)(2,1)S(1)} %pad.18.refs_4_.refs_6_) | copy-start | bytes 786436
  65.1 61.3 %copy-start.40 = (bf16[768,2048]{1,0:T(8,128)(2,1)}, bf16[768,2048]{1,0:T(8,128)(2,1)S(1)}, u32[]{:S(2)}) copy-start(bf16[768,2048]{1,0:T(8,128)(2,1)S(1)} %constant_dynamic-update-slice_fusion) | copy-start | bytes 9437188
  73.5 50.2 %copy-start.5 = (f32[1024,128]{1,0:T(8,128)}, f32[1024,128]{1,0:T(8,128)S(1)}, u32[]{:S(2)}) copy-start(f32[1024,128]{1,0:T(8,128)S(1)} %get-tuple-element.188.refs_2_.refs_4_) | copy-start | bytes 1572868
  73.5 50.2 %copy-start.6 = (f32[1024,128]{1,0:T(8,128)}, f32[1024,128]{1,0:T(8,128)S(1)}, u32[]{:S(2)}) copy-start(f32[1024,128]{1,0:T(8,128)S(1)} %get-tuple-element.189.refs_3_.refs_5_) | copy-start | bytes 1572868
  179.3 34.1 %copy-start.26 = (bf16[2,1,256,2048]{3,2,1,0:T(8,128)(2,1)S(1)}, bf16[2,1,256,2048]{3,2,1,0:T(8,128)(2,1)}, u32[]{:S(2)}) copy-start(bf16[2,1,256,2048]{3,2,1,0:T(8,128)(2,1)} %param.13) | copy-start | bytes 6291460
  217.2 66.9 %copy-start.28 = (bf16[2,1,256,2048]{3,2,1,0:T(8,128)(2,1)S(1)}, bf16[2,1,256,2048]{3,2,1,0:T(8,128)(2,1)}, u32[]{:S(2)}) copy-start(bf16[2,1,256,2048]{3,2,1,0:T(8,128)(2,1)} %param.23) | copy-start | bytes 6291460
  414.4 24.6 %copy-start.57 = (bf16[2048,2048]{1,0:T(8,128)(2,1)S(1)}, bf16[2048,2048]{1,0:T(8,128)(2,1)}, u32[]{:S(2)}) copy-start(bf16[2048,2048]{1,0:T(8,128)(2,1)} %refs_2_.1) | copy-start | bytes 25165828
  463.4 131.6 %copy-start.22 = (f32[256,2048]{1,0:T(8,128)S(1)}, f32[256,2048]{1,0:T(8,128)}, u32[]{:S(2)}) copy-start(f32[256,2048]{1,0:T(8,128)} %copy-done.21) | copy-start | bytes 6291460
  463.4 131.6 %copy-start.47 = (f32[1,4,4,128]{3,1,2,0:T(4,128)S(1)}, f32[1,4,4,128]{3,1,2,0:T(4,128)}, u32[]{:S(2)}) copy-start(f32[1,4,4,128]{3,1,2,0:T(4,128)} %copy-done.46) | copy-start | bytes 24580
  463.4 131.6 %copy-start.49 = (f32[256]{0:T(256)S(1)}, f32[256]{0:T(256)}, u32[]{:S(2)}) copy-start(f32[256]{0:T(256)} %copy-done.48) | copy-start | bytes 3076
  463.4 131.6 %copy-start.51 = (f32[256]{0:T(256)S(1)}, f32[256]{0:T(256)}, u32[]{:S(2)}) copy-start(f32[256]{0:T(256)} %copy-done.50) | copy-start | bytes 3076
  986.4 19.2 %collective-permute-start = (f32[2,512]{1,0:T(2,128)S(1)}, f32[2,512]{1,0:T(2,128)S(1)}, u32[]{:S(2)}, u32[]{:S(2)}) collective-permute-start(f32[2,512]{1,0:T(2,128)S(1)} %bitcast.147), channel_id=1, source_target_pairs={{0,8},{8,0},{16,24},{24,16},{1,9},{9,1},{17,25},{25,17},{2,10},{10... | collective-permute-start | bytes 12296 | tf_op jit(solution)/shard_map/ppermute | solution.py:1044
  987.6 18.0 %collective-permute-start.1 = (f32[2,512]{1,0:T(2,128)S(1)}, f32[2,512]{1,0:T(2,128)S(1)}, u32[]{:S(2)}, u32[]{:S(2)}) collective-permute-start(f32[2,512]{1,0:T(2,128)S(1)} %bitcast.148), channel_id=1, source_target_pairs={{0,16},{8,24},{16,0},{24,8},{1,17},{9,25},{17,1},{25,9},{2,18},{10... | collective-permute-start | bytes 12296 | tf_op jit(solution)/shard_map/ppermute | solution.py:1044
  988.9 16.6 %collective-permute-start.2 = (f32[2,512]{1,0:T(2,128)S(1)}, f32[2,512]{1,0:T(2,128)S(1)}, u32[]{:S(2)}, u32[]{:S(2)}) collective-permute-start(f32[2,512]{1,0:T(2,128)S(1)} %bitcast.149), channel_id=1, source_target_pairs={{0,24},{8,16},{16,8},{24,0},{1,25},{9,17},{17,9},{25,1},{2,26},{10... | collective-permute-start | bytes 12296 | tf_op jit(solution)/shard_map/ppermute | solution.py:1044
  1005.6 13.3 %collective-permute-start.3 = (f32[2,512]{1,0:T(2,128)S(1)}, f32[2,512]{1,0:T(2,128)S(1)}, u32[]{:S(2)}, u32[]{:S(2)}) collective-permute-start(f32[2,512]{1,0:T(2,128)S(1)} %add_add_fusion), channel_id=1, source_target_pairs={{0,1},{1,0},{2,3},{3,2},{4,5},{5,4},{6,7},{7,6},{8,9},{9,8},{10,11... | collective-permute-start | bytes 12296 | tf_op jit(solution)/shard_map/ppermute | solution.py:1044
  1018.9 14.2 %collective-permute-start.4 = (f32[2,512]{1,0:T(2,128)S(1)}, f32[2,512]{1,0:T(2,128)S(1)}, u32[]{:S(2)}, u32[]{:S(2)}) collective-permute-start(f32[2,512]{1,0:T(2,128)S(1)} %add.234), channel_id=1, source_target_pairs={{0,2},{1,3},{2,0},{3,1},{4,6},{5,7},{6,4},{7,5},{8,10},{9,11},{10,... | collective-permute-start | bytes 12296 | tf_op jit(solution)/shard_map/ppermute | solution.py:1044
  1021.3 15.9 %copy-start.36 = (bf16[1,256,2048]{2,1,0:T(8,128)(2,1)S(1)}, bf16[1,256,2048]{2,1,0:T(8,128)(2,1)}, u32[]{:S(2)}) copy-start(bf16[1,256,2048]{2,1,0:T(8,128)(2,1)} %get-tuple-element.159) | copy-start | bytes 3145732
  1021.3 15.9 %copy-start.37 = (bf16[1,256,2048]{2,1,0:T(8,128)(2,1)S(1)}, bf16[1,256,2048]{2,1,0:T(8,128)(2,1)}, u32[]{:S(2)}) copy-start(bf16[1,256,2048]{2,1,0:T(8,128)(2,1)} %get-tuple-element.161) | copy-start | bytes 3145732
  1033.1 5.7 collective-permute-start.5
  (44 other events, 175.3 us)
Sparse Core Ops, SparseCore 0:
  872.9 86.8 reduce-scatter.1

commit v8 on v7

--- a/solution.py
+++ b/solution.py
@@ -140,40 +140,6 @@
             for copy in self.to_x[t] + self.to_y[t] + self.on_x[t] + self.on_y[t]:
                 copy.wait_send()
             self.local[t].wait()
-
-
-class SmallJob:
-    def __init__(self, own):
-        self.operand = own
-        self.rows, self.width = own.shape
-        self.out_shape = jax.ShapeDtypeStruct((4 * self.rows, self.width), own.dtype)
-        self.out_spec = pl.BlockSpec(memory_space=pl.ANY)
-
-    def scratch(self):
-        return [pltpu.SemaphoreType.DMA((2, 3)), pltpu.SemaphoreType.DMA(())]
-
-    def bind(self, operand, out, scratch, x, y):
-        sems, local = scratch
-        shard = lax.axis_index("shard")
-        mine = out.at[pl.ds(pl.multiple_of(shard * self.rows, self.rows), self.rows), :]
-        self.local = pltpu.make_async_copy(operand, mine, local)
-        self.sends = [
-            remote(operand, mine, sems, k, device)
-            for k, device in enumerate((x, y, (3 - shard, x[1])))
-        ]
-
-    def begin(self):
-        for send in self.sends:
-            send.start()
-        self.local.start()
-
-    def stages(self):
-        return []
-
-    def finish(self):
-        for send in self.sends:
-            send.wait()
-        self.local.wait()
 
 
 class SumJob:
@@ -260,11 +226,15 @@
 
 
 class LineJob:
-    def __init__(self, grad, rows, lag):
+    LINE_ROWS = 32
+    BATCH = 4
+    LAG = 2
+
+    def __init__(self, grad):
         self.operand = grad
-        self.LINE_ROWS, self.LAG = rows, lag
         self.half, self.width = grad.shape[0] // 2, grad.shape[1]
         self.chunks = self.half // self.LINE_ROWS
+        self.batches = self.chunks // self.BATCH
         self.steps = self.chunks + 1 + 3 * self.LAG
         self.out_shape = jax.ShapeDtypeStruct(grad.shape, BF16)
         self.out_spec = pl.BlockSpec(memory_space=pl.ANY)
@@ -287,10 +257,13 @@
     def chunk(self, c):
         return pl.ds(pl.multiple_of(c * self.LINE_ROWS, self.LINE_ROWS), self.LINE_ROWS)
 
-    def at(self, core, c):
-        return pl.ds(
-            pl.multiple_of(core * self.half + c * self.LINE_ROWS, self.LINE_ROWS), self.LINE_ROWS
-        )
+    def batch(self, b):
+        size = self.BATCH * self.LINE_ROWS
+        return pl.ds(pl.multiple_of(b * size, size), size)
+
+    def at(self, core, b):
+        size = self.BATCH * self.LINE_ROWS
+        return pl.ds(pl.multiple_of(core * self.half + b * size, size), size)
 
     def send(self, source, target, index, arrival, device, c):
         return pltpu.make_async_remote_copy(
@@ -302,13 +275,13 @@
             device_id_type=MESH,
         )
 
-    def to_twin(self, c):
-        source = self.grad.at[self.at(1 - self.core, c), :]
-        return self.send(source, self.from_core.at[self.chunk(c), :], 0, 1, self.twin, c)
-
-    def load(self, c):
-        source = self.grad.at[self.at(self.core, c), :]
-        return pltpu.make_async_copy(source, self.own.at[self.chunk(c), :], self.sems.at[2, c])
+    def to_twin(self, b):
+        source = self.grad.at[self.at(1 - self.core, b), :]
+        return self.send(source, self.from_core.at[self.batch(b), :], 0, 1, self.twin, b)
+
+    def load(self, b):
+        source = self.grad.at[self.at(self.core, b), :]
+        return pltpu.make_async_copy(source, self.own.at[self.batch(b), :], self.sems.at[2, b])
 
     def inward(self, c):
         rows = self.chunk(c)
@@ -322,13 +295,19 @@
         rows = self.chunk(c)
         return self.send(self.from_core.at[rows, :], self.from_line.at[rows, :], 6, 4, self.pair, c)
 
-    def store(self, source, c):
-        target = self.out.at[self.at(self.core, c), :]
-        return pltpu.make_async_copy(source.at[self.chunk(c), :], target, self.sems.at[2, c])
-
-    def give(self, source, c):
-        target = self.out.at[self.at(self.core, c), :]
-        return self.send(source.at[self.chunk(c), :], target, 7, 8, self.twin, c)
+    def store(self, source, b):
+        target = self.out.at[self.at(self.core, b), :]
+        return pltpu.make_async_copy(source.at[self.batch(b), :], target, self.sems.at[2, b])
+
+    def give(self, source, b):
+        target = self.out.at[self.at(self.core, b), :]
+        return self.send(source.at[self.batch(b), :], target, 7, 8, self.twin, b)
+
+    def hand_out(self, source, c):
+        @pl.when(c % self.BATCH == self.BATCH - 1)
+        def _():
+            self.store(source, c // self.BATCH).start()
+            self.give(source, c // self.BATCH).start()
 
     def begin(self):
         pass
@@ -341,17 +320,21 @@
         live = lambda begin: (s >= begin) & (s < n + begin)
         add = lambda a, b: (a.astype(F32) + b.astype(F32)).astype(BF16)
 
-        @pl.when(live(0))
+        @pl.when(live(0) & (s % self.BATCH == 0))
         def _():
-            self.to_twin(s).start()
-            self.load(s).start()
+            self.to_twin(s // self.BATCH).start()
+            self.load(s // self.BATCH).start()
 
         @pl.when(live(1))
         def _():
             c = s - 1
             rows = self.chunk(c)
-            self.to_twin(c).wait()
-            self.load(c).wait()
+
+            @pl.when(c % self.BATCH == 0)
+            def _():
+                self.to_twin(c // self.BATCH).wait()
+                self.load(c // self.BATCH).wait()
+
             self.own[rows, :] = add(self.own[rows, :], self.from_core[rows, :])
             pl.when(self.outer)(lambda: self.inward(c).start())
 
@@ -370,21 +353,21 @@
             self.between(c).wait_recv()
             self.from_core[rows, :] = add(self.own[rows, :], self.from_inner[rows, :])
             self.outward(c).start()
-            self.store(self.from_core, c).start()
-            self.give(self.from_core, c).start()
+            self.hand_out(self.from_core, c)
 
         @pl.when(live(1 + 3 * lag) & self.outer)
         def _():
             c = s - 1 - 3 * lag
             self.outward(c).wait_recv()
-            self.store(self.from_line, c).start()
-            self.give(self.from_line, c).start()
+            self.hand_out(self.from_line, c)
 
     def finish(self):
+        def inside(b, carry):
+            self.store(self.from_line, b).wait()
+            self.give(self.from_line, b).wait()
+            return carry
+
         def body(c, carry):
-            self.store(self.from_line, c).wait()
-            self.give(self.from_line, c).wait()
-
             @pl.when(self.inner)
             def _():
                 self.between(c).wait_send()
@@ -393,6 +376,7 @@
             pl.when(self.outer)(lambda: self.inward(c).wait_send())
             return carry
 
+        lax.fori_loop(0, self.batches, inside, 0)
         lax.fori_loop(0, self.chunks, body, 0)
 
 
@@ -426,8 +410,6 @@
                 pl.semaphore_signal(barrier, inc=1, device_id=device, device_id_type=MESH)
 
             near = ([x, y] if square else []) + ([lines[0].twin, lines[0].pair] if lines else [])
-            if any(isinstance(job, SmallJob) for job in self.jobs):
-                near.append((3 - shard, replica))
             for device in near:
                 greet(device)
             if lines:
@@ -999,12 +981,6 @@
     return lax.optimization_barrier(values)
 
 
-def sum_beside(part, trees):
-    return lax.psum_scatter(
-        part.reshape(trees, -1, part.shape[1]), "shard", scatter_dimension=1, tiled=True
-    )
-
-
 class Square:
     def __init__(self, shard, replica):
         self.shard, self.replica = shard, replica
@@ -1012,10 +988,6 @@
         self.y = [(i, i ^ 2) for i in range(shard)]
         self.d = [(i, i ^ 3) for i in range(shard)]
 
-    def natural(self, rows, trees):
-        blocks = rows.reshape(trees, self.shard, -1, rows.shape[1])
-        return self.reorder(blocks, 1).reshape(rows.shape)
-
     def place(self, block):
         shard = lax.axis_index("shard")
         return (block + shard) % 2 + 2 * ((block // 2 + shard // 2) % 2)
@@ -1026,11 +998,14 @@
             [lax.dynamic_slice_in_dim(blocks, n ^ me, 1, axis) for n in range(self.shard)], axis=axis
         )
 
-    def first(self, small, own):
-        padded = jnp.pad(small, (0, -small.shape[0] % 2048)).reshape(16, -1)
-        self.kernels += 1
-        smalls, rows = transfer(Comm([SmallJob(padded), GatherJob(own, 1)], self.kernels))
-        return smalls.reshape(self.shard, -1)[:, : small.shape[0]], rows
+    def gather_small(self, own):
+        parts = [
+            own,
+            lax.ppermute(own, "shard", self.x),
+            lax.ppermute(own, "shard", self.y),
+            lax.ppermute(own, "shard", self.d),
+        ]
+        return self.reorder(jnp.stack(parts), 0)
 
     def sum_small(self, values, beside):
         share = values.shape[1] // self.shard
@@ -1048,11 +1023,11 @@
                 done.append(beside[number](total))
                 got, done[-1] = sync(got, done[-1])
             total = total + sum(got)
-        return total, done + [f(total) for f in beside[len(hops) :]]
+        return total, done
 
     def carry(self, compute, gathers=(), sums=(), totals=()):
         jobs = [GatherJob(*own) for own in gathers] + [SumJob(*part) for part in sums]
-        jobs += [LineJob(grad, *((32, 2) if compute is None else (64, 1))) for grad in totals]
+        jobs += [LineJob(grad) for grad in totals]
         self.kernels += 1
         comm = Comm(jobs, self.kernels)
         if compute is None:
@@ -1072,12 +1047,8 @@
     def place(self, block):
         return block
 
-    def natural(self, rows, trees):
-        return rows
-
-    def first(self, small, own):
-        rows = lax.all_gather(own, "shard", axis=0, tiled=True)
-        return lax.all_gather(small, "shard", axis=0, tiled=False), rows
+    def gather_small(self, own):
+        return lax.all_gather(own, "shard", axis=0, tiled=False)
 
     def carry(self, compute, gathers=(), sums=(), totals=()):
         results = None if compute is None else compute(NoComm())[0]
@@ -1147,7 +1118,8 @@
     small = jnp.concatenate(
         [gain_attn, gain_ff] + [segment_ids[t, 0].astype(BF16) for t in range(trees)]
     )
-    smalls, rows_0 = links.first(small, token_rows[0])
+    smalls = links.gather_small(small)
+    _, (rows_0,), _, _ = links.carry(None, gathers=[(token_rows[0], 1)])
     gain_first = smalls[:, :share].reshape(width).astype(F32)
     gain_second = smalls[:, share : 2 * share].reshape(width).astype(F32)
     masks, tables = [], []
@@ -1225,8 +1197,7 @@
     results = [
         (middle + RESIDUAL * down).astype(BF16) for middle, down in zip((middle_0, middle_1), downs)
     ]
-    normed_part = dot_nn(links.natural(qkv_grad, trees), w_qkv).astype(BF16)
-    normed_sums = sum_beside(normed_part, trees)
+    normed_part = dot_nn(qkv_grad, w_qkv).astype(BF16)
     (grad_attn,), _ = products(
         [
             ((saved_0[0], saved_1[0]), out_all, True),
@@ -1236,9 +1207,9 @@
         NoComm(),
         joined=True,
     )
-    _, _, _, (total_attn,) = links.carry(None, totals=[grad_attn])
-    normed_sums, total_attn = sync(normed_sums, total_attn)
-    normed_grads = [normed_sums[t].astype(F32) for t in range(trees)]
+    _, _, normed_grads, (total_attn,) = links.carry(
+        None, sums=parts(normed_part), totals=[grad_attn]
+    )
     input_grads = []
     gain_attn_sum = jnp.zeros((width,), F32)
     for t in range(trees):

time: 1050 us -> 1020 us (0.971)
  Pallas kernels: 773 us -> 743 us
  between operations: 15.5 us -> 1.83 us
    pallas_call x3, Pallas kernels: 271 us -> 257 us  [products(): pl.pallas_call(kernel, grid=(total,), in_specs=specs + right_specs + list...]
    pallas_call x1, Pallas kernels: 131 us -> 120 us  [attention_backward(): pl.pallas_call(functools.partial(attention_backward_kernel, kv_heads, blo...]
  transfers between devices with their start and end apart: 7 -> 9, of which waited for: 1 -> 1; matrix products, arithmetic and copies ran while one was open for 5% -> 6% of each run, Pallas kernels for 9% -> 4%
where the time goes in v8:
time: 1020 us; the launch traced here: 1010 us
  Pallas kernels  743 us (73%)
  matrix products  147 us (14%)
  other arithmetic  85 us (8%)
  local copies, waits for them, and re-layouts  19 us (2%)
  starting transfers between devices  11.5 us (1%)
    pallas_call x3, Pallas kernels, products(): pl.pallas_call(kernel, grid=(total,), in_specs=specs + right_specs + list...  257 us
    pallas_call x4, Pallas kernels, transfer(): pl.pallas_call(kernel, grid=(steps,), in_specs=comm.in_specs, out_specs=c...  211 us
    pallas_call x1, Pallas kernels, attention_backward(): pl.pallas_call(functools.partial(attention_backward_kernel, kv_heads, blo...  120 us
    pallas_call x2, Pallas kernels, attention_forward(): pl.pallas_call(functools.partial(attention_forward_kernel, kv_heads, bloc...  83.2 us
    pallas_call x1, Pallas kernels, feed_forward(): pl.pallas_call(kernel, grid=(steps,), in_specs=[pl.BlockSpec((rows, width...  71.4 us
    dot_general x7, matrix products, dot_nn(): lax.dot_general(left, right, (((1,), (0,)), ((), ())), preferred_element_...  67.8 us
    dot_general x5, matrix products, dot_nt(): lax.dot_general(left, right, (((1,), (1,)), ((), ())), preferred_element_...  54.7 us
    convert_element_type x3, other arithmetic, convert(): return lambda after: sync(totals[index], after)[0].astype(F32)  35.2 us
  transfers between devices with their start and end apart: 9, of which 1 were waited for; matrix products, arithmetic and copies ran while one was open for 6% of the time, Pallas kernels for 4%

profile of v8, /device:TPU:0, one launch (start us, length us, event | category | flops | bytes accessed | tf_op | source)
XLA Modules:
  0.0 1006.7 jit_solution(4537403712023974453)
XLA Ops:
  13.3 36.9 %transfer.4 = bf16[1024,2048]{1,0:T(8,128)(2,1)S(1)} custom-call(bf16[256,2048]{1,0:T(8,128)(2,1)S(1)} %get-tuple-element.165.refs_0_), custom_call_target="tpu_custom_call" | custom-call | tf_op jit(solution)/shard_map/transfer/pallas_call | solution.py:503
  67.6 6.9 fusion.64.refs_0_.refs_1_
  78.4 48.4 %attention_forward.2 = (bf16[1024,512]{1,0:T(8,128)(2,1)S(1)}, bf16[1024,512]{1,0:T(8,128)(2,1)S(1)}, bf16[1024,256]{1,0:T(8,128)(2,1)S(1)}, f32[1024,128]{1,0:T(8,128)S(1)}, bf16[1024,2048]{1,0:T(8,128)(2,1)S(1)}) custom-call(f32[1024,768]{1,0:T(8,128)S(1)} %fusion.64.refs_0_.refs_1_, f32[1024,768]{1,0:T(8,128)S(1)} %fusion.64.refs_0_.refs_1_, ...), custom_call_target="tpu_custom_call" | custom-call | flops 10000000000 | bytes 12000000 | tf_op jit(solution)/shard_map/attention_forward/pallas_call | solution.py:770
  129.1 6.9 fusion.65.refs_0_.refs_1_
  138.5 34.8 %attention_forward.3 = (bf16[1024,512]{1,0:T(8,128)(2,1)S(1)}, bf16[1024,512]{1,0:T(8,128)(2,1)S(1)}, bf16[1024,256]{1,0:T(8,128)(2,1)S(1)}, f32[1024,128]{1,0:T(8,128)S(1)}, f32[256,2048]{1,0:T(8,128)S(1)}) custom-call(f32[1024,768]{1,0:T(8,128)S(1)} %fusion.65.refs_0_.refs_1_, f32[1024,768]{1,0:T(8,128)S(1)} %fusion.65.refs_0_.refs_1_, ...), custom_call_target="tpu_custom_call" | custom-call | flops 10000000000 | bytes 12000000 | tf_op jit(solution)/shard_map/attention_forward/pallas_call | solution.py:770
  178.7 33.2 %transfer.5 = f32[256,2048]{1,0:T(8,128)S(1)} custom-call(bf16[1024,2048]{1,0:T(8,128)(2,1)} %convolution_convert_fusion.2.refs_0_), custom_call_target="tpu_custom_call" | custom-call | tf_op jit(solution)/shard_map/transfer/pallas_call | solution.py:503
  215.7 65.9 %transfer.6.refs_0_.refs_2_ = bf16[2048,2048]{1,0:T(8,128)(2,1)} custom-call(bf16[512,2048]{1,0:T(8,128)(2,1)S(1)} %pad_maximum_fusion.refs_0_), custom_call_target="tpu_custom_call" | custom-call | tf_op jit(solution)/shard_map/transfer/pallas_call | solution.py:503
  281.6 71.4 %feed_forward.1 = (bf16[2048,2048]{1,0:T(8,128)(2,1)}, bf16[2048,2048]{1,0:T(8,128)(2,1)}, bf16[2048,2048]{1,0:T(8,128)(2,1)}, bf16[2048,2048]{1,0:T(8,128)(2,1)}) custom-call(bf16[2048,2048]{1,0:T(8,128)(2,1)} %transfer.6.refs_0_.refs_2_, bf16[2048,2048]{1,0:T(8,128)(2,1)} %refs_1_.2, bf16[2048,2048]{1,0:T(8,128)(2,1)} %refs_2_.1, ...), custom_call_target="tpu_custom_call" | custom-call | flops 34359738368 | bytes 48000000 | tf_op jit(solution)/shard_map/feed_forward/pallas_call | solution.py:632
  353.1 24.0 %convolution_convert_fusion.1.refs_5_ = bf16[2048,2048]{1,0:T(8,128)(2,1)} fusion(bf16[2048,2048]{1,0:T(8,128)(2,1)} %get-tuple-element.55.refs_0_, bf16[2048,2048]{1,0:T(8,128)(2,1)} %get-tuple-element.56), kind=kOutput, calls=%fused_computation.23 | convolution fusion | flops 17184063488 | bytes 25165824 | tf_op jit(solution)/shard_map/dot_general | solution.py:35
  377.0 31.9 %fusion.7 = (bf16[2048,2048]{1,0:T(8,128)(2,1)}, bf16[2048,2048]{1,0:T(8,128)(2,1)}) fusion(bf16[2048,2048]{1,0:T(8,128)(2,1)} %get-tuple-element.58, bf16[2048,2048]{1,0:T(8,128)(2,1)} %get-tuple-element.57, bf16[2048,2048]{1,0:T(8,128)(2,1)} %get-tuple-element.56, bf16[2048,2048]{1,0:T(8,128)(2,1)} %refs_1_.3), kind=kOutput, calls=%fused_computation.10 | convolution fusion | flops 17242783744 | bytes 50331648 | tf_op jit(solution)/shard_map/dot_general | solution.py:27
  408.9 24.8 %fusion.66 = f32[2048,2048]{1,0:T(8,128)} fusion(bf16[2048,2048]{1,0:T(8,128)(2,1)} %get-tuple-element.147.refs_0_, bf16[2048,2048]{1,0:T(8,128)(2,1)} %refs_1_.2), kind=kOutput, calls=%fused_computation.177 | convolution fusion | flops 17179869184 | bytes 33554432 | tf_op jit(solution)/shard_map/dot_general | solution.py:31
  433.6 24.4 %add_convert_fusion.refs_3_.refs_4_ = bf16[2048,2048]{1,0:T(8,128)(2,1)} fusion(f32[2048,2048]{1,0:T(8,128)} %fusion.66, bf16[2048,2048]{1,0:T(8,128)(2,1)} %get-tuple-element.146.refs_1_, bf16[2048,2048]{1,0:T(8,128)(2,1)S(1)} %copy-done.52), kind=kOutput, calls=%fused_computation.11 | convolution fusion | flops 17188257792 | bytes 41943040 | tf_op jit(solution)/shard_map/dot_general | solution.py:31
  458.1 118.5 %products.3 = (bf16[2048,2048]{1,0:T(8,128)(2,1)}, bf16[2048,2048]{1,0:T(8,128)(2,1)}, f32[256,2048]{1,0:T(8,128)}, f32[256,2048]{1,0:T(8,128)}, bf16[2048,2048]{1,0:T(8,128)(2,1)}) custom-call(bf16[2048,2048]{1,0:T(8,128)(2,1)} %get-tuple-element.147.refs_0_, bf16[2048,2048]{1,0:T(8,128)(2,1)} %get-tuple-element.146.refs_1_, ...), custom_call_target="tpu_custom_call" | custom-call | flops 34359738368 | bytes 30000000 | tf_op jit(solution)/shard_map/products/pallas_call | solution.py:594
  585.1 115.3 %products.4 = (bf16[2048,2048]{1,0:T(8,128)(2,1)}, bf16[2048,2048]{1,0:T(8,128)(2,1)}, bf16[2048,2048]{1,0:T(8,128)(2,1)}) custom-call(bf16[2048,2048]{1,0:T(8,128)(2,1)} %get-tuple-element.55.refs_0_, bf16[2048,2048]{1,0:T(8,128)(2,1)} %refs_1_.3, bf16[512,2048]{1,0:T(8,128)(2,1)} %pad_maximum_fusion.2.refs_2_, bf16[2048,2048]{1,0:T(8,128)(2,1)} %get-tuple-element.61.refs_3_), custom_call_target="tpu_custom_call" | custom-call | flops 17179869184 | bytes 30000000 | tf_op jit(solution)/shard_map/products/pallas_call | solution.py:594
  700.4 5.7 fusion.43.refs_8_
  709.4 120.0 %attention_backward.1 = (bf16[2048,768]{1,0:T(8,128)(2,1)}, f32[256,2048]{1,0:T(8,128)}, f32[256,2048]{1,0:T(8,128)}, bf16[2048,2048]{1,0:T(8,128)(2,1)}) custom-call(bf16[1024,512]{1,0:T(8,128)(2,1)} %fusion.40.refs_0_, bf16[1024,512]{1,0:T(8,128)(2,1)} %copy-done.16, bf16[1024,256]{1,0:T(8,128)(2,1)} %copy-done.19, f32[1024,128]{1,0:T(8,128)} %copy-done.20, ...), custom_call_target="tpu_custom_call" | custom-call | flops 40000000000 | bytes 24000000 | tf_op jit(solution)/shard_map/attention_backward/pallas_call | solution.py:956
  829.4 23.0 %products.5.refs_2_ = bf16[1280,2048]{1,0:T(8,128)(2,1)} custom-call(bf16[1024,512]{1,0:T(8,128)(2,1)} %copy-done.13, bf16[1024,512]{1,0:T(8,128)(2,1)} %copy-done.14, bf16[2048,768]{1,0:T(8,128)(2,1)} %get-tuple-element.73.refs_2_, bf16[2048,2048]{1,0:T(8,128)(2,1)} %get-tuple-element.62.refs_3_, bf16[1024,2048]{1,0:T(8,128)(2,1)} %copy-done.35, ...), custom_call_target="tpu_custom_call" | custom-call | flops 10737418240 | bytes 30000000 | tf_op jit(solution)/shard_map/products/pallas_call | solution.py:594
  852.4 11.3 %convolution_convert_fusion.refs_0_.refs_1_ = bf16[2048,2048]{1,0:T(8,128)(2,1)} fusion(bf16[2048,768]{1,0:T(8,128)(2,1)} %get-tuple-element.73.refs_2_, bf16[768,2048]{1,0:T(8,128)(2,1)} %constant_dynamic-update-slice_fusion), kind=kOutput, calls=%fused_computation.22 | convolution fusion | flops 6446645248 | bytes 14680064 | tf_op jit(solution)/shard_map/dot_general | solution.py:31
  863.8 75.4 %transfer.7 = (f32[256,2048]{1,0:T(8,128)S(1)}, f32[256,2048]{1,0:T(8,128)S(1)}, bf16[1280,2048]{1,0:T(8,128)(2,1)}) custom-call(bf16[2048,2048]{1,0:T(8,128)(2,1)} %convolution_convert_fusion.refs_0_.refs_1_, bf16[2048,2048]{1,0:T(8,128)(2,1)} %convolution_convert_fusion.refs_0_.refs_1_, bf16[1280,2048]{1,0:T(8,128)(2,1)} %products.5.refs_2_), custom_call_target="tpu_custom_call" | custom-call | tf_op jit(solution)/shard_map/transfer/pallas_call | solution.py:503
  944.8 5.6 fusion.36
  956.3 4.4 slice_convert_fusion
  960.7 11.7 %convert_element_type.259 = f32[2048,2048]{1,0:T(8,128)} convert(bf16[2048,2048]{1,0:T(8,128)(2,1)} %get-tuple-element.77) | non-fusion elementwise | flops 4194304 | bytes 25165824 | tf_op jit(solution)/shard_map/convert_element_type | solution.py:1223
  975.3 11.7 %convert_element_type.260 = f32[2048,2048]{1,0:T(8,128)} convert(bf16[2048,2048]{1,0:T(8,128)(2,1)} %get-tuple-element.82) | non-fusion elementwise | flops 4194304 | bytes 25165824 | tf_op jit(solution)/shard_map/convert_element_type | solution.py:1223
  989.3 11.8 %convert_element_type.261 = f32[2048,2048]{1,0:T(8,128)} convert(bf16[2048,2048]{1,0:T(8,128)(2,1)} %get-tuple-element.85) | non-fusion elementwise | flops 4194304 | bytes 25165824 | tf_op jit(solution)/shard_map/convert_element_type | solution.py:1223
  (221 shorter events, 81.1 us)
Async XLA Ops:
  0.6 135.5 %copy-start = (bf16[512,2048]{1,0:T(8,128)(2,1)S(1)}, bf16[512,2048]{1,0:T(8,128)(2,1)}, u32[]{:S(2)}) copy-start(bf16[512,2048]{1,0:T(8,128)(2,1)} %param.18) | copy-start | bytes 6291460
  2.2 53.4 %collective-permute-start.2 = (bf16[1536]{0:T(1024)(128)(2,1)S(1)}, bf16[1536]{0:T(1024)(128)(2,1)S(1)}, u32[]{:S(2)}, u32[]{:S(2)}) collective-permute-start(bf16[1536]{0:T(1024)(128)(2,1)S(1)} %pad_maximum_fusion.5), channel_id=1, source_target_pairs={{0,24},{8,16},{16,8},{24,0},{1,25},{9,17},{17,9},{25,1},{2,26},{10... | collective-permute-start | bytes 9224 | tf_op jit(solution)/shard_map/ppermute | solution.py:1006
  6.2 49.4 %collective-permute-start.1 = (bf16[1536]{0:T(1024)(128)(2,1)S(1)}, bf16[1536]{0:T(1024)(128)(2,1)S(1)}, u32[]{:S(2)}, u32[]{:S(2)}) collective-permute-start(bf16[1536]{0:T(1024)(128)(2,1)S(1)} %pad_maximum_fusion.5), channel_id=1, source_target_pairs={{0,16},{8,24},{16,0},{24,8},{1,17},{9,25},{17,1},{25,9},{2,18},{10... | collective-permute-start | bytes 9224 | tf_op jit(solution)/shard_map/ppermute | solution.py:1005
  6.7 49.0 %collective-permute-start = (bf16[1536]{0:T(1024)(128)(2,1)S(1)}, bf16[1536]{0:T(1024)(128)(2,1)S(1)}, u32[]{:S(2)}, u32[]{:S(2)}) collective-permute-start(bf16[1536]{0:T(1024)(128)(2,1)S(1)} %pad_maximum_fusion.5), channel_id=1, source_target_pairs={{0,8},{8,0},{16,24},{24,16},{1,9},{9,1},{17,25},{25,17},{2,10},{10... | collective-permute-start | bytes 9224 | tf_op jit(solution)/shard_map/ppermute | solution.py:1004
  58.1 155.4 %copy-start.42 = (f32[1,4,4,128]{3,1,2,0:T(4,128)}, f32[1,4,4,128]{3,1,2,0:T(4,128)S(1)}, u32[]{:S(2)}) copy-start(f32[1,4,4,128]{3,1,2,0:T(4,128)S(1)} %copy.43) | copy-start | bytes 24580
  58.1 70.0 %copy-start.44 = (f32[1,4,4,128]{3,1,2,0:T(4,128)}, f32[1,4,4,128]{3,1,2,0:T(4,128)S(1)}, u32[]{:S(2)}) copy-start(f32[1,4,4,128]{3,1,2,0:T(4,128)S(1)} %copy.40) | copy-start | bytes 24580
  61.0 77.5 %copy-start.9 = (bf16[1024,128]{1,0:T(8,128)(2,1)}, bf16[1024,128]{1,0:T(8,128)(2,1)S(1)}, u32[]{:S(2)}) copy-start(bf16[1024,128]{1,0:T(8,128)(2,1)S(1)} %pad.16.refs_5_.refs_15_) | copy-start | bytes 786436
  63.2 75.3 %copy-start.11 = (bf16[1024,128]{1,0:T(8,128)(2,1)}, bf16[1024,128]{1,0:T(8,128)(2,1)S(1)}, u32[]{:S(2)}) copy-start(bf16[1024,128]{1,0:T(8,128)(2,1)S(1)} %pad.15.refs_4_.refs_14_) | copy-start | bytes 786436
  78.3 48.5 %copy-start.7 = (f32[1024,128]{1,0:T(8,128)}, f32[1024,128]{1,0:T(8,128)S(1)}, u32[]{:S(2)}) copy-start(f32[1024,128]{1,0:T(8,128)S(1)} %get-tuple-element.186.refs_2_.refs_4_) | copy-start | bytes 1572868
  78.3 48.5 %copy-start.8 = (f32[1024,128]{1,0:T(8,128)}, f32[1024,128]{1,0:T(8,128)S(1)}, u32[]{:S(2)}) copy-start(f32[1024,128]{1,0:T(8,128)S(1)} %get-tuple-element.187.refs_3_.refs_5_) | copy-start | bytes 1572868
  78.3 60.2 %copy-start.5 = (f32[1024,128]{1,0:T(8,128)}, f32[1024,128]{1,0:T(8,128)S(1)}, u32[]{:S(2)}) copy-start(f32[1024,128]{1,0:T(8,128)S(1)} %get-tuple-element.180.refs_3_.refs_13_) | copy-start | bytes 1572868
  78.3 60.2 %copy-start.6 = (f32[1024,128]{1,0:T(8,128)}, f32[1024,128]{1,0:T(8,128)S(1)}, u32[]{:S(2)}) copy-start(f32[1024,128]{1,0:T(8,128)S(1)} %get-tuple-element.181.refs_2_.refs_12_) | copy-start | bytes 1572868
  458.0 118.5 %copy-start.22 = (f32[256,2048]{1,0:T(8,128)S(1)}, f32[256,2048]{1,0:T(8,128)}, u32[]{:S(2)}) copy-start(f32[256,2048]{1,0:T(8,128)} %copy-done.21) | copy-start | bytes 6291460
  458.0 118.5 %copy-start.43 = (f32[1,4,4,128]{3,1,2,0:T(4,128)S(1)}, f32[1,4,4,128]{3,1,2,0:T(4,128)}, u32[]{:S(2)}) copy-start(f32[1,4,4,128]{3,1,2,0:T(4,128)} %copy-done.42) | copy-start | bytes 24580
  458.1 118.5 %copy-start.47 = (f32[256]{0:T(256)S(1)}, f32[256]{0:T(256)}, u32[]{:S(2)}) copy-start(f32[256]{0:T(256)} %copy-done.46) | copy-start | bytes 3076
  458.1 118.5 %copy-start.49 = (f32[256]{0:T(256)S(1)}, f32[256]{0:T(256)}, u32[]{:S(2)}) copy-start(f32[256]{0:T(256)} %copy-done.48) | copy-start | bytes 3076
  863.7 75.4 %copy-start.28 = (bf16[2,1,256,2048]{3,2,1,0:T(8,128)(2,1)S(1)}, bf16[2,1,256,2048]{3,2,1,0:T(8,128)(2,1)}, u32[]{:S(2)}) copy-start(bf16[2,1,256,2048]{3,2,1,0:T(8,128)(2,1)} %param.13) | copy-start | bytes 6291460
  863.7 75.4 %copy-start.45 = (f32[1,4,4,128]{3,1,2,0:T(4,128)S(1)}, f32[1,4,4,128]{3,1,2,0:T(4,128)}, u32[]{:S(2)}) copy-start(f32[1,4,4,128]{3,1,2,0:T(4,128)} %copy-done.44) | copy-start | bytes 24580
  941.2 31.1 %collective-permute-start.3 = (f32[2,512]{1,0:T(2,128)S(1)}, f32[2,512]{1,0:T(2,128)S(1)}, u32[]{:S(2)}, u32[]{:S(2)}) collective-permute-start(f32[2,512]{1,0:T(2,128)S(1)} %bitcast.131), channel_id=1, source_target_pairs={{0,8},{8,0},{16,24},{24,16},{1,9},{9,1},{17,25},{25,17},{2,10},{10... | collective-permute-start | bytes 12296 | tf_op jit(solution)/shard_map/ppermute | solution.py:1019
  942.7 29.7 %collective-permute-start.4 = (f32[2,512]{1,0:T(2,128)S(1)}, f32[2,512]{1,0:T(2,128)S(1)}, u32[]{:S(2)}, u32[]{:S(2)}) collective-permute-start(f32[2,512]{1,0:T(2,128)S(1)} %bitcast.130), channel_id=1, source_target_pairs={{0,16},{8,24},{16,0},{24,8},{1,17},{9,25},{17,1},{25,9},{2,18},{10... | collective-permute-start | bytes 12296 | tf_op jit(solution)/shard_map/ppermute | solution.py:1019
  943.4 29.0 %collective-permute-start.5 = (f32[2,512]{1,0:T(2,128)S(1)}, f32[2,512]{1,0:T(2,128)S(1)}, u32[]{:S(2)}, u32[]{:S(2)}) collective-permute-start(f32[2,512]{1,0:T(2,128)S(1)} %bitcast.129), channel_id=1, source_target_pairs={{0,24},{8,16},{16,8},{24,0},{1,25},{9,17},{17,9},{25,1},{2,26},{10... | collective-permute-start | bytes 12296 | tf_op jit(solution)/shard_map/ppermute | solution.py:1019
  972.4 14.5 %collective-permute-start.6 = (f32[2,512]{1,0:T(2,128)S(1)}, f32[2,512]{1,0:T(2,128)S(1)}, u32[]{:S(2)}, u32[]{:S(2)}) collective-permute-start(f32[2,512]{1,0:T(2,128)S(1)} %add_add_fusion), channel_id=1, source_target_pairs={{0,1},{1,0},{2,3},{3,2},{4,5},{5,4},{6,7},{7,6},{8,9},{9,8},{10,11... | collective-permute-start | bytes 12296 | tf_op jit(solution)/shard_map/ppermute | solution.py:1019
  986.9 14.2 %collective-permute-start.7 = (f32[2,512]{1,0:T(2,128)S(1)}, f32[2,512]{1,0:T(2,128)S(1)}, u32[]{:S(2)}, u32[]{:S(2)}) collective-permute-start(f32[2,512]{1,0:T(2,128)S(1)} %add.230), channel_id=1, source_target_pairs={{0,2},{1,3},{2,0},{3,1},{4,6},{5,7},{6,4},{7,5},{8,10},{9,11},{10,... | collective-permute-start | bytes 12296 | tf_op jit(solution)/shard_map/ppermute | solution.py:1019
  1001.1 4.8 collective-permute-start.8
  (41 other events, 273.3 us)

commit v9 on v8

--- a/solution.py
+++ b/solution.py
@@ -140,6 +140,40 @@
             for copy in self.to_x[t] + self.to_y[t] + self.on_x[t] + self.on_y[t]:
                 copy.wait_send()
             self.local[t].wait()
+
+
+class SmallJob:
+    def __init__(self, own):
+        self.operand = own
+        self.rows, self.width = own.shape
+        self.out_shape = jax.ShapeDtypeStruct((4 * self.rows, self.width), own.dtype)
+        self.out_spec = pl.BlockSpec(memory_space=pl.ANY)
+
+    def scratch(self):
+        return [pltpu.SemaphoreType.DMA((2, 3)), pltpu.SemaphoreType.DMA(())]
+
+    def bind(self, operand, out, scratch, x, y):
+        sems, local = scratch
+        shard = lax.axis_index("shard")
+        mine = out.at[pl.ds(pl.multiple_of(shard * self.rows, self.rows), self.rows), :]
+        self.local = pltpu.make_async_copy(operand, mine, local)
+        self.sends = [
+            remote(operand, mine, sems, k, device)
+            for k, device in enumerate((x, y, (3 - shard, x[1])))
+        ]
+
+    def begin(self):
+        for send in self.sends:
+            send.start()
+        self.local.start()
+
+    def stages(self):
+        return []
+
+    def finish(self):
+        for send in self.sends:
+            send.wait()
+        self.local.wait()
 
 
 class SumJob:
@@ -410,6 +444,8 @@
                 pl.semaphore_signal(barrier, inc=1, device_id=device, device_id_type=MESH)
 
             near = ([x, y] if square else []) + ([lines[0].twin, lines[0].pair] if lines else [])
+            if any(isinstance(job, SmallJob) for job in self.jobs):
+                near.append((3 - shard, replica))
             for device in near:
                 greet(device)
             if lines:
@@ -443,7 +479,9 @@
                 lax.fori_loop(slot * job.steps // slots, (slot + 1) * job.steps // slots, body, 0)
         for index, stage in enumerate(stages):
             if slots <= 4:
-                due = min(slots - 1, slots // 2 + index * (slots - slots // 2) // len(stages))
+                due = slots - 1
+            elif slots <= 8:
+                due = slots * 3 // 4
             else:
                 due = min(slots - 1, max(1, int(slots * (0.25 + 0.5 * index / len(stages)))))
             pl.when(slot == due)(stage)
@@ -550,6 +588,7 @@
     ]
     firsts = [sum(len(l) for l, _, _ in items[:k]) for k in range(len(items))]
     n = sum(len(l) for l, _, _ in items)
+    slots = 1 if comm.number is None else SLOTS
     if joined:
         width = items[0][1][0].shape[1]
         out_specs = [pl.BlockSpec((block, width), lambda i: (i, 0))]
@@ -562,10 +601,10 @@
         )
         step = pl.program_id(0)
         comm.enter(operands, comm_outs, scratch, step == 0)
-        width = items[0][1][0].shape[1] // SLOTS
+        width = items[0][1][0].shape[1] // slots
 
         def part(slot, carry):
-            comm.advance(step * SLOTS + slot, total * SLOTS)
+            comm.advance(step * slots + slot, total * slots)
             columns = pl.ds(pl.multiple_of(slot * width, width), width)
             for k, (left, right, transposed) in enumerate(items):
                 begin, count = steps[k]
@@ -586,7 +625,7 @@
 
             return carry
 
-        lax.fori_loop(0, SLOTS, part, 0)
+        lax.fori_loop(0, slots, part, 0)
 
         comm.finish(step == total - 1)
 
@@ -998,14 +1037,11 @@
             [lax.dynamic_slice_in_dim(blocks, n ^ me, 1, axis) for n in range(self.shard)], axis=axis
         )
 
-    def gather_small(self, own):
-        parts = [
-            own,
-            lax.ppermute(own, "shard", self.x),
-            lax.ppermute(own, "shard", self.y),
-            lax.ppermute(own, "shard", self.d),
-        ]
-        return self.reorder(jnp.stack(parts), 0)
+    def first(self, small, own):
+        padded = jnp.pad(small, (0, -small.shape[0] % 2048)).reshape(16, -1)
+        self.kernels += 1
+        smalls, rows = transfer(Comm([SmallJob(padded), GatherJob(own, 1)], self.kernels))
+        return smalls.reshape(self.shard, -1)[:, : small.shape[0]], rows
 
     def sum_small(self, values, beside):
         share = values.shape[1] // self.shard
@@ -1047,8 +1083,9 @@
     def place(self, block):
         return block
 
-    def gather_small(self, own):
-        return lax.all_gather(own, "shard", axis=0, tiled=False)
+    def first(self, small, own):
+        rows = lax.all_gather(own, "shard", axis=0, tiled=True)
+        return lax.all_gather(small, "shard", axis=0, tiled=False), rows
 
     def carry(self, compute, gathers=(), sums=(), totals=()):
         results = None if compute is None else compute(NoComm())[0]
@@ -1118,8 +1155,7 @@
     small = jnp.concatenate(
         [gain_attn, gain_ff] + [segment_ids[t, 0].astype(BF16) for t in range(trees)]
     )
-    smalls = links.gather_small(small)
-    _, (rows_0,), _, _ = links.carry(None, gathers=[(token_rows[0], 1)])
+    smalls, rows_0 = links.first(small, token_rows[0])
     gain_first = smalls[:, :share].reshape(width).astype(F32)
     gain_second = smalls[:, share : 2 * share].reshape(width).astype(F32)
     masks, tables = [], []

time: 1020 us -> 1010 us (level)
  transfers between devices with their start and end apart: 9 -> 6, of which waited for: 1 -> 1; matrix products, arithmetic and copies ran while one was open for 6% -> 6% of each run, Pallas kernels for 4% -> 0%
where the time goes in v9:
time: 1010 us; the launch traced here: 1000 us
  Pallas kernels  747 us (74%)
  matrix products  141 us (14%)
  other arithmetic  86.2 us (9%)
  local copies, waits for them, and re-layouts  19.2 us (2%)
    pallas_call x3, Pallas kernels, products(): pl.pallas_call(kernel, grid=(total,), in_specs=specs + right_specs + list...  254 us
    pallas_call x4, Pallas kernels, transfer(): pl.pallas_call(kernel, grid=(steps,), in_specs=comm.in_specs, out_specs=c...  216 us
    pallas_call x1, Pallas kernels, attention_backward(): pl.pallas_call(functools.partial(attention_backward_kernel, kv_heads, blo...  120 us
    pallas_call x2, Pallas kernels, attention_forward(): pl.pallas_call(functools.partial(attention_forward_kernel, kv_heads, bloc...  85.7 us
    pallas_call x1, Pallas kernels, feed_forward(): pl.pallas_call(kernel, grid=(steps,), in_specs=[pl.BlockSpec((rows, width...  72.4 us
    dot_general x7, matrix products, dot_nn(): lax.dot_general(left, right, (((1,), (0,)), ((), ())), preferred_element_...  67.1 us
    dot_general x5, matrix products, dot_nt(): lax.dot_general(left, right, (((1,), (1,)), ((), ())), preferred_element_...  49.6 us
    convert_element_type x3, other arithmetic, convert(): return lambda after: sync(totals[index], after)[0].astype(F32)  35.2 us
  transfers between devices with their start and end apart: 6, of which 1 were waited for; matrix products, arithmetic and copies ran while one was open for 6% of the time, Pallas kernels for 0%

profile of v9, /device:TPU:0, one launch (start us, length us, event | category | flops | bytes accessed | tf_op | source)
XLA Modules:
  0.0 1002.2 jit_solution(12007855173924804130)
XLA Ops:
  3.3 39.1 %transfer.4 = (bf16[64,128]{1,0:T(8,128)(2,1)S(1)}, bf16[1024,2048]{1,0:T(8,128)(2,1)S(1)}) custom-call(bf16[16,128]{1,0:T(8,128)(2,1)S(1)} %fusion.64.refs_0_, bf16[256,2048]{1,0:T(8,128)(2,1)S(1)} %get-tuple-element.169.refs_1_), custom_call_target="tpu_custom_call" | custom-call | tf_op jit(solution)/shard_map/transfer/pallas_call | solution.py:541
  62.0 4.9 fusion.49
  66.9 50.1 %attention_forward.2 = (bf16[1024,512]{1,0:T(8,128)(2,1)S(1)}, bf16[1024,512]{1,0:T(8,128)(2,1)S(1)}, bf16[1024,256]{1,0:T(8,128)(2,1)S(1)}, f32[1024,128]{1,0:T(8,128)S(1)}, bf16[1024,2048]{1,0:T(8,128)(2,1)S(1)}) custom-call(f32[1024,768]{1,0:T(8,128)S(1)} %fusion.72.refs_0_.refs_1_, f32[1024,768]{1,0:T(8,128)S(1)} %fusion.72.refs_0_.refs_1_, ...), custom_call_target="tpu_custom_call" | custom-call | flops 10000000000 | bytes 12000000 | tf_op jit(solution)/shard_map/attention_forward/pallas_call | solution.py:809
  121.8 5.2 fusion.73.refs_0_.refs_1_
  130.8 35.5 %attention_forward.3 = (bf16[1024,512]{1,0:T(8,128)(2,1)S(1)}, bf16[1024,512]{1,0:T(8,128)(2,1)S(1)}, bf16[1024,256]{1,0:T(8,128)(2,1)S(1)}, f32[1024,128]{1,0:T(8,128)S(1)}, f32[256,2048]{1,0:T(8,128)S(1)}) custom-call(f32[1024,768]{1,0:T(8,128)S(1)} %copy-done.16, f32[1024,768]{1,0:T(8,128)S(1)} %copy-done.16, f32[1024,128]{1,0:T(8,128)S(1)} %copy-done.6, ...), custom_call_target="tpu_custom_call" | custom-call | flops 10000000000 | bytes 12000000 | tf_op jit(solution)/shard_map/attention_forward/pallas_call | solution.py:809
  172.7 34.1 %transfer.5 = f32[256,2048]{1,0:T(8,128)S(1)} custom-call(bf16[1024,2048]{1,0:T(8,128)(2,1)} %convolution_convert_fusion.2.refs_0_), custom_call_target="tpu_custom_call" | custom-call | tf_op jit(solution)/shard_map/transfer/pallas_call | solution.py:541
  210.6 66.9 %transfer.6.refs_0_.refs_2_ = bf16[2048,2048]{1,0:T(8,128)(2,1)} custom-call(bf16[512,2048]{1,0:T(8,128)(2,1)S(1)} %pad_maximum_fusion.refs_0_), custom_call_target="tpu_custom_call" | custom-call | tf_op jit(solution)/shard_map/transfer/pallas_call | solution.py:541
  279.7 72.4 %feed_forward.1 = (bf16[2048,2048]{1,0:T(8,128)(2,1)}, bf16[2048,2048]{1,0:T(8,128)(2,1)}, bf16[2048,2048]{1,0:T(8,128)(2,1)}, bf16[2048,2048]{1,0:T(8,128)(2,1)}) custom-call(bf16[2048,2048]{1,0:T(8,128)(2,1)} %transfer.6.refs_0_.refs_2_, bf16[2048,2048]{1,0:T(8,128)(2,1)} %refs_1_.2, bf16[2048,2048]{1,0:T(8,128)(2,1)} %refs_2_.1, ...), custom_call_target="tpu_custom_call" | custom-call | flops 34359738368 | bytes 48000000 | tf_op jit(solution)/shard_map/feed_forward/pallas_call | solution.py:671
  352.0 23.9 %convolution_convert_fusion.1.refs_5_ = bf16[2048,2048]{1,0:T(8,128)(2,1)} fusion(bf16[2048,2048]{1,0:T(8,128)(2,1)} %get-tuple-element.59.refs_0_, bf16[2048,2048]{1,0:T(8,128)(2,1)} %get-tuple-element.60), kind=kOutput, calls=%fused_computation.23 | convolution fusion | flops 17184063488 | bytes 25165824 | tf_op jit(solution)/shard_map/dot_general | solution.py:35
  375.9 31.9 %fusion.7 = (bf16[2048,2048]{1,0:T(8,128)(2,1)}, bf16[2048,2048]{1,0:T(8,128)(2,1)}) fusion(bf16[2048,2048]{1,0:T(8,128)(2,1)} %get-tuple-element.62, bf16[2048,2048]{1,0:T(8,128)(2,1)} %get-tuple-element.61, bf16[2048,2048]{1,0:T(8,128)(2,1)} %get-tuple-element.60, bf16[2048,2048]{1,0:T(8,128)(2,1)} %refs_1_.3), kind=kOutput, calls=%fused_computation.10 | convolution fusion | flops 17242783744 | bytes 50331648 | tf_op jit(solution)/shard_map/dot_general | solution.py:27
  407.8 24.6 %fusion.74 = f32[2048,2048]{1,0:T(8,128)} fusion(bf16[2048,2048]{1,0:T(8,128)(2,1)} %get-tuple-element.151.refs_0_, bf16[2048,2048]{1,0:T(8,128)(2,1)} %refs_1_.2), kind=kOutput, calls=%fused_computation.179 | convolution fusion | flops 17179869184 | bytes 33554432 | tf_op jit(solution)/shard_map/dot_general | solution.py:31
  432.4 24.4 %add_convert_fusion.refs_3_.refs_4_ = bf16[2048,2048]{1,0:T(8,128)(2,1)} fusion(f32[2048,2048]{1,0:T(8,128)} %fusion.74, bf16[2048,2048]{1,0:T(8,128)(2,1)} %get-tuple-element.150.refs_1_, bf16[2048,2048]{1,0:T(8,128)(2,1)S(1)} %copy-done.60), kind=kOutput, calls=%fused_computation.11 | convolution fusion | flops 17188257792 | bytes 41943040 | tf_op jit(solution)/shard_map/dot_general | solution.py:31
  456.8 118.8 %products.3 = (bf16[2048,2048]{1,0:T(8,128)(2,1)}, bf16[2048,2048]{1,0:T(8,128)(2,1)}, f32[256,2048]{1,0:T(8,128)}, f32[256,2048]{1,0:T(8,128)}, bf16[2048,2048]{1,0:T(8,128)(2,1)}) custom-call(bf16[2048,2048]{1,0:T(8,128)(2,1)} %get-tuple-element.151.refs_0_, bf16[2048,2048]{1,0:T(8,128)(2,1)} %get-tuple-element.150.refs_1_, ...), custom_call_target="tpu_custom_call" | custom-call | flops 34359738368 | bytes 30000000 | tf_op jit(solution)/shard_map/products/pallas_call | solution.py:633
  584.1 114.9 %products.4 = (bf16[2048,2048]{1,0:T(8,128)(2,1)}, bf16[2048,2048]{1,0:T(8,128)(2,1)}, bf16[2048,2048]{1,0:T(8,128)(2,1)}) custom-call(bf16[2048,2048]{1,0:T(8,128)(2,1)} %get-tuple-element.59.refs_0_, bf16[2048,2048]{1,0:T(8,128)(2,1)} %refs_1_.3, bf16[512,2048]{1,0:T(8,128)(2,1)} %pad_maximum_fusion.2.refs_2_, bf16[2048,2048]{1,0:T(8,128)(2,1)} %get-tuple-element.65.refs_3_), custom_call_target="tpu_custom_call" | custom-call | flops 17179869184 | bytes 30000000 | tf_op jit(solution)/shard_map/products/pallas_call | solution.py:633
  699.0 5.7 fusion.40.refs_0_
  708.0 119.7 %attention_backward.1 = (bf16[2048,768]{1,0:T(8,128)(2,1)}, f32[256,2048]{1,0:T(8,128)}, f32[256,2048]{1,0:T(8,128)}, bf16[2048,2048]{1,0:T(8,128)(2,1)}) custom-call(bf16[1024,512]{1,0:T(8,128)(2,1)} %fusion.40.refs_0_, bf16[1024,512]{1,0:T(8,128)(2,1)} %copy-done.18, bf16[1024,256]{1,0:T(8,128)(2,1)} %copy-done.21, f32[1024,128]{1,0:T(8,128)} %copy-done.22, ...), custom_call_target="tpu_custom_call" | custom-call | flops 40000000000 | bytes 24000000 | tf_op jit(solution)/shard_map/attention_backward/pallas_call | solution.py:995
  827.7 19.9 %products.5.refs_2_ = bf16[1280,2048]{1,0:T(8,128)(2,1)} custom-call(bf16[1024,512]{1,0:T(8,128)(2,1)} %copy-done.13, bf16[1024,512]{1,0:T(8,128)(2,1)} %copy-done.15, bf16[2048,768]{1,0:T(8,128)(2,1)} %get-tuple-element.77.refs_2_, bf16[2048,2048]{1,0:T(8,128)(2,1)} %get-tuple-element.66.refs_3_, bf16[1024,2048]{1,0:T(8,128)(2,1)} %copy-done.37, ...), custom_call_target="tpu_custom_call" | custom-call | flops 10737418240 | bytes 30000000 | tf_op jit(solution)/shard_map/products/pallas_call | solution.py:633
  847.6 10.8 %convolution_convert_fusion.refs_0_.refs_1_ = bf16[2048,2048]{1,0:T(8,128)(2,1)} fusion(bf16[2048,768]{1,0:T(8,128)(2,1)} %get-tuple-element.77.refs_2_, bf16[768,2048]{1,0:T(8,128)(2,1)S(1)} %copy-done.44), kind=kOutput, calls=%fused_computation.22 | convolution fusion | flops 6446645248 | bytes 14680064 | tf_op jit(solution)/shard_map/dot_general | solution.py:31
  858.5 75.7 %transfer.7 = (f32[256,2048]{1,0:T(8,128)S(1)}, f32[256,2048]{1,0:T(8,128)S(1)}, bf16[1280,2048]{1,0:T(8,128)(2,1)}) custom-call(bf16[2048,2048]{1,0:T(8,128)(2,1)} %convolution_convert_fusion.refs_0_.refs_1_, bf16[2048,2048]{1,0:T(8,128)(2,1)} %convolution_convert_fusion.refs_0_.refs_1_, bf16[1280,2048]{1,0:T(8,128)(2,1)} %products.5.refs_2_), custom_call_target="tpu_custom_call" | custom-call | tf_op jit(solution)/shard_map/transfer/pallas_call | solution.py:541
  939.9 5.6 fusion.36
  951.4 4.4 slice_convert_fusion
  955.8 11.7 %convert_element_type.261 = f32[2048,2048]{1,0:T(8,128)} convert(bf16[2048,2048]{1,0:T(8,128)(2,1)} %get-tuple-element.81) | non-fusion elementwise | flops 4194304 | bytes 25165824 | tf_op jit(solution)/shard_map/convert_element_type | solution.py:1259
  970.4 11.7 %convert_element_type.262 = f32[2048,2048]{1,0:T(8,128)} convert(bf16[2048,2048]{1,0:T(8,128)(2,1)} %get-tuple-element.86) | non-fusion elementwise | flops 4194304 | bytes 25165824 | tf_op jit(solution)/shard_map/convert_element_type | solution.py:1259
  984.4 11.8 %convert_element_type.263 = f32[2048,2048]{1,0:T(8,128)} convert(bf16[2048,2048]{1,0:T(8,128)(2,1)} %get-tuple-element.89) | non-fusion elementwise | flops 4194304 | bytes 25165824 | tf_op jit(solution)/shard_map/convert_element_type | solution.py:1259
  (224 shorter events, 76.7 us)
Async XLA Ops:
  0.6 127.7 %copy-start = (bf16[512,2048]{1,0:T(8,128)(2,1)S(1)}, bf16[512,2048]{1,0:T(8,128)(2,1)}, u32[]{:S(2)}) copy-start(bf16[512,2048]{1,0:T(8,128)(2,1)} %param.18) | copy-start | bytes 6291460
  1.5 45.2 %copy-start.59 = (s32[2,1,13]{2,1,0:T(1,128)S(1)}, s32[2,1,13]{2,1,0:T(1,128)}, u32[]{:S(2)}) copy-start(s32[2,1,13]{2,1,0:T(1,128)} %param.25) | copy-start | bytes 316
  48.9 69.9 %copy-start.47 = (f32[1,4,4,128]{3,1,2,0:T(4,128)}, f32[1,4,4,128]{3,1,2,0:T(4,128)S(1)}, u32[]{:S(2)}) copy-start(f32[1,4,4,128]{3,1,2,0:T(4,128)S(1)} %copy.40) | copy-start | bytes 24580
  58.5 61.3 %copy-start.43 = (bf16[768,2048]{1,0:T(8,128)(2,1)}, bf16[768,2048]{1,0:T(8,128)(2,1)S(1)}, u32[]{:S(2)}) copy-start(bf16[768,2048]{1,0:T(8,128)(2,1)S(1)} %constant_dynamic-update-slice_fusion) | copy-start | bytes 9437188
  66.9 50.2 %copy-start.7 = (f32[1024,128]{1,0:T(8,128)}, f32[1024,128]{1,0:T(8,128)S(1)}, u32[]{:S(2)}) copy-start(f32[1024,128]{1,0:T(8,128)S(1)} %get-tuple-element.188.refs_2_.refs_4_) | copy-start | bytes 1572868
  66.9 50.2 %copy-start.8 = (f32[1024,128]{1,0:T(8,128)}, f32[1024,128]{1,0:T(8,128)S(1)}, u32[]{:S(2)}) copy-start(f32[1024,128]{1,0:T(8,128)S(1)} %get-tuple-element.189.refs_3_.refs_5_) | copy-start | bytes 1572868
  172.7 34.1 %copy-start.28 = (bf16[2,1,256,2048]{3,2,1,0:T(8,128)(2,1)S(1)}, bf16[2,1,256,2048]{3,2,1,0:T(8,128)(2,1)}, u32[]{:S(2)}) copy-start(bf16[2,1,256,2048]{3,2,1,0:T(8,128)(2,1)} %param.13) | copy-start | bytes 6291460
  210.6 66.9 %copy-start.34 = (bf16[2,1,256,2048]{3,2,1,0:T(8,128)(2,1)S(1)}, bf16[2,1,256,2048]{3,2,1,0:T(8,128)(2,1)}, u32[]{:S(2)}) copy-start(bf16[2,1,256,2048]{3,2,1,0:T(8,128)(2,1)} %param.23) | copy-start | bytes 6291460
  407.8 24.6 %copy-start.60 = (bf16[2048,2048]{1,0:T(8,128)(2,1)S(1)}, bf16[2048,2048]{1,0:T(8,128)(2,1)}, u32[]{:S(2)}) copy-start(bf16[2048,2048]{1,0:T(8,128)(2,1)} %refs_2_.1) | copy-start | bytes 25165828
  456.8 118.8 %copy-start.24 = (f32[256,2048]{1,0:T(8,128)S(1)}, f32[256,2048]{1,0:T(8,128)}, u32[]{:S(2)}) copy-start(f32[256,2048]{1,0:T(8,128)} %copy-done.23) | copy-start | bytes 6291460
  456.8 118.9 %copy-start.50 = (f32[1,4,4,128]{3,1,2,0:T(4,128)S(1)}, f32[1,4,4,128]{3,1,2,0:T(4,128)}, u32[]{:S(2)}) copy-start(f32[1,4,4,128]{3,1,2,0:T(4,128)} %copy-done.49) | copy-start | bytes 24580
  456.8 118.9 %copy-start.52 = (f32[256]{0:T(256)S(1)}, f32[256]{0:T(256)}, u32[]{:S(2)}) copy-start(f32[256]{0:T(256)} %copy-done.51) | copy-start | bytes 3076
  456.8 118.9 %copy-start.54 = (f32[256]{0:T(256)S(1)}, f32[256]{0:T(256)}, u32[]{:S(2)}) copy-start(f32[256]{0:T(256)} %copy-done.53) | copy-start | bytes 3076
  827.7 19.9 %copy-start.44 = (bf16[768,2048]{1,0:T(8,128)(2,1)S(1)}, bf16[768,2048]{1,0:T(8,128)(2,1)}, u32[]{:S(2)}) copy-start(bf16[768,2048]{1,0:T(8,128)(2,1)} %copy-done.43) | copy-start | bytes 9437188
  858.5 75.7 %copy-start.29 = (bf16[2,1,256,2048]{3,2,1,0:T(8,128)(2,1)S(1)}, bf16[2,1,256,2048]{3,2,1,0:T(8,128)(2,1)}, u32[]{:S(2)}) copy-start(bf16[2,1,256,2048]{3,2,1,0:T(8,128)(2,1)} %param.13) | copy-start | bytes 6291460
  858.5 75.7 %copy-start.48 = (f32[1,4,4,128]{3,1,2,0:T(4,128)S(1)}, f32[1,4,4,128]{3,1,2,0:T(4,128)}, u32[]{:S(2)}) copy-start(f32[1,4,4,128]{3,1,2,0:T(4,128)} %copy-done.47) | copy-start | bytes 24580
  936.2 31.3 %collective-permute-start = (f32[2,512]{1,0:T(2,128)S(1)}, f32[2,512]{1,0:T(2,128)S(1)}, u32[]{:S(2)}, u32[]{:S(2)}) collective-permute-start(f32[2,512]{1,0:T(2,128)S(1)} %bitcast.131), channel_id=1, source_target_pairs={{0,8},{8,0},{16,24},{24,16},{1,9},{9,1},{17,25},{25,17},{2,10},{10... | collective-permute-start | bytes 12296 | tf_op jit(solution)/shard_map/ppermute | solution.py:1055
  937.4 30.2 %collective-permute-start.1 = (f32[2,512]{1,0:T(2,128)S(1)}, f32[2,512]{1,0:T(2,128)S(1)}, u32[]{:S(2)}, u32[]{:S(2)}) collective-permute-start(f32[2,512]{1,0:T(2,128)S(1)} %bitcast.132), channel_id=1, source_target_pairs={{0,16},{8,24},{16,0},{24,8},{1,17},{9,25},{17,1},{25,9},{2,18},{10... | collective-permute-start | bytes 12296 | tf_op jit(solution)/shard_map/ppermute | solution.py:1055
  938.4 29.2 %collective-permute-start.2 = (f32[2,512]{1,0:T(2,128)S(1)}, f32[2,512]{1,0:T(2,128)S(1)}, u32[]{:S(2)}, u32[]{:S(2)}) collective-permute-start(f32[2,512]{1,0:T(2,128)S(1)} %bitcast.133), channel_id=1, source_target_pairs={{0,24},{8,16},{16,8},{24,0},{1,25},{9,17},{17,9},{25,1},{2,26},{10... | collective-permute-start | bytes 12296 | tf_op jit(solution)/shard_map/ppermute | solution.py:1055
  967.5 14.5 %collective-permute-start.3 = (f32[2,512]{1,0:T(2,128)S(1)}, f32[2,512]{1,0:T(2,128)S(1)}, u32[]{:S(2)}, u32[]{:S(2)}) collective-permute-start(f32[2,512]{1,0:T(2,128)S(1)} %add_add_fusion), channel_id=1, source_target_pairs={{0,1},{1,0},{2,3},{3,2},{4,5},{5,4},{6,7},{7,6},{8,9},{9,8},{10,11... | collective-permute-start | bytes 12296 | tf_op jit(solution)/shard_map/ppermute | solution.py:1055
  982.1 14.2 %collective-permute-start.4 = (f32[2,512]{1,0:T(2,128)S(1)}, f32[2,512]{1,0:T(2,128)S(1)}, u32[]{:S(2)}, u32[]{:S(2)}) collective-permute-start(f32[2,512]{1,0:T(2,128)S(1)} %add.228), channel_id=1, source_target_pairs={{0,2},{1,3},{2,0},{3,1},{4,6},{5,7},{6,4},{7,5},{8,10},{9,11},{10,... | collective-permute-start | bytes 12296 | tf_op jit(solution)/shard_map/ppermute | solution.py:1055
  984.4 15.2 %copy-start.39 = (bf16[1,256,2048]{2,1,0:T(8,128)(2,1)S(1)}, bf16[1,256,2048]{2,1,0:T(8,128)(2,1)}, u32[]{:S(2)}) copy-start(bf16[1,256,2048]{2,1,0:T(8,128)(2,1)} %get-tuple-element.159) | copy-start | bytes 3145732
  984.4 15.2 %copy-start.40 = (bf16[1,256,2048]{2,1,0:T(8,128)(2,1)S(1)}, bf16[1,256,2048]{2,1,0:T(8,128)(2,1)}, u32[]{:S(2)}) copy-start(bf16[1,256,2048]{2,1,0:T(8,128)(2,1)} %get-tuple-element.161) | copy-start | bytes 3145732
  996.3 4.9 collective-permute-start.5
  (46 other events, 191.3 us)

commit v10 on v9

--- a/solution.py
+++ b/solution.py
@@ -840,7 +840,7 @@
             jax.ShapeDtypeStruct((tree, PAIR), F32),
             *comm.out_shapes,
         ],
-        compiler_params=comm_params(comm, 40),
+        compiler_params=comm_params(comm, 58),
         cost_estimate=pl.CostEstimate(
             flops=10_000_000_000, bytes_accessed=12_000_000, transcendentals=5_000_000
         ),

time: 1010 us -> 1020 us (level)
  transfers between devices with their start and end apart: 6 -> 6, of which waited for: 1 -> 1; matrix products, arithmetic and copies ran while one was open for 6% -> 5% of each run, Pallas kernels for 0% -> 0%
where the time goes in v10:
time: 1020 us
  Pallas kernels  754 us (74%)
  matrix products  147 us (14%)
  other arithmetic  87.7 us (9%)
  local copies, waits for them, and re-layouts  18.3 us (2%)
    pallas_call x3, Pallas kernels, products(): pl.pallas_call(kernel, grid=(total,), in_specs=specs + right_specs + list...  253 us
    pallas_call x4, Pallas kernels, transfer(): pl.pallas_call(kernel, grid=(steps,), in_specs=comm.in_specs, out_specs=c...  216 us
    pallas_call x1, Pallas kernels, attention_backward(): pl.pallas_call(functools.partial(attention_backward_kernel, kv_heads, blo...  120 us
    pallas_call x2, Pallas kernels, attention_forward(): pl.pallas_call(functools.partial(attention_forward_kernel, kv_heads, bloc...  93.1 us
    pallas_call x1, Pallas kernels, feed_forward(): pl.pallas_call(kernel, grid=(steps,), in_specs=[pl.BlockSpec((rows, width...  72.3 us
    dot_general x7, matrix products, dot_nn(): lax.dot_general(left, right, (((1,), (0,)), ((), ())), preferred_element_...  71.6 us
    dot_general x5, matrix products, dot_nt(): lax.dot_general(left, right, (((1,), (1,)), ((), ())), preferred_element_...  51.2 us
    convert_element_type x3, other arithmetic, convert(): return lambda after: sync(totals[index], after)[0].astype(F32)  35.2 us
  transfers between devices with their start and end apart: 6, of which 1 were waited for; matrix products, arithmetic and copies ran while one was open for 5% of the time, Pallas kernels for 0%

profile of v10, /device:TPU:0, one launch (start us, length us, event | category | flops | bytes accessed | tf_op | source)
XLA Modules:
  0.0 1016.1 jit_solution(2189335689862723167)
XLA Ops:
  4.4 39.1 %transfer.4 = (bf16[64,128]{1,0:T(8,128)(2,1)S(1)}, bf16[1024,2048]{1,0:T(8,128)(2,1)S(1)}) custom-call(bf16[16,128]{1,0:T(8,128)(2,1)S(1)} %fusion.64.refs_0_, bf16[256,2048]{1,0:T(8,128)(2,1)S(1)} %get-tuple-element.169.refs_1_), custom_call_target="tpu_custom_call" | custom-call | tf_op jit(solution)/shard_map/transfer/pallas_call | solution.py:541
  63.6 5.5 fusion.49
  69.1 53.3 %attention_forward.2 = (bf16[1024,512]{1,0:T(8,128)(2,1)}, bf16[1024,512]{1,0:T(8,128)(2,1)}, bf16[1024,256]{1,0:T(8,128)(2,1)}, f32[1024,128]{1,0:T(8,128)}, bf16[1024,2048]{1,0:T(8,128)(2,1)}) custom-call(f32[1024,768]{1,0:T(8,128)} %fusion.72.refs_0_.refs_1_, f32[1024,768]{1,0:T(8,128)} %fusion.72.refs_0_.refs_1_, ...), custom_call_target="tpu_custom_call" | custom-call | flops 10000000000 | bytes 12000000 | tf_op jit(solution)/shard_map/attention_forward/pallas_call | solution.py:809
  135.8 5.6 convolution_convert_fusion.3.refs_6_
  141.4 39.8 %attention_forward.3 = (bf16[1024,512]{1,0:T(8,128)(2,1)}, bf16[1024,512]{1,0:T(8,128)(2,1)}, bf16[1024,256]{1,0:T(8,128)(2,1)}, f32[1024,128]{1,0:T(8,128)}, f32[256,2048]{1,0:T(8,128)}) custom-call(f32[1024,768]{1,0:T(8,128)} %fusion.73.refs_0_.refs_1_, f32[1024,768]{1,0:T(8,128)} %fusion.73.refs_0_.refs_1_, ...), custom_call_target="tpu_custom_call" | custom-call | flops 10000000000 | bytes 12000000 | tf_op jit(solution)/shard_map/attention_forward/pallas_call | solution.py:809
  181.2 5.6 convolution_convert_fusion.2.refs_0_
  186.8 34.1 %transfer.5 = f32[256,2048]{1,0:T(8,128)S(1)} custom-call(bf16[1024,2048]{1,0:T(8,128)(2,1)} %convolution_convert_fusion.2.refs_0_), custom_call_target="tpu_custom_call" | custom-call | tf_op jit(solution)/shard_map/transfer/pallas_call | solution.py:541
  224.7 66.9 %transfer.6.refs_0_.refs_2_ = bf16[2048,2048]{1,0:T(8,128)(2,1)} custom-call(bf16[512,2048]{1,0:T(8,128)(2,1)S(1)} %pad_maximum_fusion.refs_0_), custom_call_target="tpu_custom_call" | custom-call | tf_op jit(solution)/shard_map/transfer/pallas_call | solution.py:541
  293.7 72.3 %feed_forward.1 = (bf16[2048,2048]{1,0:T(8,128)(2,1)}, bf16[2048,2048]{1,0:T(8,128)(2,1)}, bf16[2048,2048]{1,0:T(8,128)(2,1)}, bf16[2048,2048]{1,0:T(8,128)(2,1)}) custom-call(bf16[2048,2048]{1,0:T(8,128)(2,1)} %transfer.6.refs_0_.refs_2_, bf16[2048,2048]{1,0:T(8,128)(2,1)} %refs_1_.2, bf16[2048,2048]{1,0:T(8,128)(2,1)} %refs_2_.1, ...), custom_call_target="tpu_custom_call" | custom-call | flops 34359738368 | bytes 48000000 | tf_op jit(solution)/shard_map/feed_forward/pallas_call | solution.py:671
  366.0 23.9 %convolution_convert_fusion.1.refs_5_ = bf16[2048,2048]{1,0:T(8,128)(2,1)} fusion(bf16[2048,2048]{1,0:T(8,128)(2,1)} %get-tuple-element.59.refs_0_, bf16[2048,2048]{1,0:T(8,128)(2,1)} %get-tuple-element.60), kind=kOutput, calls=%fused_computation.23 | convolution fusion | flops 17184063488 | bytes 25165824 | tf_op jit(solution)/shard_map/dot_general | solution.py:35
  389.9 31.9 %fusion.7 = (bf16[2048,2048]{1,0:T(8,128)(2,1)}, bf16[2048,2048]{1,0:T(8,128)(2,1)}) fusion(bf16[2048,2048]{1,0:T(8,128)(2,1)} %get-tuple-element.62, bf16[2048,2048]{1,0:T(8,128)(2,1)} %get-tuple-element.61, bf16[2048,2048]{1,0:T(8,128)(2,1)} %get-tuple-element.60, bf16[2048,2048]{1,0:T(8,128)(2,1)} %refs_1_.3), kind=kOutput, calls=%fused_computation.10 | convolution fusion | flops 17242783744 | bytes 50331648 | tf_op jit(solution)/shard_map/dot_general | solution.py:27
  421.8 24.6 %fusion.74 = f32[2048,2048]{1,0:T(8,128)} fusion(bf16[2048,2048]{1,0:T(8,128)(2,1)} %get-tuple-element.151.refs_0_, bf16[2048,2048]{1,0:T(8,128)(2,1)} %refs_1_.2), kind=kOutput, calls=%fused_computation.179 | convolution fusion | flops 17179869184 | bytes 33554432 | tf_op jit(solution)/shard_map/dot_general | solution.py:31
  446.4 24.4 %add_convert_fusion.refs_3_.refs_4_ = bf16[2048,2048]{1,0:T(8,128)(2,1)} fusion(f32[2048,2048]{1,0:T(8,128)} %fusion.74, bf16[2048,2048]{1,0:T(8,128)(2,1)} %get-tuple-element.150.refs_1_, bf16[2048,2048]{1,0:T(8,128)(2,1)S(1)} %copy-done.44), kind=kOutput, calls=%fused_computation.11 | convolution fusion | flops 17188257792 | bytes 41943040 | tf_op jit(solution)/shard_map/dot_general | solution.py:31
  470.8 118.7 %products.3 = (bf16[2048,2048]{1,0:T(8,128)(2,1)}, bf16[2048,2048]{1,0:T(8,128)(2,1)}, f32[256,2048]{1,0:T(8,128)}, f32[256,2048]{1,0:T(8,128)}, bf16[2048,2048]{1,0:T(8,128)(2,1)}) custom-call(bf16[2048,2048]{1,0:T(8,128)(2,1)} %get-tuple-element.151.refs_0_, bf16[2048,2048]{1,0:T(8,128)(2,1)} %get-tuple-element.150.refs_1_, ...), custom_call_target="tpu_custom_call" | custom-call | flops 34359738368 | bytes 30000000 | tf_op jit(solution)/shard_map/products/pallas_call | solution.py:633
  598.0 114.8 %products.4 = (bf16[2048,2048]{1,0:T(8,128)(2,1)}, bf16[2048,2048]{1,0:T(8,128)(2,1)}, bf16[2048,2048]{1,0:T(8,128)(2,1)}) custom-call(bf16[2048,2048]{1,0:T(8,128)(2,1)} %get-tuple-element.59.refs_0_, bf16[2048,2048]{1,0:T(8,128)(2,1)} %refs_1_.3, bf16[512,2048]{1,0:T(8,128)(2,1)} %pad_maximum_fusion.2.refs_2_, bf16[2048,2048]{1,0:T(8,128)(2,1)} %get-tuple-element.65.refs_3_), custom_call_target="tpu_custom_call" | custom-call | flops 17179869184 | bytes 30000000 | tf_op jit(solution)/shard_map/products/pallas_call | solution.py:633
  712.8 5.7 fusion.40.refs_0_
  721.8 119.7 %attention_backward.1 = (bf16[2048,768]{1,0:T(8,128)(2,1)}, f32[256,2048]{1,0:T(8,128)}, f32[256,2048]{1,0:T(8,128)}, bf16[2048,2048]{1,0:T(8,128)(2,1)}) custom-call(bf16[1024,512]{1,0:T(8,128)(2,1)} %fusion.40.refs_0_, bf16[1024,512]{1,0:T(8,128)(2,1)} %get-tuple-element.67.refs_1_, bf16[1024,256]{1,0:T(8,128)(2,1)} %get-tuple-element.68.refs_2_, ...), custom_call_target="tpu_custom_call" | custom-call | flops 40000000000 | bytes 24000000 | tf_op jit(solution)/shard_map/attention_backward/pallas_call | solution.py:995
  841.6 19.8 %products.5.refs_2_ = bf16[1280,2048]{1,0:T(8,128)(2,1)} custom-call(bf16[1024,512]{1,0:T(8,128)(2,1)} %get-tuple-element.56.refs_0_, bf16[1024,512]{1,0:T(8,128)(2,1)} %get-tuple-element.58.refs_1_, bf16[2048,768]{1,0:T(8,128)(2,1)} %get-tuple-element.77.refs_2_, bf16[2048,2048]{1,0:T(8,128)(2,1)} %get-tuple-element.66.refs_3_, ...), custom_call_target="tpu_custom_call" | custom-call | flops 10737418240 | bytes 30000000 | tf_op jit(solution)/shard_map/products/pallas_call | solution.py:633
  861.4 10.8 %convolution_convert_fusion.refs_0_.refs_1_ = bf16[2048,2048]{1,0:T(8,128)(2,1)} fusion(bf16[2048,768]{1,0:T(8,128)(2,1)} %get-tuple-element.77.refs_2_, bf16[768,2048]{1,0:T(8,128)(2,1)S(1)} %copy-done.28), kind=kOutput, calls=%fused_computation.22 | convolution fusion | flops 6446645248 | bytes 14680064 | tf_op jit(solution)/shard_map/dot_general | solution.py:31
  872.3 75.7 %transfer.7 = (f32[256,2048]{1,0:T(8,128)S(1)}, f32[256,2048]{1,0:T(8,128)S(1)}, bf16[1280,2048]{1,0:T(8,128)(2,1)}) custom-call(bf16[2048,2048]{1,0:T(8,128)(2,1)} %convolution_convert_fusion.refs_0_.refs_1_, bf16[2048,2048]{1,0:T(8,128)(2,1)} %convolution_convert_fusion.refs_0_.refs_1_, bf16[1280,2048]{1,0:T(8,128)(2,1)} %products.5.refs_2_), custom_call_target="tpu_custom_call" | custom-call | tf_op jit(solution)/shard_map/transfer/pallas_call | solution.py:541
  953.8 5.5 fusion.36
  969.7 11.7 %convert_element_type.261 = f32[2048,2048]{1,0:T(8,128)} convert(bf16[2048,2048]{1,0:T(8,128)(2,1)} %get-tuple-element.81) | non-fusion elementwise | flops 4194304 | bytes 25165824 | tf_op jit(solution)/shard_map/convert_element_type | solution.py:1259
  984.3 11.7 %convert_element_type.262 = f32[2048,2048]{1,0:T(8,128)} convert(bf16[2048,2048]{1,0:T(8,128)(2,1)} %get-tuple-element.86) | non-fusion elementwise | flops 4194304 | bytes 25165824 | tf_op jit(solution)/shard_map/convert_element_type | solution.py:1259
  998.3 11.8 %convert_element_type.263 = f32[2048,2048]{1,0:T(8,128)} convert(bf16[2048,2048]{1,0:T(8,128)(2,1)} %get-tuple-element.89) | non-fusion elementwise | flops 4194304 | bytes 25165824 | tf_op jit(solution)/shard_map/convert_element_type | solution.py:1259
  (192 shorter events, 81.4 us)
Async XLA Ops:
  0.6 135.2 %copy-start = (bf16[512,2048]{1,0:T(8,128)(2,1)S(1)}, bf16[512,2048]{1,0:T(8,128)(2,1)}, u32[]{:S(2)}) copy-start(bf16[512,2048]{1,0:T(8,128)(2,1)} %param.18) | copy-start | bytes 6291460
  1.5 44.8 %copy-start.43 = (s32[2,1,13]{2,1,0:T(1,128)S(1)}, s32[2,1,13]{2,1,0:T(1,128)}, u32[]{:S(2)}) copy-start(s32[2,1,13]{2,1,0:T(1,128)} %param.25) | copy-start | bytes 316
  48.5 77.2 %copy-start.31 = (f32[1,4,4,128]{3,1,2,0:T(4,128)}, f32[1,4,4,128]{3,1,2,0:T(4,128)S(1)}, u32[]{:S(2)}) copy-start(f32[1,4,4,128]{3,1,2,0:T(4,128)S(1)} %copy.40) | copy-start | bytes 24580
  58.4 68.5 %copy-start.27 = (bf16[768,2048]{1,0:T(8,128)(2,1)}, bf16[768,2048]{1,0:T(8,128)(2,1)S(1)}, u32[]{:S(2)}) copy-start(bf16[768,2048]{1,0:T(8,128)(2,1)S(1)} %constant_dynamic-update-slice_fusion) | copy-start | bytes 9437188
  186.7 34.1 %copy-start.10 = (bf16[2,1,256,2048]{3,2,1,0:T(8,128)(2,1)S(1)}, bf16[2,1,256,2048]{3,2,1,0:T(8,128)(2,1)}, u32[]{:S(2)}) copy-start(bf16[2,1,256,2048]{3,2,1,0:T(8,128)(2,1)} %param.13) | copy-start | bytes 6291460
  186.8 34.1 %copy-start.24 = (f32[256,2048]{1,0:T(8,128)S(1)}, f32[256,2048]{1,0:T(8,128)}, u32[]{:S(2)}) copy-start(f32[256,2048]{1,0:T(8,128)} %get-tuple-element.57) | copy-start | bytes 6291460
  224.7 66.9 %copy-start.16 = (bf16[2,1,256,2048]{3,2,1,0:T(8,128)(2,1)S(1)}, bf16[2,1,256,2048]{3,2,1,0:T(8,128)(2,1)}, u32[]{:S(2)}) copy-start(bf16[2,1,256,2048]{3,2,1,0:T(8,128)(2,1)} %param.23) | copy-start | bytes 6291460
  421.8 24.6 %copy-start.44 = (bf16[2048,2048]{1,0:T(8,128)(2,1)S(1)}, bf16[2048,2048]{1,0:T(8,128)(2,1)}, u32[]{:S(2)}) copy-start(bf16[2048,2048]{1,0:T(8,128)(2,1)} %refs_2_.1) | copy-start | bytes 25165828
  470.7 118.7 %copy-start.6 = (f32[256,2048]{1,0:T(8,128)S(1)}, f32[256,2048]{1,0:T(8,128)}, u32[]{:S(2)}) copy-start(f32[256,2048]{1,0:T(8,128)} %copy-done.5) | copy-start | bytes 6291460
  470.7 118.8 %copy-start.34 = (f32[1,4,4,128]{3,1,2,0:T(4,128)S(1)}, f32[1,4,4,128]{3,1,2,0:T(4,128)}, u32[]{:S(2)}) copy-start(f32[1,4,4,128]{3,1,2,0:T(4,128)} %copy-done.33) | copy-start | bytes 24580
  470.7 118.8 %copy-start.36 = (f32[256]{0:T(256)S(1)}, f32[256]{0:T(256)}, u32[]{:S(2)}) copy-start(f32[256]{0:T(256)} %copy-done.35) | copy-start | bytes 3076
  470.7 118.8 %copy-start.38 = (f32[256]{0:T(256)S(1)}, f32[256]{0:T(256)}, u32[]{:S(2)}) copy-start(f32[256]{0:T(256)} %copy-done.37) | copy-start | bytes 3076
  841.6 19.9 %copy-start.28 = (bf16[768,2048]{1,0:T(8,128)(2,1)S(1)}, bf16[768,2048]{1,0:T(8,128)(2,1)}, u32[]{:S(2)}) copy-start(bf16[768,2048]{1,0:T(8,128)(2,1)} %copy-done.27) | copy-start | bytes 9437188
  872.3 75.8 %copy-start.11 = (bf16[2,1,256,2048]{3,2,1,0:T(8,128)(2,1)S(1)}, bf16[2,1,256,2048]{3,2,1,0:T(8,128)(2,1)}, u32[]{:S(2)}) copy-start(bf16[2,1,256,2048]{3,2,1,0:T(8,128)(2,1)} %param.13) | copy-start | bytes 6291460
  872.3 75.8 %copy-start.32 = (f32[1,4,4,128]{3,1,2,0:T(4,128)S(1)}, f32[1,4,4,128]{3,1,2,0:T(4,128)}, u32[]{:S(2)}) copy-start(f32[1,4,4,128]{3,1,2,0:T(4,128)} %copy-done.31) | copy-start | bytes 24580
  950.1 31.3 %collective-permute-start = (f32[2,512]{1,0:T(2,128)S(1)}, f32[2,512]{1,0:T(2,128)S(1)}, u32[]{:S(2)}, u32[]{:S(2)}) collective-permute-start(f32[2,512]{1,0:T(2,128)S(1)} %bitcast.131), channel_id=1, source_target_pairs={{0,8},{8,0},{16,24},{24,16},{1,9},{9,1},{17,25},{25,17},{2,10},{10... | collective-permute-start | bytes 12296 | tf_op jit(solution)/shard_map/ppermute | solution.py:1055
  951.2 30.2 %collective-permute-start.1 = (f32[2,512]{1,0:T(2,128)S(1)}, f32[2,512]{1,0:T(2,128)S(1)}, u32[]{:S(2)}, u32[]{:S(2)}) collective-permute-start(f32[2,512]{1,0:T(2,128)S(1)} %bitcast.132), channel_id=1, source_target_pairs={{0,16},{8,24},{16,0},{24,8},{1,17},{9,25},{17,1},{25,9},{2,18},{10... | collective-permute-start | bytes 12296 | tf_op jit(solution)/shard_map/ppermute | solution.py:1055
  952.2 29.2 %collective-permute-start.2 = (f32[2,512]{1,0:T(2,128)S(1)}, f32[2,512]{1,0:T(2,128)S(1)}, u32[]{:S(2)}, u32[]{:S(2)}) collective-permute-start(f32[2,512]{1,0:T(2,128)S(1)} %bitcast.133), channel_id=1, source_target_pairs={{0,24},{8,16},{16,8},{24,0},{1,25},{9,17},{17,9},{25,1},{2,26},{10... | collective-permute-start | bytes 12296 | tf_op jit(solution)/shard_map/ppermute | solution.py:1055
  953.7 11.5 %slice-start = ((s8[5242880]{0:T(1024)(128)(4,1)}), s8[4194304]{0:T(1024)(128)(4,1)S(1)}, s32[]{:S(2)}) async-start(s8[5242880]{0:T(1024)(128)(4,1)} %bitcast.111), calls=%async_computation | async-start | bytes 8388608
  981.4 14.5 %collective-permute-start.3 = (f32[2,512]{1,0:T(2,128)S(1)}, f32[2,512]{1,0:T(2,128)S(1)}, u32[]{:S(2)}, u32[]{:S(2)}) collective-permute-start(f32[2,512]{1,0:T(2,128)S(1)} %add_add_fusion), channel_id=1, source_target_pairs={{0,1},{1,0},{2,3},{3,2},{4,5},{5,4},{6,7},{7,6},{8,9},{9,8},{10,11... | collective-permute-start | bytes 12296 | tf_op jit(solution)/shard_map/ppermute | solution.py:1055
  995.9 14.2 %collective-permute-start.4 = (f32[2,512]{1,0:T(2,128)S(1)}, f32[2,512]{1,0:T(2,128)S(1)}, u32[]{:S(2)}, u32[]{:S(2)}) collective-permute-start(f32[2,512]{1,0:T(2,128)S(1)} %add.228), channel_id=1, source_target_pairs={{0,2},{1,3},{2,0},{3,1},{4,6},{5,7},{6,4},{7,5},{8,10},{9,11},{10,... | collective-permute-start | bytes 12296 | tf_op jit(solution)/shard_map/ppermute | solution.py:1055
  998.3 15.2 %copy-start.22 = (bf16[1,256,2048]{2,1,0:T(8,128)(2,1)S(1)}, bf16[1,256,2048]{2,1,0:T(8,128)(2,1)}, u32[]{:S(2)}) copy-start(bf16[1,256,2048]{2,1,0:T(8,128)(2,1)} %get-tuple-element.159) | copy-start | bytes 3145732
  998.3 15.2 %copy-start.23 = (bf16[1,256,2048]{2,1,0:T(8,128)(2,1)S(1)}, bf16[1,256,2048]{2,1,0:T(8,128)(2,1)}, u32[]{:S(2)}) copy-start(bf16[1,256,2048]{2,1,0:T(8,128)(2,1)} %get-tuple-element.161) | copy-start | bytes 3145732
  1010.1 4.9 collective-permute-start.5
  (30 other events, 125.9 us)
